TPU v7x, 32 devices: a whole 2x2x4 slice. The times are simulated.
32 devices in a mesh: groups: 2 (over x), gx: 16 (over z, y, core).
Axes of the slice: x: 2, y: 2, z: 4, core: 2. Of those that a mesh axis runs over, the one named last changes fastest.
Arguments:
- inputs: bfloat16 [2, 32, 12288], P(None, 'groups', 'gx'), parts along dimension 1
- norm_gain: float32 [12288], replicated, may hold values from 0.1 to 1.9
- qkv_weight: bfloat16 [12288, 18432], P(None, 'gx'), may hold values from -0.0546875 to 0.0546875
- head_lambda: float32 [24], replicated, may hold values from 0.2 to 0.8
- head_gain: float32 [6144], replicated, may hold values from 0.1 to 1.9
- out_weight: bfloat16 [6144, 12288], P(None, 'gx'), may hold values from -0.078125 to 0.078125
- key_one_pages: bfloat16 [192, 16, 3072], P(('groups', 'gx')), parts along dimension 0, may hold values from -110 to 110
- key_two_pages: bfloat16 [192, 16, 3072], P(('groups', 'gx')), parts along dimension 0, may hold values from -110 to 110
- value_pages: bfloat16 [192, 16, 6144], P(('groups', 'gx')), parts along dimension 0, may hold values from -6 to 6
- page_table: int32 [32, 6], P(('groups', 'gx')), parts along dimension 0, may hold values from 0 to 5, as said below
- context_len: int32 [32], P(('groups', 'gx')), parts along dimension 0, may hold values from 1 to 96, as said below
- positions: int32 [32], P(('groups', 'gx')), parts along dimension 0, may hold values from 1 to 4191, as said below
Outputs:
- outputs: bfloat16 [2, 32, 12288], P(None, 'groups', 'gx'), parts along dimension 1
There are 2 independent parts, one for each index of `groups`. A program takes and returns all parts, laid end to end along the dimension named above; an argument that names none is the same for every part. Nothing has to cross between parts.
Inputs may be any that keep to these rules, and one draw needn't show every extreme that they name: `page_table`: each device's 1 x 6 entries are all its 6 pages, each once, counted from the start of that device's block of the pools. `context_len`: some sequence fills all of its pages. `positions`: at least the sequence's context length.
All inputs are finite; a program needn't handle non-finite values.
Results may differ from a plain program's by a relative error of at most 0.0077.
Values may be sent and summed in bfloat16 or wider, within the bound.
No kernel may reach another device: no remote copies, remote signals or barrier semaphores. Data moves between devices by JAX's collectives and lax.ppermute only.
A program may use at most 128 MiB of HBM per device.

v0:
```python
import math

import jax
import jax.numpy as jnp
from jax import lax
from jax.sharding import PartitionSpec as P

H = 24
HD = 128


epsilon = 1e-05
rope_base = 10000.0


def rotary(vectors, places):
    half_dim = vectors.shape[-1] // 2
    frequency = jnp.exp(
        -math.log(rope_base) * 2.0 * jnp.arange(half_dim, dtype=jnp.float32) / vectors.shape[-1]
    )
    angles = places[:, None] * frequency[None, :]
    cosine = jnp.cos(angles)[:, None, :]
    sine_values = jnp.sin(angles)[:, None, :]
    lower_half = vectors[..., :half_dim]
    upper_half = vectors[..., half_dim:]
    return jnp.concatenate(
        [
            lower_half * cosine - upper_half * sine_values,
            upper_half * cosine + lower_half * sine_values,
        ],
        axis=-1,
    )


def split_heads(qkv_rows):
    head_width = H * HD
    row_count = qkv_rows.shape[0]
    query_one = qkv_rows[:, :head_width].reshape(row_count, H, HD)
    query_two = qkv_rows[:, head_width : 2 * head_width].reshape(row_count, H, HD)
    key_one = qkv_rows[:, 2 * head_width : 3 * head_width].reshape(row_count, H, HD)
    key_two = qkv_rows[:, 3 * head_width : 4 * head_width].reshape(row_count, H, HD)
    value_rows = qkv_rows[:, 4 * head_width :].reshape(row_count, H, 2 * HD)
    return (query_one, query_two, key_one, key_two, value_rows)


def attend(step_rows, step_index, fresh, cached, allowed, starts, head_lambda, head_gain):
    query_one, query_two, key_one, key_two, value_rows = split_heads(step_rows)
    places = (starts + step_index).astype(jnp.float32)
    query_one = rotary(query_one.astype(jnp.float32), places).astype(jnp.bfloat16)
    query_two = rotary(query_two.astype(jnp.float32), places).astype(jnp.bfloat16)
    key_one = rotary(key_one.astype(jnp.float32), places).astype(jnp.bfloat16)
    key_two = rotary(key_two.astype(jnp.float32), places).astype(jnp.bfloat16)
    fresh.append((key_one, key_two, value_rows))
    fresh_one = jnp.stack([entry[0] for entry in fresh])
    fresh_two = jnp.stack([entry[1] for entry in fresh])
    fresh_value = jnp.stack([entry[2] for entry in fresh])
    capacity = cached[0].shape[1]
    newest = fresh_one.shape[0]
    allowed_all = jnp.concatenate(
        [allowed, jnp.ones((allowed.shape[0], newest), dtype=bool)], axis=1
    )[:, None, :]
    factor = 1.0 / math.sqrt(HD)

    def softmax_map(query, cache_keys, new_keys):
        older = jnp.einsum("shd,sjhd->shj", query, cache_keys, preferred_element_type=jnp.float32)
        newer = jnp.einsum("shd,eshd->she", query, new_keys, preferred_element_type=jnp.float32)
        scores = jnp.concatenate([older, newer], axis=-1) * factor
        return jax.nn.softmax(jnp.where(allowed_all, scores, -jnp.inf), axis=-1)

    first_map = softmax_map(query_one, cached[0], fresh_one)
    second_map = softmax_map(query_two, cached[1], fresh_two)
    mix = (first_map - head_lambda[None, :, None] * second_map).astype(jnp.bfloat16)
    mixed_out = jnp.einsum(
        "shj,sjhf->shf", mix[..., :capacity], cached[2], preferred_element_type=jnp.float32
    )
    mixed_out = mixed_out + jnp.einsum(
        "she,eshf->shf", mix[..., capacity:], fresh_value, preferred_element_type=jnp.float32
    )
    norms = lax.rsqrt(jnp.mean(mixed_out * mixed_out, axis=-1, keepdims=True) + epsilon)
    grouped = (mixed_out * norms * head_gain.reshape(H, 2 * HD)).astype(jnp.bfloat16)
    return grouped.reshape(grouped.shape[0], H * 2 * HD)


def project(step_inputs, norm_gain, qkv_weight):
    whole = lax.all_gather(step_inputs, "gx", axis=2, tiled=True)
    values = whole.astype(jnp.float32)
    factor_rows = lax.rsqrt(jnp.mean(values * values, axis=-1, keepdims=True) + epsilon)
    normed = (values * factor_rows * norm_gain).astype(jnp.bfloat16)
    return jnp.einsum("sbd,dc->sbc", normed, qkv_weight, preferred_element_type=jnp.float32)


def local(
    inputs,
    norm_gain,
    qkv_weight,
    head_lambda,
    head_gain,
    out_weight,
    key_one_pages,
    key_two_pages,
    value_pages,
    page_table,
    context_len,
    positions,
):
    sequences = page_table.shape[0]
    capacity = page_table.shape[1] * key_one_pages.shape[1]
    cached = tuple(
        (
            page_pool[page_table].reshape(sequences, capacity, H, -1)
            for page_pool in (key_one_pages, key_two_pages, value_pages)
        )
    )
    allowed = jnp.arange(capacity, dtype=jnp.int32)[None, :] < context_len[:, None]
    groups_in = [inputs[step_index : step_index + 1] for step_index in range(inputs.shape[0])]
    fresh = []
    produced = []
    for step_inputs in groups_in:
        projected = project(step_inputs, norm_gain, qkv_weight).astype(jnp.bfloat16)
        received = lax.all_to_all(projected, "gx", split_axis=1, concat_axis=2, tiled=True)
        step_index = len(fresh)
        attended_rows = [
            attend(
                received[0], step_index, fresh, cached, allowed, positions, head_lambda, head_gain
            )
        ]
        attended = jnp.stack(attended_rows)
        branch = jnp.einsum(
            "sbf,fd->sbd",
            lax.all_gather(attended, "gx", axis=1, tiled=True),
            out_weight,
            preferred_element_type=jnp.float32,
        )
        produced.append((step_inputs.astype(jnp.float32) + branch).astype(jnp.bfloat16))
    return jnp.concatenate(produced, axis=0)


def solution(mesh):
    placed = (
        P(None, "groups", "gx"),
        P(),
        P(None, "gx"),
        P(),
        P(),
        P(None, "gx"),
        P(("groups", "gx"), None, None),
        P(("groups", "gx"), None, None),
        P(("groups", "gx"), None, None),
        P(("groups", "gx"), None),
        P(("groups", "gx")),
        P(("groups", "gx")),
    )
    return jax.shard_map(
        local, mesh=mesh, in_specs=placed, out_specs=P(None, "groups", "gx"), check_vma=False
    )
```

profile of v0, /device:TPU:0, one launch (start us, length us, event | category | flops | bytes accessed | tf_op | source)
XLA Modules:
  0.0 174.0 jit_solution(11627546530046853365)
XLA Ops:
  0.9 24.1 %all_gather.12 = bf16[1,16,12288]{2,1,0:T(8,128)(2,1)S(1)} all-gather(bf16[1,16,768]{2,1,0:T(8,128)(2,1)S(1)} %get-tuple-element.21), channel_id=1, replica_groups=mesh['groups'=2,'gx'=16] {'gx'}, dimensions={2}, use_global_device_ids=true | all-gather | bytes 417792 | tf_op jit(solution)/shard_map/all_gather | solution.py:85
  25.2 11.1 %fusion = bf16[1,16,1152]{2,1,0:T(8,128)(2,1)S(1)} fusion(bf16[12288,1152]{1,0:T(8,128)(2,1)} %param.14, bf16[1,16,12288]{2,1,0:T(8,128)(2,1)S(1)} %all_gather.12, f32[12288]{0:T(1024)} %param.13, f32[16]{0:T(128)S(1)} %add_rsqrt_fusion.3), kind=kOutput, calls=%fused_computation.5 | convolution fusion | flops 453789696 | bytes 28790848 | tf_op jit(solution)/shard_map/sbd,dc->sbc/dot_general | solution.py:89
  38.4 4.1 %all-to-all-start = ((bf16[16,2,576]{2,1,0:T(2,128)(2,1)}), bf16[16,2,576]{2,1,0:T(2,128)(2,1)}, u32[]{:S(2)}, u32[]{:S(2)}) async-start(bf16[16,2,576]{2,1,0:T(2,128)(2,1)} %reshape.1540), calls=%async_computation | async-start | bytes 81920 | tf_op jit(solution)/shard_map/all_to_all | solution.py:120
  46.3 22.7 %all_gather.14 = bf16[1,16,12288]{2,1,0:T(8,128)(2,1)S(1)} all-gather(bf16[1,16,768]{2,1,0:T(8,128)(2,1)S(1)} %get-tuple-element.22), channel_id=1, replica_groups=mesh['groups'=2,'gx'=16] {'gx'}, dimensions={2}, use_global_device_ids=true | all-gather | bytes 417792 | tf_op jit(solution)/shard_map/all_gather | solution.py:85
  69.3 11.1 %fusion.1 = bf16[1,16,1152]{2,1,0:T(8,128)(2,1)S(1)} fusion(bf16[12288,1152]{1,0:T(8,128)(2,1)} %param.14, bf16[1,16,12288]{2,1,0:T(8,128)(2,1)S(1)} %all_gather.14, f32[16]{0:T(128)S(1)} %add_rsqrt_fusion.1, f32[12288]{0:T(1024)S(1)} %copy-done.5), kind=kOutput, calls=%fused_computation.6 | convolution fusion | flops 453789696 | bytes 28790848 | tf_op jit(solution)/shard_map/sbd,dc->sbc/dot_general | solution.py:89
  86.4 4.1 %all-to-all-start.1 = ((bf16[16,2,576]{2,1,0:T(2,128)(2,1)}), bf16[16,2,576]{2,1,0:T(2,128)(2,1)}, u32[]{:S(2)}, u32[]{:S(2)}) async-start(bf16[16,2,576]{2,1,0:T(2,128)(2,1)} %reshape.1538), calls=%async_computation.1 | async-start | bytes 81920 | tf_op jit(solution)/shard_map/all_to_all | solution.py:120
  90.6 1.5 reshape.1541
  92.1 1.5 slice_reduce_fusion.1
  93.6 1.4 slice_convert_fusion.5
  95.0 1.4 convert_reduce_fusion
  97.3 1.5 reshape.1539
  98.8 1.4 slice_reduce_fusion
  100.2 1.4 slice_convert_fusion.1
  101.6 1.5 fusion.62
  104.5 1.3 copy.21
  105.8 1.4 fusion.72
  107.2 1.5 fusion.42
  108.6 1.3 copy.22
  110.0 1.5 fusion.18
  114.6 1.3 fusion.68
  125.6 21.8 %all_gather.15 = bf16[1,16,6144]{2,0,1:T(2,128)(2,1)S(1)} all-gather(bf16[1,1,6144]{2,0,1:T(2,128)(2,1)S(1)} %stack_reshape.16), channel_id=1, replica_groups=mesh['groups'=2,'gx'=16] {'gx'}, dimensions={1}, use_global_device_ids=true | all-gather | bytes 208896 | tf_op jit(solution)/shard_map/all_gather | solution.py:130
  147.4 18.5 %all_gather.13 = bf16[1,16,6144]{2,0,1:T(2,128)(2,1)S(1)} all-gather(bf16[1,1,6144]{2,0,1:T(2,128)(2,1)S(1)} %stack_reshape.13), channel_id=1, replica_groups=mesh['groups'=2,'gx'=16] {'gx'}, dimensions={1}, use_global_device_ids=true | all-gather | bytes 208896 | tf_op jit(solution)/shard_map/all_gather | solution.py:130
  165.9 5.2 %fusion.5 = bf16[1,16,768]{2,1,0:T(8,128)(2,1)S(1)} fusion(bf16[6144,768]{1,0:T(8,128)(2,1)} %param.17, bf16[1,16,6144]{2,0,1:T(2,128)(2,1)S(1)} %all_gather.15, bf16[2,16,768]{2,1,0:T(8,128)(2,1)S(1)} %copy-done.6), kind=kOutput, calls=%fused_computation.12 | convolution fusion | flops 151031808 | bytes 9682944 | tf_op jit(solution)/shard_map/sbf,fd->sbd/dot_general | solution.py:128
  172.0 1.4 fusion.4
  (129 shorter events, 28.2 us)
Async XLA Ops:
  0.0 84.9 %copy-start = (bf16[6,16,6144]{2,1,0:T(8,128)(2,1)S(1)}, bf16[6,16,6144]{2,1,0:T(8,128)(2,1)}, u32[]{:S(2)}) copy-start(bf16[6,16,6144]{2,1,0:T(8,128)(2,1)} %param.20) | copy-start | bytes 3538948
  25.2 18.7 %copy-start.24 = (s32[1,6]{1,0:T(1,128)S(1)}, s32[1,6]{1,0:T(1,128)}, u32[]{:S(2)}) copy-start(s32[1,6]{1,0:T(1,128)} %param.21) | copy-start | bytes 76
  25.2 20.5 %copy-start.20 = (f32[6144]{0:T(1024)S(1)}, f32[6144]{0:T(1024)}, u32[]{:S(2)}) copy-start(f32[6144]{0:T(1024)} %param.16) | copy-start | bytes 73732
  36.4 32.9 %copy-start.5 = (f32[12288]{0:T(1024)S(1)}, f32[12288]{0:T(1024)}, u32[]{:S(2)}) copy-start(f32[12288]{0:T(1024)} %param.13) | copy-start | bytes 147460
  38.4 48.0 %all-to-all-start = ((bf16[16,2,576]{2,1,0:T(2,128)(2,1)}), bf16[16,2,576]{2,1,0:T(2,128)(2,1)}, u32[]{:S(2)}, u32[]{:S(2)}) async-start(bf16[16,2,576]{2,1,0:T(2,128)(2,1)} %reshape.1540), calls=%async_computation | async-start | bytes 81920 | tf_op jit(solution)/shard_map/all_to_all | solution.py:120
  69.3 12.7 %copy-start.1 = (bf16[6,16,3072]{2,1,0:T(8,128)(2,1)S(1)}, bf16[6,16,3072]{2,1,0:T(8,128)(2,1)}, u32[]{:S(2)}) copy-start(bf16[6,16,3072]{2,1,0:T(8,128)(2,1)} %param.19) | copy-start | bytes 1769476
  85.8 25.7 %copy-start.3 = (bf16[12,8,24,128]{3,2,1,0:T(8,128)(2,1)S(1)}, bf16[12,8,24,128]{3,2,1,0:T(8,128)(2,1)}, u32[]{:S(2)}) copy-start(bf16[12,8,24,128]{3,2,1,0:T(8,128)(2,1)} %copy.59) | copy-start | bytes 1769476
  85.8 27.4 %copy-start.22 = (f32[24]{0:T(128)S(1)}, f32[24]{0:T(128)}, u32[]{:S(2)}) copy-start(f32[24]{0:T(128)} %param.15) | copy-start | bytes 292
  86.4 10.8 %all-to-all-start.1 = ((bf16[16,2,576]{2,1,0:T(2,128)(2,1)}), bf16[16,2,576]{2,1,0:T(2,128)(2,1)}, u32[]{:S(2)}, u32[]{:S(2)}) async-start(bf16[16,2,576]{2,1,0:T(2,128)(2,1)} %reshape.1538), calls=%async_computation.1 | async-start | bytes 81920 | tf_op jit(solution)/shard_map/all_to_all | solution.py:120
  92.1 23.9 %copy-start.4 = (bf16[12,8,24,128]{3,2,1,0:T(8,128)(2,1)S(1)}, bf16[12,8,24,128]{3,2,1,0:T(8,128)(2,1)}, u32[]{:S(2)}) copy-start(bf16[12,8,24,128]{3,2,1,0:T(8,128)(2,1)} %copy.60) | copy-start | bytes 1769476
  109.9 2.7 %copy-start.16 = (f32[1,24,1]{2,1,0:T(8,128)S(1)}, f32[1,24,1]{2,1,0:T(8,128)}, u32[]{:S(2)}) copy-start(f32[1,24,1]{2,1,0:T(8,128)} %copy.21) | copy-start | bytes 292
  109.9 2.7 %copy-start.17 = (f32[1,24,1]{2,1,0:T(8,128)S(1)}, f32[1,24,1]{2,1,0:T(8,128)}, u32[]{:S(2)}) copy-start(f32[1,24,1]{2,1,0:T(8,128)} %copy.22) | copy-start | bytes 292
  109.9 2.7 %copy-start.23 = (pred[97]{0:T(512)(128)(4,1)S(1)}, pred[97]{0:T(512)(128)(4,1)}, u32[]{:S(2)}) copy-start(pred[97]{0:T(512)(128)(4,1)} %add_bitcast_fusion) | copy-start | bytes 295
  109.9 4.7 %copy-start.7 = (f32[1,3072]{1,0:T(1,128)S(1)}, f32[1,3072]{1,0:T(1,128)}, u32[]{:S(2)}) copy-start(f32[1,3072]{1,0:T(1,128)} %get-tuple-element.18) | copy-start | bytes 36868
  109.9 4.7 %copy-start.8 = (f32[1,3072]{1,0:T(1,128)S(1)}, f32[1,3072]{1,0:T(1,128)}, u32[]{:S(2)}) copy-start(f32[1,3072]{1,0:T(1,128)} %get-tuple-element.19) | copy-start | bytes 36868
  109.9 4.7 %copy-start.9 = (f32[1,3072]{1,0:T(1,128)S(1)}, f32[1,3072]{1,0:T(1,128)}, u32[]{:S(2)}) copy-start(f32[1,3072]{1,0:T(1,128)} %get-tuple-element.20) | copy-start | bytes 36868
  109.9 7.1 %copy-start.14 = (bf16[1,24,64]{2,1,0:T(8,128)(2,1)S(1)}, bf16[1,24,64]{2,1,0:T(8,128)(2,1)}, u32[]{:S(2)}) copy-start(bf16[1,24,64]{2,1,0:T(8,128)(2,1)} %get-tuple-element.43) | copy-start | bytes 9220
  110.0 7.1 %copy-start.15 = (bf16[1,24,64]{2,1,0:T(8,128)(2,1)S(1)}, bf16[1,24,64]{2,1,0:T(8,128)(2,1)}, u32[]{:S(2)}) copy-start(bf16[1,24,64]{2,1,0:T(8,128)(2,1)} %get-tuple-element.44) | copy-start | bytes 9220
  116.0 2.6 %copy-start.19 = (bf16[1,1,24,64]{3,2,1,0:T(8,128)(2,1)S(1)}, bf16[1,1,24,64]{3,2,1,0:T(8,128)(2,1)}, u32[]{:S(2)}) copy-start(bf16[1,1,24,64]{3,2,1,0:T(8,128)(2,1)} %get-tuple-element.48) | copy-start | bytes 9220
  117.4 7.2 %copy-start.11 = (bf16[24,96,1]{1,0,2:T(8,128)(2,1)S(1)}, bf16[24,96,1]{1,0,2:T(8,128)(2,1)}, u32[]{:S(2)}) copy-start(bf16[24,96,1]{1,0,2:T(8,128)(2,1)} %slice_bitcast_fusion.1) | copy-start | bytes 13828
  124.6 41.3 %copy-start.6 = (bf16[2,16,768]{2,1,0:T(8,128)(2,1)S(1)}, bf16[2,16,768]{2,1,0:T(8,128)(2,1)}, u32[]{:S(2)}) copy-start(bf16[2,16,768]{2,1,0:T(8,128)(2,1)} %param.12) | copy-start | bytes 147460
  125.1 46.0 %slice-start = ((s8[9437184]{0:T(1024)(128)(4,1)}), s8[1048576]{0:T(1024)(128)(4,1)S(1)}, s32[]{:S(2)}) async-start(s8[9437184]{0:T(1024)(128)(4,1)} %bitcast.160), calls=%async_computation.2 | async-start | bytes 2097152
  165.9 5.2 %slice-start.1 = ((s8[9437184]{0:T(1024)(128)(4,1)}), s8[4194304]{0:T(1024)(128)(4,1)S(1)}, s32[]{:S(2)}) async-start(s8[9437184]{0:T(1024)(128)(4,1)} %bitcast.160), calls=%async_computation.3 | async-start | bytes 8388608
  165.9 6.1 %slice-start.2 = ((s8[9437184]{0:T(1024)(128)(4,1)}), s8[4194304]{0:T(1024)(128)(4,1)S(1)}, s32[]{:S(2)}) async-start(s8[9437184]{0:T(1024)(128)(4,1)} %bitcast.160), calls=%async_computation.4 | async-start | bytes 8388608
  (6 other events, 7.9 us)
where the time goes:
time: 175 us; the launch traced here: 174 us
  blocking collectives  87.2 us (50%)
  matrix products  33.8 us (19%)
  other arithmetic  21.3 us (12%)
  local copies, waits for them, and re-layouts  20.9 us (12%)
  starting transfers between devices  8.27 us (5%)
    all_gather x2, blocking collectives, project(): whole = lax.all_gather(step_inputs, 'gx', axis=2, tiled=True)  46.8 us
    all_gather x2, blocking collectives, local(): lax.all_gather(attended, 'gx', axis=1, tiled=True)  40.3 us
    dot_general x2, matrix products, project(): jnp.einsum('sbd,dc->sbc', normed, qkv_weight, preferred_element_type=jnp....  22.2 us
    all_to_all x2, starting transfers between devices, local(): lax.all_to_all(projected, 'gx', split_axis=1, concat_axis=2, tiled=True)  8.27 us
    unnamed x64, local copies, waits for them, and re-layouts  8.17 us
    dot_general x2, matrix products, local(): jnp.einsum('sbf,fd->sbd', lax.all_gather(attended, 'gx', axis=1, tiled=Tr...  6.56 us
    concatenate x6, other arithmetic, rotary(): jnp.concatenate([lower_half * cosine - upper_half * sine_values, upper_ha...  5.77 us
    dot_general x4, matrix products, softmax_map(): jnp.einsum('shd,sjhd->shj', query, cache_keys, preferred_element_type=jnp...  4.05 us
  transfers between devices with their start and end apart: 2, of which 1 were waited for; matrix products, arithmetic and copies ran while one was open for 15% of the time, Pallas kernels for 0%

commit v1 on v0

v1 whole, which is shorter than its diff:
```python
import functools
import math

import jax
import jax.numpy as jnp
from jax import lax
from jax.experimental import pallas as pl
from jax.experimental.pallas import tpu as pltpu
from jax.sharding import PartitionSpec as P

H = 24
HD = 128
EPS = 1e-05
ROPE_BASE = 10000.0
F32 = jnp.float32
BF16 = jnp.bfloat16
VMEM_LIMIT = 16 * 1024 * 1024


def radices(n):
    rest = n // 2
    middle = 1
    while middle * middle * 4 <= rest:
        middle *= 2
    return rest // middle, middle


def swap(block, n, mask):
    return lax.ppermute(block, "gx", [(i, i ^ mask) for i in range(n)])


def gather_blocks(block, n):
    outer, middle = radices(n)
    rows = jnp.stack([block] + [swap(block, n, o * 2 * middle) for o in range(1, outer)])
    mine = jnp.concatenate([rows] + [swap(rows, n, m * 2) for m in range(1, middle)])
    return mine, swap(mine, n, 1)


def owner(me, entry, core, n):
    outer, middle = radices(n)
    mask = (entry % outer) * (2 * middle) + (entry // outer) * 2 + core
    return jnp.bitwise_xor(me, mask)


def project_kernel(n, me_ref, mine_ref, other_ref, gain_ref, weight_ref, out_ref, total, spread):
    me = me_ref[0]
    half, rows, part = mine_ref.shape
    columns = weight_ref.shape[1]
    blocks = columns // 128
    squares = jnp.zeros((rows, part), F32)
    for entry in range(half):
        for ref in (mine_ref, other_ref):
            values = ref[entry].astype(F32)
            squares = squares + values * values
    mean = jnp.sum(squares, axis=1, keepdims=True) * (1.0 / (n * part))
    factor = lax.rsqrt(mean + EPS)
    total[...] = jnp.zeros_like(total)

    @pl.loop(0, half)
    def _(entry):
        for core, ref in ((0, mine_ref), (1, other_ref)):
            shard = owner(me, entry, core, n)
            normed = (ref[entry].astype(F32) * factor * gain_ref[shard]).astype(BF16)
            start = pl.multiple_of(shard * part, part)
            total[...] += jnp.dot(
                normed, weight_ref[pl.ds(start, part), :], preferred_element_type=F32
            )

    steps = rows // n
    for step in range(steps):
        for block in range(blocks):
            spread[:, step * blocks + block, :] = total[
                step * n : (step + 1) * n, block * 128 : (block + 1) * 128
            ]
    for target in range(n):
        out_ref[target] = spread[target, : steps * blocks, :].astype(BF16)


def project(me, mine, other, gain, weight, n):
    half, rows, part = mine.shape
    columns = weight.shape[1]
    pieces = rows // n * (columns // 128)
    vmem = pl.BlockSpec(memory_space=pltpu.VMEM)
    return pl.pallas_call(
        functools.partial(project_kernel, n),
        out_shape=jax.ShapeDtypeStruct((n, pieces, 128), BF16),
        in_specs=[pl.BlockSpec(memory_space=pltpu.SMEM), vmem, vmem, vmem, vmem],
        out_specs=vmem,
        scratch_shapes=[
            pltpu.VMEM((rows, columns), F32),
            pltpu.VMEM((n, -(-pieces // 8) * 8, 128), F32),
        ],
        compiler_params=pltpu.CompilerParams(vmem_limit_bytes=VMEM_LIMIT),
        cost_estimate=pl.CostEstimate(
            flops=2 * rows * weight.shape[0] * columns, bytes_accessed=0, transcendentals=0
        ),
    )(me, mine, other, gain, pltpu.with_memory_space_constraint(weight, pltpu.VMEM))


def attend_kernel(
    table_ref, length_ref, received_ref, cos_ref, sin_ref, lambda_ref, gain_ref,
    keys_one_ref, keys_two_ref, values_ref, out_ref, fresh,
):
    sources, pieces, _ = received_ref.shape
    steps = cos_ref.shape[0]
    blocks = pieces // steps
    pages, page, _ = keys_one_ref.shape
    capacity = pages * page
    for source in range(sources):
        piece = received_ref[source].astype(F32)
        for step in range(steps):
            fresh[step, source * blocks : (source + 1) * blocks, :] = piece[
                step * blocks : (step + 1) * blocks
            ]

    def heads(step, kind):
        return fresh[step, kind * H : (kind + 1) * H, :]

    def rotated(step, kind):
        values = heads(step, kind)
        turned = values * cos_ref[step] + pltpu.roll(values, HD // 2, 1) * sin_ref[step]
        return turned.astype(BF16).astype(F32)

    row = lax.broadcasted_iota(jnp.int32, (1, capacity), 1)
    place = jnp.zeros((1, capacity), jnp.int32)
    for index in range(pages):
        first = table_ref[0, index] * page
        inside = (row >= first) & (row < first + page)
        place = jnp.where(inside, row - first + index * page, place)
    allowed = place < length_ref[0]

    scale = 1.0 / math.sqrt(HD)
    head_row = lax.rem(lax.broadcasted_iota(jnp.int32, (steps * H, HD), 0), H)

    def softmax_map(kind, keys_ref):
        queries = [rotated(step, kind) for step in range(steps)]
        news = [rotated(step, kind + 2) for step in range(steps)]
        stacked = jnp.concatenate(queries, axis=0)
        apart = jnp.concatenate(
            [jnp.where(head_row == h, stacked, 0.0).astype(BF16) for h in range(H)], axis=1
        )
        older = lax.dot_general(
            apart, keys_ref[...].reshape(capacity, H * HD), (((1,), (1,)), ((), ())),
            preferred_element_type=F32,
        )
        older = jnp.where(allowed, older * scale, -1e38)
        parts = []
        for step in range(steps):
            cached = older[step * H : (step + 1) * H]
            newer = [
                jnp.sum(queries[step] * news[e], axis=1, keepdims=True) * scale
                for e in range(step + 1)
            ]
            top = jnp.max(cached, axis=1, keepdims=True)
            for value in newer:
                top = jnp.maximum(top, value)
            cached = jnp.exp(cached - top)
            newer = [jnp.exp(value - top) for value in newer]
            whole = jnp.sum(cached, axis=1, keepdims=True)
            for value in newer:
                whole = whole + value
            parts.append((cached / whole, [value / whole for value in newer]))
        return parts

    first = softmax_map(0, keys_one_ref)
    second = softmax_map(1, keys_two_ref)
    weight = lambda_ref[...]
    mix = jnp.concatenate(
        [first[step][0] - weight * second[step][0] for step in range(steps)], axis=0
    ).astype(BF16)
    spread = jnp.dot(mix, values_ref[...].reshape(capacity, -1), preferred_element_type=F32)
    wide_row = lax.broadcasted_iota(jnp.int32, (H, 2 * HD), 0)
    fresh_values = [
        jnp.concatenate(
            [fresh[e, pl.ds(4 * H + half, H, stride=2), :] for half in range(2)], axis=1
        )
        for e in range(steps)
    ]
    for step in range(steps):
        mixed = jnp.zeros((H, 2 * HD), F32)
        for h in range(H):
            block = spread[step * H : (step + 1) * H, h * 2 * HD : (h + 1) * 2 * HD]
            mixed = jnp.where(wide_row == h, block, mixed)
        for e in range(step + 1):
            share = first[step][1][e] - weight * second[step][1][e]
            mixed = mixed + share.astype(BF16).astype(F32) * fresh_values[e]
        norm = lax.rsqrt(jnp.mean(mixed * mixed, axis=1, keepdims=True) + EPS)
        out_ref[step * H : (step + 1) * H, :] = (mixed * norm * gain_ref[...]).astype(BF16)


def attend(table, length, received, cos, sin, weights, gain, keys_one, keys_two, values):
    steps = cos.shape[0]
    sources, pieces, _ = received.shape
    vmem = pl.BlockSpec(memory_space=pltpu.VMEM)
    smem = pl.BlockSpec(memory_space=pltpu.SMEM)
    held = [pltpu.with_memory_space_constraint(x, pltpu.VMEM) for x in (keys_one, keys_two, values)]
    return pl.pallas_call(
        attend_kernel,
        out_shape=jax.ShapeDtypeStruct((steps * H, 2 * HD), BF16),
        in_specs=[smem, smem] + [vmem] * 8,
        out_specs=vmem,
        scratch_shapes=[pltpu.VMEM((steps, sources * (pieces // steps), 128), F32)],
        compiler_params=pltpu.CompilerParams(vmem_limit_bytes=VMEM_LIMIT),
    )(table, length, received, cos, sin, weights, gain, *held)


def output_kernel(n, me_ref, mine_ref, other_ref, inputs_ref, weight_ref, out_ref, rows_ref, total):
    me = me_ref[0]
    half, heads, width = mine_ref.shape
    steps = heads // H
    lanes = width // 128
    for entry in range(half):
        for core, ref in ((0, mine_ref), (1, other_ref)):
            start = pl.multiple_of(owner(me, entry, core, n) * heads, 8)
            block = ref[entry].astype(F32)
            for lane in range(lanes):
                rows_ref[lane, pl.ds(start, heads), :] = block[:, lane * 128 : (lane + 1) * 128]
    total[...] = jnp.zeros_like(total)
    for h in range(H):
        left = jnp.concatenate(
            [
                jnp.concatenate(
                    [rows_ref[lane, pl.ds(step * H + h, n, stride=heads), :] for lane in range(lanes)],
                    axis=1,
                )
                for step in range(steps)
            ],
            axis=0,
        ).astype(BF16)
        total[...] += jnp.dot(
            left, weight_ref[h * width : (h + 1) * width, :], preferred_element_type=F32
        )
    for step in range(steps):
        out_ref[step] = (
            inputs_ref[step].astype(F32) + total[step * n : (step + 1) * n]
        ).astype(BF16)


def output(me, mine, other, inputs, weight, n):
    half, heads, width = mine.shape
    vmem = pl.BlockSpec(memory_space=pltpu.VMEM)
    steps, rows, columns = inputs.shape
    return pl.pallas_call(
        functools.partial(output_kernel, n),
        out_shape=jax.ShapeDtypeStruct(inputs.shape, BF16),
        in_specs=[pl.BlockSpec(memory_space=pltpu.SMEM), vmem, vmem, vmem, vmem],
        out_specs=vmem,
        scratch_shapes=[
            pltpu.VMEM((width // 128, n * heads, 128), F32),
            pltpu.VMEM((steps * rows, columns), F32),
        ],
        compiler_params=pltpu.CompilerParams(vmem_limit_bytes=VMEM_LIMIT),
    )(me, mine, other, inputs, pltpu.with_memory_space_constraint(weight, pltpu.VMEM))


def angles(positions, steps):
    half = HD // 2
    frequency = jnp.exp(-math.log(ROPE_BASE) * 2.0 * jnp.arange(half, dtype=F32) / HD)
    places = (positions + jnp.arange(steps, dtype=jnp.int32)).astype(F32)
    turns = places[:, None] * frequency[None, :]
    cosine, sine = jnp.cos(turns), jnp.sin(turns)
    cos = jnp.concatenate([cosine, cosine], axis=-1)
    sin = jnp.concatenate([-sine, sine], axis=-1)
    return cos[:, None, :], sin[:, None, :]


def local(
    n, inputs, norm_gain, qkv_weight, head_lambda, head_gain, out_weight,
    key_one_pages, key_two_pages, value_pages, page_table, context_len, positions,
):
    steps, rows, part = inputs.shape
    me = lax.axis_index("gx").astype(jnp.int32).reshape(1)
    mine, other = gather_blocks(inputs.reshape(steps * rows, part), n)
    sent = project(me, mine, other, norm_gain.reshape(n, 1, part), qkv_weight, n)
    received = lax.all_to_all(sent, "gx", 0, 0)
    cos, sin = angles(positions, steps)
    attended = attend(
        page_table, context_len, received, cos, sin, head_lambda.reshape(H, 1),
        head_gain.reshape(H, 2 * HD), key_one_pages, key_two_pages, value_pages,
    )
    mine, other = gather_blocks(attended, n)
    return output(me, mine, other, inputs, out_weight, n)


def rotary(vectors, cos, sin):
    return vectors * cos + jnp.roll(vectors, HD // 2, axis=-1) * sin


def local_any(
    n, inputs, norm_gain, qkv_weight, head_lambda, head_gain, out_weight,
    key_one_pages, key_two_pages, value_pages, page_table, context_len, positions,
):
    steps = inputs.shape[0]
    own = page_table.shape[0]
    capacity = page_table.shape[1] * key_one_pages.shape[1]
    values = lax.all_gather(inputs, "gx", axis=2, tiled=True).astype(F32)
    factor = lax.rsqrt(jnp.mean(values * values, axis=-1, keepdims=True) + EPS)
    normed = (values * factor * norm_gain).astype(BF16)
    projected = jnp.einsum("sbd,dc->sbc", normed, qkv_weight, preferred_element_type=F32)
    received = lax.all_to_all(
        projected.astype(BF16), "gx", split_axis=1, concat_axis=2, tiled=True
    )
    cached = tuple(
        pool[page_table].reshape(own, capacity, H, -1)
        for pool in (key_one_pages, key_two_pages, value_pages)
    )
    both = received[..., : 4 * H * HD].reshape(steps, own, 4, H, HD).astype(F32)
    new_values = received[..., 4 * H * HD :].reshape(steps, own, H, 2 * HD)
    cos, sin = jax.vmap(lambda p: angles(p, steps))(positions.reshape(own, 1))
    cos, sin = (jnp.moveaxis(x, 0, 1)[:, :, None] for x in (cos, sin))
    turned = rotary(both, cos, sin).astype(BF16)
    place = jnp.arange(capacity, dtype=jnp.int32)
    allowed = (place[None, :] < context_len[:, None])[None, :, None, :]
    step = jnp.arange(steps)
    newer_allowed = (step[None, :] <= step[:, None])[:, None, None, :]

    def softmax_map(query, keys, news):
        older = jnp.einsum("tshd,sjhd->tshj", query, keys, preferred_element_type=F32)
        newer = jnp.einsum("tshd,eshd->tshe", query, news, preferred_element_type=F32)
        scores = jnp.concatenate(
            [jnp.where(allowed, older, -jnp.inf), jnp.where(newer_allowed, newer, -jnp.inf)], axis=-1
        )
        return jax.nn.softmax(scores * (1.0 / math.sqrt(HD)), axis=-1)

    first = softmax_map(turned[:, :, 0], cached[0], turned[:, :, 2])
    second = softmax_map(turned[:, :, 1], cached[1], turned[:, :, 3])
    mix = (first - head_lambda[:, None] * second).astype(BF16)
    mixed = jnp.einsum(
        "tshj,sjhf->tshf", mix[..., :capacity], cached[2], preferred_element_type=F32
    ) + jnp.einsum("tshe,eshf->tshf", mix[..., capacity:], new_values, preferred_element_type=F32)
    norm = lax.rsqrt(jnp.mean(mixed * mixed, axis=-1, keepdims=True) + EPS)
    grouped = (mixed * norm * head_gain.reshape(H, 2 * HD)).astype(BF16)
    whole = lax.all_gather(grouped.reshape(steps, own, -1), "gx", axis=1, tiled=True)
    branch = jnp.einsum("sbf,fd->sbd", whole, out_weight, preferred_element_type=F32)
    return (inputs.astype(F32) + branch).astype(BF16)


def solution(mesh):
    n = mesh.shape["gx"]
    placed = (
        P(None, "groups", "gx"),
        P(),
        P(None, "gx"),
        P(),
        P(),
        P(None, "gx"),
        P(("groups", "gx"), None, None),
        P(("groups", "gx"), None, None),
        P(("groups", "gx"), None, None),
        P(("groups", "gx"), None),
        P(("groups", "gx")),
        P(("groups", "gx")),
    )

    def chosen(inputs, norm_gain, qkv_weight, *rest):
        aligned = inputs.shape[2] % 128 == 0 and qkv_weight.shape[1] % 128 == 0
        single = rest[6].shape[0] == 1
        power = n >= 2 and n & (n - 1) == 0
        body = local if aligned and single and power else local_any
        return body(n, inputs, norm_gain, qkv_weight, *rest)

    return jax.shard_map(
        chosen, mesh=mesh, in_specs=placed, out_specs=P(None, "groups", "gx"), check_vma=False
    )
```

time: 175 us -> 68.3 us (0.39)
  blocking collectives: 87.2 us -> 0 us
  matrix products: 33.8 us -> 0 us
  waiting for transfers between devices: 0.89 us -> 24.5 us
  other arithmetic: 21.3 us -> 1.04 us
  Pallas kernels: 0 us -> 10.2 us
  starting transfers between devices: 8.27 us -> 16.1 us
  local copies, waits for them, and re-layouts: 20.9 us -> 14.6 us
    all_gather x4 -> x0, blocking collectives: 87.2 us -> none  [the longest x2 46.8 us: project(): whole = lax.all_gather(step_inputs, 'gx', axis=2, tiled=True)]
    dot_general x13 -> x0, matrix products: 33.8 us -> none  [the longest x2 22.2 us: project(): jnp.einsum('sbd,dc->sbc', normed, qkv_weight, preferred_element_type=jnp....]
    ppermute x0 -> x10, waiting for transfers between devices: none -> 18.1 us  [swap(): return lax.ppermute(block, 'gx', [(i, i ^ mask) for i in range(n)])]
    ppermute x0 -> x10, starting transfers between devices: none -> 12.6 us  [swap(): return lax.ppermute(block, 'gx', [(i, i ^ mask) for i in range(n)])]
    pallas_call x0 -> x3, Pallas kernels: none -> 10.2 us  [the longest x1 6.21 us: project(): pl.pallas_call(functools.partial(project_kernel, n), out_shape=jax.ShapeD...]
    concatenate x7 -> x1, other arithmetic: 6.4 us -> 0.08 us  [angles(): cos = jnp.concatenate([cosine, cosine], axis=-1)]
    unnamed x64 -> x28, local copies, waits for them, and re-layouts: 8.17 us -> 14.5 us
    all_to_all x2 -> x1, waiting for transfers between devices: 0.89 us -> 6.41 us  [local(): received = lax.all_to_all(sent, 'gx', 0, 0)]
  transfers between devices with their start and end apart: 2 -> 11, of which waited for: 1 -> 9; matrix products, arithmetic and copies ran while one was open for 15% -> 2% of each run, Pallas kernels for 0% -> 0%
where the time goes in v1:
time: 68.3 us; the launch traced here: 67.9 us
  waiting for transfers between devices  24.5 us (36%)
  starting transfers between devices  16.1 us (24%)
  local copies, waits for them, and re-layouts  14.6 us (21%)
  Pallas kernels  10.2 us (15%)
  between operations  1.46 us (2%)
  other arithmetic  1.04 us (2%)
    ppermute x10, waiting for transfers between devices, swap(): return lax.ppermute(block, 'gx', [(i, i ^ mask) for i in range(n)])  18.1 us
    unnamed x28, local copies, waits for them, and re-layouts  14.5 us
    ppermute x10, starting transfers between devices, swap(): return lax.ppermute(block, 'gx', [(i, i ^ mask) for i in range(n)])  12.6 us
    all_to_all x1, waiting for transfers between devices, local(): received = lax.all_to_all(sent, 'gx', 0, 0)  6.41 us
    pallas_call x1, Pallas kernels, project(): pl.pallas_call(functools.partial(project_kernel, n), out_shape=jax.ShapeD...  6.21 us
    all_to_all x1, starting transfers between devices, local(): received = lax.all_to_all(sent, 'gx', 0, 0)  3.51 us
    pallas_call x1, Pallas kernels, output(): pl.pallas_call(functools.partial(output_kernel, n), out_shape=jax.ShapeDt...  2.37 us
    pallas_call x1, Pallas kernels, attend(): pl.pallas_call(attend_kernel, out_shape=jax.ShapeDtypeStruct((steps * H,...  1.67 us
  transfers between devices with their start and end apart: 11, of which 9 were waited for; matrix products, arithmetic and copies ran while one was open for 2% of the time, Pallas kernels for 0%

profile of v1, /device:TPU:0, one launch (start us, length us, event | category | flops | bytes accessed | tf_op | source)
XLA Modules:
  0.0 67.9 jit_solution(16698508195322176393)
XLA Ops:
  0.0 3.0 %collective-permute-start = (bf16[32,768]{1,0:T(8,128)(2,1)}, bf16[32,768]{1,0:T(8,128)(2,1)S(1)}, u32[]{:S(2)}, u32[]{:S(2)}) collective-permute-start(bf16[32,768]{1,0:T(8,128)(2,1)} %bitcast.27), channel_id=1, source_target_pairs={{0,4},{1,5},{2,6},{3,7},{4,0},{5,1},{6,2},{7,3},{8,12},{9,13},{10,... | collective-permute-start | bytes 147464 | tf_op jit(solution)/shard_map/ppermute | solution.py:29
  3.0 2.6 %collective-permute-start.1 = (bf16[32,768]{1,0:T(8,128)(2,1)}, bf16[32,768]{1,0:T(8,128)(2,1)S(1)}, u32[]{:S(2)}, u32[]{:S(2)}) collective-permute-start(bf16[32,768]{1,0:T(8,128)(2,1)} %bitcast.28), channel_id=1, source_target_pairs={{0,8},{1,9},{2,10},{3,11},{4,12},{5,13},{6,14},{7,15},{8,0},{9,1},... | collective-permute-start | bytes 147464 | tf_op jit(solution)/shard_map/ppermute | solution.py:29
  5.6 0.9 %constant_dynamic-update-slice_fusion.4 = bf16[8,32,768]{2,1,0:T(8,128)(2,1)S(1)} fusion(bf16[1,32,768]{2,1,0:T(8,128)(2,1)} %bitcast.30), kind=kLoop, calls=%fused_computation.6 | loop fusion | bytes 98304
  6.5 2.7 %collective-permute-done.1 = bf16[32,768]{1,0:T(8,128)(2,1)S(1)} collective-permute-done((bf16[32,768]{1,0:T(8,128)(2,1)}, bf16[32,768]{1,0:T(8,128)(2,1)S(1)}, u32[]{:S(2)}, u32[]{:S(2)}) %collective-permute-start.1) | collective-permute-done | bytes 49184 | tf_op jit(solution)/shard_map/ppermute | solution.py:29
  9.2 2.6 %collective-permute-done.2 = bf16[32,768]{1,0:T(8,128)(2,1)S(1)} collective-permute-done((bf16[32,768]{1,0:T(8,128)(2,1)}, bf16[32,768]{1,0:T(8,128)(2,1)S(1)}, u32[]{:S(2)}, u32[]{:S(2)}) %collective-permute-start.2) | collective-permute-done | bytes 49184 | tf_op jit(solution)/shard_map/ppermute | solution.py:29
  11.7 0.8 %pad_maximum_fusion = bf16[4,32,768]{2,1,0:T(8,128)(2,1)S(1)} fusion(bf16[1,32,768]{2,1,0:T(8,128)(2,1)S(1)} %bitcast.38, bf16[1,32,768]{2,1,0:T(8,128)(2,1)S(1)} %bitcast.37, bf16[1,32,768]{2,1,0:T(8,128)(2,1)S(1)} %bitcast.36, bf16[1,32,768]{2,1,0:T(8,128)(2,1)} %bitcast.31), kind=kLoop, calls=%fused_computation | loop fusion | flops 294912 | bytes 393216 | tf_op jit(solution)/shard_map/stack | solution.py:34
  12.5 1.6 %collective-permute-start.3 = (bf16[4,32,768]{2,1,0:T(8,128)(2,1)S(1)}, bf16[4,32,768]{2,1,0:T(8,128)(2,1)S(1)}, u32[]{:S(2)}, u32[]{:S(2)}) collective-permute-start(bf16[4,32,768]{2,1,0:T(8,128)(2,1)S(1)} %pad_maximum_fusion), channel_id=1, source_target_pairs={{0,2},{1,3},{2,0},{3,1},{4,6},{5,7},{6,4},{7,5},{8,10},{9,11},{10,... | collective-permute-start | bytes 589832 | tf_op jit(solution)/shard_map/ppermute | solution.py:29
  14.2 4.1 %collective-permute-done.3 = bf16[4,32,768]{2,1,0:T(8,128)(2,1)S(1)} collective-permute-done((bf16[4,32,768]{2,1,0:T(8,128)(2,1)S(1)}, bf16[4,32,768]{2,1,0:T(8,128)(2,1)S(1)}, u32[]{:S(2)}, u32[]{:S(2)}) %collective-permute-start.3) | collective-permute-done | bytes 196640 | tf_op jit(solution)/shard_map/ppermute | solution.py:29
  19.1 1.0 %collective-permute-done.4.other_ref = bf16[8,32,768]{2,1,0:T(8,128)(2,1)S(1)} collective-permute-done((bf16[8,32,768]{2,1,0:T(8,128)(2,1)S(1)}, bf16[8,32,768]{2,1,0:T(8,128)(2,1)S(1)}, u32[]{:S(2)}, u32[]{:S(2)}) %collective-permute-start.4) | collective-permute-done | bytes 393248 | tf_op jit(solution)/shard_map/ppermute | solution.py:29
  20.1 9.1 %copy-done = bf16[12288,1152]{1,0:T(8,128)(2,1)S(1)} copy-done((bf16[12288,1152]{1,0:T(8,128)(2,1)S(1)}, bf16[12288,1152]{1,0:T(8,128)(2,1)}, u32[]{:S(2)}) %copy-start) | copy-done | bytes 28311576
  29.1 0.8 %copy-done.6 = f32[12288]{0:T(1024)S(1)} copy-done((f32[12288]{0:T(1024)S(1)}, f32[12288]{0:T(1024)}, u32[]{:S(2)}) %copy-start.6) | copy-done | bytes 49176
  30.0 6.2 %shard_map.118 = bf16[16,18,128]{2,1,0:T(8,128)(2,1)} custom-call(s32[1]{0:T(128)} %bitcast.me_ref, bf16[8,32,768]{2,1,0:T(8,128)(2,1)S(1)} %constant_dynamic-update-slice_fusion.mine_ref, bf16[8,32,768]{2,1,0:T(8,128)(2,1)S(1)} %collective-permute-done.4.other_ref, f32[16,1,768]{2,1,0:T(1,128)S(1)} %bitcast.33, bf16[12288,1152]{1,0:T(8,128)(2,1)S(1)} %copy-done), custom_call_target="tpu_custom_call" | custom-call | flops 905969664 | tf_op jit(solution)/shard_map/pallas_call | solution.py:84
  36.2 3.5 %all-to-all-start = ((bf16[16,18,128]{2,1,0:T(8,128)(2,1)}), bf16[16,18,128]{2,1,0:T(8,128)(2,1)S(1)}, u32[]{:S(2)}, u32[]{:S(2)}) async-start(bf16[16,18,128]{2,1,0:T(8,128)(2,1)} %shard_map.118), calls=%async_computation | async-start | bytes 196608 | tf_op jit(solution)/shard_map/all_to_all | solution.py:275
  40.7 6.4 %all-to-all-done.received_ref = bf16[16,18,128]{2,1,0:T(8,128)(2,1)S(1)} async-done(((bf16[16,18,128]{2,1,0:T(8,128)(2,1)}), bf16[16,18,128]{2,1,0:T(8,128)(2,1)S(1)}, u32[]{:S(2)}, u32[]{:S(2)}) %all-to-all-start) | async-done | bytes 73760 | tf_op jit(solution)/shard_map/all_to_all | solution.py:275
  47.1 1.7 %shard_map.119 = bf16[48,256]{1,0:T(8,128)(2,1)S(1)} custom-call(s32[1,6]{1,0:T(1,128)S(1)} %copy-done.7, s32[1]{0:T(128)S(6)} %copy.23.length_ref, bf16[16,18,128]{2,1,0:T(8,128)(2,1)S(1)} %all-to-all-done.received_ref, f32[2,1,128]{2,1,0:T(1,128)S(1)} %bitcast.34, f32[2,1,128]{2,1,0:T(1,128)S(1)} %bitcast.35, f32[24,1]{1,0:T(8,128)S(1)} %copy.14.lambda_ref, ...), custom_call_target="tpu_custom_call" | custom-call | tf_op jit(solution)/shard_map/pallas_call | solution.py:197
  48.9 1.1 %collective-permute-start.6 = (bf16[48,256]{1,0:T(8,128)(2,1)S(1)}, bf16[48,256]{1,0:T(8,128)(2,1)S(1)}, u32[]{:S(2)}, u32[]{:S(2)}) collective-permute-start(bf16[48,256]{1,0:T(8,128)(2,1)S(1)} %shard_map.119), channel_id=1, source_target_pairs={{0,8},{1,9},{2,10},{3,11},{4,12},{5,13},{6,14},{7,15},{8,0},{9,1},... | collective-permute-start | bytes 73736 | tf_op jit(solution)/shard_map/ppermute | solution.py:29
  50.0 3.2 %collective-permute-start.7 = (bf16[48,256]{1,0:T(8,128)(2,1)S(1)}, bf16[48,256]{1,0:T(8,128)(2,1)S(1)}, u32[]{:S(2)}, u32[]{:S(2)}) collective-permute-start(bf16[48,256]{1,0:T(8,128)(2,1)S(1)} %shard_map.119), channel_id=1, source_target_pairs={{0,12},{1,13},{2,14},{3,15},{4,8},{5,9},{6,10},{7,11},{8,4},{9,5},... | collective-permute-start | bytes 73736 | tf_op jit(solution)/shard_map/ppermute | solution.py:29
  53.2 0.4 collective-permute-done.6
  53.6 2.0 %collective-permute-done.7 = bf16[48,256]{1,0:T(8,128)(2,1)S(1)} collective-permute-done((bf16[48,256]{1,0:T(8,128)(2,1)S(1)}, bf16[48,256]{1,0:T(8,128)(2,1)S(1)}, u32[]{:S(2)}, u32[]{:S(2)}) %collective-permute-start.7) | collective-permute-done | bytes 24608 | tf_op jit(solution)/shard_map/ppermute | solution.py:29
  55.6 0.8 %collective-permute-start.8 = (bf16[4,48,256]{2,1,0:T(8,128)(2,1)S(1)}, bf16[4,48,256]{2,1,0:T(8,128)(2,1)S(1)}, u32[]{:S(2)}, u32[]{:S(2)}) collective-permute-start(bf16[4,48,256]{2,1,0:T(8,128)(2,1)S(1)} %pad_maximum_fusion.1), channel_id=1, source_target_pairs={{0,2},{1,3},{2,0},{3,1},{4,6},{5,7},{6,4},{7,5},{8,10},{9,11},{10,... | collective-permute-start | bytes 294920 | tf_op jit(solution)/shard_map/ppermute | solution.py:29
  56.4 3.9 %collective-permute-done.8 = bf16[4,48,256]{2,1,0:T(8,128)(2,1)S(1)} collective-permute-done((bf16[4,48,256]{2,1,0:T(8,128)(2,1)S(1)}, bf16[4,48,256]{2,1,0:T(8,128)(2,1)S(1)}, u32[]{:S(2)}, u32[]{:S(2)}) %collective-permute-start.8) | collective-permute-done | bytes 98336 | tf_op jit(solution)/shard_map/ppermute | solution.py:29
  60.4 1.4 %collective-permute-done.9.other_ref = bf16[8,48,256]{2,1,0:T(8,128)(2,1)S(1)} collective-permute-done((bf16[8,48,256]{2,1,0:T(8,128)(2,1)S(1)}, bf16[8,48,256]{2,1,0:T(8,128)(2,1)S(1)}, u32[]{:S(2)}, u32[]{:S(2)}) %collective-permute-start.9) | collective-permute-done | bytes 196640 | tf_op jit(solution)/shard_map/ppermute | solution.py:29
  61.8 3.7 %copy-done.1 = bf16[6144,768]{1,0:T(8,128)(2,1)S(1)} copy-done((bf16[6144,768]{1,0:T(8,128)(2,1)S(1)}, bf16[6144,768]{1,0:T(8,128)(2,1)}, u32[]{:S(2)}) %copy-start.1) | copy-done | bytes 9437208
  65.5 2.4 %shard_map.120 = bf16[2,16,768]{2,1,0:T(8,128)(2,1)} custom-call(s32[1]{0:T(128)} %bitcast.me_ref, bf16[8,48,256]{2,1,0:T(8,128)(2,1)S(1)} %constant_dynamic-update-slice_fusion.5.mine_ref, bf16[8,48,256]{2,1,0:T(8,128)(2,1)S(1)} %collective-permute-done.9.other_ref, bf16[2,16,768]{2,1,0:T(8,128)(2,1)S(1)} %copy-done.5, bf16[6144,768]{1,0:T(8,128)(2,1)S(1)} %copy-done.1), custom_call_target="tpu_custom_call" | custom-call | tf_op jit(solution)/shard_map/pallas_call | solution.py:243
  (39 shorter events, 0.6 us)
Async XLA Ops:
  0.0 6.5 %collective-permute-start = (bf16[32,768]{1,0:T(8,128)(2,1)}, bf16[32,768]{1,0:T(8,128)(2,1)S(1)}, u32[]{:S(2)}, u32[]{:S(2)}) collective-permute-start(bf16[32,768]{1,0:T(8,128)(2,1)} %bitcast.27), channel_id=1, source_target_pairs={{0,4},{1,5},{2,6},{3,7},{4,0},{5,1},{6,2},{7,3},{8,12},{9,13},{10,... | collective-permute-start | bytes 147464 | tf_op jit(solution)/shard_map/ppermute | solution.py:29
  3.0 6.1 %collective-permute-start.1 = (bf16[32,768]{1,0:T(8,128)(2,1)}, bf16[32,768]{1,0:T(8,128)(2,1)S(1)}, u32[]{:S(2)}, u32[]{:S(2)}) collective-permute-start(bf16[32,768]{1,0:T(8,128)(2,1)} %bitcast.28), channel_id=1, source_target_pairs={{0,8},{1,9},{2,10},{3,11},{4,12},{5,13},{6,14},{7,15},{8,0},{9,1},... | collective-permute-start | bytes 147464 | tf_op jit(solution)/shard_map/ppermute | solution.py:29
  5.6 6.1 %collective-permute-start.2 = (bf16[32,768]{1,0:T(8,128)(2,1)}, bf16[32,768]{1,0:T(8,128)(2,1)S(1)}, u32[]{:S(2)}, u32[]{:S(2)}) collective-permute-start(bf16[32,768]{1,0:T(8,128)(2,1)} %bitcast.29), channel_id=1, source_target_pairs={{0,12},{1,13},{2,14},{3,15},{4,8},{5,9},{6,10},{7,11},{8,4},{9,5},... | collective-permute-start | bytes 147464 | tf_op jit(solution)/shard_map/ppermute | solution.py:29
  12.5 5.7 %collective-permute-start.3 = (bf16[4,32,768]{2,1,0:T(8,128)(2,1)S(1)}, bf16[4,32,768]{2,1,0:T(8,128)(2,1)S(1)}, u32[]{:S(2)}, u32[]{:S(2)}) collective-permute-start(bf16[4,32,768]{2,1,0:T(8,128)(2,1)S(1)} %pad_maximum_fusion), channel_id=1, source_target_pairs={{0,2},{1,3},{2,0},{3,1},{4,6},{5,7},{6,4},{7,5},{8,10},{9,11},{10,... | collective-permute-start | bytes 589832 | tf_op jit(solution)/shard_map/ppermute | solution.py:29
  18.3 1.8 %collective-permute-start.4 = (bf16[8,32,768]{2,1,0:T(8,128)(2,1)S(1)}, bf16[8,32,768]{2,1,0:T(8,128)(2,1)S(1)}, u32[]{:S(2)}, u32[]{:S(2)}) collective-permute-start(bf16[8,32,768]{2,1,0:T(8,128)(2,1)S(1)} %constant_dynamic-update-slice_fusion.mine_ref), channel_id=1, source_target_pairs={{0,1},{1,0},{2,3},{3,2},{4,5},{5,4},{6,7},{7,6},{8,9},{9,8},{10,11... | collective-permute-start | bytes 1179656 | tf_op jit(solution)/shard_map/ppermute | solution.py:29
  20.1 9.1 %copy-start = (bf16[12288,1152]{1,0:T(8,128)(2,1)S(1)}, bf16[12288,1152]{1,0:T(8,128)(2,1)}, u32[]{:S(2)}) copy-start(bf16[12288,1152]{1,0:T(8,128)(2,1)} %weight_ref.2) | copy-start | bytes 84934656
  29.1 0.8 %copy-start.6 = (f32[12288]{0:T(1024)S(1)}, f32[12288]{0:T(1024)}, u32[]{:S(2)}) copy-start(f32[12288]{0:T(1024)} %param.13) | copy-start | bytes 147460
  29.9 9.9 %copy-start.8 = (f32[6144]{0:T(1024)S(1)}, f32[6144]{0:T(1024)}, u32[]{:S(2)}) copy-start(f32[6144]{0:T(1024)} %param.16) | copy-start | bytes 73732
  29.9 9.9 %copy-start.9 = (f32[24]{0:T(128)S(1)}, f32[24]{0:T(128)}, u32[]{:S(2)}) copy-start(f32[24]{0:T(128)} %param.15) | copy-start | bytes 292
  29.9 17.1 %copy-start.2 = (bf16[6,16,6144]{2,1,0:T(8,128)(2,1)S(1)}, bf16[6,16,6144]{2,1,0:T(8,128)(2,1)}, u32[]{:S(2)}) copy-start(bf16[6,16,6144]{2,1,0:T(8,128)(2,1)} %values_ref.1) | copy-start | bytes 3538948
  29.9 17.1 %copy-start.3 = (bf16[6,16,3072]{2,1,0:T(8,128)(2,1)S(1)}, bf16[6,16,3072]{2,1,0:T(8,128)(2,1)}, u32[]{:S(2)}) copy-start(bf16[6,16,3072]{2,1,0:T(8,128)(2,1)} %keys_one_ref.1) | copy-start | bytes 1769476
  29.9 17.1 %copy-start.4 = (bf16[6,16,3072]{2,1,0:T(8,128)(2,1)S(1)}, bf16[6,16,3072]{2,1,0:T(8,128)(2,1)}, u32[]{:S(2)}) copy-start(bf16[6,16,3072]{2,1,0:T(8,128)(2,1)} %keys_two_ref.1) | copy-start | bytes 1769476
  30.0 17.1 %copy-start.7 = (s32[1,6]{1,0:T(1,128)S(1)}, s32[1,6]{1,0:T(1,128)}, u32[]{:S(2)}) copy-start(s32[1,6]{1,0:T(1,128)} %table_ref.1) | copy-start | bytes 76
  30.0 31.9 %copy-start.5 = (bf16[2,16,768]{2,1,0:T(8,128)(2,1)S(1)}, bf16[2,16,768]{2,1,0:T(8,128)(2,1)}, u32[]{:S(2)}) copy-start(bf16[2,16,768]{2,1,0:T(8,128)(2,1)} %inputs_ref.1) | copy-start | bytes 147460
  36.2 10.9 %all-to-all-start = ((bf16[16,18,128]{2,1,0:T(8,128)(2,1)}), bf16[16,18,128]{2,1,0:T(8,128)(2,1)S(1)}, u32[]{:S(2)}, u32[]{:S(2)}) async-start(bf16[16,18,128]{2,1,0:T(8,128)(2,1)} %shard_map.118), calls=%async_computation | async-start | bytes 196608 | tf_op jit(solution)/shard_map/all_to_all | solution.py:275
  48.8 4.5 %collective-permute-start.5 = (bf16[48,256]{1,0:T(8,128)(2,1)S(1)}, bf16[48,256]{1,0:T(8,128)(2,1)S(1)}, u32[]{:S(2)}, u32[]{:S(2)}) collective-permute-start(bf16[48,256]{1,0:T(8,128)(2,1)S(1)} %shard_map.119), channel_id=1, source_target_pairs={{0,4},{1,5},{2,6},{3,7},{4,0},{5,1},{6,2},{7,3},{8,12},{9,13},{10,... | collective-permute-start | bytes 73736 | tf_op jit(solution)/shard_map/ppermute | solution.py:29
  48.9 4.8 %collective-permute-start.6 = (bf16[48,256]{1,0:T(8,128)(2,1)S(1)}, bf16[48,256]{1,0:T(8,128)(2,1)S(1)}, u32[]{:S(2)}, u32[]{:S(2)}) collective-permute-start(bf16[48,256]{1,0:T(8,128)(2,1)S(1)} %shard_map.119), channel_id=1, source_target_pairs={{0,8},{1,9},{2,10},{3,11},{4,12},{5,13},{6,14},{7,15},{8,0},{9,1},... | collective-permute-start | bytes 73736 | tf_op jit(solution)/shard_map/ppermute | solution.py:29
  50.0 5.6 %collective-permute-start.7 = (bf16[48,256]{1,0:T(8,128)(2,1)S(1)}, bf16[48,256]{1,0:T(8,128)(2,1)S(1)}, u32[]{:S(2)}, u32[]{:S(2)}) collective-permute-start(bf16[48,256]{1,0:T(8,128)(2,1)S(1)} %shard_map.119), channel_id=1, source_target_pairs={{0,12},{1,13},{2,14},{3,15},{4,8},{5,9},{6,10},{7,11},{8,4},{9,5},... | collective-permute-start | bytes 73736 | tf_op jit(solution)/shard_map/ppermute | solution.py:29
  55.6 4.7 %collective-permute-start.8 = (bf16[4,48,256]{2,1,0:T(8,128)(2,1)S(1)}, bf16[4,48,256]{2,1,0:T(8,128)(2,1)S(1)}, u32[]{:S(2)}, u32[]{:S(2)}) collective-permute-start(bf16[4,48,256]{2,1,0:T(8,128)(2,1)S(1)} %pad_maximum_fusion.1), channel_id=1, source_target_pairs={{0,2},{1,3},{2,0},{3,1},{4,6},{5,7},{6,4},{7,5},{8,10},{9,11},{10,... | collective-permute-start | bytes 294920 | tf_op jit(solution)/shard_map/ppermute | solution.py:29
  60.3 1.5 %collective-permute-start.9 = (bf16[8,48,256]{2,1,0:T(8,128)(2,1)S(1)}, bf16[8,48,256]{2,1,0:T(8,128)(2,1)S(1)}, u32[]{:S(2)}, u32[]{:S(2)}) collective-permute-start(bf16[8,48,256]{2,1,0:T(8,128)(2,1)S(1)} %constant_dynamic-update-slice_fusion.5.mine_ref), channel_id=1, source_target_pairs={{0,1},{1,0},{2,3},{3,2},{4,5},{5,4},{6,7},{7,6},{8,9},{9,8},{10,11... | collective-permute-start | bytes 589832 | tf_op jit(solution)/shard_map/ppermute | solution.py:29
  61.8 3.7 %copy-start.1 = (bf16[6144,768]{1,0:T(8,128)(2,1)S(1)}, bf16[6144,768]{1,0:T(8,128)(2,1)}, u32[]{:S(2)}) copy-start(bf16[6144,768]{1,0:T(8,128)(2,1)} %weight_ref.3) | copy-start | bytes 28311556

commit v2 on v1

--- a/solution.py
+++ b/solution.py
@@ -29,9 +29,15 @@
     return lax.ppermute(block, "gx", [(i, i ^ mask) for i in range(n)])
 
 
-def gather_blocks(block, n):
+def outer_row(block, n, held=None):
     outer, middle = radices(n)
-    rows = jnp.stack([block] + [swap(block, n, o * 2 * middle) for o in range(1, outer)])
+    arrived = [swap(block, n, o * 2 * middle) for o in range(1, outer)]
+    return jnp.stack([block if held is None else held] + arrived)
+
+
+def gather_blocks(block, n, held=None):
+    _, middle = radices(n)
+    rows = outer_row(block, n, held)
     mine = jnp.concatenate([rows] + [swap(rows, n, m * 2) for m in range(1, middle)])
     return mine, swap(mine, n, 1)
 
@@ -42,59 +48,159 @@
     return jnp.bitwise_xor(me, mask)
 
 
-def project_kernel(n, me_ref, mine_ref, other_ref, gain_ref, weight_ref, out_ref, total, spread):
+def far(x):
+    return pltpu.with_memory_space_constraint(x, pltpu.HBM)
+
+
+def hint(us):
+    return pl.CostEstimate(flops=0, bytes_accessed=int(us * 3_000_000), transcendentals=0)
+
+
+def fetches(n, first, count, cores, me, from_ref, to_ref, sems):
+    part = from_ref.shape[0] // n
+    copies = []
+    for index, core in enumerate(cores):
+        for entry in range(count):
+            slot = index * count + entry
+            start = pl.multiple_of(owner(me, first + entry, core, n) * part, part)
+            copies.append(
+                pltpu.make_async_copy(
+                    from_ref.at[pl.ds(start, part), :],
+                    to_ref.at[slot],
+                    sems.at[slot],
+                )
+            )
+    return copies
+
+
+def fetch_kernel(
+    n, count, me_ref, block_ref, gain_ref, weight_ref, held, gain_out, weight_out, sems, other_sems
+):
+    copies = fetches(n, 0, count, (0, 1), me_ref[0], weight_ref, weight_out, sems)
+    copies = [
+        pltpu.make_async_copy(block_ref, held, other_sems.at[0]),
+        pltpu.make_async_copy(gain_ref, gain_out, other_sems.at[1]),
+    ] + copies
+    for copy in copies:
+        copy.start()
+    for copy in copies:
+        copy.wait()
+
+
+def add_products(n, first, base, core, me, ref, gain_ref, weight_ref, total, squares):
+    @pl.loop(0, ref.shape[0])
+    def _(entry):
+        shard = owner(me, first + entry, core, n)
+        values = ref[entry].astype(F32)
+        squares[...] += values * values
+        scaled = (values * gain_ref[shard]).astype(BF16)
+        total[...] += jnp.dot(scaled, weight_ref[base + entry], preferred_element_type=F32)
+
+
+def open_kernel(
+    n, me_ref, mine_ref, other_ref, gain_ref, held_ref, weight_ref, total, squares, later_ref, sems
+):
     me = me_ref[0]
-    half, rows, part = mine_ref.shape
-    columns = weight_ref.shape[1]
-    blocks = columns // 128
-    squares = jnp.zeros((rows, part), F32)
-    for entry in range(half):
-        for ref in (mine_ref, other_ref):
-            values = ref[entry].astype(F32)
-            squares = squares + values * values
-    mean = jnp.sum(squares, axis=1, keepdims=True) * (1.0 / (n * part))
+    outer = mine_ref.shape[0]
+    copies = fetches(n, outer, n // 2 - outer, (0, 1), me, weight_ref, later_ref, sems)
+    for copy in copies:
+        copy.start()
+    total[...] = jnp.zeros_like(total)
+    squares[...] = jnp.zeros_like(squares)
+    for core, ref in ((0, mine_ref), (1, other_ref)):
+        add_products(n, 0, core * outer, core, me, ref, gain_ref, held_ref, total, squares)
+    for copy in copies:
+        copy.wait()
+
+
+def more_kernel(
+    n, first, base, core, me_ref, block_ref, gain_ref, weight_ref, total_in, squares_in, total, squares
+):
+    total[...] = total_in[...]
+    squares[...] = squares_in[...]
+    add_products(
+        n, first, base, core, me_ref[0], block_ref, gain_ref, weight_ref, total, squares
+    )
+
+
+def close_kernel(
+    n, first, base, core, me_ref, block_ref, gain_ref, weight_ref, total_in, squares_in, out_ref,
+    total, squares, spread,
+):
+    more_kernel(
+        n, first, base, core, me_ref, block_ref, gain_ref, weight_ref, total_in, squares_in,
+        total, squares,
+    )
+    rows, part = squares.shape
+    mean = jnp.sum(squares[...], axis=1, keepdims=True) * (1.0 / (n * part))
     factor = lax.rsqrt(mean + EPS)
-    total[...] = jnp.zeros_like(total)
-
-    @pl.loop(0, half)
-    def _(entry):
-        for core, ref in ((0, mine_ref), (1, other_ref)):
-            shard = owner(me, entry, core, n)
-            normed = (ref[entry].astype(F32) * factor * gain_ref[shard]).astype(BF16)
-            start = pl.multiple_of(shard * part, part)
-            total[...] += jnp.dot(
-                normed, weight_ref[pl.ds(start, part), :], preferred_element_type=F32
-            )
-
+    blocks = total.shape[1] // 128
     steps = rows // n
-    for step in range(steps):
-        for block in range(blocks):
-            spread[:, step * blocks + block, :] = total[
-                step * n : (step + 1) * n, block * 128 : (block + 1) * 128
-            ]
+    for block in range(blocks):
+        scaled = total[:, block * 128 : (block + 1) * 128] * factor
+        for step in range(steps):
+            spread[:, step * blocks + block, :] = scaled[step * n : (step + 1) * n]
     for target in range(n):
         out_ref[target] = spread[target, : steps * blocks, :].astype(BF16)
 
 
-def project(me, mine, other, gain, weight, n):
-    half, rows, part = mine.shape
+def project(me, block, gain, weight, n):
+    rows, part = block.shape
     columns = weight.shape[1]
     pieces = rows // n * (columns // 128)
+    outer, middle = radices(n)
     vmem = pl.BlockSpec(memory_space=pltpu.VMEM)
-    return pl.pallas_call(
-        functools.partial(project_kernel, n),
-        out_shape=jax.ShapeDtypeStruct((n, pieces, 128), BF16),
-        in_specs=[pl.BlockSpec(memory_space=pltpu.SMEM), vmem, vmem, vmem, vmem],
-        out_specs=vmem,
-        scratch_shapes=[
-            pltpu.VMEM((rows, columns), F32),
-            pltpu.VMEM((n, -(-pieces // 8) * 8, 128), F32),
-        ],
-        compiler_params=pltpu.CompilerParams(vmem_limit_bytes=VMEM_LIMIT),
-        cost_estimate=pl.CostEstimate(
-            flops=2 * rows * weight.shape[0] * columns, bytes_accessed=0, transcendentals=0
+    smem = pl.BlockSpec(memory_space=pltpu.SMEM)
+    hbm = pl.BlockSpec(memory_space=pltpu.HBM)
+    params = pltpu.CompilerParams(vmem_limit_bytes=VMEM_LIMIT)
+    sums = (jax.ShapeDtypeStruct((rows, columns), F32), jax.ShapeDtypeStruct((rows, part), F32))
+    now, later_count = 2 * outer, n - 2 * outer
+
+    held, gain, weight_now = pl.pallas_call(
+        functools.partial(fetch_kernel, n, outer),
+        out_shape=(
+            pltpu.VMEM(block.shape, BF16),
+            pltpu.VMEM(gain.shape, F32),
+            pltpu.VMEM((now, part, columns), BF16),
         ),
-    )(me, mine, other, gain, pltpu.with_memory_space_constraint(weight, pltpu.VMEM))
+        in_specs=[smem, hbm, hbm, hbm],
+        out_specs=(vmem,) * 3,
+        scratch_shapes=[pltpu.SemaphoreType.DMA((now,)), pltpu.SemaphoreType.DMA((2,))],
+        compiler_params=params,
+        cost_estimate=hint(5),
+    )(me, far(block), far(gain), far(weight))
+    row = outer_row(block, n, held)
+    later = [swap(row, n, m * 2) for m in range(1, middle)]
+    *partial, weight_later = pl.pallas_call(
+        functools.partial(open_kernel, n),
+        out_shape=sums + (pltpu.VMEM((later_count, part, columns), BF16),),
+        in_specs=[smem] + [vmem] * 4 + [hbm],
+        out_specs=(vmem,) * 3,
+        scratch_shapes=[pltpu.SemaphoreType.DMA((later_count,))],
+        compiler_params=params,
+        cost_estimate=hint(5),
+    )(
+        me, row, swap(row, n, 1), gain, pltpu.with_memory_space_constraint(weight_now, pltpu.VMEM),
+        far(weight),
+    )
+    later, partial = lax.optimization_barrier((later, partial))
+    weight_later = pltpu.with_memory_space_constraint(weight_later, pltpu.VMEM)
+    for m in range(1, middle):
+        across = swap(later[m - 1], n, 1)
+        for core, blocks in ((0, later[m - 1]), (1, across)):
+            last = m == middle - 1 and core == 1
+            spread = pltpu.VMEM((n, -(-pieces // 8) * 8, 128), F32)
+            base = core * (later_count // 2) + (m - 1) * outer
+            partial = pl.pallas_call(
+                functools.partial(close_kernel if last else more_kernel, n, m * outer, base, core),
+                out_shape=jax.ShapeDtypeStruct((n, pieces, 128), BF16) if last else sums,
+                in_specs=[smem] + [vmem] * 5,
+                out_specs=vmem if last else (vmem, vmem),
+                scratch_shapes=[pltpu.VMEM(x.shape, F32) for x in sums] + [spread] if last else (),
+                compiler_params=params,
+                cost_estimate=hint(2),
+            )(me, blocks, gain, weight_later, *partial)
+    return partial
 
 
 def attend_kernel(
@@ -201,6 +307,7 @@
         out_specs=vmem,
         scratch_shapes=[pltpu.VMEM((steps, sources * (pieces // steps), 128), F32)],
         compiler_params=pltpu.CompilerParams(vmem_limit_bytes=VMEM_LIMIT),
+        cost_estimate=hint(10),
     )(table, length, received, cos, sin, weights, gain, *held)
 
 
@@ -236,6 +343,29 @@
         ).astype(BF16)
 
 
+def keep_kernel(block_ref, from_ref, held, to_ref, sem):
+    copy = pltpu.make_async_copy(from_ref, to_ref, sem)
+    copy.start()
+    held[...] = block_ref[...]
+    copy.wait()
+
+
+def keep(block, weight):
+    vmem = pl.BlockSpec(memory_space=pltpu.VMEM)
+    return pl.pallas_call(
+        keep_kernel,
+        out_shape=(
+            jax.ShapeDtypeStruct(block.shape, block.dtype),
+            pltpu.VMEM(weight.shape, weight.dtype),
+        ),
+        in_specs=[vmem, pl.BlockSpec(memory_space=pltpu.HBM)],
+        out_specs=(vmem, vmem),
+        scratch_shapes=[pltpu.SemaphoreType.DMA],
+        compiler_params=pltpu.CompilerParams(vmem_limit_bytes=4 * 1024 * 1024),
+        cost_estimate=hint(3),
+    )(block, far(weight))
+
+
 def output(me, mine, other, inputs, weight, n):
     half, heads, width = mine.shape
     vmem = pl.BlockSpec(memory_space=pltpu.VMEM)
@@ -270,16 +400,17 @@
 ):
     steps, rows, part = inputs.shape
     me = lax.axis_index("gx").astype(jnp.int32).reshape(1)
-    mine, other = gather_blocks(inputs.reshape(steps * rows, part), n)
-    sent = project(me, mine, other, norm_gain.reshape(n, 1, part), qkv_weight, n)
+    block = inputs.reshape(steps * rows, part)
+    sent = project(me, block, norm_gain.reshape(n, 1, part), qkv_weight, n)
     received = lax.all_to_all(sent, "gx", 0, 0)
     cos, sin = angles(positions, steps)
     attended = attend(
         page_table, context_len, received, cos, sin, head_lambda.reshape(H, 1),
         head_gain.reshape(H, 2 * HD), key_one_pages, key_two_pages, value_pages,
     )
-    mine, other = gather_blocks(attended, n)
-    return output(me, mine, other, inputs, out_weight, n)
+    held, weight = keep(attended, out_weight)
+    mine, other = gather_blocks(attended, n, held)
+    return output(me, mine, other, inputs, weight, n)
 
 
 def rotary(vectors, cos, sin):
@@ -355,7 +486,7 @@
     def chosen(inputs, norm_gain, qkv_weight, *rest):
         aligned = inputs.shape[2] % 128 == 0 and qkv_weight.shape[1] % 128 == 0
         single = rest[6].shape[0] == 1
-        power = n >= 2 and n & (n - 1) == 0
+        power = n >= 4 and n & (n - 1) == 0
         body = local if aligned and single and power else local_any
         return body(n, inputs, norm_gain, qkv_weight, *rest)
 

time: 68.3 us -> 55.1 us (0.81)
  local copies, waits for them, and re-layouts: 14.6 us -> 0.16 us
  Pallas kernels: 10.2 us -> 22.4 us
  waiting for transfers between devices: 24.5 us -> 13.3 us
  starting transfers between devices: 16.1 us -> 17.2 us
  other arithmetic: 1.04 us -> 0.24 us
    unnamed x28 -> x18, local copies, waits for them, and re-layouts: 14.5 us -> 0.06 us
    pallas_call x1 -> x5, Pallas kernels: 6.21 us -> 18.3 us  [the longest x1 5.21 us: project(): pl.pallas_call(functools.partial(fetch_kernel, n, outer), out_shape=(pltp...]
    ppermute x10 -> x11, waiting for transfers between devices: 18.1 us -> 6.88 us  [swap(): return lax.ppermute(block, 'gx', [(i, i ^ mask) for i in range(n)])]
    all_to_all x1, starting transfers between devices: 3.51 us -> 5.09 us  [local(): received = lax.all_to_all(sent, 'gx', 0, 0)]
    another operation x2, other arithmetic: 0.84 us -> 0.04 us  [outer_row(): return jnp.stack([block if held is None else held] + arrived)]
    ppermute x10 -> x11, starting transfers between devices: 12.6 us -> 12.1 us  [swap(): return lax.ppermute(block, 'gx', [(i, i ^ mask) for i in range(n)])]
  transfers between devices with their start and end apart: 11 -> 12, of which waited for: 9 -> 4; matrix products, arithmetic and copies ran while one was open for 2% -> 1% of each run, Pallas kernels for 0% -> 29%
where the time goes in v2:
time: 55.1 us; the launch traced here: 54.9 us
  Pallas kernels  22.4 us (41%)
  starting transfers between devices  17.2 us (31%)
  waiting for transfers between devices  13.3 us (24%)
  between operations  1.59 us (3%)
    ppermute x11, starting transfers between devices, swap(): return lax.ppermute(block, 'gx', [(i, i ^ mask) for i in range(n)])  12.1 us
    ppermute x11, waiting for transfers between devices, swap(): return lax.ppermute(block, 'gx', [(i, i ^ mask) for i in range(n)])  6.88 us
    all_to_all x1, waiting for transfers between devices, local(): received = lax.all_to_all(sent, 'gx', 0, 0)  6.45 us
    pallas_call x1, Pallas kernels, project(): pl.pallas_call(functools.partial(fetch_kernel, n, outer), out_shape=(pltp...  5.21 us
    pallas_call x1, Pallas kernels, project(): pl.pallas_call(functools.partial(open_kernel, n), out_shape=sums + (pltpu...  5.17 us
    all_to_all x1, starting transfers between devices, local(): received = lax.all_to_all(sent, 'gx', 0, 0)  5.09 us
    pallas_call x2, Pallas kernels, project(): pl.pallas_call(functools.partial(close_kernel if last else more_kernel, n...  4.27 us
    pallas_call x1, Pallas kernels, keep(): pl.pallas_call(keep_kernel, out_shape=(jax.ShapeDtypeStruct(block.shape,...  3.69 us
  transfers between devices with their start and end apart: 12, of which 4 were waited for; matrix products, arithmetic and copies ran while one was open for 1% of the time, Pallas kernels for 29%

profile of v2, /device:TPU:0, one launch (start us, length us, event | category | flops | bytes accessed | tf_op | source)
XLA Modules:
  0.0 54.9 jit_solution(1635166722845791388)
XLA Ops:
  0.0 3.0 %collective-permute-start = (bf16[32,768]{1,0:T(8,128)(2,1)}, bf16[32,768]{1,0:T(8,128)(2,1)S(1)}, u32[]{:S(2)}, u32[]{:S(2)}) collective-permute-start(bf16[32,768]{1,0:T(8,128)(2,1)} %bitcast.22), channel_id=1, source_target_pairs={{0,4},{1,5},{2,6},{3,7},{4,0},{5,1},{6,2},{7,3},{8,12},{9,13},{10,... | collective-permute-start | bytes 147464 | tf_op jit(solution)/shard_map/ppermute | solution.py:29
  3.0 2.6 %collective-permute-start.1 = (bf16[32,768]{1,0:T(8,128)(2,1)}, bf16[32,768]{1,0:T(8,128)(2,1)S(1)}, u32[]{:S(2)}, u32[]{:S(2)}) collective-permute-start(bf16[32,768]{1,0:T(8,128)(2,1)} %bitcast.23), channel_id=1, source_target_pairs={{0,8},{1,9},{2,10},{3,11},{4,12},{5,13},{6,14},{7,15},{8,0},{9,1},... | collective-permute-start | bytes 147464 | tf_op jit(solution)/shard_map/ppermute | solution.py:29
  5.6 5.2 %shard_map.118 = (bf16[32,768]{1,0:T(8,128)(2,1)S(1)}, f32[16,1,768]{2,1,0:T(1,128)S(1)}, bf16[8,768,1152]{2,1,0:T(8,128)(2,1)S(1)}) custom-call(s32[1]{0:T(128)} %bitcast.me_ref, bf16[32,768]{1,0:T(8,128)(2,1)} %bitcast.25, f32[16,1,768]{2,1,0:T(1,128)} %bitcast.33, bf16[12288,1152]{1,0:T(8,128)(2,1)} %weight_ref.3), custom_call_target="tpu_custom_call" | custom-call | bytes 15000000 | tf_op jit(solution)/shard_map/pallas_call | solution.py:159
  10.9 0.9 %collective-permute-done.2 = bf16[32,768]{1,0:T(8,128)(2,1)S(1)} collective-permute-done((bf16[32,768]{1,0:T(8,128)(2,1)}, bf16[32,768]{1,0:T(8,128)(2,1)S(1)}, u32[]{:S(2)}, u32[]{:S(2)}) %collective-permute-start.2) | collective-permute-done | bytes 49184 | tf_op jit(solution)/shard_map/ppermute | solution.py:29
  11.7 0.1 collective-permute-start.4
  11.8 1.6 %collective-permute-start.3 = (bf16[4,32,768]{2,1,0:T(8,128)(2,1)S(1)}, bf16[4,32,768]{2,1,0:T(8,128)(2,1)S(1)}, u32[]{:S(2)}, u32[]{:S(2)}) collective-permute-start(bf16[4,32,768]{2,1,0:T(8,128)(2,1)S(1)} %pad_maximum_fusion.mine_ref), channel_id=1, source_target_pairs={{0,2},{1,3},{2,0},{3,1},{4,6},{5,7},{6,4},{7,5},{8,10},{9,11},{10,... | collective-permute-start | bytes 589832 | tf_op jit(solution)/shard_map/ppermute | solution.py:29
  14.1 5.2 %shard_map.119 = (f32[32,1152]{1,0:T(8,128)S(1)}, f32[32,768]{1,0:T(8,128)S(1)}, bf16[8,768,1152]{2,1,0:T(8,128)(2,1)S(1)}) custom-call(s32[1]{0:T(128)} %bitcast.me_ref, bf16[4,32,768]{2,1,0:T(8,128)(2,1)S(1)} %pad_maximum_fusion.mine_ref, bf16[4,32,768]{2,1,0:T(8,128)(2,1)S(1)} %collective-permute-done.4.other_ref, ...), custom_call_target="tpu_custom_call" | custom-call | bytes 15000000 | tf_op jit(solution)/shard_map/pallas_call | solution.py:174
  19.3 0.2 collective-permute-start.5
  19.6 1.7 %shard_map.120 = (f32[32,1152]{1,0:T(8,128)S(1)}, f32[32,768]{1,0:T(8,128)S(1)}) custom-call(s32[1]{0:T(128)} %bitcast.me_ref, bf16[4,32,768]{2,1,0:T(8,128)(2,1)S(1)} %collective-permute-done.3.block_ref, f32[16,1,768]{2,1,0:T(1,128)S(1)} %get-tuple-element.19.gain_ref, bf16[8,768,1152]{2,1,0:T(8,128)(2,1)S(1)} %get-tuple-element.24.weight_ref, ...), custom_call_target="tpu_custom_call" | custom-call | bytes 6000000 | tf_op jit(solution)/shard_map/pallas_call | solution.py:194
  21.3 2.6 %shard_map.121 = bf16[16,18,128]{2,1,0:T(8,128)(2,1)} custom-call(s32[1]{0:T(128)} %bitcast.me_ref, bf16[4,32,768]{2,1,0:T(8,128)(2,1)S(1)} %collective-permute-done.5.block_ref, f32[16,1,768]{2,1,0:T(1,128)S(1)} %get-tuple-element.19.gain_ref, bf16[8,768,1152]{2,1,0:T(8,128)(2,1)S(1)} %get-tuple-element.24.weight_ref, ...), custom_call_target="tpu_custom_call" | custom-call | bytes 6000000 | tf_op jit(solution)/shard_map/pallas_call | solution.py:194
  23.9 5.1 %all-to-all-start = ((bf16[16,18,128]{2,1,0:T(8,128)(2,1)}), bf16[16,18,128]{2,1,0:T(8,128)(2,1)S(1)}, u32[]{:S(2)}, u32[]{:S(2)}) async-start(bf16[16,18,128]{2,1,0:T(8,128)(2,1)} %shard_map.121), calls=%async_computation | async-start | bytes 196608 | tf_op jit(solution)/shard_map/all_to_all | solution.py:405
  29.0 0.1 fusion
  29.1 0.1 copy.14.lambda_ref
  29.9 0.1 pad_maximum_fusion.2
  29.9 6.4 %all-to-all-done.received_ref = bf16[16,18,128]{2,1,0:T(8,128)(2,1)S(1)} async-done(((bf16[16,18,128]{2,1,0:T(8,128)(2,1)}), bf16[16,18,128]{2,1,0:T(8,128)(2,1)S(1)}, u32[]{:S(2)}, u32[]{:S(2)}) %all-to-all-start) | async-done | bytes 73760 | tf_op jit(solution)/shard_map/all_to_all | solution.py:405
  36.4 1.7 %shard_map.122.block_ref = bf16[48,256]{1,0:T(8,128)(2,1)S(1)} custom-call(s32[1,6]{1,0:T(1,128)S(1)} %copy-done.4, s32[1]{0:T(128)S(6)} %copy.19.length_ref, bf16[16,18,128]{2,1,0:T(8,128)(2,1)S(1)} %all-to-all-done.received_ref, f32[2,1,128]{2,1,0:T(1,128)S(1)} %bitcast.28, f32[2,1,128]{2,1,0:T(1,128)S(1)} %bitcast.29, f32[24,1]{1,0:T(8,128)S(1)} %copy.14.lambda_ref, ...), custom_call_target="tpu_custom_call" | custom-call | bytes 30000000 | tf_op jit(solution)/shard_map/pallas_call | solution.py:303
  38.1 0.1 collective-permute-start.6
  38.2 1.2 %collective-permute-start.7 = (bf16[48,256]{1,0:T(8,128)(2,1)S(1)}, bf16[48,256]{1,0:T(8,128)(2,1)S(1)}, u32[]{:S(2)}, u32[]{:S(2)}) collective-permute-start(bf16[48,256]{1,0:T(8,128)(2,1)S(1)} %shard_map.122.block_ref), channel_id=1, source_target_pairs={{0,8},{1,9},{2,10},{3,11},{4,12},{5,13},{6,14},{7,15},{8,0},{9,1},... | collective-permute-start | bytes 73736 | tf_op jit(solution)/shard_map/ppermute | solution.py:29
  39.3 3.2 %collective-permute-start.8 = (bf16[48,256]{1,0:T(8,128)(2,1)S(1)}, bf16[48,256]{1,0:T(8,128)(2,1)S(1)}, u32[]{:S(2)}, u32[]{:S(2)}) collective-permute-start(bf16[48,256]{1,0:T(8,128)(2,1)S(1)} %shard_map.122.block_ref), channel_id=1, source_target_pairs={{0,12},{1,13},{2,14},{3,15},{4,8},{5,9},{6,10},{7,11},{8,4},{9,5},... | collective-permute-start | bytes 73736 | tf_op jit(solution)/shard_map/ppermute | solution.py:29
  42.5 3.7 %shard_map.123 = (bf16[48,256]{1,0:T(8,128)(2,1)S(1)}, bf16[6144,768]{1,0:T(8,128)(2,1)S(1)}) custom-call(bf16[48,256]{1,0:T(8,128)(2,1)S(1)} %shard_map.122.block_ref, bf16[6144,768]{1,0:T(8,128)(2,1)} %from_ref.1), custom_call_target="tpu_custom_call" | custom-call | bytes 9000000 | tf_op jit(solution)/shard_map/pallas_call | solution.py:355
  46.3 0.1 collective-permute-start.9
  46.4 4.6 %collective-permute-done.9 = bf16[4,48,256]{2,1,0:T(8,128)(2,1)S(1)} collective-permute-done((bf16[4,48,256]{2,1,0:T(8,128)(2,1)S(1)}, bf16[4,48,256]{2,1,0:T(8,128)(2,1)S(1)}, u32[]{:S(2)}, u32[]{:S(2)}) %collective-permute-start.9) | collective-permute-done | bytes 98336 | tf_op jit(solution)/shard_map/ppermute | solution.py:29
  51.1 1.4 %collective-permute-done.10.other_ref = bf16[8,48,256]{2,1,0:T(8,128)(2,1)S(1)} collective-permute-done((bf16[8,48,256]{2,1,0:T(8,128)(2,1)S(1)}, bf16[8,48,256]{2,1,0:T(8,128)(2,1)S(1)}, u32[]{:S(2)}, u32[]{:S(2)}) %collective-permute-start.10) | collective-permute-done | bytes 196640 | tf_op jit(solution)/shard_map/ppermute | solution.py:29
  52.5 2.4 %shard_map.124 = bf16[2,16,768]{2,1,0:T(8,128)(2,1)} custom-call(s32[1]{0:T(128)} %bitcast.me_ref, bf16[8,48,256]{2,1,0:T(8,128)(2,1)S(1)} %constant_dynamic-update-slice_fusion.mine_ref, bf16[8,48,256]{2,1,0:T(8,128)(2,1)S(1)} %collective-permute-done.10.other_ref, bf16[2,16,768]{2,1,0:T(8,128)(2,1)S(1)} %copy-done.3, ...), custom_call_target="tpu_custom_call" | custom-call | tf_op jit(solution)/shard_map/pallas_call | solution.py:373
  (34 shorter events, 0.2 us)
Async XLA Ops:
  0.0 10.8 %collective-permute-start = (bf16[32,768]{1,0:T(8,128)(2,1)}, bf16[32,768]{1,0:T(8,128)(2,1)S(1)}, u32[]{:S(2)}, u32[]{:S(2)}) collective-permute-start(bf16[32,768]{1,0:T(8,128)(2,1)} %bitcast.22), channel_id=1, source_target_pairs={{0,4},{1,5},{2,6},{3,7},{4,0},{5,1},{6,2},{7,3},{8,12},{9,13},{10,... | collective-permute-start | bytes 147464 | tf_op jit(solution)/shard_map/ppermute | solution.py:29
  3.0 7.8 %collective-permute-start.1 = (bf16[32,768]{1,0:T(8,128)(2,1)}, bf16[32,768]{1,0:T(8,128)(2,1)S(1)}, u32[]{:S(2)}, u32[]{:S(2)}) collective-permute-start(bf16[32,768]{1,0:T(8,128)(2,1)} %bitcast.23), channel_id=1, source_target_pairs={{0,8},{1,9},{2,10},{3,11},{4,12},{5,13},{6,14},{7,15},{8,0},{9,1},... | collective-permute-start | bytes 147464 | tf_op jit(solution)/shard_map/ppermute | solution.py:29
  5.6 6.1 %collective-permute-start.2 = (bf16[32,768]{1,0:T(8,128)(2,1)}, bf16[32,768]{1,0:T(8,128)(2,1)S(1)}, u32[]{:S(2)}, u32[]{:S(2)}) collective-permute-start(bf16[32,768]{1,0:T(8,128)(2,1)} %bitcast.24), channel_id=1, source_target_pairs={{0,12},{1,13},{2,14},{3,15},{4,8},{5,9},{6,10},{7,11},{8,4},{9,5},... | collective-permute-start | bytes 147464 | tf_op jit(solution)/shard_map/ppermute | solution.py:29
  11.7 2.3 %collective-permute-start.4 = (bf16[4,32,768]{2,1,0:T(8,128)(2,1)S(1)}, bf16[4,32,768]{2,1,0:T(8,128)(2,1)S(1)}, u32[]{:S(2)}, u32[]{:S(2)}) collective-permute-start(bf16[4,32,768]{2,1,0:T(8,128)(2,1)S(1)} %pad_maximum_fusion.mine_ref), channel_id=1, source_target_pairs={{0,1},{1,0},{2,3},{3,2},{4,5},{5,4},{6,7},{7,6},{8,9},{9,8},{10,11... | collective-permute-start | bytes 589832 | tf_op jit(solution)/shard_map/ppermute | solution.py:29
  11.8 7.4 %collective-permute-start.3 = (bf16[4,32,768]{2,1,0:T(8,128)(2,1)S(1)}, bf16[4,32,768]{2,1,0:T(8,128)(2,1)S(1)}, u32[]{:S(2)}, u32[]{:S(2)}) collective-permute-start(bf16[4,32,768]{2,1,0:T(8,128)(2,1)S(1)} %pad_maximum_fusion.mine_ref), channel_id=1, source_target_pairs={{0,2},{1,3},{2,0},{3,1},{4,6},{5,7},{6,4},{7,5},{8,10},{9,11},{10,... | collective-permute-start | bytes 589832 | tf_op jit(solution)/shard_map/ppermute | solution.py:29
  19.3 2.1 %collective-permute-start.5 = (bf16[4,32,768]{2,1,0:T(8,128)(2,1)S(1)}, bf16[4,32,768]{2,1,0:T(8,128)(2,1)S(1)}, u32[]{:S(2)}, u32[]{:S(2)}) collective-permute-start(bf16[4,32,768]{2,1,0:T(8,128)(2,1)S(1)} %collective-permute-done.3.block_ref), channel_id=1, source_target_pairs={{0,1},{1,0},{2,3},{3,2},{4,5},{5,4},{6,7},{7,6},{8,9},{9,8},{10,11... | collective-permute-start | bytes 589832 | tf_op jit(solution)/shard_map/ppermute | solution.py:29
  19.5 9.6 %copy-start.5 = (f32[6144]{0:T(1024)S(1)}, f32[6144]{0:T(1024)}, u32[]{:S(2)}) copy-start(f32[6144]{0:T(1024)} %param.16) | copy-start | bytes 73732
  19.5 9.6 %copy-start.6 = (f32[24]{0:T(128)S(1)}, f32[24]{0:T(128)}, u32[]{:S(2)}) copy-start(f32[24]{0:T(128)} %param.15) | copy-start | bytes 292
  19.5 16.9 %copy-start = (bf16[6,16,6144]{2,1,0:T(8,128)(2,1)S(1)}, bf16[6,16,6144]{2,1,0:T(8,128)(2,1)}, u32[]{:S(2)}) copy-start(bf16[6,16,6144]{2,1,0:T(8,128)(2,1)} %values_ref.1) | copy-start | bytes 3538948
  19.5 16.8 %copy-start.1 = (bf16[6,16,3072]{2,1,0:T(8,128)(2,1)S(1)}, bf16[6,16,3072]{2,1,0:T(8,128)(2,1)}, u32[]{:S(2)}) copy-start(bf16[6,16,3072]{2,1,0:T(8,128)(2,1)} %keys_one_ref.1) | copy-start | bytes 1769476
  19.5 16.8 %copy-start.2 = (bf16[6,16,3072]{2,1,0:T(8,128)(2,1)S(1)}, bf16[6,16,3072]{2,1,0:T(8,128)(2,1)}, u32[]{:S(2)}) copy-start(bf16[6,16,3072]{2,1,0:T(8,128)(2,1)} %keys_two_ref.1) | copy-start | bytes 1769476
  19.6 16.8 %copy-start.4 = (s32[1,6]{1,0:T(1,128)S(1)}, s32[1,6]{1,0:T(1,128)}, u32[]{:S(2)}) copy-start(s32[1,6]{1,0:T(1,128)} %table_ref.1) | copy-start | bytes 76
  21.3 31.2 %copy-start.3 = (bf16[2,16,768]{2,1,0:T(8,128)(2,1)S(1)}, bf16[2,16,768]{2,1,0:T(8,128)(2,1)}, u32[]{:S(2)}) copy-start(bf16[2,16,768]{2,1,0:T(8,128)(2,1)} %inputs_ref.1) | copy-start | bytes 147460
  23.9 12.5 %all-to-all-start = ((bf16[16,18,128]{2,1,0:T(8,128)(2,1)}), bf16[16,18,128]{2,1,0:T(8,128)(2,1)S(1)}, u32[]{:S(2)}, u32[]{:S(2)}) async-start(bf16[16,18,128]{2,1,0:T(8,128)(2,1)} %shard_map.121), calls=%async_computation | async-start | bytes 196608 | tf_op jit(solution)/shard_map/all_to_all | solution.py:405
  38.1 8.2 %collective-permute-start.6 = (bf16[48,256]{1,0:T(8,128)(2,1)S(1)}, bf16[48,256]{1,0:T(8,128)(2,1)S(1)}, u32[]{:S(2)}, u32[]{:S(2)}) collective-permute-start(bf16[48,256]{1,0:T(8,128)(2,1)S(1)} %shard_map.122.block_ref), channel_id=1, source_target_pairs={{0,4},{1,5},{2,6},{3,7},{4,0},{5,1},{6,2},{7,3},{8,12},{9,13},{10,... | collective-permute-start | bytes 73736 | tf_op jit(solution)/shard_map/ppermute | solution.py:29
  38.2 8.1 %collective-permute-start.7 = (bf16[48,256]{1,0:T(8,128)(2,1)S(1)}, bf16[48,256]{1,0:T(8,128)(2,1)S(1)}, u32[]{:S(2)}, u32[]{:S(2)}) collective-permute-start(bf16[48,256]{1,0:T(8,128)(2,1)S(1)} %shard_map.122.block_ref), channel_id=1, source_target_pairs={{0,8},{1,9},{2,10},{3,11},{4,12},{5,13},{6,14},{7,15},{8,0},{9,1},... | collective-permute-start | bytes 73736 | tf_op jit(solution)/shard_map/ppermute | solution.py:29
  39.3 6.9 %collective-permute-start.8 = (bf16[48,256]{1,0:T(8,128)(2,1)S(1)}, bf16[48,256]{1,0:T(8,128)(2,1)S(1)}, u32[]{:S(2)}, u32[]{:S(2)}) collective-permute-start(bf16[48,256]{1,0:T(8,128)(2,1)S(1)} %shard_map.122.block_ref), channel_id=1, source_target_pairs={{0,12},{1,13},{2,14},{3,15},{4,8},{5,9},{6,10},{7,11},{8,4},{9,5},... | collective-permute-start | bytes 73736 | tf_op jit(solution)/shard_map/ppermute | solution.py:29
  46.3 4.7 %collective-permute-start.9 = (bf16[4,48,256]{2,1,0:T(8,128)(2,1)S(1)}, bf16[4,48,256]{2,1,0:T(8,128)(2,1)S(1)}, u32[]{:S(2)}, u32[]{:S(2)}) collective-permute-start(bf16[4,48,256]{2,1,0:T(8,128)(2,1)S(1)} %pad_maximum_fusion.1), channel_id=1, source_target_pairs={{0,2},{1,3},{2,0},{3,1},{4,6},{5,7},{6,4},{7,5},{8,10},{9,11},{10,... | collective-permute-start | bytes 294920 | tf_op jit(solution)/shard_map/ppermute | solution.py:29
  51.0 1.5 %collective-permute-start.10 = (bf16[8,48,256]{2,1,0:T(8,128)(2,1)S(1)}, bf16[8,48,256]{2,1,0:T(8,128)(2,1)S(1)}, u32[]{:S(2)}, u32[]{:S(2)}) collective-permute-start(bf16[8,48,256]{2,1,0:T(8,128)(2,1)S(1)} %constant_dynamic-update-slice_fusion.mine_ref), channel_id=1, source_target_pairs={{0,1},{1,0},{2,3},{3,2},{4,5},{5,4},{6,7},{7,6},{8,9},{9,8},{10,11... | collective-permute-start | bytes 589832 | tf_op jit(solution)/shard_map/ppermute | solution.py:29

commit v3 on v2

--- a/solution.py
+++ b/solution.py
@@ -29,16 +29,13 @@
     return lax.ppermute(block, "gx", [(i, i ^ mask) for i in range(n)])
 
 
-def outer_row(block, n, held=None):
+def gather_blocks(block, n, first_aside, second_aside):
     outer, middle = radices(n)
     arrived = [swap(block, n, o * 2 * middle) for o in range(1, outer)]
-    return jnp.stack([block if held is None else held] + arrived)
-
-
-def gather_blocks(block, n, held=None):
-    _, middle = radices(n)
-    rows = outer_row(block, n, held)
-    mine = jnp.concatenate([rows] + [swap(rows, n, m * 2) for m in range(1, middle)])
+    rows = jnp.stack([first_aside(block)] + arrived)
+    others = [swap(rows, n, m * 2) for m in range(1, middle)]
+    rows, others = lax.optimization_barrier((second_aside(rows), others))
+    mine = jnp.concatenate([rows] + others)
     return mine, swap(mine, n, 1)
 
 
@@ -73,64 +70,125 @@
     return copies
 
 
+def slots(n):
+    outer, middle = radices(n)
+    return [
+        (m * outer + entry, core) for m in range(middle) for core in range(2) for entry in range(outer)
+    ]
+
+
+def fetches(n, order, me, from_ref, to_ref, sems):
+    part = from_ref.shape[0] // n
+    copies = []
+    for slot, (entry, core) in enumerate(order):
+        start = pl.multiple_of(owner(me, entry, core, n) * part, part)
+        copies.append(
+            pltpu.make_async_copy(
+                from_ref.at[pl.ds(start, part), :], to_ref.at[slot], sems.at[slot]
+            )
+        )
+    return copies
+
+
 def fetch_kernel(
-    n, count, me_ref, block_ref, gain_ref, weight_ref, held, gain_out, weight_out, sems, other_sems
+    n, order, me_ref, block_ref, gain_ref, weight_ref, held, gain_out, weight_out, sems, other_sems
 ):
-    copies = fetches(n, 0, count, (0, 1), me_ref[0], weight_ref, weight_out, sems)
     copies = [
         pltpu.make_async_copy(block_ref, held, other_sems.at[0]),
         pltpu.make_async_copy(gain_ref, gain_out, other_sems.at[1]),
-    ] + copies
+    ] + fetches(n, order, me_ref[0], weight_ref, weight_out, sems)
     for copy in copies:
         copy.start()
     for copy in copies:
         copy.wait()
 
 
-def add_products(n, first, base, core, me, ref, gain_ref, weight_ref, total, squares):
-    @pl.loop(0, ref.shape[0])
-    def _(entry):
-        shard = owner(me, first + entry, core, n)
-        values = ref[entry].astype(F32)
-        squares[...] += values * values
-        scaled = (values * gain_ref[shard]).astype(BF16)
-        total[...] += jnp.dot(scaled, weight_ref[base + entry], preferred_element_type=F32)
-
-
-def open_kernel(
-    n, me_ref, mine_ref, other_ref, gain_ref, held_ref, weight_ref, total, squares, later_ref, sems
-):
+def fetch(me, block, gain, weight, n, order):
+    part, columns = weight.shape[0] // n, weight.shape[1]
+    vmem = pl.BlockSpec(memory_space=pltpu.VMEM)
+    hbm = pl.BlockSpec(memory_space=pltpu.HBM)
+    return pl.pallas_call(
+        functools.partial(fetch_kernel, n, order),
+        out_shape=(
+            pltpu.VMEM(block.shape, BF16),
+            pltpu.VMEM(gain.shape, F32),
+            pltpu.VMEM((len(order), part, columns), BF16),
+        ),
+        in_specs=[pl.BlockSpec(memory_space=pltpu.SMEM), hbm, hbm, hbm],
+        out_specs=(vmem,) * 3,
+        scratch_shapes=[
+            pltpu.SemaphoreType.DMA((len(order),)),
+            pltpu.SemaphoreType.DMA((2,)),
+        ],
+        compiler_params=pltpu.CompilerParams(vmem_limit_bytes=4 * 1024 * 1024),
+        cost_estimate=hint(5),
+    )(me, far(block), far(gain), far(weight))
+
+
+def near(x):
+    return pltpu.with_memory_space_constraint(x, pltpu.VMEM)
+
+
+def add_products(n, order, me, refs, gain_ref, weights, total, squares):
+    rows = total.shape[0]
+    sums = None
+    square = squares[...]
+    for (entry, core), ref, (held, slot) in zip(order, refs, weights, strict=True):
+        values = ref[...].astype(F32)
+        square = square + values * values
+        scaled = values * gain_ref[owner(me, entry, core, n)]
+        high = scaled.astype(BF16)
+        low = (scaled - high.astype(F32)).astype(BF16)
+        product = jnp.dot(
+            jnp.concatenate([high, low], axis=0), held[slot], preferred_element_type=F32
+        )
+        sums = product if sums is None else sums + product
+    squares[...] = square
+    total[...] += sums[:rows] + sums[rows:]
+
+
+def open_kernel(n, cuts, me_ref, mine_ref, other_ref, gain_ref, weight_ref, *rest):
+    *helds, total, squares, later_ref, sems = rest
     me = me_ref[0]
     outer = mine_ref.shape[0]
-    copies = fetches(n, outer, n // 2 - outer, (0, 1), me, weight_ref, later_ref, sems)
+    order = slots(n)
+    copies = fetches(n, order[cuts[-1] :], me, weight_ref, later_ref, sems)
     for copy in copies:
         copy.start()
     total[...] = jnp.zeros_like(total)
     squares[...] = jnp.zeros_like(squares)
-    for core, ref in ((0, mine_ref), (1, other_ref)):
-        add_products(n, 0, core * outer, core, me, ref, gain_ref, held_ref, total, squares)
+    refs = [mine_ref.at[e] for e in range(outer)] + [other_ref.at[e] for e in range(outer)]
+    add_products(
+        n, order[: 2 * outer], me, refs, gain_ref, places(helds, cuts)[: 2 * outer], total, squares
+    )
     for copy in copies:
         copy.wait()
 
 
+def places(helds, cuts):
+    found = []
+    for held, start, stop in zip(helds, (0,) + cuts[:-1], cuts, strict=True):
+        found += [(held, slot) for slot in range(stop - start)]
+    return found
+
+
 def more_kernel(
-    n, first, base, core, me_ref, block_ref, gain_ref, weight_ref, total_in, squares_in, total, squares
+    n, cuts, first, me_ref, block_ref, gain_ref, *rest,
 ):
+    *helds, total_in, squares_in, total, squares = rest
     total[...] = total_in[...]
     squares[...] = squares_in[...]
+    outer = block_ref.shape[0]
+    picked = slice(first, first + outer)
     add_products(
-        n, first, base, core, me_ref[0], block_ref, gain_ref, weight_ref, total, squares
-    )
-
-
-def close_kernel(
-    n, first, base, core, me_ref, block_ref, gain_ref, weight_ref, total_in, squares_in, out_ref,
-    total, squares, spread,
-):
-    more_kernel(
-        n, first, base, core, me_ref, block_ref, gain_ref, weight_ref, total_in, squares_in,
-        total, squares,
-    )
+        n, slots(n)[picked], me_ref[0], [block_ref.at[e] for e in range(outer)], gain_ref,
+        places(helds, cuts)[picked], total, squares,
+    )
+
+
+def close_kernel(n, cuts, first, me_ref, block_ref, gain_ref, *rest):
+    *refs, out_ref, total, squares, spread = rest
+    more_kernel(n, cuts, first, me_ref, block_ref, gain_ref, *refs, total, squares)
     rows, part = squares.shape
     mean = jnp.sum(squares[...], axis=1, keepdims=True) * (1.0 / (n * part))
     factor = lax.rsqrt(mean + EPS)
@@ -154,52 +212,42 @@
     hbm = pl.BlockSpec(memory_space=pltpu.HBM)
     params = pltpu.CompilerParams(vmem_limit_bytes=VMEM_LIMIT)
     sums = (jax.ShapeDtypeStruct((rows, columns), F32), jax.ShapeDtypeStruct((rows, part), F32))
-    now, later_count = 2 * outer, n - 2 * outer
-
-    held, gain, weight_now = pl.pallas_call(
-        functools.partial(fetch_kernel, n, outer),
-        out_shape=(
-            pltpu.VMEM(block.shape, BF16),
-            pltpu.VMEM(gain.shape, F32),
-            pltpu.VMEM((now, part, columns), BF16),
-        ),
-        in_specs=[smem, hbm, hbm, hbm],
+    order = slots(n)
+    cut = 2 * outer
+    cuts = (cut,)
+
+    arrived = [swap(block, n, o * 2 * middle) for o in range(1, outer)]
+    held, gain_held, weight_now = fetch(me, block, gain, weight, n, order[:cut])
+    row = jnp.stack([held] + arrived)
+    later = [swap(row, n, m * 2) for m in range(1, middle)]
+    helds = (near(weight_now),)
+    *partial, weight_later = pl.pallas_call(
+        functools.partial(open_kernel, n, cuts),
+        out_shape=sums + (pltpu.VMEM((n - cut, part, columns), BF16),),
+        in_specs=[smem] + [vmem] * 3 + [hbm, vmem],
         out_specs=(vmem,) * 3,
-        scratch_shapes=[pltpu.SemaphoreType.DMA((now,)), pltpu.SemaphoreType.DMA((2,))],
+        scratch_shapes=[pltpu.SemaphoreType.DMA((n - cut,))],
         compiler_params=params,
         cost_estimate=hint(5),
-    )(me, far(block), far(gain), far(weight))
-    row = outer_row(block, n, held)
-    later = [swap(row, n, m * 2) for m in range(1, middle)]
-    *partial, weight_later = pl.pallas_call(
-        functools.partial(open_kernel, n),
-        out_shape=sums + (pltpu.VMEM((later_count, part, columns), BF16),),
-        in_specs=[smem] + [vmem] * 4 + [hbm],
-        out_specs=(vmem,) * 3,
-        scratch_shapes=[pltpu.SemaphoreType.DMA((later_count,))],
-        compiler_params=params,
-        cost_estimate=hint(5),
-    )(
-        me, row, swap(row, n, 1), gain, pltpu.with_memory_space_constraint(weight_now, pltpu.VMEM),
-        far(weight),
-    )
+    )(me, row, swap(row, n, 1), gain_held, far(weight), *helds)
     later, partial = lax.optimization_barrier((later, partial))
-    weight_later = pltpu.with_memory_space_constraint(weight_later, pltpu.VMEM)
+    helds += (near(weight_later),)
+    cuts += (n,)
     for m in range(1, middle):
         across = swap(later[m - 1], n, 1)
         for core, blocks in ((0, later[m - 1]), (1, across)):
             last = m == middle - 1 and core == 1
             spread = pltpu.VMEM((n, -(-pieces // 8) * 8, 128), F32)
-            base = core * (later_count // 2) + (m - 1) * outer
+            first = (2 * m + core) * outer
             partial = pl.pallas_call(
-                functools.partial(close_kernel if last else more_kernel, n, m * outer, base, core),
+                functools.partial(close_kernel if last else more_kernel, n, cuts, first),
                 out_shape=jax.ShapeDtypeStruct((n, pieces, 128), BF16) if last else sums,
-                in_specs=[smem] + [vmem] * 5,
+                in_specs=[smem] + [vmem] * 6,
                 out_specs=vmem if last else (vmem, vmem),
                 scratch_shapes=[pltpu.VMEM(x.shape, F32) for x in sums] + [spread] if last else (),
                 compiler_params=params,
                 cost_estimate=hint(2),
-            )(me, blocks, gain, weight_later, *partial)
+            )(me, blocks, gain_held, *helds, *partial)
     return partial
 
 
@@ -299,7 +347,7 @@
     sources, pieces, _ = received.shape
     vmem = pl.BlockSpec(memory_space=pltpu.VMEM)
     smem = pl.BlockSpec(memory_space=pltpu.SMEM)
-    held = [pltpu.with_memory_space_constraint(x, pltpu.VMEM) for x in (keys_one, keys_two, values)]
+    held = [near(x) for x in (keys_one, keys_two, values)]
     return pl.pallas_call(
         attend_kernel,
         out_shape=jax.ShapeDtypeStruct((steps * H, 2 * HD), BF16),
@@ -311,7 +359,8 @@
     )(table, length, received, cos, sin, weights, gain, *held)
 
 
-def output_kernel(n, me_ref, mine_ref, other_ref, inputs_ref, weight_ref, out_ref, rows_ref, total):
+def output_kernel(n, me_ref, mine_ref, other_ref, inputs_ref, *rest):
+    *weights, out_ref, rows_ref = rest
     me = me_ref[0]
     half, heads, width = mine_ref.shape
     steps = heads // H
@@ -322,7 +371,7 @@
             block = ref[entry].astype(F32)
             for lane in range(lanes):
                 rows_ref[lane, pl.ds(start, heads), :] = block[:, lane * 128 : (lane + 1) * 128]
-    total[...] = jnp.zeros_like(total)
+    total = None
     for h in range(H):
         left = jnp.concatenate(
             [
@@ -334,53 +383,61 @@
             ],
             axis=0,
         ).astype(BF16)
-        total[...] += jnp.dot(
-            left, weight_ref[h * width : (h + 1) * width, :], preferred_element_type=F32
-        )
+        held = weights[h * len(weights) // H]
+        at = h * width % held.shape[0]
+        product = jnp.dot(left, held[at : at + width, :], preferred_element_type=F32)
+        total = product if total is None else total + product
     for step in range(steps):
         out_ref[step] = (
             inputs_ref[step].astype(F32) + total[step * n : (step + 1) * n]
         ).astype(BF16)
 
 
-def keep_kernel(block_ref, from_ref, held, to_ref, sem):
-    copy = pltpu.make_async_copy(from_ref, to_ref, sem)
+def keep_kernel(half, block_ref, from_ref, held, to_ref, sem):
+    rows = to_ref.shape[0]
+    copy = pltpu.make_async_copy(from_ref.at[pl.ds(half * rows, rows), :], to_ref, sem)
     copy.start()
     held[...] = block_ref[...]
     copy.wait()
 
 
-def keep(block, weight):
+def keep(block, weight, half, us):
     vmem = pl.BlockSpec(memory_space=pltpu.VMEM)
     return pl.pallas_call(
-        keep_kernel,
+        functools.partial(keep_kernel, half),
         out_shape=(
             jax.ShapeDtypeStruct(block.shape, block.dtype),
-            pltpu.VMEM(weight.shape, weight.dtype),
+            pltpu.VMEM((weight.shape[0] // 2, weight.shape[1]), weight.dtype),
         ),
         in_specs=[vmem, pl.BlockSpec(memory_space=pltpu.HBM)],
         out_specs=(vmem, vmem),
         scratch_shapes=[pltpu.SemaphoreType.DMA],
         compiler_params=pltpu.CompilerParams(vmem_limit_bytes=4 * 1024 * 1024),
-        cost_estimate=hint(3),
+        cost_estimate=hint(us),
     )(block, far(weight))
 
 
-def output(me, mine, other, inputs, weight, n):
+def output(me, attended, inputs, weight, n):
+    kept = []
+
+    def aside(half, block):
+        block, part = keep(block, weight, half, 2)
+        kept.append(near(part))
+        return block
+
+    mine, other = gather_blocks(
+        attended, n, functools.partial(aside, 0), functools.partial(aside, 1)
+    )
     half, heads, width = mine.shape
     vmem = pl.BlockSpec(memory_space=pltpu.VMEM)
-    steps, rows, columns = inputs.shape
     return pl.pallas_call(
         functools.partial(output_kernel, n),
         out_shape=jax.ShapeDtypeStruct(inputs.shape, BF16),
-        in_specs=[pl.BlockSpec(memory_space=pltpu.SMEM), vmem, vmem, vmem, vmem],
+        in_specs=[pl.BlockSpec(memory_space=pltpu.SMEM)] + [vmem] * 5,
         out_specs=vmem,
-        scratch_shapes=[
-            pltpu.VMEM((width // 128, n * heads, 128), F32),
-            pltpu.VMEM((steps * rows, columns), F32),
-        ],
+        scratch_shapes=[pltpu.VMEM((width // 128, n * heads, 128), F32)],
         compiler_params=pltpu.CompilerParams(vmem_limit_bytes=VMEM_LIMIT),
-    )(me, mine, other, inputs, pltpu.with_memory_space_constraint(weight, pltpu.VMEM))
+    )(me, mine, other, inputs, *kept)
 
 
 def angles(positions, steps):
@@ -394,6 +451,32 @@
     return cos[:, None, :], sin[:, None, :]
 
 
+def turn_kernel(positions_ref, after_ref, cos_ref, sin_ref):
+    steps = cos_ref.shape[0]
+    lane = lax.broadcasted_iota(jnp.int32, (8, HD), 1)
+    step = lax.broadcasted_iota(jnp.int32, (8, HD), 0)
+    pair = lax.rem(lane, HD // 2).astype(F32)
+    frequency = jnp.exp(-math.log(ROPE_BASE) * 2.0 * pair / HD)
+    turns = (positions_ref[0] + step).astype(F32) * frequency
+    cos = jnp.cos(turns)
+    sin = jnp.where(lane < HD // 2, -1.0, 1.0) * jnp.sin(turns)
+    for index in range(steps):
+        cos_ref[index] = cos[index : index + 1]
+        sin_ref[index] = sin[index : index + 1]
+
+
+def turn(positions, after, steps):
+    vmem = pl.BlockSpec(memory_space=pltpu.VMEM)
+    return pl.pallas_call(
+        turn_kernel,
+        out_shape=(jax.ShapeDtypeStruct((steps, 1, HD), F32),) * 2,
+        in_specs=[pl.BlockSpec(memory_space=pltpu.SMEM), pl.BlockSpec(memory_space=pl.ANY)],
+        out_specs=(vmem, vmem),
+        compiler_params=pltpu.CompilerParams(vmem_limit_bytes=4 * 1024 * 1024),
+        cost_estimate=hint(1),
+    )(positions, after)
+
+
 def local(
     n, inputs, norm_gain, qkv_weight, head_lambda, head_gain, out_weight,
     key_one_pages, key_two_pages, value_pages, page_table, context_len, positions,
@@ -403,14 +486,12 @@
     block = inputs.reshape(steps * rows, part)
     sent = project(me, block, norm_gain.reshape(n, 1, part), qkv_weight, n)
     received = lax.all_to_all(sent, "gx", 0, 0)
-    cos, sin = angles(positions, steps)
+    cos, sin = turn(positions, sent, steps)
     attended = attend(
         page_table, context_len, received, cos, sin, head_lambda.reshape(H, 1),
         head_gain.reshape(H, 2 * HD), key_one_pages, key_two_pages, value_pages,
     )
-    held, weight = keep(attended, out_weight)
-    mine, other = gather_blocks(attended, n, held)
-    return output(me, mine, other, inputs, weight, n)
+    return output(me, attended, inputs, out_weight, n)
 
 
 def rotary(vectors, cos, sin):

time: 55.1 us -> 53.5 us (0.971)
  waiting for transfers between devices: 13.3 us -> 10.1 us
  Pallas kernels: 22.4 us -> 24.4 us
    pallas_call x3 -> x5, Pallas kernels: 14.1 us -> 17.2 us  [the longest x1 7.3 us: project(): pl.pallas_call(functools.partial(open_kernel, n, cuts), out_shape=sums +...]
    ppermute x11, waiting for transfers between devices: 6.88 us -> 4.18 us  [swap(): return lax.ppermute(block, 'gx', [(i, i ^ mask) for i in range(n)])]
    pallas_call x2, Pallas kernels: 4.27 us -> 3.09 us  [project(): pl.pallas_call(functools.partial(close_kernel if last else more_kernel, n...]
  transfers between devices with their start and end apart: 12 -> 12, of which waited for: 4 -> 6; matrix products, arithmetic and copies ran while one was open for 1% -> 0% of each run, Pallas kernels for 29% -> 35%
where the time goes in v3:
time: 53.5 us; the launch traced here: 53.2 us
  Pallas kernels  24.4 us (46%)
  starting transfers between devices  17 us (32%)
  waiting for transfers between devices  10.1 us (19%)
  between operations  1.51 us (3%)
    ppermute x11, starting transfers between devices, swap(): return lax.ppermute(block, 'gx', [(i, i ^ mask) for i in range(n)])  11.9 us
    pallas_call x1, Pallas kernels, project(): pl.pallas_call(functools.partial(open_kernel, n, cuts), out_shape=sums +...  7.3 us
    all_to_all x1, waiting for transfers between devices, local(): received = lax.all_to_all(sent, 'gx', 0, 0)  5.93 us
    pallas_call x1, Pallas kernels, fetch(): pl.pallas_call(functools.partial(fetch_kernel, n, order), out_shape=(pltp...  5.21 us
    all_to_all x1, starting transfers between devices, local(): received = lax.all_to_all(sent, 'gx', 0, 0)  5.16 us
    pallas_call x2, Pallas kernels, keep(): pl.pallas_call(functools.partial(keep_kernel, half), out_shape=(jax.Shape...  4.69 us
    ppermute x11, waiting for transfers between devices, swap(): return lax.ppermute(block, 'gx', [(i, i ^ mask) for i in range(n)])  4.18 us
    pallas_call x2, Pallas kernels, project(): pl.pallas_call(functools.partial(close_kernel if last else more_kernel, n...  3.09 us
  transfers between devices with their start and end apart: 12, of which 6 were waited for; matrix products, arithmetic and copies ran while one was open for 0% of the time, Pallas kernels for 35%

profile of v3, /device:TPU:0, one launch (start us, length us, event | category | flops | bytes accessed | tf_op | source)
XLA Modules:
  0.0 53.2 jit_solution(12407778733872078206)
XLA Ops:
  0.0 3.0 %collective-permute-start = (bf16[32,768]{1,0:T(8,128)(2,1)}, bf16[32,768]{1,0:T(8,128)(2,1)S(1)}, u32[]{:S(2)}, u32[]{:S(2)}) collective-permute-start(bf16[32,768]{1,0:T(8,128)(2,1)} %bitcast.12), channel_id=1, source_target_pairs={{0,4},{1,5},{2,6},{3,7},{4,0},{5,1},{6,2},{7,3},{8,12},{9,13},{10,... | collective-permute-start | bytes 147464 | tf_op jit(solution)/shard_map/ppermute | solution.py:29
  3.0 2.6 %collective-permute-start.1 = (bf16[32,768]{1,0:T(8,128)(2,1)}, bf16[32,768]{1,0:T(8,128)(2,1)S(1)}, u32[]{:S(2)}, u32[]{:S(2)}) collective-permute-start(bf16[32,768]{1,0:T(8,128)(2,1)} %bitcast.13), channel_id=1, source_target_pairs={{0,8},{1,9},{2,10},{3,11},{4,12},{5,13},{6,14},{7,15},{8,0},{9,1},... | collective-permute-start | bytes 147464 | tf_op jit(solution)/shard_map/ppermute | solution.py:29
  5.6 5.2 %shard_map.118 = (bf16[32,768]{1,0:T(8,128)(2,1)S(1)}, f32[16,1,768]{2,1,0:T(1,128)S(1)}, bf16[8,768,1152]{2,1,0:T(8,128)(2,1)S(1)}) custom-call(s32[1]{0:T(128)} %bitcast.me_ref, bf16[32,768]{1,0:T(8,128)(2,1)} %bitcast.15, f32[16,1,768]{2,1,0:T(1,128)} %bitcast.18, bf16[12288,1152]{1,0:T(8,128)(2,1)} %weight_ref.3), custom_call_target="tpu_custom_call" | custom-call | bytes 15000000 | tf_op jit(solution)/shard_map/pallas_call | solution.py:110
  10.9 0.9 %collective-permute-done.2 = bf16[32,768]{1,0:T(8,128)(2,1)S(1)} collective-permute-done((bf16[32,768]{1,0:T(8,128)(2,1)}, bf16[32,768]{1,0:T(8,128)(2,1)S(1)}, u32[]{:S(2)}, u32[]{:S(2)}) %collective-permute-start.2) | collective-permute-done | bytes 49184 | tf_op jit(solution)/shard_map/ppermute | solution.py:29
  11.8 1.6 %collective-permute-start.3 = (bf16[4,32,768]{2,1,0:T(8,128)(2,1)S(1)}, bf16[4,32,768]{2,1,0:T(8,128)(2,1)S(1)}, u32[]{:S(2)}, u32[]{:S(2)}) collective-permute-start(bf16[4,32,768]{2,1,0:T(8,128)(2,1)S(1)} %pad_maximum_fusion.mine_ref), channel_id=1, source_target_pairs={{0,2},{1,3},{2,0},{3,1},{4,6},{5,7},{6,4},{7,5},{8,10},{9,11},{10,... | collective-permute-start | bytes 589832 | tf_op jit(solution)/shard_map/ppermute | solution.py:29
  13.4 7.3 %shard_map.119 = (f32[32,1152]{1,0:T(8,128)S(1)}, f32[32,768]{1,0:T(8,128)S(1)}, bf16[8,768,1152]{2,1,0:T(8,128)(2,1)S(1)}) custom-call(s32[1]{0:T(128)} %bitcast.me_ref, bf16[4,32,768]{2,1,0:T(8,128)(2,1)S(1)} %pad_maximum_fusion.mine_ref, bf16[4,32,768]{2,1,0:T(8,128)(2,1)S(1)} %collective-permute-done.4.other_ref, ...), custom_call_target="tpu_custom_call" | custom-call | bytes 15000000 | tf_op jit(solution)/shard_map/pallas_call | solution.py:224
  20.7 0.2 collective-permute-start.5
  21.0 1.2 %shard_map.120 = (f32[32,1152]{1,0:T(8,128)S(1)}, f32[32,768]{1,0:T(8,128)S(1)}) custom-call(s32[1]{0:T(128)} %bitcast.me_ref, bf16[4,32,768]{2,1,0:T(8,128)(2,1)S(1)} %collective-permute-done.3.block_ref, f32[16,1,768]{2,1,0:T(1,128)S(1)} %get-tuple-element.25.gain_ref, bf16[8,768,1152]{2,1,0:T(8,128)(2,1)S(1)} %get-tuple-element.26.rest_0_, ...), custom_call_target="tpu_custom_call" | custom-call | bytes 6000000 | tf_op jit(solution)/shard_map/pallas_call | solution.py:242
  22.3 1.9 %shard_map.121.after_ref = bf16[16,18,128]{2,1,0:T(8,128)(2,1)} custom-call(s32[1]{0:T(128)} %bitcast.me_ref, bf16[4,32,768]{2,1,0:T(8,128)(2,1)S(1)} %collective-permute-done.5.block_ref, f32[16,1,768]{2,1,0:T(1,128)S(1)} %get-tuple-element.25.gain_ref, bf16[8,768,1152]{2,1,0:T(8,128)(2,1)S(1)} %get-tuple-element.26.rest_0_, ...), custom_call_target="tpu_custom_call" | custom-call | bytes 6000000 | tf_op jit(solution)/shard_map/pallas_call | solution.py:242
  24.2 5.2 %all-to-all-start = ((bf16[16,18,128]{2,1,0:T(8,128)(2,1)}), bf16[16,18,128]{2,1,0:T(8,128)(2,1)S(1)}, u32[]{:S(2)}, u32[]{:S(2)}) async-start(bf16[16,18,128]{2,1,0:T(8,128)(2,1)} %shard_map.121.after_ref), calls=%async_computation | async-start | bytes 196608 | tf_op jit(solution)/shard_map/all_to_all | solution.py:488
  30.0 0.1 copy.13.lambda_ref
  30.8 5.9 %all-to-all-done.received_ref = bf16[16,18,128]{2,1,0:T(8,128)(2,1)S(1)} async-done(((bf16[16,18,128]{2,1,0:T(8,128)(2,1)}), bf16[16,18,128]{2,1,0:T(8,128)(2,1)S(1)}, u32[]{:S(2)}, u32[]{:S(2)}) %all-to-all-start) | async-done | bytes 73760 | tf_op jit(solution)/shard_map/all_to_all | solution.py:488
  36.8 1.7 %shard_map.123.block_ref = bf16[48,256]{1,0:T(8,128)(2,1)S(1)} custom-call(s32[1,6]{1,0:T(1,128)S(1)} %copy-done.4, s32[1]{0:T(128)S(6)} %copy.15.length_ref, bf16[16,18,128]{2,1,0:T(8,128)(2,1)S(1)} %all-to-all-done.received_ref, f32[2,1,128]{2,1,0:T(1,128)S(1)} %get-tuple-element.35.cos_ref, f32[2,1,128]{2,1,0:T(1,128)S(1)} %get-tuple-element.36.sin_ref, ...), custom_call_target="tpu_custom_call" | custom-call | bytes 30000000 | tf_op jit(solution)/shard_map/pallas_call | solution.py:351
  38.5 0.2 collective-permute-start.7
  38.7 1.9 %collective-permute-start.8 = (bf16[48,256]{1,0:T(8,128)(2,1)S(1)}, bf16[48,256]{1,0:T(8,128)(2,1)S(1)}, u32[]{:S(2)}, u32[]{:S(2)}) collective-permute-start(bf16[48,256]{1,0:T(8,128)(2,1)S(1)} %shard_map.123.block_ref), channel_id=1, source_target_pairs={{0,12},{1,13},{2,14},{3,15},{4,8},{5,9},{6,10},{7,11},{8,4},{9,5},... | collective-permute-start | bytes 73736 | tf_op jit(solution)/shard_map/ppermute | solution.py:29
  40.6 1.4 %collective-permute-start.6 = (bf16[48,256]{1,0:T(8,128)(2,1)S(1)}, bf16[48,256]{1,0:T(8,128)(2,1)S(1)}, u32[]{:S(2)}, u32[]{:S(2)}) collective-permute-start(bf16[48,256]{1,0:T(8,128)(2,1)S(1)} %shard_map.123.block_ref), channel_id=1, source_target_pairs={{0,4},{1,5},{2,6},{3,7},{4,0},{5,1},{6,2},{7,3},{8,12},{9,13},{10,... | collective-permute-start | bytes 73736 | tf_op jit(solution)/shard_map/ppermute | solution.py:29
  42.0 2.3 %shard_map.124 = (bf16[48,256]{1,0:T(8,128)(2,1)S(1)}, bf16[3072,768]{1,0:T(8,128)(2,1)S(1)}) custom-call(bf16[48,256]{1,0:T(8,128)(2,1)S(1)} %shard_map.123.block_ref, bf16[6144,768]{1,0:T(8,128)(2,1)} %from_ref.3), custom_call_target="tpu_custom_call" | custom-call | bytes 6000000 | tf_op jit(solution)/shard_map/pallas_call | solution.py:406
  44.4 0.2 collective-permute-done.6
  44.6 0.7 %collective-permute-start.9 = (bf16[4,48,256]{2,1,0:T(8,128)(2,1)S(1)}, bf16[4,48,256]{2,1,0:T(8,128)(2,1)S(1)}, u32[]{:S(2)}, u32[]{:S(2)}) collective-permute-start(bf16[4,48,256]{2,1,0:T(8,128)(2,1)S(1)} %pad_maximum_fusion.1.block_ref), channel_id=1, source_target_pairs={{0,2},{1,3},{2,0},{3,1},{4,6},{5,7},{6,4},{7,5},{8,10},{9,11},{10,... | collective-permute-start | bytes 294920 | tf_op jit(solution)/shard_map/ppermute | solution.py:29
  45.3 2.3 %shard_map.125 = (bf16[4,48,256]{2,1,0:T(8,128)(2,1)S(1)}, bf16[3072,768]{1,0:T(8,128)(2,1)S(1)}) custom-call(bf16[4,48,256]{2,1,0:T(8,128)(2,1)S(1)} %pad_maximum_fusion.1.block_ref, bf16[6144,768]{1,0:T(8,128)(2,1)} %from_ref.3), custom_call_target="tpu_custom_call" | custom-call | bytes 6000000 | tf_op jit(solution)/shard_map/pallas_call | solution.py:406
  47.7 1.6 %collective-permute-done.9 = bf16[4,48,256]{2,1,0:T(8,128)(2,1)S(1)} collective-permute-done((bf16[4,48,256]{2,1,0:T(8,128)(2,1)S(1)}, bf16[4,48,256]{2,1,0:T(8,128)(2,1)S(1)}, u32[]{:S(2)}, u32[]{:S(2)}) %collective-permute-start.9) | collective-permute-done | bytes 98336 | tf_op jit(solution)/shard_map/ppermute | solution.py:29
  49.3 0.1 collective-permute-start.10
  49.4 1.4 %collective-permute-done.10.other_ref = bf16[8,48,256]{2,1,0:T(8,128)(2,1)S(1)} collective-permute-done((bf16[8,48,256]{2,1,0:T(8,128)(2,1)S(1)}, bf16[8,48,256]{2,1,0:T(8,128)(2,1)S(1)}, u32[]{:S(2)}, u32[]{:S(2)}) %collective-permute-start.10) | collective-permute-done | bytes 196640 | tf_op jit(solution)/shard_map/ppermute | solution.py:29
  50.8 2.4 %shard_map.126 = bf16[2,16,768]{2,1,0:T(8,128)(2,1)} custom-call(s32[1]{0:T(128)} %bitcast.me_ref, bf16[8,48,256]{2,1,0:T(8,128)(2,1)S(1)} %constant_dynamic-update-slice_fusion.mine_ref, bf16[8,48,256]{2,1,0:T(8,128)(2,1)S(1)} %collective-permute-done.10.other_ref, bf16[2,16,768]{2,1,0:T(8,128)(2,1)S(1)} %copy-done.3, ...), custom_call_target="tpu_custom_call" | custom-call | tf_op jit(solution)/shard_map/pallas_call | solution.py:433
  (29 shorter events, 0.3 us)
Async XLA Ops:
  0.0 10.8 %collective-permute-start = (bf16[32,768]{1,0:T(8,128)(2,1)}, bf16[32,768]{1,0:T(8,128)(2,1)S(1)}, u32[]{:S(2)}, u32[]{:S(2)}) collective-permute-start(bf16[32,768]{1,0:T(8,128)(2,1)} %bitcast.12), channel_id=1, source_target_pairs={{0,4},{1,5},{2,6},{3,7},{4,0},{5,1},{6,2},{7,3},{8,12},{9,13},{10,... | collective-permute-start | bytes 147464 | tf_op jit(solution)/shard_map/ppermute | solution.py:29
  3.0 7.8 %collective-permute-start.1 = (bf16[32,768]{1,0:T(8,128)(2,1)}, bf16[32,768]{1,0:T(8,128)(2,1)S(1)}, u32[]{:S(2)}, u32[]{:S(2)}) collective-permute-start(bf16[32,768]{1,0:T(8,128)(2,1)} %bitcast.13), channel_id=1, source_target_pairs={{0,8},{1,9},{2,10},{3,11},{4,12},{5,13},{6,14},{7,15},{8,0},{9,1},... | collective-permute-start | bytes 147464 | tf_op jit(solution)/shard_map/ppermute | solution.py:29
  5.6 6.1 %collective-permute-start.2 = (bf16[32,768]{1,0:T(8,128)(2,1)}, bf16[32,768]{1,0:T(8,128)(2,1)S(1)}, u32[]{:S(2)}, u32[]{:S(2)}) collective-permute-start(bf16[32,768]{1,0:T(8,128)(2,1)} %bitcast.14), channel_id=1, source_target_pairs={{0,12},{1,13},{2,14},{3,15},{4,8},{5,9},{6,10},{7,11},{8,4},{9,5},... | collective-permute-start | bytes 147464 | tf_op jit(solution)/shard_map/ppermute | solution.py:29
  11.7 1.7 %collective-permute-start.4 = (bf16[4,32,768]{2,1,0:T(8,128)(2,1)S(1)}, bf16[4,32,768]{2,1,0:T(8,128)(2,1)S(1)}, u32[]{:S(2)}, u32[]{:S(2)}) collective-permute-start(bf16[4,32,768]{2,1,0:T(8,128)(2,1)S(1)} %pad_maximum_fusion.mine_ref), channel_id=1, source_target_pairs={{0,1},{1,0},{2,3},{3,2},{4,5},{5,4},{6,7},{7,6},{8,9},{9,8},{10,11... | collective-permute-start | bytes 589832 | tf_op jit(solution)/shard_map/ppermute | solution.py:29
  11.8 8.9 %collective-permute-start.3 = (bf16[4,32,768]{2,1,0:T(8,128)(2,1)S(1)}, bf16[4,32,768]{2,1,0:T(8,128)(2,1)S(1)}, u32[]{:S(2)}, u32[]{:S(2)}) collective-permute-start(bf16[4,32,768]{2,1,0:T(8,128)(2,1)S(1)} %pad_maximum_fusion.mine_ref), channel_id=1, source_target_pairs={{0,2},{1,3},{2,0},{3,1},{4,6},{5,7},{6,4},{7,5},{8,10},{9,11},{10,... | collective-permute-start | bytes 589832 | tf_op jit(solution)/shard_map/ppermute | solution.py:29
  20.7 1.5 %collective-permute-start.5 = (bf16[4,32,768]{2,1,0:T(8,128)(2,1)S(1)}, bf16[4,32,768]{2,1,0:T(8,128)(2,1)S(1)}, u32[]{:S(2)}, u32[]{:S(2)}) collective-permute-start(bf16[4,32,768]{2,1,0:T(8,128)(2,1)S(1)} %collective-permute-done.3.block_ref), channel_id=1, source_target_pairs={{0,1},{1,0},{2,3},{3,2},{4,5},{5,4},{6,7},{7,6},{8,9},{9,8},{10,11... | collective-permute-start | bytes 589832 | tf_op jit(solution)/shard_map/ppermute | solution.py:29
  22.2 7.7 %copy-start.5 = (f32[6144]{0:T(1024)S(1)}, f32[6144]{0:T(1024)}, u32[]{:S(2)}) copy-start(f32[6144]{0:T(1024)} %param.16) | copy-start | bytes 73732
  22.2 7.8 %copy-start.6 = (f32[24]{0:T(128)S(1)}, f32[24]{0:T(128)}, u32[]{:S(2)}) copy-start(f32[24]{0:T(128)} %param.15) | copy-start | bytes 292
  22.2 14.5 %copy-start = (bf16[6,16,6144]{2,1,0:T(8,128)(2,1)S(1)}, bf16[6,16,6144]{2,1,0:T(8,128)(2,1)}, u32[]{:S(2)}) copy-start(bf16[6,16,6144]{2,1,0:T(8,128)(2,1)} %values_ref.1) | copy-start | bytes 3538948
  22.2 14.5 %copy-start.1 = (bf16[6,16,3072]{2,1,0:T(8,128)(2,1)S(1)}, bf16[6,16,3072]{2,1,0:T(8,128)(2,1)}, u32[]{:S(2)}) copy-start(bf16[6,16,3072]{2,1,0:T(8,128)(2,1)} %keys_one_ref.1) | copy-start | bytes 1769476
  22.3 14.5 %copy-start.2 = (bf16[6,16,3072]{2,1,0:T(8,128)(2,1)S(1)}, bf16[6,16,3072]{2,1,0:T(8,128)(2,1)}, u32[]{:S(2)}) copy-start(bf16[6,16,3072]{2,1,0:T(8,128)(2,1)} %keys_two_ref.1) | copy-start | bytes 1769476
  22.3 14.5 %copy-start.4 = (s32[1,6]{1,0:T(1,128)S(1)}, s32[1,6]{1,0:T(1,128)}, u32[]{:S(2)}) copy-start(s32[1,6]{1,0:T(1,128)} %table_ref.1) | copy-start | bytes 76
  24.2 12.6 %all-to-all-start = ((bf16[16,18,128]{2,1,0:T(8,128)(2,1)}), bf16[16,18,128]{2,1,0:T(8,128)(2,1)S(1)}, u32[]{:S(2)}, u32[]{:S(2)}) async-start(bf16[16,18,128]{2,1,0:T(8,128)(2,1)} %shard_map.121.after_ref), calls=%async_computation | async-start | bytes 196608 | tf_op jit(solution)/shard_map/all_to_all | solution.py:488
  38.4 12.4 %copy-start.3 = (bf16[2,16,768]{2,1,0:T(8,128)(2,1)S(1)}, bf16[2,16,768]{2,1,0:T(8,128)(2,1)}, u32[]{:S(2)}) copy-start(bf16[2,16,768]{2,1,0:T(8,128)(2,1)} %inputs_ref.1) | copy-start | bytes 147460
  38.5 5.9 %collective-permute-start.7 = (bf16[48,256]{1,0:T(8,128)(2,1)S(1)}, bf16[48,256]{1,0:T(8,128)(2,1)S(1)}, u32[]{:S(2)}, u32[]{:S(2)}) collective-permute-start(bf16[48,256]{1,0:T(8,128)(2,1)S(1)} %shard_map.123.block_ref), channel_id=1, source_target_pairs={{0,8},{1,9},{2,10},{3,11},{4,12},{5,13},{6,14},{7,15},{8,0},{9,1},... | collective-permute-start | bytes 73736 | tf_op jit(solution)/shard_map/ppermute | solution.py:29
  38.7 5.7 %collective-permute-start.8 = (bf16[48,256]{1,0:T(8,128)(2,1)S(1)}, bf16[48,256]{1,0:T(8,128)(2,1)S(1)}, u32[]{:S(2)}, u32[]{:S(2)}) collective-permute-start(bf16[48,256]{1,0:T(8,128)(2,1)S(1)} %shard_map.123.block_ref), channel_id=1, source_target_pairs={{0,12},{1,13},{2,14},{3,15},{4,8},{5,9},{6,10},{7,11},{8,4},{9,5},... | collective-permute-start | bytes 73736 | tf_op jit(solution)/shard_map/ppermute | solution.py:29
  40.6 4.0 %collective-permute-start.6 = (bf16[48,256]{1,0:T(8,128)(2,1)S(1)}, bf16[48,256]{1,0:T(8,128)(2,1)S(1)}, u32[]{:S(2)}, u32[]{:S(2)}) collective-permute-start(bf16[48,256]{1,0:T(8,128)(2,1)S(1)} %shard_map.123.block_ref), channel_id=1, source_target_pairs={{0,4},{1,5},{2,6},{3,7},{4,0},{5,1},{6,2},{7,3},{8,12},{9,13},{10,... | collective-permute-start | bytes 73736 | tf_op jit(solution)/shard_map/ppermute | solution.py:29
  44.6 4.7 %collective-permute-start.9 = (bf16[4,48,256]{2,1,0:T(8,128)(2,1)S(1)}, bf16[4,48,256]{2,1,0:T(8,128)(2,1)S(1)}, u32[]{:S(2)}, u32[]{:S(2)}) collective-permute-start(bf16[4,48,256]{2,1,0:T(8,128)(2,1)S(1)} %pad_maximum_fusion.1.block_ref), channel_id=1, source_target_pairs={{0,2},{1,3},{2,0},{3,1},{4,6},{5,7},{6,4},{7,5},{8,10},{9,11},{10,... | collective-permute-start | bytes 294920 | tf_op jit(solution)/shard_map/ppermute | solution.py:29
  49.3 1.5 %collective-permute-start.10 = (bf16[8,48,256]{2,1,0:T(8,128)(2,1)S(1)}, bf16[8,48,256]{2,1,0:T(8,128)(2,1)S(1)}, u32[]{:S(2)}, u32[]{:S(2)}) collective-permute-start(bf16[8,48,256]{2,1,0:T(8,128)(2,1)S(1)} %constant_dynamic-update-slice_fusion.mine_ref), channel_id=1, source_target_pairs={{0,1},{1,0},{2,3},{3,2},{4,5},{5,4},{6,7},{7,6},{8,9},{9,8},{10,11... | collective-permute-start | bytes 589832 | tf_op jit(solution)/shard_map/ppermute | solution.py:29

commit v4 on v3

--- a/solution.py
+++ b/solution.py
@@ -129,77 +129,69 @@
     return pltpu.with_memory_space_constraint(x, pltpu.VMEM)
 
 
-def add_products(n, order, me, refs, gain_ref, weights, total, squares):
-    rows = total.shape[0]
-    sums = None
-    square = squares[...]
-    for (entry, core), ref, (held, slot) in zip(order, refs, weights, strict=True):
-        values = ref[...].astype(F32)
-        square = square + values * values
-        scaled = values * gain_ref[owner(me, entry, core, n)]
-        high = scaled.astype(BF16)
-        low = (scaled - high.astype(F32)).astype(BF16)
-        product = jnp.dot(
-            jnp.concatenate([high, low], axis=0), held[slot], preferred_element_type=F32
-        )
-        sums = product if sums is None else sums + product
-    squares[...] = square
-    total[...] += sums[:rows] + sums[rows:]
-
-
-def open_kernel(n, cuts, me_ref, mine_ref, other_ref, gain_ref, weight_ref, *rest):
-    *helds, total, squares, later_ref, sems = rest
-    me = me_ref[0]
-    outer = mine_ref.shape[0]
-    order = slots(n)
-    copies = fetches(n, order[cuts[-1] :], me, weight_ref, later_ref, sems)
+def add_squares(refs, square):
+    for ref in refs:
+        for entry in range(ref.shape[0]):
+            values = ref[entry].astype(F32)
+            square = square + values * values
+    return square
+
+
+def squares_kernel(n, order, count, me_ref, weight_ref, *rest):
+    blocks, (before, squares, weight_out, sems) = rest[:count], rest[count:]
+    copies = fetches(n, order, me_ref[0], weight_ref, weight_out, sems)
     for copy in copies:
         copy.start()
-    total[...] = jnp.zeros_like(total)
-    squares[...] = jnp.zeros_like(squares)
-    refs = [mine_ref.at[e] for e in range(outer)] + [other_ref.at[e] for e in range(outer)]
-    add_products(
-        n, order[: 2 * outer], me, refs, gain_ref, places(helds, cuts)[: 2 * outer], total, squares
-    )
+    squares[...] = add_squares(blocks, before[...])
     for copy in copies:
         copy.wait()
 
 
-def places(helds, cuts):
-    found = []
-    for held, start, stop in zip(helds, (0,) + cuts[:-1], cuts, strict=True):
-        found += [(held, slot) for slot in range(stop - start)]
-    return found
-
-
-def more_kernel(
-    n, cuts, first, me_ref, block_ref, gain_ref, *rest,
-):
-    *helds, total_in, squares_in, total, squares = rest
-    total[...] = total_in[...]
-    squares[...] = squares_in[...]
-    outer = block_ref.shape[0]
-    picked = slice(first, first + outer)
-    add_products(
-        n, slots(n)[picked], me_ref[0], [block_ref.at[e] for e in range(outer)], gain_ref,
-        places(helds, cuts)[picked], total, squares,
-    )
-
-
-def close_kernel(n, cuts, first, me_ref, block_ref, gain_ref, *rest):
-    *refs, out_ref, total, squares, spread = rest
-    more_kernel(n, cuts, first, me_ref, block_ref, gain_ref, *refs, total, squares)
-    rows, part = squares.shape
-    mean = jnp.sum(squares[...], axis=1, keepdims=True) * (1.0 / (n * part))
+def squares_beside(me, weight, blocks, before, n, order):
+    part, columns = weight.shape[0] // n, weight.shape[1]
+    vmem = pl.BlockSpec(memory_space=pltpu.VMEM)
+    return pl.pallas_call(
+        functools.partial(squares_kernel, n, order, len(blocks)),
+        out_shape=(
+            jax.ShapeDtypeStruct(before.shape, F32),
+            pltpu.VMEM((len(order), part, columns), BF16),
+        ),
+        in_specs=[
+            pl.BlockSpec(memory_space=pltpu.SMEM),
+            pl.BlockSpec(memory_space=pltpu.HBM),
+        ]
+        + [vmem] * (len(blocks) + 1),
+        out_specs=(vmem, vmem),
+        scratch_shapes=[pltpu.SemaphoreType.DMA((len(order),))],
+        compiler_params=pltpu.CompilerParams(vmem_limit_bytes=4 * 1024 * 1024),
+        cost_estimate=hint(len(order) * 0.7),
+    )(me, far(weight), *blocks, before)
+
+
+def project_kernel(n, count, me_ref, gain_ref, before_ref, *rest):
+    blocks, (*helds, out_ref, spread) = rest[:count], rest[count:]
+    me = me_ref[0]
+    rows, part = before_ref.shape
+    square = add_squares(blocks[-1:], before_ref[...])
+    mean = jnp.sum(square, axis=1, keepdims=True) * (1.0 / (n * part))
     factor = lax.rsqrt(mean + EPS)
-    blocks = total.shape[1] // 128
+    refs = [(ref, entry) for ref in blocks for entry in range(ref.shape[0])]
+    places = [(held, slot) for held in helds for slot in range(held.shape[0])]
+    total = None
+    for (entry, core), (ref, at), (held, slot) in zip(slots(n), refs, places, strict=True):
+        gain = gain_ref[owner(me, entry, core, n)]
+        normed = (ref[at].astype(F32) * factor * gain).astype(BF16)
+        product = jnp.dot(normed, held[slot], preferred_element_type=F32)
+        total = product if total is None else total + product
+    columns = total.shape[1] // 128
     steps = rows // n
-    for block in range(blocks):
-        scaled = total[:, block * 128 : (block + 1) * 128] * factor
+    for block in range(columns):
         for step in range(steps):
-            spread[:, step * blocks + block, :] = scaled[step * n : (step + 1) * n]
+            spread[:, step * columns + block, :] = total[
+                step * n : (step + 1) * n, block * 128 : (block + 1) * 128
+            ]
     for target in range(n):
-        out_ref[target] = spread[target, : steps * blocks, :].astype(BF16)
+        out_ref[target] = spread[target, : steps * columns, :].astype(BF16)
 
 
 def project(me, block, gain, weight, n):
@@ -207,48 +199,31 @@
     columns = weight.shape[1]
     pieces = rows // n * (columns // 128)
     outer, middle = radices(n)
-    vmem = pl.BlockSpec(memory_space=pltpu.VMEM)
-    smem = pl.BlockSpec(memory_space=pltpu.SMEM)
-    hbm = pl.BlockSpec(memory_space=pltpu.HBM)
-    params = pltpu.CompilerParams(vmem_limit_bytes=VMEM_LIMIT)
-    sums = (jax.ShapeDtypeStruct((rows, columns), F32), jax.ShapeDtypeStruct((rows, part), F32))
     order = slots(n)
-    cut = 2 * outer
-    cuts = (cut,)
+    first, second = 2 * outer, n - max(1, outer // 2)
 
     arrived = [swap(block, n, o * 2 * middle) for o in range(1, outer)]
-    held, gain_held, weight_now = fetch(me, block, gain, weight, n, order[:cut])
+    held, gain, weight_a = fetch(me, block, gain, weight, n, order[:first])
     row = jnp.stack([held] + arrived)
     later = [swap(row, n, m * 2) for m in range(1, middle)]
-    helds = (near(weight_now),)
-    *partial, weight_later = pl.pallas_call(
-        functools.partial(open_kernel, n, cuts),
-        out_shape=sums + (pltpu.VMEM((n - cut, part, columns), BF16),),
-        in_specs=[smem] + [vmem] * 3 + [hbm, vmem],
-        out_specs=(vmem,) * 3,
-        scratch_shapes=[pltpu.SemaphoreType.DMA((n - cut,))],
-        compiler_params=params,
-        cost_estimate=hint(5),
-    )(me, row, swap(row, n, 1), gain_held, far(weight), *helds)
-    later, partial = lax.optimization_barrier((later, partial))
-    helds += (near(weight_later),)
-    cuts += (n,)
-    for m in range(1, middle):
-        across = swap(later[m - 1], n, 1)
-        for core, blocks in ((0, later[m - 1]), (1, across)):
-            last = m == middle - 1 and core == 1
-            spread = pltpu.VMEM((n, -(-pieces // 8) * 8, 128), F32)
-            first = (2 * m + core) * outer
-            partial = pl.pallas_call(
-                functools.partial(close_kernel if last else more_kernel, n, cuts, first),
-                out_shape=jax.ShapeDtypeStruct((n, pieces, 128), BF16) if last else sums,
-                in_specs=[smem] + [vmem] * 6,
-                out_specs=vmem if last else (vmem, vmem),
-                scratch_shapes=[pltpu.VMEM(x.shape, F32) for x in sums] + [spread] if last else (),
-                compiler_params=params,
-                cost_estimate=hint(2),
-            )(me, blocks, gain_held, *helds, *partial)
-    return partial
+    blocks = [row, swap(row, n, 1)]
+    squares = jnp.zeros((rows, part), F32)
+    squares, weight_b = squares_beside(me, weight, blocks, squares, n, order[first:second])
+    later, squares = lax.optimization_barrier((later, squares))
+    across = [swap(each, n, 1) for each in later]
+    for each, other in zip(later, across, strict=True):
+        blocks += [each, other]
+    squares, weight_c = squares_beside(me, weight, blocks[2:-1], squares, n, order[second:])
+    vmem = pl.BlockSpec(memory_space=pltpu.VMEM)
+    return pl.pallas_call(
+        functools.partial(project_kernel, n, len(blocks)),
+        out_shape=jax.ShapeDtypeStruct((n, pieces, 128), BF16),
+        in_specs=[pl.BlockSpec(memory_space=pltpu.SMEM)] + [vmem] * (len(blocks) + 5),
+        out_specs=vmem,
+        scratch_shapes=[pltpu.VMEM((n, -(-pieces // 8) * 8, 128), F32)],
+        compiler_params=pltpu.CompilerParams(vmem_limit_bytes=VMEM_LIMIT),
+        cost_estimate=hint(6),
+    )(me, gain, squares, *blocks, near(weight_a), near(weight_b), near(weight_c))
 
 
 def attend_kernel(

time: 53.5 us -> 56 us (1.047)
  waiting for transfers between devices: 10.1 us -> 11.6 us
  Pallas kernels: 24.4 us -> 25.3 us
    ppermute x11, waiting for transfers between devices: 4.18 us -> 5.7 us  [swap(): return lax.ppermute(block, 'gx', [(i, i ^ mask) for i in range(n)])]
    pallas_call x3, Pallas kernels: 10.4 us -> 11.3 us  [the longest x2 6.17 us: squares_beside(): pl.pallas_call(functools.partial(squares_kernel, n, order, len(blocks)),...]
  transfers between devices with their start and end apart: 12 -> 12, of which waited for: 6 -> 6; matrix products, arithmetic and copies ran while one was open for 0% -> 0% of each run, Pallas kernels for 35% -> 29%
where the time goes in v4:
time: 56 us; the launch traced here: 55.7 us
  Pallas kernels  25.3 us (45%)
  starting transfers between devices  17 us (30%)
  waiting for transfers between devices  11.6 us (21%)
  between operations  1.54 us (3%)
    ppermute x11, starting transfers between devices, swap(): return lax.ppermute(block, 'gx', [(i, i ^ mask) for i in range(n)])  11.6 us
    pallas_call x2, Pallas kernels, squares_beside(): pl.pallas_call(functools.partial(squares_kernel, n, order, len(blocks)),...  6.17 us
    all_to_all x1, waiting for transfers between devices, local(): received = lax.all_to_all(sent, 'gx', 0, 0)  5.93 us
    ppermute x11, waiting for transfers between devices, swap(): return lax.ppermute(block, 'gx', [(i, i ^ mask) for i in range(n)])  5.7 us
    all_to_all x1, starting transfers between devices, local(): received = lax.all_to_all(sent, 'gx', 0, 0)  5.42 us
    pallas_call x1, Pallas kernels, fetch(): pl.pallas_call(functools.partial(fetch_kernel, n, order), out_shape=(pltp...  5.21 us
    pallas_call x1, Pallas kernels, project(): pl.pallas_call(functools.partial(project_kernel, n, len(blocks)), out_sha...  5.14 us
    pallas_call x2, Pallas kernels, keep(): pl.pallas_call(functools.partial(keep_kernel, half), out_shape=(jax.Shape...  4.69 us
  transfers between devices with their start and end apart: 12, of which 6 were waited for; matrix products, arithmetic and copies ran while one was open for 0% of the time, Pallas kernels for 29%

profile of v4, /device:TPU:0, one launch (start us, length us, event | category | flops | bytes accessed | tf_op | source)
XLA Modules:
  0.0 55.7 jit_solution(8285605381580839741)
XLA Ops:
  0.0 3.0 %collective-permute-start = (bf16[32,768]{1,0:T(8,128)(2,1)}, bf16[32,768]{1,0:T(8,128)(2,1)S(1)}, u32[]{:S(2)}, u32[]{:S(2)}) collective-permute-start(bf16[32,768]{1,0:T(8,128)(2,1)} %bitcast.12), channel_id=1, source_target_pairs={{0,4},{1,5},{2,6},{3,7},{4,0},{5,1},{6,2},{7,3},{8,12},{9,13},{10,... | collective-permute-start | bytes 147464 | tf_op jit(solution)/shard_map/ppermute | solution.py:29
  3.0 2.6 %collective-permute-start.1 = (bf16[32,768]{1,0:T(8,128)(2,1)}, bf16[32,768]{1,0:T(8,128)(2,1)S(1)}, u32[]{:S(2)}, u32[]{:S(2)}) collective-permute-start(bf16[32,768]{1,0:T(8,128)(2,1)} %bitcast.13), channel_id=1, source_target_pairs={{0,8},{1,9},{2,10},{3,11},{4,12},{5,13},{6,14},{7,15},{8,0},{9,1},... | collective-permute-start | bytes 147464 | tf_op jit(solution)/shard_map/ppermute | solution.py:29
  5.6 5.2 %shard_map.118 = (bf16[32,768]{1,0:T(8,128)(2,1)S(1)}, f32[16,1,768]{2,1,0:T(1,128)S(1)}, bf16[8,768,1152]{2,1,0:T(8,128)(2,1)S(1)}) custom-call(s32[1]{0:T(128)} %bitcast.me_ref, bf16[32,768]{1,0:T(8,128)(2,1)} %bitcast.15, f32[16,1,768]{2,1,0:T(1,128)} %bitcast.18, bf16[12288,1152]{1,0:T(8,128)(2,1)} %weight_ref.5), custom_call_target="tpu_custom_call" | custom-call | bytes 15000000 | tf_op jit(solution)/shard_map/pallas_call | solution.py:110
  10.9 0.9 %collective-permute-done.2 = bf16[32,768]{1,0:T(8,128)(2,1)S(1)} collective-permute-done((bf16[32,768]{1,0:T(8,128)(2,1)}, bf16[32,768]{1,0:T(8,128)(2,1)S(1)}, u32[]{:S(2)}, u32[]{:S(2)}) %collective-permute-start.2) | collective-permute-done | bytes 49184 | tf_op jit(solution)/shard_map/ppermute | solution.py:29
  11.7 0.1 collective-permute-start.4
  11.8 1.6 %collective-permute-start.3 = (bf16[4,32,768]{2,1,0:T(8,128)(2,1)S(1)}, bf16[4,32,768]{2,1,0:T(8,128)(2,1)S(1)}, u32[]{:S(2)}, u32[]{:S(2)}) collective-permute-start(bf16[4,32,768]{2,1,0:T(8,128)(2,1)S(1)} %pad_maximum_fusion.rest_0_), channel_id=1, source_target_pairs={{0,2},{1,3},{2,0},{3,1},{4,6},{5,7},{6,4},{7,5},{8,10},{9,11},{10,... | collective-permute-start | bytes 589832 | tf_op jit(solution)/shard_map/ppermute | solution.py:29
  13.4 4.1 %shard_map.119 = (f32[32,768]{1,0:T(8,128)S(1)}, bf16[6,768,1152]{2,1,0:T(8,128)(2,1)S(1)}) custom-call(s32[1]{0:T(128)} %bitcast.me_ref, bf16[12288,1152]{1,0:T(8,128)(2,1)} %weight_ref.5, bf16[4,32,768]{2,1,0:T(8,128)(2,1)S(1)} %pad_maximum_fusion.rest_0_, bf16[4,32,768]{2,1,0:T(8,128)(2,1)S(1)} %collective-permute-done.4.rest_1_, ...), custom_call_target="tpu_custom_call" | custom-call | bytes 12599999 | tf_op jit(solution)/shard_map/pallas_call | solution.py:153
  17.6 1.6 %collective-permute-done.3.rest_0_.rest_2_ = bf16[4,32,768]{2,1,0:T(8,128)(2,1)S(1)} collective-permute-done((bf16[4,32,768]{2,1,0:T(8,128)(2,1)S(1)}, bf16[4,32,768]{2,1,0:T(8,128)(2,1)S(1)}, u32[]{:S(2)}, u32[]{:S(2)}) %collective-permute-start.3) | collective-permute-done | bytes 196640 | tf_op jit(solution)/shard_map/ppermute | solution.py:29
  19.1 2.0 %shard_map.120 = (f32[32,768]{1,0:T(8,128)S(1)}, bf16[2,768,1152]{2,1,0:T(8,128)(2,1)S(1)}) custom-call(s32[1]{0:T(128)} %bitcast.me_ref, bf16[12288,1152]{1,0:T(8,128)(2,1)} %weight_ref.5, bf16[4,32,768]{2,1,0:T(8,128)(2,1)S(1)} %collective-permute-done.3.rest_0_.rest_2_, f32[32,768]{1,0:T(8,128)S(1)} %get-tuple-element.26.rest_1_), custom_call_target="tpu_custom_call" | custom-call | bytes 4200000 | tf_op jit(solution)/shard_map/pallas_call | solution.py:153
  21.3 5.1 %shard_map.121.after_ref = bf16[16,18,128]{2,1,0:T(8,128)(2,1)} custom-call(s32[1]{0:T(128)} %bitcast.me_ref, f32[16,1,768]{2,1,0:T(1,128)S(1)} %get-tuple-element.22.gain_ref, f32[32,768]{1,0:T(8,128)S(1)} %get-tuple-element.27.before_ref, bf16[4,32,768]{2,1,0:T(8,128)(2,1)S(1)} %pad_maximum_fusion.rest_0_, ...), custom_call_target="tpu_custom_call" | custom-call | bytes 18000000 | tf_op jit(solution)/shard_map/pallas_call | solution.py:218
  26.4 5.4 %all-to-all-start = ((bf16[16,18,128]{2,1,0:T(8,128)(2,1)}), bf16[16,18,128]{2,1,0:T(8,128)(2,1)S(1)}, u32[]{:S(2)}, u32[]{:S(2)}) async-start(bf16[16,18,128]{2,1,0:T(8,128)(2,1)} %shard_map.121.after_ref), calls=%async_computation | async-start | bytes 196608 | tf_op jit(solution)/shard_map/all_to_all | solution.py:463
  32.5 0.1 copy.13.lambda_ref
  33.3 5.9 %all-to-all-done.received_ref = bf16[16,18,128]{2,1,0:T(8,128)(2,1)S(1)} async-done(((bf16[16,18,128]{2,1,0:T(8,128)(2,1)}), bf16[16,18,128]{2,1,0:T(8,128)(2,1)S(1)}, u32[]{:S(2)}, u32[]{:S(2)}) %all-to-all-start) | async-done | bytes 73760 | tf_op jit(solution)/shard_map/all_to_all | solution.py:463
  39.3 1.7 %shard_map.123.block_ref = bf16[48,256]{1,0:T(8,128)(2,1)S(1)} custom-call(s32[1,6]{1,0:T(1,128)S(1)} %copy-done.4, s32[1]{0:T(128)S(6)} %copy.15.length_ref, bf16[16,18,128]{2,1,0:T(8,128)(2,1)S(1)} %all-to-all-done.received_ref, f32[2,1,128]{2,1,0:T(1,128)S(1)} %get-tuple-element.31.cos_ref, f32[2,1,128]{2,1,0:T(1,128)S(1)} %get-tuple-element.32.sin_ref, ...), custom_call_target="tpu_custom_call" | custom-call | bytes 30000000 | tf_op jit(solution)/shard_map/pallas_call | solution.py:326
  41.0 0.3 collective-permute-start.7
  41.2 1.9 %collective-permute-start.8 = (bf16[48,256]{1,0:T(8,128)(2,1)S(1)}, bf16[48,256]{1,0:T(8,128)(2,1)S(1)}, u32[]{:S(2)}, u32[]{:S(2)}) collective-permute-start(bf16[48,256]{1,0:T(8,128)(2,1)S(1)} %shard_map.123.block_ref), channel_id=1, source_target_pairs={{0,12},{1,13},{2,14},{3,15},{4,8},{5,9},{6,10},{7,11},{8,4},{9,5},... | collective-permute-start | bytes 73736 | tf_op jit(solution)/shard_map/ppermute | solution.py:29
  43.1 1.4 %collective-permute-start.6 = (bf16[48,256]{1,0:T(8,128)(2,1)S(1)}, bf16[48,256]{1,0:T(8,128)(2,1)S(1)}, u32[]{:S(2)}, u32[]{:S(2)}) collective-permute-start(bf16[48,256]{1,0:T(8,128)(2,1)S(1)} %shard_map.123.block_ref), channel_id=1, source_target_pairs={{0,4},{1,5},{2,6},{3,7},{4,0},{5,1},{6,2},{7,3},{8,12},{9,13},{10,... | collective-permute-start | bytes 73736 | tf_op jit(solution)/shard_map/ppermute | solution.py:29
  44.5 2.3 %shard_map.124 = (bf16[48,256]{1,0:T(8,128)(2,1)S(1)}, bf16[3072,768]{1,0:T(8,128)(2,1)S(1)}) custom-call(bf16[48,256]{1,0:T(8,128)(2,1)S(1)} %shard_map.123.block_ref, bf16[6144,768]{1,0:T(8,128)(2,1)} %from_ref.3), custom_call_target="tpu_custom_call" | custom-call | bytes 6000000 | tf_op jit(solution)/shard_map/pallas_call | solution.py:381
  46.9 0.2 collective-permute-done.6
  47.1 0.7 %collective-permute-start.9 = (bf16[4,48,256]{2,1,0:T(8,128)(2,1)S(1)}, bf16[4,48,256]{2,1,0:T(8,128)(2,1)S(1)}, u32[]{:S(2)}, u32[]{:S(2)}) collective-permute-start(bf16[4,48,256]{2,1,0:T(8,128)(2,1)S(1)} %pad_maximum_fusion.1.block_ref), channel_id=1, source_target_pairs={{0,2},{1,3},{2,0},{3,1},{4,6},{5,7},{6,4},{7,5},{8,10},{9,11},{10,... | collective-permute-start | bytes 294920 | tf_op jit(solution)/shard_map/ppermute | solution.py:29
  47.8 2.3 %shard_map.125 = (bf16[4,48,256]{2,1,0:T(8,128)(2,1)S(1)}, bf16[3072,768]{1,0:T(8,128)(2,1)S(1)}) custom-call(bf16[4,48,256]{2,1,0:T(8,128)(2,1)S(1)} %pad_maximum_fusion.1.block_ref, bf16[6144,768]{1,0:T(8,128)(2,1)} %from_ref.3), custom_call_target="tpu_custom_call" | custom-call | bytes 6000000 | tf_op jit(solution)/shard_map/pallas_call | solution.py:381
  50.2 1.6 %collective-permute-done.9 = bf16[4,48,256]{2,1,0:T(8,128)(2,1)S(1)} collective-permute-done((bf16[4,48,256]{2,1,0:T(8,128)(2,1)S(1)}, bf16[4,48,256]{2,1,0:T(8,128)(2,1)S(1)}, u32[]{:S(2)}, u32[]{:S(2)}) %collective-permute-start.9) | collective-permute-done | bytes 98336 | tf_op jit(solution)/shard_map/ppermute | solution.py:29
  51.9 1.4 %collective-permute-done.10.other_ref = bf16[8,48,256]{2,1,0:T(8,128)(2,1)S(1)} collective-permute-done((bf16[8,48,256]{2,1,0:T(8,128)(2,1)S(1)}, bf16[8,48,256]{2,1,0:T(8,128)(2,1)S(1)}, u32[]{:S(2)}, u32[]{:S(2)}) %collective-permute-start.10) | collective-permute-done | bytes 196640 | tf_op jit(solution)/shard_map/ppermute | solution.py:29
  53.3 2.4 %shard_map.126 = bf16[2,16,768]{2,1,0:T(8,128)(2,1)} custom-call(s32[1]{0:T(128)} %bitcast.me_ref, bf16[8,48,256]{2,1,0:T(8,128)(2,1)S(1)} %constant_dynamic-update-slice_fusion.mine_ref, bf16[8,48,256]{2,1,0:T(8,128)(2,1)S(1)} %collective-permute-done.10.other_ref, bf16[2,16,768]{2,1,0:T(8,128)(2,1)S(1)} %copy-done.3, ...), custom_call_target="tpu_custom_call" | custom-call | tf_op jit(solution)/shard_map/pallas_call | solution.py:408
  (30 shorter events, 0.3 us)
Async XLA Ops:
  0.0 10.8 %collective-permute-start = (bf16[32,768]{1,0:T(8,128)(2,1)}, bf16[32,768]{1,0:T(8,128)(2,1)S(1)}, u32[]{:S(2)}, u32[]{:S(2)}) collective-permute-start(bf16[32,768]{1,0:T(8,128)(2,1)} %bitcast.12), channel_id=1, source_target_pairs={{0,4},{1,5},{2,6},{3,7},{4,0},{5,1},{6,2},{7,3},{8,12},{9,13},{10,... | collective-permute-start | bytes 147464 | tf_op jit(solution)/shard_map/ppermute | solution.py:29
  3.0 7.8 %collective-permute-start.1 = (bf16[32,768]{1,0:T(8,128)(2,1)}, bf16[32,768]{1,0:T(8,128)(2,1)S(1)}, u32[]{:S(2)}, u32[]{:S(2)}) collective-permute-start(bf16[32,768]{1,0:T(8,128)(2,1)} %bitcast.13), channel_id=1, source_target_pairs={{0,8},{1,9},{2,10},{3,11},{4,12},{5,13},{6,14},{7,15},{8,0},{9,1},... | collective-permute-start | bytes 147464 | tf_op jit(solution)/shard_map/ppermute | solution.py:29
  5.6 6.1 %collective-permute-start.2 = (bf16[32,768]{1,0:T(8,128)(2,1)}, bf16[32,768]{1,0:T(8,128)(2,1)S(1)}, u32[]{:S(2)}, u32[]{:S(2)}) collective-permute-start(bf16[32,768]{1,0:T(8,128)(2,1)} %bitcast.14), channel_id=1, source_target_pairs={{0,12},{1,13},{2,14},{3,15},{4,8},{5,9},{6,10},{7,11},{8,4},{9,5},... | collective-permute-start | bytes 147464 | tf_op jit(solution)/shard_map/ppermute | solution.py:29
  11.7 1.7 %collective-permute-start.4 = (bf16[4,32,768]{2,1,0:T(8,128)(2,1)S(1)}, bf16[4,32,768]{2,1,0:T(8,128)(2,1)S(1)}, u32[]{:S(2)}, u32[]{:S(2)}) collective-permute-start(bf16[4,32,768]{2,1,0:T(8,128)(2,1)S(1)} %pad_maximum_fusion.rest_0_), channel_id=1, source_target_pairs={{0,1},{1,0},{2,3},{3,2},{4,5},{5,4},{6,7},{7,6},{8,9},{9,8},{10,11... | collective-permute-start | bytes 589832 | tf_op jit(solution)/shard_map/ppermute | solution.py:29
  11.8 7.3 %collective-permute-start.3 = (bf16[4,32,768]{2,1,0:T(8,128)(2,1)S(1)}, bf16[4,32,768]{2,1,0:T(8,128)(2,1)S(1)}, u32[]{:S(2)}, u32[]{:S(2)}) collective-permute-start(bf16[4,32,768]{2,1,0:T(8,128)(2,1)S(1)} %pad_maximum_fusion.rest_0_), channel_id=1, source_target_pairs={{0,2},{1,3},{2,0},{3,1},{4,6},{5,7},{6,4},{7,5},{8,10},{9,11},{10,... | collective-permute-start | bytes 589832 | tf_op jit(solution)/shard_map/ppermute | solution.py:29
  19.1 2.0 %collective-permute-start.5 = (bf16[4,32,768]{2,1,0:T(8,128)(2,1)S(1)}, bf16[4,32,768]{2,1,0:T(8,128)(2,1)S(1)}, u32[]{:S(2)}, u32[]{:S(2)}) collective-permute-start(bf16[4,32,768]{2,1,0:T(8,128)(2,1)S(1)} %collective-permute-done.3.rest_0_.rest_2_), channel_id=1, source_target_pairs={{0,1},{1,0},{2,3},{3,2},{4,5},{5,4},{6,7},{7,6},{8,9},{9,8},{10,11... | collective-permute-start | bytes 589832 | tf_op jit(solution)/shard_map/ppermute | solution.py:29
  21.2 11.3 %copy-start.5 = (f32[6144]{0:T(1024)S(1)}, f32[6144]{0:T(1024)}, u32[]{:S(2)}) copy-start(f32[6144]{0:T(1024)} %param.16) | copy-start | bytes 73732
  21.2 11.3 %copy-start.6 = (f32[24]{0:T(128)S(1)}, f32[24]{0:T(128)}, u32[]{:S(2)}) copy-start(f32[24]{0:T(128)} %param.15) | copy-start | bytes 292
  21.2 18.0 %copy-start = (bf16[6,16,6144]{2,1,0:T(8,128)(2,1)S(1)}, bf16[6,16,6144]{2,1,0:T(8,128)(2,1)}, u32[]{:S(2)}) copy-start(bf16[6,16,6144]{2,1,0:T(8,128)(2,1)} %values_ref.1) | copy-start | bytes 3538948
  21.2 18.0 %copy-start.1 = (bf16[6,16,3072]{2,1,0:T(8,128)(2,1)S(1)}, bf16[6,16,3072]{2,1,0:T(8,128)(2,1)}, u32[]{:S(2)}) copy-start(bf16[6,16,3072]{2,1,0:T(8,128)(2,1)} %keys_one_ref.1) | copy-start | bytes 1769476
  21.2 18.0 %copy-start.2 = (bf16[6,16,3072]{2,1,0:T(8,128)(2,1)S(1)}, bf16[6,16,3072]{2,1,0:T(8,128)(2,1)}, u32[]{:S(2)}) copy-start(bf16[6,16,3072]{2,1,0:T(8,128)(2,1)} %keys_two_ref.1) | copy-start | bytes 1769476
  21.3 18.0 %copy-start.4 = (s32[1,6]{1,0:T(1,128)S(1)}, s32[1,6]{1,0:T(1,128)}, u32[]{:S(2)}) copy-start(s32[1,6]{1,0:T(1,128)} %table_ref.1) | copy-start | bytes 76
  26.4 12.8 %all-to-all-start = ((bf16[16,18,128]{2,1,0:T(8,128)(2,1)}), bf16[16,18,128]{2,1,0:T(8,128)(2,1)S(1)}, u32[]{:S(2)}, u32[]{:S(2)}) async-start(bf16[16,18,128]{2,1,0:T(8,128)(2,1)} %shard_map.121.after_ref), calls=%async_computation | async-start | bytes 196608 | tf_op jit(solution)/shard_map/all_to_all | solution.py:463
  40.9 12.4 %copy-start.3 = (bf16[2,16,768]{2,1,0:T(8,128)(2,1)S(1)}, bf16[2,16,768]{2,1,0:T(8,128)(2,1)}, u32[]{:S(2)}) copy-start(bf16[2,16,768]{2,1,0:T(8,128)(2,1)} %inputs_ref.1) | copy-start | bytes 147460
  41.0 5.9 %collective-permute-start.7 = (bf16[48,256]{1,0:T(8,128)(2,1)S(1)}, bf16[48,256]{1,0:T(8,128)(2,1)S(1)}, u32[]{:S(2)}, u32[]{:S(2)}) collective-permute-start(bf16[48,256]{1,0:T(8,128)(2,1)S(1)} %shard_map.123.block_ref), channel_id=1, source_target_pairs={{0,8},{1,9},{2,10},{3,11},{4,12},{5,13},{6,14},{7,15},{8,0},{9,1},... | collective-permute-start | bytes 73736 | tf_op jit(solution)/shard_map/ppermute | solution.py:29
  41.2 5.7 %collective-permute-start.8 = (bf16[48,256]{1,0:T(8,128)(2,1)S(1)}, bf16[48,256]{1,0:T(8,128)(2,1)S(1)}, u32[]{:S(2)}, u32[]{:S(2)}) collective-permute-start(bf16[48,256]{1,0:T(8,128)(2,1)S(1)} %shard_map.123.block_ref), channel_id=1, source_target_pairs={{0,12},{1,13},{2,14},{3,15},{4,8},{5,9},{6,10},{7,11},{8,4},{9,5},... | collective-permute-start | bytes 73736 | tf_op jit(solution)/shard_map/ppermute | solution.py:29
  43.1 4.0 %collective-permute-start.6 = (bf16[48,256]{1,0:T(8,128)(2,1)S(1)}, bf16[48,256]{1,0:T(8,128)(2,1)S(1)}, u32[]{:S(2)}, u32[]{:S(2)}) collective-permute-start(bf16[48,256]{1,0:T(8,128)(2,1)S(1)} %shard_map.123.block_ref), channel_id=1, source_target_pairs={{0,4},{1,5},{2,6},{3,7},{4,0},{5,1},{6,2},{7,3},{8,12},{9,13},{10,... | collective-permute-start | bytes 73736 | tf_op jit(solution)/shard_map/ppermute | solution.py:29
  47.1 4.7 %collective-permute-start.9 = (bf16[4,48,256]{2,1,0:T(8,128)(2,1)S(1)}, bf16[4,48,256]{2,1,0:T(8,128)(2,1)S(1)}, u32[]{:S(2)}, u32[]{:S(2)}) collective-permute-start(bf16[4,48,256]{2,1,0:T(8,128)(2,1)S(1)} %pad_maximum_fusion.1.block_ref), channel_id=1, source_target_pairs={{0,2},{1,3},{2,0},{3,1},{4,6},{5,7},{6,4},{7,5},{8,10},{9,11},{10,... | collective-permute-start | bytes 294920 | tf_op jit(solution)/shard_map/ppermute | solution.py:29
  51.8 1.5 %collective-permute-start.10 = (bf16[8,48,256]{2,1,0:T(8,128)(2,1)S(1)}, bf16[8,48,256]{2,1,0:T(8,128)(2,1)S(1)}, u32[]{:S(2)}, u32[]{:S(2)}) collective-permute-start(bf16[8,48,256]{2,1,0:T(8,128)(2,1)S(1)} %constant_dynamic-update-slice_fusion.mine_ref), channel_id=1, source_target_pairs={{0,1},{1,0},{2,3},{3,2},{4,5},{5,4},{6,7},{7,6},{8,9},{9,8},{10,11... | collective-permute-start | bytes 589832 | tf_op jit(solution)/shard_map/ppermute | solution.py:29

commit v5 on v4

--- a/solution.py
+++ b/solution.py
@@ -71,10 +71,7 @@
 
 
 def slots(n):
-    outer, middle = radices(n)
-    return [
-        (m * outer + entry, core) for m in range(middle) for core in range(2) for entry in range(outer)
-    ]
+    return [(entry, core) for core in range(2) for entry in range(n // 2)]
 
 
 def fetches(n, order, me, from_ref, to_ref, sems):
@@ -206,14 +203,12 @@
     held, gain, weight_a = fetch(me, block, gain, weight, n, order[:first])
     row = jnp.stack([held] + arrived)
     later = [swap(row, n, m * 2) for m in range(1, middle)]
-    blocks = [row, swap(row, n, 1)]
     squares = jnp.zeros((rows, part), F32)
-    squares, weight_b = squares_beside(me, weight, blocks, squares, n, order[first:second])
+    squares, weight_b = squares_beside(me, weight, [row], squares, n, order[first:second])
     later, squares = lax.optimization_barrier((later, squares))
-    across = [swap(each, n, 1) for each in later]
-    for each, other in zip(later, across, strict=True):
-        blocks += [each, other]
-    squares, weight_c = squares_beside(me, weight, blocks[2:-1], squares, n, order[second:])
+    mine = jnp.concatenate([row] + later)
+    blocks = [mine, swap(mine, n, 1)]
+    squares, weight_c = squares_beside(me, weight, later, squares, n, order[second:])
     vmem = pl.BlockSpec(memory_space=pltpu.VMEM)
     return pl.pallas_call(
         functools.partial(project_kernel, n, len(blocks)),

time: 56 us -> 55.3 us (0.987)
  waiting for transfers between devices: 11.6 us -> 9.79 us
  starting transfers between devices: 17 us -> 18.1 us
    ppermute x11 -> x10, waiting for transfers between devices: 5.7 us -> 3.84 us  [swap(): return lax.ppermute(block, 'gx', [(i, i ^ mask) for i in range(n)])]
    ppermute x11 -> x10, starting transfers between devices: 11.6 us -> 12.1 us  [swap(): return lax.ppermute(block, 'gx', [(i, i ^ mask) for i in range(n)])]
  transfers between devices with their start and end apart: 12 -> 11, of which waited for: 6 -> 4; matrix products, arithmetic and copies ran while one was open for 0% -> 0% of each run, Pallas kernels for 29% -> 29%
where the time goes in v5:
time: 55.3 us; the launch traced here: 55 us
  Pallas kernels  25.3 us (46%)
  starting transfers between devices  18.1 us (33%)
  waiting for transfers between devices  9.79 us (18%)
  between operations  1.58 us (3%)
    ppermute x10, starting transfers between devices, swap(): return lax.ppermute(block, 'gx', [(i, i ^ mask) for i in range(n)])  12.1 us
    pallas_call x2, Pallas kernels, squares_beside(): pl.pallas_call(functools.partial(squares_kernel, n, order, len(blocks)),...  6.17 us
    all_to_all x1, starting transfers between devices, local(): received = lax.all_to_all(sent, 'gx', 0, 0)  5.97 us
    all_to_all x1, waiting for transfers between devices, local(): received = lax.all_to_all(sent, 'gx', 0, 0)  5.95 us
    pallas_call x1, Pallas kernels, fetch(): pl.pallas_call(functools.partial(fetch_kernel, n, order), out_shape=(pltp...  5.2 us
    pallas_call x1, Pallas kernels, project(): pl.pallas_call(functools.partial(project_kernel, n, len(blocks)), out_sha...  5.18 us
    pallas_call x2, Pallas kernels, keep(): pl.pallas_call(functools.partial(keep_kernel, half), out_shape=(jax.Shape...  4.69 us
    ppermute x10, waiting for transfers between devices, swap(): return lax.ppermute(block, 'gx', [(i, i ^ mask) for i in range(n)])  3.84 us
  transfers between devices with their start and end apart: 11, of which 4 were waited for; matrix products, arithmetic and copies ran while one was open for 0% of the time, Pallas kernels for 29%

profile of v5, /device:TPU:0, one launch (start us, length us, event | category | flops | bytes accessed | tf_op | source)
XLA Modules:
  0.0 55.0 jit_solution(4599702492626535967)
XLA Ops:
  0.0 5.0 %collective-permute-start.2 = (bf16[32,768]{1,0:T(8,128)(2,1)}, bf16[32,768]{1,0:T(8,128)(2,1)S(1)}, u32[]{:S(2)}, u32[]{:S(2)}) collective-permute-start(bf16[32,768]{1,0:T(8,128)(2,1)} %bitcast.16), channel_id=1, source_target_pairs={{0,12},{1,13},{2,14},{3,15},{4,8},{5,9},{6,10},{7,11},{8,4},{9,5},... | collective-permute-start | bytes 147464 | tf_op jit(solution)/shard_map/ppermute | solution.py:29
  5.1 0.6 %collective-permute-start = (bf16[32,768]{1,0:T(8,128)(2,1)}, bf16[32,768]{1,0:T(8,128)(2,1)S(1)}, u32[]{:S(2)}, u32[]{:S(2)}) collective-permute-start(bf16[32,768]{1,0:T(8,128)(2,1)} %bitcast.18), channel_id=1, source_target_pairs={{0,4},{1,5},{2,6},{3,7},{4,0},{5,1},{6,2},{7,3},{8,12},{9,13},{10,... | collective-permute-start | bytes 147464 | tf_op jit(solution)/shard_map/ppermute | solution.py:29
  5.6 5.2 %shard_map.118 = (bf16[32,768]{1,0:T(8,128)(2,1)S(1)}, f32[16,1,768]{2,1,0:T(1,128)S(1)}, bf16[8,768,1152]{2,1,0:T(8,128)(2,1)S(1)}) custom-call(s32[1]{0:T(128)} %bitcast.me_ref, bf16[32,768]{1,0:T(8,128)(2,1)} %bitcast.19, f32[16,1,768]{2,1,0:T(1,128)} %bitcast.25, bf16[12288,1152]{1,0:T(8,128)(2,1)} %weight_ref.5), custom_call_target="tpu_custom_call" | custom-call | bytes 15000000 | tf_op jit(solution)/shard_map/pallas_call | solution.py:107
  10.9 1.8 %collective-permute-start.3 = (bf16[4,32,768]{2,1,0:T(8,128)(2,1)S(1)}, bf16[4,32,768]{2,1,0:T(8,128)(2,1)S(1)}, u32[]{:S(2)}, u32[]{:S(2)}) collective-permute-start(bf16[4,32,768]{2,1,0:T(8,128)(2,1)S(1)} %pad_maximum_fusion.rest_0_), channel_id=1, source_target_pairs={{0,2},{1,3},{2,0},{3,1},{4,6},{5,7},{6,4},{7,5},{8,10},{9,11},{10,... | collective-permute-start | bytes 589832 | tf_op jit(solution)/shard_map/ppermute | solution.py:29
  12.7 4.1 %shard_map.119 = (f32[32,768]{1,0:T(8,128)S(1)}, bf16[6,768,1152]{2,1,0:T(8,128)(2,1)S(1)}) custom-call(s32[1]{0:T(128)} %bitcast.me_ref, bf16[12288,1152]{1,0:T(8,128)(2,1)} %weight_ref.5, bf16[4,32,768]{2,1,0:T(8,128)(2,1)S(1)} %pad_maximum_fusion.rest_0_, f32[32,768]{1,0:T(8,128)S(1)} %broadcast_in_dim.3.rest_1_), custom_call_target="tpu_custom_call" | custom-call | bytes 12599999 | tf_op jit(solution)/shard_map/pallas_call | solution.py:150
  16.9 0.1 collective-permute-done.3.rest_0_
  17.1 0.1 collective-permute-start.4
  17.2 2.0 %shard_map.120 = (f32[32,768]{1,0:T(8,128)S(1)}, bf16[2,768,1152]{2,1,0:T(8,128)(2,1)S(1)}) custom-call(s32[1]{0:T(128)} %bitcast.me_ref, bf16[12288,1152]{1,0:T(8,128)(2,1)} %weight_ref.5, bf16[4,32,768]{2,1,0:T(8,128)(2,1)S(1)} %collective-permute-done.3.rest_0_, f32[32,768]{1,0:T(8,128)S(1)} %get-tuple-element.26.rest_1_), custom_call_target="tpu_custom_call" | custom-call | bytes 4200000 | tf_op jit(solution)/shard_map/pallas_call | solution.py:150
  19.3 5.2 %shard_map.121.after_ref = bf16[16,18,128]{2,1,0:T(8,128)(2,1)} custom-call(s32[1]{0:T(128)} %bitcast.me_ref, f32[16,1,768]{2,1,0:T(1,128)S(1)} %get-tuple-element.22.gain_ref, f32[32,768]{1,0:T(8,128)S(1)} %get-tuple-element.27.before_ref, bf16[8,32,768]{2,1,0:T(8,128)(2,1)S(1)} %constant_dynamic-update-slice_fusion.rest_0_, ...), custom_call_target="tpu_custom_call" | custom-call | bytes 18000000 | tf_op jit(solution)/shard_map/pallas_call | solution.py:213
  24.5 6.0 %all-to-all-start = ((bf16[16,18,128]{2,1,0:T(8,128)(2,1)}), bf16[16,18,128]{2,1,0:T(8,128)(2,1)S(1)}, u32[]{:S(2)}, u32[]{:S(2)}) async-start(bf16[16,18,128]{2,1,0:T(8,128)(2,1)} %shard_map.121.after_ref), calls=%async_computation | async-start | bytes 196608 | tf_op jit(solution)/shard_map/all_to_all | solution.py:458
  31.7 0.1 copy.13.lambda_ref
  31.9 0.1 shard_map.122
  31.9 5.9 %all-to-all-done.received_ref = bf16[16,18,128]{2,1,0:T(8,128)(2,1)S(1)} async-done(((bf16[16,18,128]{2,1,0:T(8,128)(2,1)}), bf16[16,18,128]{2,1,0:T(8,128)(2,1)S(1)}, u32[]{:S(2)}, u32[]{:S(2)}) %all-to-all-start) | async-done | bytes 73760 | tf_op jit(solution)/shard_map/all_to_all | solution.py:458
  37.9 1.7 %shard_map.123.block_ref = bf16[48,256]{1,0:T(8,128)(2,1)S(1)} custom-call(s32[1,6]{1,0:T(1,128)S(1)} %copy-done.4, s32[1]{0:T(128)S(6)} %copy.19.length_ref, bf16[16,18,128]{2,1,0:T(8,128)(2,1)S(1)} %all-to-all-done.received_ref, f32[2,1,128]{2,1,0:T(1,128)S(1)} %get-tuple-element.31.cos_ref, f32[2,1,128]{2,1,0:T(1,128)S(1)} %get-tuple-element.32.sin_ref, ...), custom_call_target="tpu_custom_call" | custom-call | bytes 30000000 | tf_op jit(solution)/shard_map/pallas_call | solution.py:321
  39.6 0.7 %collective-permute-start.7 = (bf16[48,256]{1,0:T(8,128)(2,1)S(1)}, bf16[48,256]{1,0:T(8,128)(2,1)S(1)}, u32[]{:S(2)}, u32[]{:S(2)}) collective-permute-start(bf16[48,256]{1,0:T(8,128)(2,1)S(1)} %shard_map.123.block_ref), channel_id=1, source_target_pairs={{0,12},{1,13},{2,14},{3,15},{4,8},{5,9},{6,10},{7,11},{8,4},{9,5},... | collective-permute-start | bytes 73736 | tf_op jit(solution)/shard_map/ppermute | solution.py:29
  40.3 0.6 %collective-permute-start.6 = (bf16[48,256]{1,0:T(8,128)(2,1)S(1)}, bf16[48,256]{1,0:T(8,128)(2,1)S(1)}, u32[]{:S(2)}, u32[]{:S(2)}) collective-permute-start(bf16[48,256]{1,0:T(8,128)(2,1)S(1)} %shard_map.123.block_ref), channel_id=1, source_target_pairs={{0,8},{1,9},{2,10},{3,11},{4,12},{5,13},{6,14},{7,15},{8,0},{9,1},... | collective-permute-start | bytes 73736 | tf_op jit(solution)/shard_map/ppermute | solution.py:29
  40.9 3.2 %collective-permute-start.5 = (bf16[48,256]{1,0:T(8,128)(2,1)S(1)}, bf16[48,256]{1,0:T(8,128)(2,1)S(1)}, u32[]{:S(2)}, u32[]{:S(2)}) collective-permute-start(bf16[48,256]{1,0:T(8,128)(2,1)S(1)} %shard_map.123.block_ref), channel_id=1, source_target_pairs={{0,4},{1,5},{2,6},{3,7},{4,0},{5,1},{6,2},{7,3},{8,12},{9,13},{10,... | collective-permute-start | bytes 73736 | tf_op jit(solution)/shard_map/ppermute | solution.py:29
  44.0 2.3 %shard_map.124 = (bf16[48,256]{1,0:T(8,128)(2,1)S(1)}, bf16[3072,768]{1,0:T(8,128)(2,1)S(1)}) custom-call(bf16[48,256]{1,0:T(8,128)(2,1)S(1)} %shard_map.123.block_ref, bf16[6144,768]{1,0:T(8,128)(2,1)} %from_ref.3), custom_call_target="tpu_custom_call" | custom-call | bytes 6000000 | tf_op jit(solution)/shard_map/pallas_call | solution.py:376
  46.4 0.1 collective-permute-start.8
  46.5 2.3 %shard_map.125 = (bf16[4,48,256]{2,1,0:T(8,128)(2,1)S(1)}, bf16[3072,768]{1,0:T(8,128)(2,1)S(1)}) custom-call(bf16[4,48,256]{2,1,0:T(8,128)(2,1)S(1)} %pad_maximum_fusion.1.block_ref, bf16[6144,768]{1,0:T(8,128)(2,1)} %from_ref.3), custom_call_target="tpu_custom_call" | custom-call | bytes 6000000 | tf_op jit(solution)/shard_map/pallas_call | solution.py:376
  48.9 2.2 %collective-permute-done.8 = bf16[4,48,256]{2,1,0:T(8,128)(2,1)S(1)} collective-permute-done((bf16[4,48,256]{2,1,0:T(8,128)(2,1)S(1)}, bf16[4,48,256]{2,1,0:T(8,128)(2,1)S(1)}, u32[]{:S(2)}, u32[]{:S(2)}) %collective-permute-start.8) | collective-permute-done | bytes 98336 | tf_op jit(solution)/shard_map/ppermute | solution.py:29
  51.1 0.1 collective-permute-start.9
  51.2 1.4 %collective-permute-done.9.other_ref = bf16[8,48,256]{2,1,0:T(8,128)(2,1)S(1)} collective-permute-done((bf16[8,48,256]{2,1,0:T(8,128)(2,1)S(1)}, bf16[8,48,256]{2,1,0:T(8,128)(2,1)S(1)}, u32[]{:S(2)}, u32[]{:S(2)}) %collective-permute-start.9) | collective-permute-done | bytes 196640 | tf_op jit(solution)/shard_map/ppermute | solution.py:29
  52.7 2.4 %shard_map.126 = bf16[2,16,768]{2,1,0:T(8,128)(2,1)} custom-call(s32[1]{0:T(128)} %bitcast.me_ref, bf16[8,48,256]{2,1,0:T(8,128)(2,1)S(1)} %constant_dynamic-update-slice_fusion.5.mine_ref, bf16[8,48,256]{2,1,0:T(8,128)(2,1)S(1)} %collective-permute-done.9.other_ref, bf16[2,16,768]{2,1,0:T(8,128)(2,1)S(1)} %copy-done.3, ...), custom_call_target="tpu_custom_call" | custom-call | tf_op jit(solution)/shard_map/pallas_call | solution.py:403
  (33 shorter events, 0.2 us)
Async XLA Ops:
  0.0 10.8 %collective-permute-start.2 = (bf16[32,768]{1,0:T(8,128)(2,1)}, bf16[32,768]{1,0:T(8,128)(2,1)S(1)}, u32[]{:S(2)}, u32[]{:S(2)}) collective-permute-start(bf16[32,768]{1,0:T(8,128)(2,1)} %bitcast.16), channel_id=1, source_target_pairs={{0,12},{1,13},{2,14},{3,15},{4,8},{5,9},{6,10},{7,11},{8,4},{9,5},... | collective-permute-start | bytes 147464 | tf_op jit(solution)/shard_map/ppermute | solution.py:29
  5.0 5.8 %collective-permute-start.1 = (bf16[32,768]{1,0:T(8,128)(2,1)}, bf16[32,768]{1,0:T(8,128)(2,1)S(1)}, u32[]{:S(2)}, u32[]{:S(2)}) collective-permute-start(bf16[32,768]{1,0:T(8,128)(2,1)} %bitcast.17), channel_id=1, source_target_pairs={{0,8},{1,9},{2,10},{3,11},{4,12},{5,13},{6,14},{7,15},{8,0},{9,1},... | collective-permute-start | bytes 147464 | tf_op jit(solution)/shard_map/ppermute | solution.py:29
  5.1 5.8 %collective-permute-start = (bf16[32,768]{1,0:T(8,128)(2,1)}, bf16[32,768]{1,0:T(8,128)(2,1)S(1)}, u32[]{:S(2)}, u32[]{:S(2)}) collective-permute-start(bf16[32,768]{1,0:T(8,128)(2,1)} %bitcast.18), channel_id=1, source_target_pairs={{0,4},{1,5},{2,6},{3,7},{4,0},{5,1},{6,2},{7,3},{8,12},{9,13},{10,... | collective-permute-start | bytes 147464 | tf_op jit(solution)/shard_map/ppermute | solution.py:29
  10.9 6.1 %collective-permute-start.3 = (bf16[4,32,768]{2,1,0:T(8,128)(2,1)S(1)}, bf16[4,32,768]{2,1,0:T(8,128)(2,1)S(1)}, u32[]{:S(2)}, u32[]{:S(2)}) collective-permute-start(bf16[4,32,768]{2,1,0:T(8,128)(2,1)S(1)} %pad_maximum_fusion.rest_0_), channel_id=1, source_target_pairs={{0,2},{1,3},{2,0},{3,1},{4,6},{5,7},{6,4},{7,5},{8,10},{9,11},{10,... | collective-permute-start | bytes 589832 | tf_op jit(solution)/shard_map/ppermute | solution.py:29
  17.1 2.1 %collective-permute-start.4 = (bf16[8,32,768]{2,1,0:T(8,128)(2,1)S(1)}, bf16[8,32,768]{2,1,0:T(8,128)(2,1)S(1)}, u32[]{:S(2)}, u32[]{:S(2)}) collective-permute-start(bf16[8,32,768]{2,1,0:T(8,128)(2,1)S(1)} %constant_dynamic-update-slice_fusion.rest_0_), channel_id=1, source_target_pairs={{0,1},{1,0},{2,3},{3,2},{4,5},{5,4},{6,7},{7,6},{8,9},{9,8},{10,11... | collective-permute-start | bytes 1179656 | tf_op jit(solution)/shard_map/ppermute | solution.py:29
  19.2 12.5 %copy-start.6 = (f32[24]{0:T(128)S(1)}, f32[24]{0:T(128)}, u32[]{:S(2)}) copy-start(f32[24]{0:T(128)} %param.15) | copy-start | bytes 292
  19.2 12.6 %copy-start.5 = (f32[6144]{0:T(1024)S(1)}, f32[6144]{0:T(1024)}, u32[]{:S(2)}) copy-start(f32[6144]{0:T(1024)} %param.16) | copy-start | bytes 73732
  19.2 18.6 %copy-start = (bf16[6,16,6144]{2,1,0:T(8,128)(2,1)S(1)}, bf16[6,16,6144]{2,1,0:T(8,128)(2,1)}, u32[]{:S(2)}) copy-start(bf16[6,16,6144]{2,1,0:T(8,128)(2,1)} %values_ref.1) | copy-start | bytes 3538948
  19.2 18.6 %copy-start.1 = (bf16[6,16,3072]{2,1,0:T(8,128)(2,1)S(1)}, bf16[6,16,3072]{2,1,0:T(8,128)(2,1)}, u32[]{:S(2)}) copy-start(bf16[6,16,3072]{2,1,0:T(8,128)(2,1)} %keys_one_ref.1) | copy-start | bytes 1769476
  19.3 18.6 %copy-start.2 = (bf16[6,16,3072]{2,1,0:T(8,128)(2,1)S(1)}, bf16[6,16,3072]{2,1,0:T(8,128)(2,1)}, u32[]{:S(2)}) copy-start(bf16[6,16,3072]{2,1,0:T(8,128)(2,1)} %keys_two_ref.1) | copy-start | bytes 1769476
  19.3 18.6 %copy-start.4 = (s32[1,6]{1,0:T(1,128)S(1)}, s32[1,6]{1,0:T(1,128)}, u32[]{:S(2)}) copy-start(s32[1,6]{1,0:T(1,128)} %table_ref.1) | copy-start | bytes 76
  24.5 13.4 %all-to-all-start = ((bf16[16,18,128]{2,1,0:T(8,128)(2,1)}), bf16[16,18,128]{2,1,0:T(8,128)(2,1)S(1)}, u32[]{:S(2)}, u32[]{:S(2)}) async-start(bf16[16,18,128]{2,1,0:T(8,128)(2,1)} %shard_map.121.after_ref), calls=%async_computation | async-start | bytes 196608 | tf_op jit(solution)/shard_map/all_to_all | solution.py:458
  39.6 13.1 %copy-start.3 = (bf16[2,16,768]{2,1,0:T(8,128)(2,1)S(1)}, bf16[2,16,768]{2,1,0:T(8,128)(2,1)}, u32[]{:S(2)}) copy-start(bf16[2,16,768]{2,1,0:T(8,128)(2,1)} %inputs_ref.1) | copy-start | bytes 147460
  39.6 6.8 %collective-permute-start.7 = (bf16[48,256]{1,0:T(8,128)(2,1)S(1)}, bf16[48,256]{1,0:T(8,128)(2,1)S(1)}, u32[]{:S(2)}, u32[]{:S(2)}) collective-permute-start(bf16[48,256]{1,0:T(8,128)(2,1)S(1)} %shard_map.123.block_ref), channel_id=1, source_target_pairs={{0,12},{1,13},{2,14},{3,15},{4,8},{5,9},{6,10},{7,11},{8,4},{9,5},... | collective-permute-start | bytes 73736 | tf_op jit(solution)/shard_map/ppermute | solution.py:29
  40.3 6.1 %collective-permute-start.6 = (bf16[48,256]{1,0:T(8,128)(2,1)S(1)}, bf16[48,256]{1,0:T(8,128)(2,1)S(1)}, u32[]{:S(2)}, u32[]{:S(2)}) collective-permute-start(bf16[48,256]{1,0:T(8,128)(2,1)S(1)} %shard_map.123.block_ref), channel_id=1, source_target_pairs={{0,8},{1,9},{2,10},{3,11},{4,12},{5,13},{6,14},{7,15},{8,0},{9,1},... | collective-permute-start | bytes 73736 | tf_op jit(solution)/shard_map/ppermute | solution.py:29
  40.9 5.5 %collective-permute-start.5 = (bf16[48,256]{1,0:T(8,128)(2,1)S(1)}, bf16[48,256]{1,0:T(8,128)(2,1)S(1)}, u32[]{:S(2)}, u32[]{:S(2)}) collective-permute-start(bf16[48,256]{1,0:T(8,128)(2,1)S(1)} %shard_map.123.block_ref), channel_id=1, source_target_pairs={{0,4},{1,5},{2,6},{3,7},{4,0},{5,1},{6,2},{7,3},{8,12},{9,13},{10,... | collective-permute-start | bytes 73736 | tf_op jit(solution)/shard_map/ppermute | solution.py:29
  46.4 4.7 %collective-permute-start.8 = (bf16[4,48,256]{2,1,0:T(8,128)(2,1)S(1)}, bf16[4,48,256]{2,1,0:T(8,128)(2,1)S(1)}, u32[]{:S(2)}, u32[]{:S(2)}) collective-permute-start(bf16[4,48,256]{2,1,0:T(8,128)(2,1)S(1)} %pad_maximum_fusion.1.block_ref), channel_id=1, source_target_pairs={{0,2},{1,3},{2,0},{3,1},{4,6},{5,7},{6,4},{7,5},{8,10},{9,11},{10,... | collective-permute-start | bytes 294920 | tf_op jit(solution)/shard_map/ppermute | solution.py:29
  51.1 1.5 %collective-permute-start.9 = (bf16[8,48,256]{2,1,0:T(8,128)(2,1)S(1)}, bf16[8,48,256]{2,1,0:T(8,128)(2,1)S(1)}, u32[]{:S(2)}, u32[]{:S(2)}) collective-permute-start(bf16[8,48,256]{2,1,0:T(8,128)(2,1)S(1)} %constant_dynamic-update-slice_fusion.5.mine_ref), channel_id=1, source_target_pairs={{0,1},{1,0},{2,3},{3,2},{4,5},{5,4},{6,7},{7,6},{8,9},{9,8},{10,11... | collective-permute-start | bytes 589832 | tf_op jit(solution)/shard_map/ppermute | solution.py:29

commit v6 on v5

--- a/solution.py
+++ b/solution.py
@@ -135,56 +135,94 @@
 
 
 def squares_kernel(n, order, count, me_ref, weight_ref, *rest):
-    blocks, (before, squares, weight_out, sems) = rest[:count], rest[count:]
+    blocks, (squares, weight_out, sems) = rest[:count], rest[count:]
     copies = fetches(n, order, me_ref[0], weight_ref, weight_out, sems)
     for copy in copies:
         copy.start()
-    squares[...] = add_squares(blocks, before[...])
+    squares[...] = add_squares(blocks, jnp.zeros(squares.shape, F32))
     for copy in copies:
         copy.wait()
 
 
-def squares_beside(me, weight, blocks, before, n, order):
+def squares_beside(me, weight, blocks, n, order):
     part, columns = weight.shape[0] // n, weight.shape[1]
     vmem = pl.BlockSpec(memory_space=pltpu.VMEM)
     return pl.pallas_call(
         functools.partial(squares_kernel, n, order, len(blocks)),
         out_shape=(
-            jax.ShapeDtypeStruct(before.shape, F32),
+            jax.ShapeDtypeStruct(blocks[0].shape[1:], F32),
             pltpu.VMEM((len(order), part, columns), BF16),
         ),
         in_specs=[
             pl.BlockSpec(memory_space=pltpu.SMEM),
             pl.BlockSpec(memory_space=pltpu.HBM),
         ]
-        + [vmem] * (len(blocks) + 1),
+        + [vmem] * len(blocks),
         out_specs=(vmem, vmem),
         scratch_shapes=[pltpu.SemaphoreType.DMA((len(order),))],
         compiler_params=pltpu.CompilerParams(vmem_limit_bytes=4 * 1024 * 1024),
         cost_estimate=hint(len(order) * 0.7),
-    )(me, far(weight), *blocks, before)
-
-
-def project_kernel(n, count, me_ref, gain_ref, before_ref, *rest):
-    blocks, (*helds, out_ref, spread) = rest[:count], rest[count:]
+    )(me, far(weight), *blocks)
+
+
+def more_squares_kernel(count, before, *rest):
+    *blocks, squares = rest
+    squares[...] = add_squares(blocks, before[...])
+
+
+def more_squares(blocks, before):
+    vmem = pl.BlockSpec(memory_space=pltpu.VMEM)
+    return pl.pallas_call(
+        functools.partial(more_squares_kernel, len(blocks)),
+        out_shape=jax.ShapeDtypeStruct(before.shape, F32),
+        in_specs=[vmem] * (len(blocks) + 1),
+        out_specs=vmem,
+        compiler_params=pltpu.CompilerParams(vmem_limit_bytes=4 * 1024 * 1024),
+        cost_estimate=hint(1),
+    )(before, *blocks)
+
+
+def project_kernel(n, order, me_ref, gain_ref, before_ref, mine_ref, other_ref, weight_ref, *rest):
+    *helds, out_ref, last, spread, total, kept, sems = rest
     me = me_ref[0]
     rows, part = before_ref.shape
-    square = add_squares(blocks[-1:], before_ref[...])
-    mean = jnp.sum(square, axis=1, keepdims=True) * (1.0 / (n * part))
-    factor = lax.rsqrt(mean + EPS)
-    refs = [(ref, entry) for ref in blocks for entry in range(ref.shape[0])]
+    copies = fetches(n, order, me, weight_ref, last, sems)
+    for copy in copies:
+        copy.start()
     places = [(held, slot) for held in helds for slot in range(held.shape[0])]
-    total = None
-    for (entry, core), (ref, at), (held, slot) in zip(slots(n), refs, places, strict=True):
-        gain = gain_ref[owner(me, entry, core, n)]
-        normed = (ref[at].astype(F32) * factor * gain).astype(BF16)
-        product = jnp.dot(normed, held[slot], preferred_element_type=F32)
-        total = product if total is None else total + product
-    columns = total.shape[1] // 128
+    early = len(places)
+    places += [(last, slot) for slot in range(len(order))]
+    blocks = list(zip(slots(n), places, strict=True))
+
+    def products(picked, factor):
+        summed = None
+        for (entry, core), (held, slot) in picked:
+            values = (mine_ref, other_ref)[core][entry].astype(F32)
+            normed = (values * factor * gain_ref[owner(me, entry, core, n)]).astype(BF16)
+            product = jnp.dot(normed, held[slot], preferred_element_type=F32)
+            summed = product if summed is None else summed + product
+        return summed
+
+    def row_factor():
+        square = add_squares([other_ref], before_ref[...])
+        mean = jnp.sum(square, axis=1, keepdims=True) * (1.0 / (n * part))
+        return lax.rsqrt(mean + EPS)
+
+    @pl.when(me >= 0)
+    def _():
+        factor = row_factor()
+        total[...] = products(blocks[:early], factor)
+        kept[...] = jnp.broadcast_to(factor, kept.shape)
+
+    for copy in copies:
+        copy.wait()
+    factor = kept[:, :1]
+    summed = total[...] + products(blocks[early:], factor)
+    columns = summed.shape[1] // 128
     steps = rows // n
     for block in range(columns):
         for step in range(steps):
-            spread[:, step * columns + block, :] = total[
+            spread[:, step * columns + block, :] = summed[
                 step * n : (step + 1) * n, block * 128 : (block + 1) * 128
             ]
     for target in range(n):
@@ -197,28 +235,34 @@
     pieces = rows // n * (columns // 128)
     outer, middle = radices(n)
     order = slots(n)
-    first, second = 2 * outer, n - max(1, outer // 2)
+    first, second = 3 * n // 8, 3 * n // 4
 
     arrived = [swap(block, n, o * 2 * middle) for o in range(1, outer)]
     held, gain, weight_a = fetch(me, block, gain, weight, n, order[:first])
     row = jnp.stack([held] + arrived)
     later = [swap(row, n, m * 2) for m in range(1, middle)]
-    squares = jnp.zeros((rows, part), F32)
-    squares, weight_b = squares_beside(me, weight, [row], squares, n, order[first:second])
+    squares, weight_b = squares_beside(me, weight, [row], n, order[first:second])
     later, squares = lax.optimization_barrier((later, squares))
     mine = jnp.concatenate([row] + later)
-    blocks = [mine, swap(mine, n, 1)]
-    squares, weight_c = squares_beside(me, weight, later, squares, n, order[second:])
-    vmem = pl.BlockSpec(memory_space=pltpu.VMEM)
-    return pl.pallas_call(
-        functools.partial(project_kernel, n, len(blocks)),
+    other = swap(mine, n, 1)
+    squares = more_squares(later, squares)
+    vmem = pl.BlockSpec(memory_space=pltpu.VMEM)
+    hbm = pl.BlockSpec(memory_space=pltpu.HBM)
+    return pl.pallas_call(
+        functools.partial(project_kernel, n, order[second:]),
         out_shape=jax.ShapeDtypeStruct((n, pieces, 128), BF16),
-        in_specs=[pl.BlockSpec(memory_space=pltpu.SMEM)] + [vmem] * (len(blocks) + 5),
+        in_specs=[pl.BlockSpec(memory_space=pltpu.SMEM)] + [vmem] * 4 + [hbm] + [vmem] * 2,
         out_specs=vmem,
-        scratch_shapes=[pltpu.VMEM((n, -(-pieces // 8) * 8, 128), F32)],
+        scratch_shapes=[
+            pltpu.VMEM((n - second, part, columns), BF16),
+            pltpu.VMEM((n, -(-pieces // 8) * 8, 128), F32),
+            pltpu.VMEM((rows, columns), F32),
+            pltpu.VMEM((rows, 128), F32),
+            pltpu.SemaphoreType.DMA((n - second,)),
+        ],
         compiler_params=pltpu.CompilerParams(vmem_limit_bytes=VMEM_LIMIT),
         cost_estimate=hint(6),
-    )(me, gain, squares, *blocks, near(weight_a), near(weight_b), near(weight_c))
+    )(me, gain, squares, mine, other, far(weight), near(weight_a), near(weight_b))
 
 
 def attend_kernel(

time: 55.3 us -> 54 us (0.976)
  Pallas kernels: 25.3 us -> 22.5 us
  waiting for transfers between devices: 9.79 us -> 11.8 us
    pallas_call x2 -> x1, Pallas kernels: 6.17 us -> 4.14 us  [squares_beside(): pl.pallas_call(functools.partial(squares_kernel, n, order, len(blocks)),...]
    ppermute x10, waiting for transfers between devices: 3.84 us -> 5.82 us  [swap(): return lax.ppermute(block, 'gx', [(i, i ^ mask) for i in range(n)])]
    pallas_call x1, Pallas kernels: 5.2 us -> 4.18 us  [fetch(): pl.pallas_call(functools.partial(fetch_kernel, n, order), out_shape=(pltp...]
    pallas_call x1 -> x2, Pallas kernels: 5.18 us -> 5.44 us  [the longest x1 5.39 us: project(): pl.pallas_call(functools.partial(project_kernel, n, order[second:]), out_...]
  transfers between devices with their start and end apart: 11 -> 11, of which waited for: 4 -> 5; matrix products, arithmetic and copies ran while one was open for 0% -> 0% of each run, Pallas kernels for 29% -> 24%
where the time goes in v6:
time: 54 us; the launch traced here: 53.7 us
  Pallas kernels  22.5 us (42%)
  starting transfers between devices  17.7 us (33%)
  waiting for transfers between devices  11.8 us (22%)
  between operations  1.54 us (3%)
    ppermute x10, starting transfers between devices, swap(): return lax.ppermute(block, 'gx', [(i, i ^ mask) for i in range(n)])  11.9 us
    all_to_all x1, waiting for transfers between devices, local(): received = lax.all_to_all(sent, 'gx', 0, 0)  5.95 us
    all_to_all x1, starting transfers between devices, local(): received = lax.all_to_all(sent, 'gx', 0, 0)  5.82 us
    ppermute x10, waiting for transfers between devices, swap(): return lax.ppermute(block, 'gx', [(i, i ^ mask) for i in range(n)])  5.82 us
    pallas_call x1, Pallas kernels, project(): pl.pallas_call(functools.partial(project_kernel, n, order[second:]), out_...  5.39 us
    pallas_call x2, Pallas kernels, keep(): pl.pallas_call(functools.partial(keep_kernel, half), out_shape=(jax.Shape...  4.69 us
    pallas_call x1, Pallas kernels, fetch(): pl.pallas_call(functools.partial(fetch_kernel, n, order), out_shape=(pltp...  4.18 us
    pallas_call x1, Pallas kernels, squares_beside(): pl.pallas_call(functools.partial(squares_kernel, n, order, len(blocks)),...  4.14 us
  transfers between devices with their start and end apart: 11, of which 5 were waited for; matrix products, arithmetic and copies ran while one was open for 0% of the time, Pallas kernels for 24%

profile of v6, /device:TPU:0, one launch (start us, length us, event | category | flops | bytes accessed | tf_op | source)
XLA Modules:
  0.0 53.7 jit_solution(17460772481759584913)
XLA Ops:
  0.0 5.0 %collective-permute-start.2 = (bf16[32,768]{1,0:T(8,128)(2,1)}, bf16[32,768]{1,0:T(8,128)(2,1)S(1)}, u32[]{:S(2)}, u32[]{:S(2)}) collective-permute-start(bf16[32,768]{1,0:T(8,128)(2,1)} %bitcast.16), channel_id=1, source_target_pairs={{0,12},{1,13},{2,14},{3,15},{4,8},{5,9},{6,10},{7,11},{8,4},{9,5},... | collective-permute-start | bytes 147464 | tf_op jit(solution)/shard_map/ppermute | solution.py:29
  5.1 0.6 %collective-permute-start = (bf16[32,768]{1,0:T(8,128)(2,1)}, bf16[32,768]{1,0:T(8,128)(2,1)S(1)}, u32[]{:S(2)}, u32[]{:S(2)}) collective-permute-start(bf16[32,768]{1,0:T(8,128)(2,1)} %bitcast.18), channel_id=1, source_target_pairs={{0,4},{1,5},{2,6},{3,7},{4,0},{5,1},{6,2},{7,3},{8,12},{9,13},{10,... | collective-permute-start | bytes 147464 | tf_op jit(solution)/shard_map/ppermute | solution.py:29
  5.6 4.2 %shard_map.118 = (bf16[32,768]{1,0:T(8,128)(2,1)S(1)}, f32[16,1,768]{2,1,0:T(1,128)S(1)}, bf16[6,768,1152]{2,1,0:T(8,128)(2,1)S(1)}) custom-call(s32[1]{0:T(128)} %bitcast.me_ref, bf16[32,768]{1,0:T(8,128)(2,1)} %bitcast.19, f32[16,1,768]{2,1,0:T(1,128)} %bitcast.25, bf16[12288,1152]{1,0:T(8,128)(2,1)} %weight_ref.5), custom_call_target="tpu_custom_call" | custom-call | bytes 15000000 | tf_op jit(solution)/shard_map/pallas_call | solution.py:107
  9.8 0.4 collective-permute-done.1
  10.3 1.6 %collective-permute-start.3 = (bf16[4,32,768]{2,1,0:T(8,128)(2,1)S(1)}, bf16[4,32,768]{2,1,0:T(8,128)(2,1)S(1)}, u32[]{:S(2)}, u32[]{:S(2)}) collective-permute-start(bf16[4,32,768]{2,1,0:T(8,128)(2,1)S(1)} %pad_maximum_fusion.rest_0_), channel_id=1, source_target_pairs={{0,2},{1,3},{2,0},{3,1},{4,6},{5,7},{6,4},{7,5},{8,10},{9,11},{10,... | collective-permute-start | bytes 589832 | tf_op jit(solution)/shard_map/ppermute | solution.py:29
  11.9 4.1 %shard_map.119 = (f32[32,768]{1,0:T(8,128)S(1)}, bf16[6,768,1152]{2,1,0:T(8,128)(2,1)S(1)}) custom-call(s32[1]{0:T(128)} %bitcast.me_ref, bf16[12288,1152]{1,0:T(8,128)(2,1)} %weight_ref.5, bf16[4,32,768]{2,1,0:T(8,128)(2,1)S(1)} %pad_maximum_fusion.rest_0_), custom_call_target="tpu_custom_call" | custom-call | bytes 12599999 | tf_op jit(solution)/shard_map/pallas_call | solution.py:150
  16.1 0.1 collective-permute-start.4
  16.3 1.7 %collective-permute-done.4.other_ref = bf16[8,32,768]{2,1,0:T(8,128)(2,1)S(1)} collective-permute-done((bf16[8,32,768]{2,1,0:T(8,128)(2,1)S(1)}, bf16[8,32,768]{2,1,0:T(8,128)(2,1)S(1)}, u32[]{:S(2)}, u32[]{:S(2)}) %collective-permute-start.4) | collective-permute-done | bytes 393248 | tf_op jit(solution)/shard_map/ppermute | solution.py:29
  17.9 5.4 %shard_map.121.after_ref = bf16[16,18,128]{2,1,0:T(8,128)(2,1)} custom-call(s32[1]{0:T(128)} %bitcast.me_ref, f32[16,1,768]{2,1,0:T(1,128)S(1)} %get-tuple-element.20.gain_ref, f32[32,768]{1,0:T(8,128)S(1)} %shard_map.120.before_ref, bf16[8,32,768]{2,1,0:T(8,128)(2,1)S(1)} %constant_dynamic-update-slice_fusion.mine_ref, ...), custom_call_target="tpu_custom_call" | custom-call | bytes 18000000 | tf_op jit(solution)/shard_map/pallas_call | solution.py:251
  23.3 5.8 %all-to-all-start = ((bf16[16,18,128]{2,1,0:T(8,128)(2,1)}), bf16[16,18,128]{2,1,0:T(8,128)(2,1)S(1)}, u32[]{:S(2)}, u32[]{:S(2)}) async-start(bf16[16,18,128]{2,1,0:T(8,128)(2,1)} %shard_map.121.after_ref), calls=%async_computation | async-start | bytes 196608 | tf_op jit(solution)/shard_map/all_to_all | solution.py:502
  30.5 0.1 copy.13.lambda_ref
  30.6 0.1 shard_map.122
  30.6 5.9 %all-to-all-done.received_ref = bf16[16,18,128]{2,1,0:T(8,128)(2,1)S(1)} async-done(((bf16[16,18,128]{2,1,0:T(8,128)(2,1)}), bf16[16,18,128]{2,1,0:T(8,128)(2,1)S(1)}, u32[]{:S(2)}, u32[]{:S(2)}) %all-to-all-start) | async-done | bytes 73760 | tf_op jit(solution)/shard_map/all_to_all | solution.py:502
  36.6 1.7 %shard_map.123.block_ref = bf16[48,256]{1,0:T(8,128)(2,1)S(1)} custom-call(s32[1,6]{1,0:T(1,128)S(1)} %copy-done.4, s32[1]{0:T(128)S(6)} %copy.19.length_ref, bf16[16,18,128]{2,1,0:T(8,128)(2,1)S(1)} %all-to-all-done.received_ref, f32[2,1,128]{2,1,0:T(1,128)S(1)} %get-tuple-element.27.cos_ref, f32[2,1,128]{2,1,0:T(1,128)S(1)} %get-tuple-element.28.sin_ref, ...), custom_call_target="tpu_custom_call" | custom-call | bytes 30000000 | tf_op jit(solution)/shard_map/pallas_call | solution.py:365
  38.3 0.7 %collective-permute-start.7 = (bf16[48,256]{1,0:T(8,128)(2,1)S(1)}, bf16[48,256]{1,0:T(8,128)(2,1)S(1)}, u32[]{:S(2)}, u32[]{:S(2)}) collective-permute-start(bf16[48,256]{1,0:T(8,128)(2,1)S(1)} %shard_map.123.block_ref), channel_id=1, source_target_pairs={{0,12},{1,13},{2,14},{3,15},{4,8},{5,9},{6,10},{7,11},{8,4},{9,5},... | collective-permute-start | bytes 73736 | tf_op jit(solution)/shard_map/ppermute | solution.py:29
  39.0 0.6 %collective-permute-start.6 = (bf16[48,256]{1,0:T(8,128)(2,1)S(1)}, bf16[48,256]{1,0:T(8,128)(2,1)S(1)}, u32[]{:S(2)}, u32[]{:S(2)}) collective-permute-start(bf16[48,256]{1,0:T(8,128)(2,1)S(1)} %shard_map.123.block_ref), channel_id=1, source_target_pairs={{0,8},{1,9},{2,10},{3,11},{4,12},{5,13},{6,14},{7,15},{8,0},{9,1},... | collective-permute-start | bytes 73736 | tf_op jit(solution)/shard_map/ppermute | solution.py:29
  39.6 3.2 %collective-permute-start.5 = (bf16[48,256]{1,0:T(8,128)(2,1)S(1)}, bf16[48,256]{1,0:T(8,128)(2,1)S(1)}, u32[]{:S(2)}, u32[]{:S(2)}) collective-permute-start(bf16[48,256]{1,0:T(8,128)(2,1)S(1)} %shard_map.123.block_ref), channel_id=1, source_target_pairs={{0,4},{1,5},{2,6},{3,7},{4,0},{5,1},{6,2},{7,3},{8,12},{9,13},{10,... | collective-permute-start | bytes 73736 | tf_op jit(solution)/shard_map/ppermute | solution.py:29
  42.8 2.3 %shard_map.124 = (bf16[48,256]{1,0:T(8,128)(2,1)S(1)}, bf16[3072,768]{1,0:T(8,128)(2,1)S(1)}) custom-call(bf16[48,256]{1,0:T(8,128)(2,1)S(1)} %shard_map.123.block_ref, bf16[6144,768]{1,0:T(8,128)(2,1)} %from_ref.3), custom_call_target="tpu_custom_call" | custom-call | bytes 6000000 | tf_op jit(solution)/shard_map/pallas_call | solution.py:420
  45.2 0.1 collective-permute-start.8
  45.2 2.3 %shard_map.125 = (bf16[4,48,256]{2,1,0:T(8,128)(2,1)S(1)}, bf16[3072,768]{1,0:T(8,128)(2,1)S(1)}) custom-call(bf16[4,48,256]{2,1,0:T(8,128)(2,1)S(1)} %pad_maximum_fusion.1.block_ref, bf16[6144,768]{1,0:T(8,128)(2,1)} %from_ref.3), custom_call_target="tpu_custom_call" | custom-call | bytes 6000000 | tf_op jit(solution)/shard_map/pallas_call | solution.py:420
  47.6 2.2 %collective-permute-done.8 = bf16[4,48,256]{2,1,0:T(8,128)(2,1)S(1)} collective-permute-done((bf16[4,48,256]{2,1,0:T(8,128)(2,1)S(1)}, bf16[4,48,256]{2,1,0:T(8,128)(2,1)S(1)}, u32[]{:S(2)}, u32[]{:S(2)}) %collective-permute-start.8) | collective-permute-done | bytes 98336 | tf_op jit(solution)/shard_map/ppermute | solution.py:29
  49.9 0.1 collective-permute-start.9
  49.9 1.4 %collective-permute-done.9.other_ref = bf16[8,48,256]{2,1,0:T(8,128)(2,1)S(1)} collective-permute-done((bf16[8,48,256]{2,1,0:T(8,128)(2,1)S(1)}, bf16[8,48,256]{2,1,0:T(8,128)(2,1)S(1)}, u32[]{:S(2)}, u32[]{:S(2)}) %collective-permute-start.9) | collective-permute-done | bytes 196640 | tf_op jit(solution)/shard_map/ppermute | solution.py:29
  51.4 2.4 %shard_map.126 = bf16[2,16,768]{2,1,0:T(8,128)(2,1)} custom-call(s32[1]{0:T(128)} %bitcast.me_ref, bf16[8,48,256]{2,1,0:T(8,128)(2,1)S(1)} %constant_dynamic-update-slice_fusion.5.mine_ref, bf16[8,48,256]{2,1,0:T(8,128)(2,1)S(1)} %collective-permute-done.9.other_ref, bf16[2,16,768]{2,1,0:T(8,128)(2,1)S(1)} %copy-done.3, ...), custom_call_target="tpu_custom_call" | custom-call | tf_op jit(solution)/shard_map/pallas_call | solution.py:447
  (32 shorter events, 0.2 us)
Async XLA Ops:
  0.0 9.8 %collective-permute-start.2 = (bf16[32,768]{1,0:T(8,128)(2,1)}, bf16[32,768]{1,0:T(8,128)(2,1)S(1)}, u32[]{:S(2)}, u32[]{:S(2)}) collective-permute-start(bf16[32,768]{1,0:T(8,128)(2,1)} %bitcast.16), channel_id=1, source_target_pairs={{0,12},{1,13},{2,14},{3,15},{4,8},{5,9},{6,10},{7,11},{8,4},{9,5},... | collective-permute-start | bytes 147464 | tf_op jit(solution)/shard_map/ppermute | solution.py:29
  5.0 5.2 %collective-permute-start.1 = (bf16[32,768]{1,0:T(8,128)(2,1)}, bf16[32,768]{1,0:T(8,128)(2,1)S(1)}, u32[]{:S(2)}, u32[]{:S(2)}) collective-permute-start(bf16[32,768]{1,0:T(8,128)(2,1)} %bitcast.17), channel_id=1, source_target_pairs={{0,8},{1,9},{2,10},{3,11},{4,12},{5,13},{6,14},{7,15},{8,0},{9,1},... | collective-permute-start | bytes 147464 | tf_op jit(solution)/shard_map/ppermute | solution.py:29
  5.1 5.2 %collective-permute-start = (bf16[32,768]{1,0:T(8,128)(2,1)}, bf16[32,768]{1,0:T(8,128)(2,1)S(1)}, u32[]{:S(2)}, u32[]{:S(2)}) collective-permute-start(bf16[32,768]{1,0:T(8,128)(2,1)} %bitcast.18), channel_id=1, source_target_pairs={{0,4},{1,5},{2,6},{3,7},{4,0},{5,1},{6,2},{7,3},{8,12},{9,13},{10,... | collective-permute-start | bytes 147464 | tf_op jit(solution)/shard_map/ppermute | solution.py:29
  10.3 5.8 %collective-permute-start.3 = (bf16[4,32,768]{2,1,0:T(8,128)(2,1)S(1)}, bf16[4,32,768]{2,1,0:T(8,128)(2,1)S(1)}, u32[]{:S(2)}, u32[]{:S(2)}) collective-permute-start(bf16[4,32,768]{2,1,0:T(8,128)(2,1)S(1)} %pad_maximum_fusion.rest_0_), channel_id=1, source_target_pairs={{0,2},{1,3},{2,0},{3,1},{4,6},{5,7},{6,4},{7,5},{8,10},{9,11},{10,... | collective-permute-start | bytes 589832 | tf_op jit(solution)/shard_map/ppermute | solution.py:29
  16.1 1.8 %collective-permute-start.4 = (bf16[8,32,768]{2,1,0:T(8,128)(2,1)S(1)}, bf16[8,32,768]{2,1,0:T(8,128)(2,1)S(1)}, u32[]{:S(2)}, u32[]{:S(2)}) collective-permute-start(bf16[8,32,768]{2,1,0:T(8,128)(2,1)S(1)} %constant_dynamic-update-slice_fusion.mine_ref), channel_id=1, source_target_pairs={{0,1},{1,0},{2,3},{3,2},{4,5},{5,4},{6,7},{7,6},{8,9},{9,8},{10,11... | collective-permute-start | bytes 1179656 | tf_op jit(solution)/shard_map/ppermute | solution.py:29
  17.9 12.6 %copy-start.6 = (f32[24]{0:T(128)S(1)}, f32[24]{0:T(128)}, u32[]{:S(2)}) copy-start(f32[24]{0:T(128)} %param.15) | copy-start | bytes 292
  17.9 12.7 %copy-start.5 = (f32[6144]{0:T(1024)S(1)}, f32[6144]{0:T(1024)}, u32[]{:S(2)}) copy-start(f32[6144]{0:T(1024)} %param.16) | copy-start | bytes 73732
  17.9 18.7 %copy-start = (bf16[6,16,6144]{2,1,0:T(8,128)(2,1)S(1)}, bf16[6,16,6144]{2,1,0:T(8,128)(2,1)}, u32[]{:S(2)}) copy-start(bf16[6,16,6144]{2,1,0:T(8,128)(2,1)} %values_ref.1) | copy-start | bytes 3538948
  17.9 18.7 %copy-start.1 = (bf16[6,16,3072]{2,1,0:T(8,128)(2,1)S(1)}, bf16[6,16,3072]{2,1,0:T(8,128)(2,1)}, u32[]{:S(2)}) copy-start(bf16[6,16,3072]{2,1,0:T(8,128)(2,1)} %keys_one_ref.1) | copy-start | bytes 1769476
  17.9 18.7 %copy-start.2 = (bf16[6,16,3072]{2,1,0:T(8,128)(2,1)S(1)}, bf16[6,16,3072]{2,1,0:T(8,128)(2,1)}, u32[]{:S(2)}) copy-start(bf16[6,16,3072]{2,1,0:T(8,128)(2,1)} %keys_two_ref.1) | copy-start | bytes 1769476
  17.9 18.7 %copy-start.4 = (s32[1,6]{1,0:T(1,128)S(1)}, s32[1,6]{1,0:T(1,128)}, u32[]{:S(2)}) copy-start(s32[1,6]{1,0:T(1,128)} %table_ref.1) | copy-start | bytes 76
  23.3 13.2 %all-to-all-start = ((bf16[16,18,128]{2,1,0:T(8,128)(2,1)}), bf16[16,18,128]{2,1,0:T(8,128)(2,1)S(1)}, u32[]{:S(2)}, u32[]{:S(2)}) async-start(bf16[16,18,128]{2,1,0:T(8,128)(2,1)} %shard_map.121.after_ref), calls=%async_computation | async-start | bytes 196608 | tf_op jit(solution)/shard_map/all_to_all | solution.py:502
  38.3 13.1 %copy-start.3 = (bf16[2,16,768]{2,1,0:T(8,128)(2,1)S(1)}, bf16[2,16,768]{2,1,0:T(8,128)(2,1)}, u32[]{:S(2)}) copy-start(bf16[2,16,768]{2,1,0:T(8,128)(2,1)} %inputs_ref.1) | copy-start | bytes 147460
  38.3 6.8 %collective-permute-start.7 = (bf16[48,256]{1,0:T(8,128)(2,1)S(1)}, bf16[48,256]{1,0:T(8,128)(2,1)S(1)}, u32[]{:S(2)}, u32[]{:S(2)}) collective-permute-start(bf16[48,256]{1,0:T(8,128)(2,1)S(1)} %shard_map.123.block_ref), channel_id=1, source_target_pairs={{0,12},{1,13},{2,14},{3,15},{4,8},{5,9},{6,10},{7,11},{8,4},{9,5},... | collective-permute-start | bytes 73736 | tf_op jit(solution)/shard_map/ppermute | solution.py:29
  39.0 6.1 %collective-permute-start.6 = (bf16[48,256]{1,0:T(8,128)(2,1)S(1)}, bf16[48,256]{1,0:T(8,128)(2,1)S(1)}, u32[]{:S(2)}, u32[]{:S(2)}) collective-permute-start(bf16[48,256]{1,0:T(8,128)(2,1)S(1)} %shard_map.123.block_ref), channel_id=1, source_target_pairs={{0,8},{1,9},{2,10},{3,11},{4,12},{5,13},{6,14},{7,15},{8,0},{9,1},... | collective-permute-start | bytes 73736 | tf_op jit(solution)/shard_map/ppermute | solution.py:29
  39.6 5.5 %collective-permute-start.5 = (bf16[48,256]{1,0:T(8,128)(2,1)S(1)}, bf16[48,256]{1,0:T(8,128)(2,1)S(1)}, u32[]{:S(2)}, u32[]{:S(2)}) collective-permute-start(bf16[48,256]{1,0:T(8,128)(2,1)S(1)} %shard_map.123.block_ref), channel_id=1, source_target_pairs={{0,4},{1,5},{2,6},{3,7},{4,0},{5,1},{6,2},{7,3},{8,12},{9,13},{10,... | collective-permute-start | bytes 73736 | tf_op jit(solution)/shard_map/ppermute | solution.py:29
  45.2 4.7 %collective-permute-start.8 = (bf16[4,48,256]{2,1,0:T(8,128)(2,1)S(1)}, bf16[4,48,256]{2,1,0:T(8,128)(2,1)S(1)}, u32[]{:S(2)}, u32[]{:S(2)}) collective-permute-start(bf16[4,48,256]{2,1,0:T(8,128)(2,1)S(1)} %pad_maximum_fusion.1.block_ref), channel_id=1, source_target_pairs={{0,2},{1,3},{2,0},{3,1},{4,6},{5,7},{6,4},{7,5},{8,10},{9,11},{10,... | collective-permute-start | bytes 294920 | tf_op jit(solution)/shard_map/ppermute | solution.py:29
  49.9 1.5 %collective-permute-start.9 = (bf16[8,48,256]{2,1,0:T(8,128)(2,1)S(1)}, bf16[8,48,256]{2,1,0:T(8,128)(2,1)S(1)}, u32[]{:S(2)}, u32[]{:S(2)}) collective-permute-start(bf16[8,48,256]{2,1,0:T(8,128)(2,1)S(1)} %constant_dynamic-update-slice_fusion.5.mine_ref), channel_id=1, source_target_pairs={{0,1},{1,0},{2,3},{3,2},{4,5},{5,4},{6,7},{7,6},{8,9},{9,8},{10,11... | collective-permute-start | bytes 589832 | tf_op jit(solution)/shard_map/ppermute | solution.py:29

commit v7 on v6

--- a/solution.py
+++ b/solution.py
@@ -235,14 +235,17 @@
     pieces = rows // n * (columns // 128)
     outer, middle = radices(n)
     order = slots(n)
-    first, second = 3 * n // 8, 3 * n // 4
+    first, second = 5 * n // 16, 11 * n // 16
 
     arrived = [swap(block, n, o * 2 * middle) for o in range(1, outer)]
+    own = [swap(block, n, m * 2) for m in range(1, middle)]
     held, gain, weight_a = fetch(me, block, gain, weight, n, order[:first])
-    row = jnp.stack([held] + arrived)
-    later = [swap(row, n, m * 2) for m in range(1, middle)]
+    arrived = jnp.stack(arrived)
+    row = jnp.concatenate([held[None], arrived])
+    later = [swap(arrived, n, m * 2) for m in range(1, middle)]
     squares, weight_b = squares_beside(me, weight, [row], n, order[first:second])
     later, squares = lax.optimization_barrier((later, squares))
+    later = [part for pair in zip([each[None] for each in own], later) for part in pair]
     mine = jnp.concatenate([row] + later)
     other = swap(mine, n, 1)
     squares = more_squares(later, squares)

time: 54 us -> 54.6 us (1.011)
  waiting for transfers between devices: 11.8 us -> 12.4 us
    all_to_all x1, starting transfers between devices: 5.82 us -> 4.87 us  [local(): received = lax.all_to_all(sent, 'gx', 0, 0)]
    ppermute x10 -> x11, starting transfers between devices: 11.9 us -> 12.6 us  [swap(): return lax.ppermute(block, 'gx', [(i, i ^ mask) for i in range(n)])]
    ppermute x10 -> x11, waiting for transfers between devices: 5.82 us -> 6.46 us  [swap(): return lax.ppermute(block, 'gx', [(i, i ^ mask) for i in range(n)])]
    pallas_call x1, Pallas kernels: 5.39 us -> 5.99 us  [project(): pl.pallas_call(functools.partial(project_kernel, n, order[second:]), out_...]
  transfers between devices with their start and end apart: 11 -> 12, of which waited for: 5 -> 6; matrix products, arithmetic and copies ran while one was open for 0% -> 0% of each run, Pallas kernels for 24% -> 23%
where the time goes in v7:
time: 54.6 us; the launch traced here: 54.3 us
  Pallas kernels  22.6 us (41%)
  starting transfers between devices  17.5 us (32%)
  waiting for transfers between devices  12.4 us (23%)
  between operations  1.55 us (3%)
    ppermute x11, starting transfers between devices, swap(): return lax.ppermute(block, 'gx', [(i, i ^ mask) for i in range(n)])  12.6 us
    ppermute x11, waiting for transfers between devices, swap(): return lax.ppermute(block, 'gx', [(i, i ^ mask) for i in range(n)])  6.46 us
    pallas_call x1, Pallas kernels, project(): pl.pallas_call(functools.partial(project_kernel, n, order[second:]), out_...  5.99 us
    all_to_all x1, waiting for transfers between devices, local(): received = lax.all_to_all(sent, 'gx', 0, 0)  5.95 us
    all_to_all x1, starting transfers between devices, local(): received = lax.all_to_all(sent, 'gx', 0, 0)  4.87 us
    pallas_call x2, Pallas kernels, keep(): pl.pallas_call(functools.partial(keep_kernel, half), out_shape=(jax.Shape...  4.69 us
    pallas_call x1, Pallas kernels, squares_beside(): pl.pallas_call(functools.partial(squares_kernel, n, order, len(blocks)),...  4.14 us
    pallas_call x1, Pallas kernels, fetch(): pl.pallas_call(functools.partial(fetch_kernel, n, order), out_shape=(pltp...  3.67 us
  transfers between devices with their start and end apart: 12, of which 6 were waited for; matrix products, arithmetic and copies ran while one was open for 0% of the time, Pallas kernels for 23%

profile of v7, /device:TPU:0, one launch (start us, length us, event | category | flops | bytes accessed | tf_op | source)
XLA Modules:
  0.0 54.3 jit_solution(8131243894720211461)
XLA Ops:
  0.0 3.0 %collective-permute-start.4 = (bf16[32,768]{1,0:T(8,128)(2,1)}, bf16[32,768]{1,0:T(8,128)(2,1)S(1)}, u32[]{:S(2)}, u32[]{:S(2)}) collective-permute-start(bf16[32,768]{1,0:T(8,128)(2,1)} %bitcast.18), channel_id=1, source_target_pairs={{0,2},{1,3},{2,0},{3,1},{4,6},{5,7},{6,4},{7,5},{8,10},{9,11},{10,... | collective-permute-start | bytes 147464 | tf_op jit(solution)/shard_map/ppermute | solution.py:29
  3.0 3.6 %collective-permute-start.2 = (bf16[32,768]{1,0:T(8,128)(2,1)}, bf16[32,768]{1,0:T(8,128)(2,1)S(1)}, u32[]{:S(2)}, u32[]{:S(2)}) collective-permute-start(bf16[32,768]{1,0:T(8,128)(2,1)} %bitcast.19), channel_id=1, source_target_pairs={{0,12},{1,13},{2,14},{3,15},{4,8},{5,9},{6,10},{7,11},{8,4},{9,5},... | collective-permute-start | bytes 147464 | tf_op jit(solution)/shard_map/ppermute | solution.py:29
  6.6 0.8 %collective-permute-start = (bf16[32,768]{1,0:T(8,128)(2,1)}, bf16[32,768]{1,0:T(8,128)(2,1)S(1)}, u32[]{:S(2)}, u32[]{:S(2)}) collective-permute-start(bf16[32,768]{1,0:T(8,128)(2,1)} %bitcast.21), channel_id=1, source_target_pairs={{0,4},{1,5},{2,6},{3,7},{4,0},{5,1},{6,2},{7,3},{8,12},{9,13},{10,... | collective-permute-start | bytes 147464 | tf_op jit(solution)/shard_map/ppermute | solution.py:29
  7.4 3.7 %shard_map.118 = (bf16[32,768]{1,0:T(8,128)(2,1)S(1)}, f32[16,1,768]{2,1,0:T(1,128)S(1)}, bf16[5,768,1152]{2,1,0:T(8,128)(2,1)S(1)}) custom-call(s32[1]{0:T(128)} %bitcast.me_ref, bf16[32,768]{1,0:T(8,128)(2,1)} %bitcast.22, f32[16,1,768]{2,1,0:T(1,128)} %bitcast.32, bf16[12288,1152]{1,0:T(8,128)(2,1)} %weight_ref.5), custom_call_target="tpu_custom_call" | custom-call | bytes 15000000 | tf_op jit(solution)/shard_map/pallas_call | solution.py:107
  11.1 0.7 %collective-permute-done.1 = bf16[32,768]{1,0:T(8,128)(2,1)S(1)} collective-permute-done((bf16[32,768]{1,0:T(8,128)(2,1)}, bf16[32,768]{1,0:T(8,128)(2,1)S(1)}, u32[]{:S(2)}, u32[]{:S(2)}) %collective-permute-start.1) | collective-permute-done | bytes 49184 | tf_op jit(solution)/shard_map/ppermute | solution.py:29
  11.8 0.6 %collective-permute-start.3 = (bf16[3,32,768]{2,1,0:T(8,128)(2,1)S(1)}, bf16[3,32,768]{2,1,0:T(8,128)(2,1)S(1)}, u32[]{:S(2)}, u32[]{:S(2)}) collective-permute-start(bf16[3,32,768]{2,1,0:T(8,128)(2,1)S(1)} %pad_maximum_fusion.1), channel_id=1, source_target_pairs={{0,2},{1,3},{2,0},{3,1},{4,6},{5,7},{6,4},{7,5},{8,10},{9,11},{10,... | collective-permute-start | bytes 442376 | tf_op jit(solution)/shard_map/ppermute | solution.py:29
  12.4 4.1 %shard_map.119 = (f32[32,768]{1,0:T(8,128)S(1)}, bf16[6,768,1152]{2,1,0:T(8,128)(2,1)S(1)}) custom-call(s32[1]{0:T(128)} %bitcast.me_ref, bf16[12288,1152]{1,0:T(8,128)(2,1)} %weight_ref.5, bf16[4,32,768]{2,1,0:T(8,128)(2,1)S(1)} %pad_maximum_fusion.rest_0_), custom_call_target="tpu_custom_call" | custom-call | bytes 12599999 | tf_op jit(solution)/shard_map/pallas_call | solution.py:150
  16.6 0.4 collective-permute-done.3.rest_1_
  17.0 0.1 collective-permute-start.5
  17.1 1.7 %collective-permute-done.5.other_ref = bf16[8,32,768]{2,1,0:T(8,128)(2,1)S(1)} collective-permute-done((bf16[8,32,768]{2,1,0:T(8,128)(2,1)S(1)}, bf16[8,32,768]{2,1,0:T(8,128)(2,1)S(1)}, u32[]{:S(2)}, u32[]{:S(2)}) %collective-permute-start.5) | collective-permute-done | bytes 393248 | tf_op jit(solution)/shard_map/ppermute | solution.py:29
  18.8 6.0 %shard_map.121.after_ref = bf16[16,18,128]{2,1,0:T(8,128)(2,1)} custom-call(s32[1]{0:T(128)} %bitcast.me_ref, f32[16,1,768]{2,1,0:T(1,128)S(1)} %get-tuple-element.20.gain_ref, f32[32,768]{1,0:T(8,128)S(1)} %shard_map.120.before_ref, bf16[8,32,768]{2,1,0:T(8,128)(2,1)S(1)} %constant_dynamic-update-slice_fusion.mine_ref, ...), custom_call_target="tpu_custom_call" | custom-call | bytes 18000000 | tf_op jit(solution)/shard_map/pallas_call | solution.py:254
  24.8 4.9 %all-to-all-start = ((bf16[16,18,128]{2,1,0:T(8,128)(2,1)}), bf16[16,18,128]{2,1,0:T(8,128)(2,1)S(1)}, u32[]{:S(2)}, u32[]{:S(2)}) async-start(bf16[16,18,128]{2,1,0:T(8,128)(2,1)} %shard_map.121.after_ref), calls=%async_computation | async-start | bytes 196608 | tf_op jit(solution)/shard_map/all_to_all | solution.py:505
  31.0 0.1 copy.13.lambda_ref
  31.2 5.9 %all-to-all-done.received_ref = bf16[16,18,128]{2,1,0:T(8,128)(2,1)S(1)} async-done(((bf16[16,18,128]{2,1,0:T(8,128)(2,1)}), bf16[16,18,128]{2,1,0:T(8,128)(2,1)S(1)}, u32[]{:S(2)}, u32[]{:S(2)}) %all-to-all-start) | async-done | bytes 73760 | tf_op jit(solution)/shard_map/all_to_all | solution.py:505
  37.2 1.7 %shard_map.123.block_ref = bf16[48,256]{1,0:T(8,128)(2,1)S(1)} custom-call(s32[1,6]{1,0:T(1,128)S(1)} %copy-done.4, s32[1]{0:T(128)S(6)} %copy.20.length_ref, bf16[16,18,128]{2,1,0:T(8,128)(2,1)S(1)} %all-to-all-done.received_ref, f32[2,1,128]{2,1,0:T(1,128)S(1)} %get-tuple-element.27.cos_ref, f32[2,1,128]{2,1,0:T(1,128)S(1)} %get-tuple-element.28.sin_ref, ...), custom_call_target="tpu_custom_call" | custom-call | bytes 30000000 | tf_op jit(solution)/shard_map/pallas_call | solution.py:368
  38.9 0.7 %collective-permute-start.8 = (bf16[48,256]{1,0:T(8,128)(2,1)S(1)}, bf16[48,256]{1,0:T(8,128)(2,1)S(1)}, u32[]{:S(2)}, u32[]{:S(2)}) collective-permute-start(bf16[48,256]{1,0:T(8,128)(2,1)S(1)} %shard_map.123.block_ref), channel_id=1, source_target_pairs={{0,12},{1,13},{2,14},{3,15},{4,8},{5,9},{6,10},{7,11},{8,4},{9,5},... | collective-permute-start | bytes 73736 | tf_op jit(solution)/shard_map/ppermute | solution.py:29
  39.5 0.6 %collective-permute-start.7 = (bf16[48,256]{1,0:T(8,128)(2,1)S(1)}, bf16[48,256]{1,0:T(8,128)(2,1)S(1)}, u32[]{:S(2)}, u32[]{:S(2)}) collective-permute-start(bf16[48,256]{1,0:T(8,128)(2,1)S(1)} %shard_map.123.block_ref), channel_id=1, source_target_pairs={{0,8},{1,9},{2,10},{3,11},{4,12},{5,13},{6,14},{7,15},{8,0},{9,1},... | collective-permute-start | bytes 73736 | tf_op jit(solution)/shard_map/ppermute | solution.py:29
  40.1 3.2 %collective-permute-start.6 = (bf16[48,256]{1,0:T(8,128)(2,1)S(1)}, bf16[48,256]{1,0:T(8,128)(2,1)S(1)}, u32[]{:S(2)}, u32[]{:S(2)}) collective-permute-start(bf16[48,256]{1,0:T(8,128)(2,1)S(1)} %shard_map.123.block_ref), channel_id=1, source_target_pairs={{0,4},{1,5},{2,6},{3,7},{4,0},{5,1},{6,2},{7,3},{8,12},{9,13},{10,... | collective-permute-start | bytes 73736 | tf_op jit(solution)/shard_map/ppermute | solution.py:29
  43.3 2.3 %shard_map.124 = (bf16[48,256]{1,0:T(8,128)(2,1)S(1)}, bf16[3072,768]{1,0:T(8,128)(2,1)S(1)}) custom-call(bf16[48,256]{1,0:T(8,128)(2,1)S(1)} %shard_map.123.block_ref, bf16[6144,768]{1,0:T(8,128)(2,1)} %from_ref.3), custom_call_target="tpu_custom_call" | custom-call | bytes 6000000 | tf_op jit(solution)/shard_map/pallas_call | solution.py:423
  45.7 0.1 collective-permute-start.9
  45.8 2.3 %shard_map.125 = (bf16[4,48,256]{2,1,0:T(8,128)(2,1)S(1)}, bf16[3072,768]{1,0:T(8,128)(2,1)S(1)}) custom-call(bf16[4,48,256]{2,1,0:T(8,128)(2,1)S(1)} %pad_maximum_fusion.2.block_ref, bf16[6144,768]{1,0:T(8,128)(2,1)} %from_ref.3), custom_call_target="tpu_custom_call" | custom-call | bytes 6000000 | tf_op jit(solution)/shard_map/pallas_call | solution.py:423
  48.2 2.2 %collective-permute-done.9 = bf16[4,48,256]{2,1,0:T(8,128)(2,1)S(1)} collective-permute-done((bf16[4,48,256]{2,1,0:T(8,128)(2,1)S(1)}, bf16[4,48,256]{2,1,0:T(8,128)(2,1)S(1)}, u32[]{:S(2)}, u32[]{:S(2)}) %collective-permute-start.9) | collective-permute-done | bytes 98336 | tf_op jit(solution)/shard_map/ppermute | solution.py:29
  50.5 1.4 %collective-permute-done.10.other_ref = bf16[8,48,256]{2,1,0:T(8,128)(2,1)S(1)} collective-permute-done((bf16[8,48,256]{2,1,0:T(8,128)(2,1)S(1)}, bf16[8,48,256]{2,1,0:T(8,128)(2,1)S(1)}, u32[]{:S(2)}, u32[]{:S(2)}) %collective-permute-start.10) | collective-permute-done | bytes 196640 | tf_op jit(solution)/shard_map/ppermute | solution.py:29
  51.9 2.4 %shard_map.126 = bf16[2,16,768]{2,1,0:T(8,128)(2,1)} custom-call(s32[1]{0:T(128)} %bitcast.me_ref, bf16[8,48,256]{2,1,0:T(8,128)(2,1)S(1)} %constant_dynamic-update-slice_fusion.6.mine_ref, bf16[8,48,256]{2,1,0:T(8,128)(2,1)S(1)} %collective-permute-done.10.other_ref, bf16[2,16,768]{2,1,0:T(8,128)(2,1)S(1)} %copy-done.3, ...), custom_call_target="tpu_custom_call" | custom-call | tf_op jit(solution)/shard_map/pallas_call | solution.py:450
  (36 shorter events, 0.3 us)
Async XLA Ops:
  0.0 16.6 %collective-permute-start.4 = (bf16[32,768]{1,0:T(8,128)(2,1)}, bf16[32,768]{1,0:T(8,128)(2,1)S(1)}, u32[]{:S(2)}, u32[]{:S(2)}) collective-permute-start(bf16[32,768]{1,0:T(8,128)(2,1)} %bitcast.18), channel_id=1, source_target_pairs={{0,2},{1,3},{2,0},{3,1},{4,6},{5,7},{6,4},{7,5},{8,10},{9,11},{10,... | collective-permute-start | bytes 147464 | tf_op jit(solution)/shard_map/ppermute | solution.py:29
  3.0 8.1 %collective-permute-start.2 = (bf16[32,768]{1,0:T(8,128)(2,1)}, bf16[32,768]{1,0:T(8,128)(2,1)S(1)}, u32[]{:S(2)}, u32[]{:S(2)}) collective-permute-start(bf16[32,768]{1,0:T(8,128)(2,1)} %bitcast.19), channel_id=1, source_target_pairs={{0,12},{1,13},{2,14},{3,15},{4,8},{5,9},{6,10},{7,11},{8,4},{9,5},... | collective-permute-start | bytes 147464 | tf_op jit(solution)/shard_map/ppermute | solution.py:29
  6.6 5.2 %collective-permute-start.1 = (bf16[32,768]{1,0:T(8,128)(2,1)}, bf16[32,768]{1,0:T(8,128)(2,1)S(1)}, u32[]{:S(2)}, u32[]{:S(2)}) collective-permute-start(bf16[32,768]{1,0:T(8,128)(2,1)} %bitcast.20), channel_id=1, source_target_pairs={{0,8},{1,9},{2,10},{3,11},{4,12},{5,13},{6,14},{7,15},{8,0},{9,1},... | collective-permute-start | bytes 147464 | tf_op jit(solution)/shard_map/ppermute | solution.py:29
  6.6 5.2 %collective-permute-start = (bf16[32,768]{1,0:T(8,128)(2,1)}, bf16[32,768]{1,0:T(8,128)(2,1)S(1)}, u32[]{:S(2)}, u32[]{:S(2)}) collective-permute-start(bf16[32,768]{1,0:T(8,128)(2,1)} %bitcast.21), channel_id=1, source_target_pairs={{0,4},{1,5},{2,6},{3,7},{4,0},{5,1},{6,2},{7,3},{8,12},{9,13},{10,... | collective-permute-start | bytes 147464 | tf_op jit(solution)/shard_map/ppermute | solution.py:29
  11.8 5.2 %collective-permute-start.3 = (bf16[3,32,768]{2,1,0:T(8,128)(2,1)S(1)}, bf16[3,32,768]{2,1,0:T(8,128)(2,1)S(1)}, u32[]{:S(2)}, u32[]{:S(2)}) collective-permute-start(bf16[3,32,768]{2,1,0:T(8,128)(2,1)S(1)} %pad_maximum_fusion.1), channel_id=1, source_target_pairs={{0,2},{1,3},{2,0},{3,1},{4,6},{5,7},{6,4},{7,5},{8,10},{9,11},{10,... | collective-permute-start | bytes 442376 | tf_op jit(solution)/shard_map/ppermute | solution.py:29
  17.0 1.8 %collective-permute-start.5 = (bf16[8,32,768]{2,1,0:T(8,128)(2,1)S(1)}, bf16[8,32,768]{2,1,0:T(8,128)(2,1)S(1)}, u32[]{:S(2)}, u32[]{:S(2)}) collective-permute-start(bf16[8,32,768]{2,1,0:T(8,128)(2,1)S(1)} %constant_dynamic-update-slice_fusion.mine_ref), channel_id=1, source_target_pairs={{0,1},{1,0},{2,3},{3,2},{4,5},{5,4},{6,7},{7,6},{8,9},{9,8},{10,11... | collective-permute-start | bytes 1179656 | tf_op jit(solution)/shard_map/ppermute | solution.py:29
  18.8 12.2 %copy-start.6 = (f32[24]{0:T(128)S(1)}, f32[24]{0:T(128)}, u32[]{:S(2)}) copy-start(f32[24]{0:T(128)} %param.15) | copy-start | bytes 292
  18.8 12.3 %copy-start.5 = (f32[6144]{0:T(1024)S(1)}, f32[6144]{0:T(1024)}, u32[]{:S(2)}) copy-start(f32[6144]{0:T(1024)} %param.16) | copy-start | bytes 73732
  18.8 18.3 %copy-start = (bf16[6,16,6144]{2,1,0:T(8,128)(2,1)S(1)}, bf16[6,16,6144]{2,1,0:T(8,128)(2,1)}, u32[]{:S(2)}) copy-start(bf16[6,16,6144]{2,1,0:T(8,128)(2,1)} %values_ref.1) | copy-start | bytes 3538948
  18.8 18.3 %copy-start.1 = (bf16[6,16,3072]{2,1,0:T(8,128)(2,1)S(1)}, bf16[6,16,3072]{2,1,0:T(8,128)(2,1)}, u32[]{:S(2)}) copy-start(bf16[6,16,3072]{2,1,0:T(8,128)(2,1)} %keys_one_ref.1) | copy-start | bytes 1769476
  18.8 18.3 %copy-start.2 = (bf16[6,16,3072]{2,1,0:T(8,128)(2,1)S(1)}, bf16[6,16,3072]{2,1,0:T(8,128)(2,1)}, u32[]{:S(2)}) copy-start(bf16[6,16,3072]{2,1,0:T(8,128)(2,1)} %keys_two_ref.1) | copy-start | bytes 1769476
  18.8 18.3 %copy-start.4 = (s32[1,6]{1,0:T(1,128)S(1)}, s32[1,6]{1,0:T(1,128)}, u32[]{:S(2)}) copy-start(s32[1,6]{1,0:T(1,128)} %table_ref.1) | copy-start | bytes 76
  24.8 12.3 %all-to-all-start = ((bf16[16,18,128]{2,1,0:T(8,128)(2,1)}), bf16[16,18,128]{2,1,0:T(8,128)(2,1)S(1)}, u32[]{:S(2)}, u32[]{:S(2)}) async-start(bf16[16,18,128]{2,1,0:T(8,128)(2,1)} %shard_map.121.after_ref), calls=%async_computation | async-start | bytes 196608 | tf_op jit(solution)/shard_map/all_to_all | solution.py:505
  38.8 13.1 %copy-start.3 = (bf16[2,16,768]{2,1,0:T(8,128)(2,1)S(1)}, bf16[2,16,768]{2,1,0:T(8,128)(2,1)}, u32[]{:S(2)}) copy-start(bf16[2,16,768]{2,1,0:T(8,128)(2,1)} %inputs_ref.1) | copy-start | bytes 147460
  38.9 6.8 %collective-permute-start.8 = (bf16[48,256]{1,0:T(8,128)(2,1)S(1)}, bf16[48,256]{1,0:T(8,128)(2,1)S(1)}, u32[]{:S(2)}, u32[]{:S(2)}) collective-permute-start(bf16[48,256]{1,0:T(8,128)(2,1)S(1)} %shard_map.123.block_ref), channel_id=1, source_target_pairs={{0,12},{1,13},{2,14},{3,15},{4,8},{5,9},{6,10},{7,11},{8,4},{9,5},... | collective-permute-start | bytes 73736 | tf_op jit(solution)/shard_map/ppermute | solution.py:29
  39.5 6.1 %collective-permute-start.7 = (bf16[48,256]{1,0:T(8,128)(2,1)S(1)}, bf16[48,256]{1,0:T(8,128)(2,1)S(1)}, u32[]{:S(2)}, u32[]{:S(2)}) collective-permute-start(bf16[48,256]{1,0:T(8,128)(2,1)S(1)} %shard_map.123.block_ref), channel_id=1, source_target_pairs={{0,8},{1,9},{2,10},{3,11},{4,12},{5,13},{6,14},{7,15},{8,0},{9,1},... | collective-permute-start | bytes 73736 | tf_op jit(solution)/shard_map/ppermute | solution.py:29
  40.1 5.5 %collective-permute-start.6 = (bf16[48,256]{1,0:T(8,128)(2,1)S(1)}, bf16[48,256]{1,0:T(8,128)(2,1)S(1)}, u32[]{:S(2)}, u32[]{:S(2)}) collective-permute-start(bf16[48,256]{1,0:T(8,128)(2,1)S(1)} %shard_map.123.block_ref), channel_id=1, source_target_pairs={{0,4},{1,5},{2,6},{3,7},{4,0},{5,1},{6,2},{7,3},{8,12},{9,13},{10,... | collective-permute-start | bytes 73736 | tf_op jit(solution)/shard_map/ppermute | solution.py:29
  45.7 4.7 %collective-permute-start.9 = (bf16[4,48,256]{2,1,0:T(8,128)(2,1)S(1)}, bf16[4,48,256]{2,1,0:T(8,128)(2,1)S(1)}, u32[]{:S(2)}, u32[]{:S(2)}) collective-permute-start(bf16[4,48,256]{2,1,0:T(8,128)(2,1)S(1)} %pad_maximum_fusion.2.block_ref), channel_id=1, source_target_pairs={{0,2},{1,3},{2,0},{3,1},{4,6},{5,7},{6,4},{7,5},{8,10},{9,11},{10,... | collective-permute-start | bytes 294920 | tf_op jit(solution)/shard_map/ppermute | solution.py:29
  50.4 1.5 %collective-permute-start.10 = (bf16[8,48,256]{2,1,0:T(8,128)(2,1)S(1)}, bf16[8,48,256]{2,1,0:T(8,128)(2,1)S(1)}, u32[]{:S(2)}, u32[]{:S(2)}) collective-permute-start(bf16[8,48,256]{2,1,0:T(8,128)(2,1)S(1)} %constant_dynamic-update-slice_fusion.6.mine_ref), channel_id=1, source_target_pairs={{0,1},{1,0},{2,3},{3,2},{4,5},{5,4},{6,7},{7,6},{8,9},{9,8},{10,11... | collective-permute-start | bytes 589832 | tf_op jit(solution)/shard_map/ppermute | solution.py:29

commit v8 on v6

--- a/solution.py
+++ b/solution.py
@@ -87,39 +87,76 @@
     return copies
 
 
-def fetch_kernel(
-    n, order, me_ref, block_ref, gain_ref, weight_ref, held, gain_out, weight_out, sems, other_sems
-):
-    copies = [
-        pltpu.make_async_copy(block_ref, held, other_sems.at[0]),
-        pltpu.make_async_copy(gain_ref, gain_out, other_sems.at[1]),
-    ] + fetches(n, order, me_ref[0], weight_ref, weight_out, sems)
-    for copy in copies:
+def fetch_kernel(n, order, *rest):
+    (
+        me_ref, block_ref, gain_ref, weight_ref, table_ref, lambda_ref, head_gain_ref,
+        held, gain_out, weight_out, place_ref, lambda_out, head_gain_out,
+        table, row_ref, wide_ref, sems, other_sems,
+    ) = rest
+    small = [
+        pltpu.make_async_copy(start, end, other_sems.at[index])
+        for index, (start, end) in enumerate(
+            (
+                (table_ref, table),
+                (lambda_ref, row_ref),
+                (head_gain_ref, wide_ref),
+                (block_ref, held),
+                (gain_ref, gain_out),
+            )
+        )
+    ]
+    large = fetches(n, order, me_ref[0], weight_ref, weight_out, sems)
+    for copy in small + large:
         copy.start()
-    for copy in copies:
+    for copy in small:
         copy.wait()
 
-
-def fetch(me, block, gain, weight, n, order):
+    capacity = place_ref.shape[1]
+    pages = table_ref.shape[1]
+    page = capacity // pages
+    row = lax.broadcasted_iota(jnp.int32, (1, capacity), 1)
+    place = jnp.zeros((1, capacity), jnp.int32)
+    for index in range(pages):
+        first = table[0, index] * page
+        inside = (row >= first) & (row < first + page)
+        place = jnp.where(inside, row - first + index * page, place)
+    place_ref[...] = place
+    across = lax.broadcasted_iota(jnp.int32, (H, H), 1) == lax.broadcasted_iota(jnp.int32, (H, H), 0)
+    lambda_out[...] = jnp.sum(jnp.where(across, row_ref[...], 0.0), axis=1, keepdims=True)
+    for h in range(H):
+        head_gain_out[h : h + 1, :] = wide_ref[:, h * 2 * HD : (h + 1) * 2 * HD]
+
+    for copy in large:
+        copy.wait()
+
+
+def fetch(me, block, gain, weight, n, order, small, capacity):
     part, columns = weight.shape[0] // n, weight.shape[1]
     vmem = pl.BlockSpec(memory_space=pltpu.VMEM)
     hbm = pl.BlockSpec(memory_space=pltpu.HBM)
+    table, weights, head_gain = small
     return pl.pallas_call(
         functools.partial(fetch_kernel, n, order),
         out_shape=(
             pltpu.VMEM(block.shape, BF16),
             pltpu.VMEM(gain.shape, F32),
             pltpu.VMEM((len(order), part, columns), BF16),
+            jax.ShapeDtypeStruct((1, capacity), jnp.int32),
+            jax.ShapeDtypeStruct((H, 1), F32),
+            jax.ShapeDtypeStruct((H, 2 * HD), F32),
         ),
-        in_specs=[pl.BlockSpec(memory_space=pltpu.SMEM), hbm, hbm, hbm],
-        out_specs=(vmem,) * 3,
+        in_specs=[pl.BlockSpec(memory_space=pltpu.SMEM)] + [hbm] * 6,
+        out_specs=(vmem,) * 6,
         scratch_shapes=[
+            pltpu.SMEM(table.shape, table.dtype),
+            pltpu.VMEM(weights.shape, F32),
+            pltpu.VMEM(head_gain.shape, F32),
             pltpu.SemaphoreType.DMA((len(order),)),
-            pltpu.SemaphoreType.DMA((2,)),
+            pltpu.SemaphoreType.DMA((5,)),
         ],
         compiler_params=pltpu.CompilerParams(vmem_limit_bytes=4 * 1024 * 1024),
         cost_estimate=hint(5),
-    )(me, far(block), far(gain), far(weight))
+    )(me, far(block), far(gain), far(weight), *map(far, small))
 
 
 def near(x):
@@ -165,21 +202,40 @@
     )(me, far(weight), *blocks)
 
 
-def more_squares_kernel(count, before, *rest):
-    *blocks, squares = rest
+def more_squares_kernel(positions_ref, length_ref, place_ref, before, *rest):
+    *blocks, squares, cos_ref, sin_ref, allowed_ref = rest
     squares[...] = add_squares(blocks, before[...])
-
-
-def more_squares(blocks, before):
+    steps = cos_ref.shape[0]
+    lane = lax.broadcasted_iota(jnp.int32, (8, HD), 1)
+    step = lax.broadcasted_iota(jnp.int32, (8, HD), 0)
+    pair = lax.rem(lane, HD // 2).astype(F32)
+    frequency = jnp.exp(-math.log(ROPE_BASE) * 2.0 * pair / HD)
+    turns = (positions_ref[0] + step).astype(F32) * frequency
+    cos = jnp.cos(turns)
+    sin = jnp.where(lane < HD // 2, -1.0, 1.0) * jnp.sin(turns)
+    for index in range(steps):
+        cos_ref[index] = cos[index : index + 1]
+        sin_ref[index] = sin[index : index + 1]
+    allowed_ref[...] = jnp.where(place_ref[...] < length_ref[0], 1.0, 0.0)
+
+
+def more_squares(blocks, before, positions, length, place, steps):
     vmem = pl.BlockSpec(memory_space=pltpu.VMEM)
+    smem = pl.BlockSpec(memory_space=pltpu.SMEM)
+    turns = jax.ShapeDtypeStruct((steps, 1, HD), F32)
     return pl.pallas_call(
-        functools.partial(more_squares_kernel, len(blocks)),
-        out_shape=jax.ShapeDtypeStruct(before.shape, F32),
-        in_specs=[vmem] * (len(blocks) + 1),
-        out_specs=vmem,
+        more_squares_kernel,
+        out_shape=(
+            jax.ShapeDtypeStruct(before.shape, F32),
+            turns,
+            turns,
+            jax.ShapeDtypeStruct(place.shape, F32),
+        ),
+        in_specs=[smem, smem] + [vmem] * (len(blocks) + 2),
+        out_specs=(vmem,) * 4,
         compiler_params=pltpu.CompilerParams(vmem_limit_bytes=4 * 1024 * 1024),
         cost_estimate=hint(1),
-    )(before, *blocks)
+    )(positions, length, place, before, *blocks)
 
 
 def project_kernel(n, order, me_ref, gain_ref, before_ref, mine_ref, other_ref, weight_ref, *rest):
@@ -229,7 +285,7 @@
         out_ref[target] = spread[target, : steps * columns, :].astype(BF16)
 
 
-def project(me, block, gain, weight, n):
+def project(me, block, gain, weight, n, scalars, small, capacity):
     rows, part = block.shape
     columns = weight.shape[1]
     pieces = rows // n * (columns // 128)
@@ -238,17 +294,19 @@
     first, second = 3 * n // 8, 3 * n // 4
 
     arrived = [swap(block, n, o * 2 * middle) for o in range(1, outer)]
-    held, gain, weight_a = fetch(me, block, gain, weight, n, order[:first])
+    held, gain, weight_a, place, weights, head_gain = fetch(
+        me, block, gain, weight, n, order[:first], small, capacity
+    )
     row = jnp.stack([held] + arrived)
     later = [swap(row, n, m * 2) for m in range(1, middle)]
     squares, weight_b = squares_beside(me, weight, [row], n, order[first:second])
     later, squares = lax.optimization_barrier((later, squares))
     mine = jnp.concatenate([row] + later)
     other = swap(mine, n, 1)
-    squares = more_squares(later, squares)
+    squares, cos, sin, allowed = more_squares(later, squares, *scalars, place, rows // n)
     vmem = pl.BlockSpec(memory_space=pltpu.VMEM)
     hbm = pl.BlockSpec(memory_space=pltpu.HBM)
-    return pl.pallas_call(
+    sent = pl.pallas_call(
         functools.partial(project_kernel, n, order[second:]),
         out_shape=jax.ShapeDtypeStruct((n, pieces, 128), BF16),
         in_specs=[pl.BlockSpec(memory_space=pltpu.SMEM)] + [vmem] * 4 + [hbm] + [vmem] * 2,
@@ -263,10 +321,11 @@
         compiler_params=pltpu.CompilerParams(vmem_limit_bytes=VMEM_LIMIT),
         cost_estimate=hint(6),
     )(me, gain, squares, mine, other, far(weight), near(weight_a), near(weight_b))
+    return sent, (cos, sin, allowed, weights, head_gain)
 
 
 def attend_kernel(
-    table_ref, length_ref, received_ref, cos_ref, sin_ref, lambda_ref, gain_ref,
+    received_ref, cos_ref, sin_ref, allowed_ref, lambda_ref, gain_ref,
     keys_one_ref, keys_two_ref, values_ref, out_ref, fresh,
 ):
     sources, pieces, _ = received_ref.shape
@@ -289,14 +348,7 @@
         turned = values * cos_ref[step] + pltpu.roll(values, HD // 2, 1) * sin_ref[step]
         return turned.astype(BF16).astype(F32)
 
-    row = lax.broadcasted_iota(jnp.int32, (1, capacity), 1)
-    place = jnp.zeros((1, capacity), jnp.int32)
-    for index in range(pages):
-        first = table_ref[0, index] * page
-        inside = (row >= first) & (row < first + page)
-        place = jnp.where(inside, row - first + index * page, place)
-    allowed = place < length_ref[0]
-
+    allowed = allowed_ref[...] > 0.0
     scale = 1.0 / math.sqrt(HD)
     head_row = lax.rem(lax.broadcasted_iota(jnp.int32, (steps * H, HD), 0), H)
 
@@ -356,21 +408,20 @@
         out_ref[step * H : (step + 1) * H, :] = (mixed * norm * gain_ref[...]).astype(BF16)
 
 
-def attend(table, length, received, cos, sin, weights, gain, keys_one, keys_two, values):
+def attend(received, cos, sin, allowed, weights, gain, keys_one, keys_two, values):
     steps = cos.shape[0]
     sources, pieces, _ = received.shape
     vmem = pl.BlockSpec(memory_space=pltpu.VMEM)
-    smem = pl.BlockSpec(memory_space=pltpu.SMEM)
     held = [near(x) for x in (keys_one, keys_two, values)]
     return pl.pallas_call(
         attend_kernel,
         out_shape=jax.ShapeDtypeStruct((steps * H, 2 * HD), BF16),
-        in_specs=[smem, smem] + [vmem] * 8,
+        in_specs=[vmem] * 9,
         out_specs=vmem,
         scratch_shapes=[pltpu.VMEM((steps, sources * (pieces // steps), 128), F32)],
         compiler_params=pltpu.CompilerParams(vmem_limit_bytes=VMEM_LIMIT),
         cost_estimate=hint(10),
-    )(table, length, received, cos, sin, weights, gain, *held)
+    )(received, cos, sin, allowed, weights, gain, *held)
 
 
 def output_kernel(n, me_ref, mine_ref, other_ref, inputs_ref, *rest):
@@ -465,32 +516,6 @@
     return cos[:, None, :], sin[:, None, :]
 
 
-def turn_kernel(positions_ref, after_ref, cos_ref, sin_ref):
-    steps = cos_ref.shape[0]
-    lane = lax.broadcasted_iota(jnp.int32, (8, HD), 1)
-    step = lax.broadcasted_iota(jnp.int32, (8, HD), 0)
-    pair = lax.rem(lane, HD // 2).astype(F32)
-    frequency = jnp.exp(-math.log(ROPE_BASE) * 2.0 * pair / HD)
-    turns = (positions_ref[0] + step).astype(F32) * frequency
-    cos = jnp.cos(turns)
-    sin = jnp.where(lane < HD // 2, -1.0, 1.0) * jnp.sin(turns)
-    for index in range(steps):
-        cos_ref[index] = cos[index : index + 1]
-        sin_ref[index] = sin[index : index + 1]
-
-
-def turn(positions, after, steps):
-    vmem = pl.BlockSpec(memory_space=pltpu.VMEM)
-    return pl.pallas_call(
-        turn_kernel,
-        out_shape=(jax.ShapeDtypeStruct((steps, 1, HD), F32),) * 2,
-        in_specs=[pl.BlockSpec(memory_space=pltpu.SMEM), pl.BlockSpec(memory_space=pl.ANY)],
-        out_specs=(vmem, vmem),
-        compiler_params=pltpu.CompilerParams(vmem_limit_bytes=4 * 1024 * 1024),
-        cost_estimate=hint(1),
-    )(positions, after)
-
-
 def local(
     n, inputs, norm_gain, qkv_weight, head_lambda, head_gain, out_weight,
     key_one_pages, key_two_pages, value_pages, page_table, context_len, positions,
@@ -498,13 +523,14 @@
     steps, rows, part = inputs.shape
     me = lax.axis_index("gx").astype(jnp.int32).reshape(1)
     block = inputs.reshape(steps * rows, part)
-    sent = project(me, block, norm_gain.reshape(n, 1, part), qkv_weight, n)
+    capacity = page_table.shape[1] * key_one_pages.shape[1]
+    small = (page_table, head_lambda.reshape(1, H), head_gain.reshape(1, H * 2 * HD))
+    sent, aside = project(
+        me, block, norm_gain.reshape(n, 1, part), qkv_weight, n, (positions, context_len), small,
+        capacity,
+    )
     received = lax.all_to_all(sent, "gx", 0, 0)
-    cos, sin = turn(positions, sent, steps)
-    attended = attend(
-        page_table, context_len, received, cos, sin, head_lambda.reshape(H, 1),
-        head_gain.reshape(H, 2 * HD), key_one_pages, key_two_pages, value_pages,
-    )
+    attended = attend(received, *aside, key_one_pages, key_two_pages, value_pages)
     return output(me, attended, inputs, out_weight, n)
 
 

time: 54 us -> 52.6 us (0.974)
  blocking collectives: 0 us -> 13.1 us
  waiting for transfers between devices: 11.8 us -> 4.42 us
  starting transfers between devices: 17.7 us -> 11.9 us
  Pallas kernels: 22.5 us -> 21.4 us
    all_to_all x0 -> x1, blocking collectives: none -> 13.1 us  [local(): received = lax.all_to_all(sent, 'gx', 0, 0)]
    all_to_all x1 -> x0, waiting for transfers between devices: 5.95 us -> none  [local(): received = lax.all_to_all(sent, 'gx', 0, 0)]
    all_to_all x1 -> x0, starting transfers between devices: 5.82 us -> none  [local(): received = lax.all_to_all(sent, 'gx', 0, 0)]
    ppermute x10, waiting for transfers between devices: 5.82 us -> 4.42 us  [swap(): return lax.ppermute(block, 'gx', [(i, i ^ mask) for i in range(n)])]
    pallas_call x1, Pallas kernels: 5.39 us -> 4.75 us  [project(): pl.pallas_call(functools.partial(project_kernel, n, order[second:]), out_...]
  transfers between devices with their start and end apart: 11 -> 10, of which waited for: 5 -> 4; matrix products, arithmetic and copies ran while one was open for 0% -> 0% of each run, Pallas kernels for 24% -> 25%
where the time goes in v8:
time: 52.6 us; the launch traced here: 52.4 us
  Pallas kernels  21.4 us (41%)
  blocking collectives  13.1 us (25%)
  starting transfers between devices  11.9 us (23%)
  waiting for transfers between devices  4.42 us (8%)
  between operations  1.48 us (3%)
    all_to_all x1, blocking collectives, local(): received = lax.all_to_all(sent, 'gx', 0, 0)  13.1 us
    ppermute x10, starting transfers between devices, swap(): return lax.ppermute(block, 'gx', [(i, i ^ mask) for i in range(n)])  11.9 us
    pallas_call x1, Pallas kernels, project(): pl.pallas_call(functools.partial(project_kernel, n, order[second:]), out_...  4.75 us
    pallas_call x2, Pallas kernels, keep(): pl.pallas_call(functools.partial(keep_kernel, half), out_shape=(jax.Shape...  4.69 us
    ppermute x10, waiting for transfers between devices, swap(): return lax.ppermute(block, 'gx', [(i, i ^ mask) for i in range(n)])  4.42 us
    pallas_call x1, Pallas kernels, fetch(): pl.pallas_call(functools.partial(fetch_kernel, n, order), out_shape=(pltp...  4.24 us
    pallas_call x1, Pallas kernels, squares_beside(): pl.pallas_call(functools.partial(squares_kernel, n, order, len(blocks)),...  4.14 us
    pallas_call x1, Pallas kernels, output(): pl.pallas_call(functools.partial(output_kernel, n), out_shape=jax.ShapeDt...  2.37 us
  transfers between devices with their start and end apart: 10, of which 4 were waited for; matrix products, arithmetic and copies ran while one was open for 0% of the time, Pallas kernels for 25%

profile of v8, /device:TPU:0, one launch (start us, length us, event | category | flops | bytes accessed | tf_op | source)
XLA Modules:
  0.0 52.4 jit_solution(5701092698693849587)
XLA Ops:
  0.0 5.0 %collective-permute-start.2 = (bf16[32,768]{1,0:T(8,128)(2,1)}, bf16[32,768]{1,0:T(8,128)(2,1)S(1)}, u32[]{:S(2)}, u32[]{:S(2)}) collective-permute-start(bf16[32,768]{1,0:T(8,128)(2,1)} %bitcast.17), channel_id=1, source_target_pairs={{0,12},{1,13},{2,14},{3,15},{4,8},{5,9},{6,10},{7,11},{8,4},{9,5},... | collective-permute-start | bytes 147464 | tf_op jit(solution)/shard_map/ppermute | solution.py:29
  5.1 0.6 %collective-permute-start = (bf16[32,768]{1,0:T(8,128)(2,1)}, bf16[32,768]{1,0:T(8,128)(2,1)S(1)}, u32[]{:S(2)}, u32[]{:S(2)}) collective-permute-start(bf16[32,768]{1,0:T(8,128)(2,1)} %bitcast.19), channel_id=1, source_target_pairs={{0,4},{1,5},{2,6},{3,7},{4,0},{5,1},{6,2},{7,3},{8,12},{9,13},{10,... | collective-permute-start | bytes 147464 | tf_op jit(solution)/shard_map/ppermute | solution.py:29
  5.6 4.2 %shard_map.118 = (bf16[32,768]{1,0:T(8,128)(2,1)S(1)}, f32[16,1,768]{2,1,0:T(1,128)S(1)}, bf16[6,768,1152]{2,1,0:T(8,128)(2,1)S(1)}, s32[1,96]{1,0:T(1,128)S(1)}...) custom-call(s32[1]{0:T(128)} %bitcast.rest_0_.me_ref, bf16[32,768]{1,0:T(8,128)(2,1)} %bitcast.20, f32[16,1,768]{2,1,0:T(1,128)} %bitcast.26, ...), custom_call_target="tpu_custom_call" | custom-call | bytes 15000000 | tf_op jit(solution)/shard_map/pallas_call | solution.py:138
  9.9 0.4 collective-permute-done.1
  10.3 1.6 %collective-permute-start.3 = (bf16[4,32,768]{2,1,0:T(8,128)(2,1)S(1)}, bf16[4,32,768]{2,1,0:T(8,128)(2,1)S(1)}, u32[]{:S(2)}, u32[]{:S(2)}) collective-permute-start(bf16[4,32,768]{2,1,0:T(8,128)(2,1)S(1)} %pad_maximum_fusion.rest_0_), channel_id=1, source_target_pairs={{0,2},{1,3},{2,0},{3,1},{4,6},{5,7},{6,4},{7,5},{8,10},{9,11},{10,... | collective-permute-start | bytes 589832 | tf_op jit(solution)/shard_map/ppermute | solution.py:29
  11.9 4.1 %shard_map.119 = (f32[32,768]{1,0:T(8,128)S(1)}, bf16[6,768,1152]{2,1,0:T(8,128)(2,1)S(1)}) custom-call(s32[1]{0:T(128)} %bitcast.rest_0_.me_ref, bf16[12288,1152]{1,0:T(8,128)(2,1)} %weight_ref.3, bf16[4,32,768]{2,1,0:T(8,128)(2,1)S(1)} %pad_maximum_fusion.rest_0_), custom_call_target="tpu_custom_call" | custom-call | bytes 12599999 | tf_op jit(solution)/shard_map/pallas_call | solution.py:187
  16.1 0.0 collective-permute-done.3.rest_0_
  16.1 0.1 collective-permute-start.4
  17.5 0.1 shard_map.120
  17.6 0.3 collective-permute-done.4.other_ref
  17.9 4.7 %shard_map.121 = bf16[16,18,128]{2,1,0:T(8,128)(2,1)S(1)} custom-call(s32[1]{0:T(128)} %bitcast.rest_0_.me_ref, f32[16,1,768]{2,1,0:T(1,128)S(1)} %get-tuple-element.25.gain_ref, f32[32,768]{1,0:T(8,128)S(1)} %get-tuple-element.31.before_ref, bf16[8,32,768]{2,1,0:T(8,128)(2,1)S(1)} %constant_dynamic-update-slice_fusion.mine_ref, ...), custom_call_target="tpu_custom_call" | custom-call | bytes 18000000 | tf_op jit(solution)/shard_map/pallas_call | solution.py:309
  22.7 13.1 %all_to_all.5.received_ref = bf16[16,18,128]{2,1,0:T(8,128)(2,1)S(1)} all-to-all(bf16[16,18,128]{2,1,0:T(8,128)(2,1)S(1)} %shard_map.121), channel_id=1, replica_groups=mesh['groups'=2,'gx'=16] {'gx'}, dimensions={0} | all-to-all | bytes 147456 | tf_op jit(solution)/shard_map/all_to_all | solution.py:532
  35.8 1.1 %shard_map.122.block_ref = bf16[48,256]{1,0:T(8,128)(2,1)S(1)} custom-call(bf16[16,18,128]{2,1,0:T(8,128)(2,1)S(1)} %all_to_all.5.received_ref, f32[2,1,128]{2,1,0:T(1,128)S(1)} %get-tuple-element.34.cos_ref, f32[2,1,128]{2,1,0:T(1,128)S(1)} %get-tuple-element.35.sin_ref, f32[1,96]{1,0:T(1,128)S(1)} %get-tuple-element.36.allowed_ref, ...), custom_call_target="tpu_custom_call" | custom-call | bytes 30000000 | tf_op jit(solution)/shard_map/pallas_call | solution.py:416
  36.9 0.0 copy-start.3
  36.9 0.7 %collective-permute-start.7 = (bf16[48,256]{1,0:T(8,128)(2,1)S(1)}, bf16[48,256]{1,0:T(8,128)(2,1)S(1)}, u32[]{:S(2)}, u32[]{:S(2)}) collective-permute-start(bf16[48,256]{1,0:T(8,128)(2,1)S(1)} %shard_map.122.block_ref), channel_id=1, source_target_pairs={{0,12},{1,13},{2,14},{3,15},{4,8},{5,9},{6,10},{7,11},{8,4},{9,5},... | collective-permute-start | bytes 73736 | tf_op jit(solution)/shard_map/ppermute | solution.py:29
  37.6 0.6 %collective-permute-start.6 = (bf16[48,256]{1,0:T(8,128)(2,1)S(1)}, bf16[48,256]{1,0:T(8,128)(2,1)S(1)}, u32[]{:S(2)}, u32[]{:S(2)}) collective-permute-start(bf16[48,256]{1,0:T(8,128)(2,1)S(1)} %shard_map.122.block_ref), channel_id=1, source_target_pairs={{0,8},{1,9},{2,10},{3,11},{4,12},{5,13},{6,14},{7,15},{8,0},{9,1},... | collective-permute-start | bytes 73736 | tf_op jit(solution)/shard_map/ppermute | solution.py:29
  38.2 3.2 %collective-permute-start.5 = (bf16[48,256]{1,0:T(8,128)(2,1)S(1)}, bf16[48,256]{1,0:T(8,128)(2,1)S(1)}, u32[]{:S(2)}, u32[]{:S(2)}) collective-permute-start(bf16[48,256]{1,0:T(8,128)(2,1)S(1)} %shard_map.122.block_ref), channel_id=1, source_target_pairs={{0,4},{1,5},{2,6},{3,7},{4,0},{5,1},{6,2},{7,3},{8,12},{9,13},{10,... | collective-permute-start | bytes 73736 | tf_op jit(solution)/shard_map/ppermute | solution.py:29
  41.4 2.3 %shard_map.123 = (bf16[48,256]{1,0:T(8,128)(2,1)S(1)}, bf16[3072,768]{1,0:T(8,128)(2,1)S(1)}) custom-call(bf16[48,256]{1,0:T(8,128)(2,1)S(1)} %shard_map.122.block_ref, bf16[6144,768]{1,0:T(8,128)(2,1)} %from_ref.3), custom_call_target="tpu_custom_call" | custom-call | bytes 6000000 | tf_op jit(solution)/shard_map/pallas_call | solution.py:471
  43.8 0.1 collective-permute-start.8
  43.9 2.3 %shard_map.124 = (bf16[4,48,256]{2,1,0:T(8,128)(2,1)S(1)}, bf16[3072,768]{1,0:T(8,128)(2,1)S(1)}) custom-call(bf16[4,48,256]{2,1,0:T(8,128)(2,1)S(1)} %pad_maximum_fusion.1.block_ref, bf16[6144,768]{1,0:T(8,128)(2,1)} %from_ref.3), custom_call_target="tpu_custom_call" | custom-call | bytes 6000000 | tf_op jit(solution)/shard_map/pallas_call | solution.py:471
  46.2 2.2 %collective-permute-done.8 = bf16[4,48,256]{2,1,0:T(8,128)(2,1)S(1)} collective-permute-done((bf16[4,48,256]{2,1,0:T(8,128)(2,1)S(1)}, bf16[4,48,256]{2,1,0:T(8,128)(2,1)S(1)}, u32[]{:S(2)}, u32[]{:S(2)}) %collective-permute-start.8) | collective-permute-done | bytes 98336 | tf_op jit(solution)/shard_map/ppermute | solution.py:29
  48.5 0.1 collective-permute-start.9
  48.6 1.4 %collective-permute-done.9.other_ref = bf16[8,48,256]{2,1,0:T(8,128)(2,1)S(1)} collective-permute-done((bf16[8,48,256]{2,1,0:T(8,128)(2,1)S(1)}, bf16[8,48,256]{2,1,0:T(8,128)(2,1)S(1)}, u32[]{:S(2)}, u32[]{:S(2)}) %collective-permute-start.9) | collective-permute-done | bytes 196640 | tf_op jit(solution)/shard_map/ppermute | solution.py:29
  50.0 2.4 %shard_map.125 = bf16[2,16,768]{2,1,0:T(8,128)(2,1)} custom-call(s32[1]{0:T(128)} %bitcast.rest_0_.me_ref, bf16[8,48,256]{2,1,0:T(8,128)(2,1)S(1)} %constant_dynamic-update-slice_fusion.5.mine_ref, bf16[8,48,256]{2,1,0:T(8,128)(2,1)S(1)} %collective-permute-done.9.other_ref, bf16[2,16,768]{2,1,0:T(8,128)(2,1)S(1)} %copy-done.3, ...), custom_call_target="tpu_custom_call" | custom-call | tf_op jit(solution)/shard_map/pallas_call | solution.py:498
  (22 shorter events, 0.1 us)
Async XLA Ops:
  0.0 9.9 %collective-permute-start.2 = (bf16[32,768]{1,0:T(8,128)(2,1)}, bf16[32,768]{1,0:T(8,128)(2,1)S(1)}, u32[]{:S(2)}, u32[]{:S(2)}) collective-permute-start(bf16[32,768]{1,0:T(8,128)(2,1)} %bitcast.17), channel_id=1, source_target_pairs={{0,12},{1,13},{2,14},{3,15},{4,8},{5,9},{6,10},{7,11},{8,4},{9,5},... | collective-permute-start | bytes 147464 | tf_op jit(solution)/shard_map/ppermute | solution.py:29
  5.0 5.2 %collective-permute-start.1 = (bf16[32,768]{1,0:T(8,128)(2,1)}, bf16[32,768]{1,0:T(8,128)(2,1)S(1)}, u32[]{:S(2)}, u32[]{:S(2)}) collective-permute-start(bf16[32,768]{1,0:T(8,128)(2,1)} %bitcast.18), channel_id=1, source_target_pairs={{0,8},{1,9},{2,10},{3,11},{4,12},{5,13},{6,14},{7,15},{8,0},{9,1},... | collective-permute-start | bytes 147464 | tf_op jit(solution)/shard_map/ppermute | solution.py:29
  5.1 5.2 %collective-permute-start = (bf16[32,768]{1,0:T(8,128)(2,1)}, bf16[32,768]{1,0:T(8,128)(2,1)S(1)}, u32[]{:S(2)}, u32[]{:S(2)}) collective-permute-start(bf16[32,768]{1,0:T(8,128)(2,1)} %bitcast.19), channel_id=1, source_target_pairs={{0,4},{1,5},{2,6},{3,7},{4,0},{5,1},{6,2},{7,3},{8,12},{9,13},{10,... | collective-permute-start | bytes 147464 | tf_op jit(solution)/shard_map/ppermute | solution.py:29
  10.3 5.8 %collective-permute-start.3 = (bf16[4,32,768]{2,1,0:T(8,128)(2,1)S(1)}, bf16[4,32,768]{2,1,0:T(8,128)(2,1)S(1)}, u32[]{:S(2)}, u32[]{:S(2)}) collective-permute-start(bf16[4,32,768]{2,1,0:T(8,128)(2,1)S(1)} %pad_maximum_fusion.rest_0_), channel_id=1, source_target_pairs={{0,2},{1,3},{2,0},{3,1},{4,6},{5,7},{6,4},{7,5},{8,10},{9,11},{10,... | collective-permute-start | bytes 589832 | tf_op jit(solution)/shard_map/ppermute | solution.py:29
  16.1 1.8 %collective-permute-start.4 = (bf16[8,32,768]{2,1,0:T(8,128)(2,1)S(1)}, bf16[8,32,768]{2,1,0:T(8,128)(2,1)S(1)}, u32[]{:S(2)}, u32[]{:S(2)}) collective-permute-start(bf16[8,32,768]{2,1,0:T(8,128)(2,1)S(1)} %constant_dynamic-update-slice_fusion.mine_ref), channel_id=1, source_target_pairs={{0,1},{1,0},{2,3},{3,2},{4,5},{5,4},{6,7},{7,6},{8,9},{9,8},{10,11... | collective-permute-start | bytes 1179656 | tf_op jit(solution)/shard_map/ppermute | solution.py:29
  17.9 17.8 %copy-start = (bf16[6,16,6144]{2,1,0:T(8,128)(2,1)S(1)}, bf16[6,16,6144]{2,1,0:T(8,128)(2,1)}, u32[]{:S(2)}) copy-start(bf16[6,16,6144]{2,1,0:T(8,128)(2,1)} %values_ref.1) | copy-start | bytes 3538948
  17.9 17.8 %copy-start.1 = (bf16[6,16,3072]{2,1,0:T(8,128)(2,1)S(1)}, bf16[6,16,3072]{2,1,0:T(8,128)(2,1)}, u32[]{:S(2)}) copy-start(bf16[6,16,3072]{2,1,0:T(8,128)(2,1)} %keys_one_ref.1) | copy-start | bytes 1769476
  17.9 17.8 %copy-start.2 = (bf16[6,16,3072]{2,1,0:T(8,128)(2,1)S(1)}, bf16[6,16,3072]{2,1,0:T(8,128)(2,1)}, u32[]{:S(2)}) copy-start(bf16[6,16,3072]{2,1,0:T(8,128)(2,1)} %keys_two_ref.1) | copy-start | bytes 1769476
  36.9 13.1 %copy-start.3 = (bf16[2,16,768]{2,1,0:T(8,128)(2,1)S(1)}, bf16[2,16,768]{2,1,0:T(8,128)(2,1)}, u32[]{:S(2)}) copy-start(bf16[2,16,768]{2,1,0:T(8,128)(2,1)} %inputs_ref.1) | copy-start | bytes 147460
  36.9 6.8 %collective-permute-start.7 = (bf16[48,256]{1,0:T(8,128)(2,1)S(1)}, bf16[48,256]{1,0:T(8,128)(2,1)S(1)}, u32[]{:S(2)}, u32[]{:S(2)}) collective-permute-start(bf16[48,256]{1,0:T(8,128)(2,1)S(1)} %shard_map.122.block_ref), channel_id=1, source_target_pairs={{0,12},{1,13},{2,14},{3,15},{4,8},{5,9},{6,10},{7,11},{8,4},{9,5},... | collective-permute-start | bytes 73736 | tf_op jit(solution)/shard_map/ppermute | solution.py:29
  37.6 6.1 %collective-permute-start.6 = (bf16[48,256]{1,0:T(8,128)(2,1)S(1)}, bf16[48,256]{1,0:T(8,128)(2,1)S(1)}, u32[]{:S(2)}, u32[]{:S(2)}) collective-permute-start(bf16[48,256]{1,0:T(8,128)(2,1)S(1)} %shard_map.122.block_ref), channel_id=1, source_target_pairs={{0,8},{1,9},{2,10},{3,11},{4,12},{5,13},{6,14},{7,15},{8,0},{9,1},... | collective-permute-start | bytes 73736 | tf_op jit(solution)/shard_map/ppermute | solution.py:29
  38.2 5.5 %collective-permute-start.5 = (bf16[48,256]{1,0:T(8,128)(2,1)S(1)}, bf16[48,256]{1,0:T(8,128)(2,1)S(1)}, u32[]{:S(2)}, u32[]{:S(2)}) collective-permute-start(bf16[48,256]{1,0:T(8,128)(2,1)S(1)} %shard_map.122.block_ref), channel_id=1, source_target_pairs={{0,4},{1,5},{2,6},{3,7},{4,0},{5,1},{6,2},{7,3},{8,12},{9,13},{10,... | collective-permute-start | bytes 73736 | tf_op jit(solution)/shard_map/ppermute | solution.py:29
  43.8 4.7 %collective-permute-start.8 = (bf16[4,48,256]{2,1,0:T(8,128)(2,1)S(1)}, bf16[4,48,256]{2,1,0:T(8,128)(2,1)S(1)}, u32[]{:S(2)}, u32[]{:S(2)}) collective-permute-start(bf16[4,48,256]{2,1,0:T(8,128)(2,1)S(1)} %pad_maximum_fusion.1.block_ref), channel_id=1, source_target_pairs={{0,2},{1,3},{2,0},{3,1},{4,6},{5,7},{6,4},{7,5},{8,10},{9,11},{10,... | collective-permute-start | bytes 294920 | tf_op jit(solution)/shard_map/ppermute | solution.py:29
  48.5 1.5 %collective-permute-start.9 = (bf16[8,48,256]{2,1,0:T(8,128)(2,1)S(1)}, bf16[8,48,256]{2,1,0:T(8,128)(2,1)S(1)}, u32[]{:S(2)}, u32[]{:S(2)}) collective-permute-start(bf16[8,48,256]{2,1,0:T(8,128)(2,1)S(1)} %constant_dynamic-update-slice_fusion.5.mine_ref), channel_id=1, source_target_pairs={{0,1},{1,0},{2,3},{3,2},{4,5},{5,4},{6,7},{7,6},{8,9},{9,8},{10,11... | collective-permute-start | bytes 589832 | tf_op jit(solution)/shard_map/ppermute | solution.py:29

commit v9 on v8

--- a/solution.py
+++ b/solution.py
@@ -291,7 +291,7 @@
     pieces = rows // n * (columns // 128)
     outer, middle = radices(n)
     order = slots(n)
-    first, second = 3 * n // 8, 3 * n // 4
+    first, second = 5 * n // 16, 3 * n // 4
 
     arrived = [swap(block, n, o * 2 * middle) for o in range(1, outer)]
     held, gain, weight_a, place, weights, head_gain = fetch(

time: 52.6 us -> 52.1 us (level)
  blocking collectives: 13.1 us -> 12.1 us
    all_to_all x1, blocking collectives: 13.1 us -> 12.1 us  [local(): received = lax.all_to_all(sent, 'gx', 0, 0)]
where the time goes in v9:
time: 52.1 us; the launch traced here: 51.8 us
  Pallas kernels  21.4 us (41%)
  blocking collectives  12.1 us (23%)
  starting transfers between devices  11.9 us (23%)
  waiting for transfers between devices  4.89 us (9%)
  between operations  1.49 us (3%)
    all_to_all x1, blocking collectives, local(): received = lax.all_to_all(sent, 'gx', 0, 0)  12.1 us
    ppermute x10, starting transfers between devices, swap(): return lax.ppermute(block, 'gx', [(i, i ^ mask) for i in range(n)])  11.9 us
    ppermute x10, waiting for transfers between devices, swap(): return lax.ppermute(block, 'gx', [(i, i ^ mask) for i in range(n)])  4.89 us
    pallas_call x1, Pallas kernels, project(): pl.pallas_call(functools.partial(project_kernel, n, order[second:]), out_...  4.75 us
    pallas_call x2, Pallas kernels, keep(): pl.pallas_call(functools.partial(keep_kernel, half), out_shape=(jax.Shape...  4.69 us
    pallas_call x1, Pallas kernels, squares_beside(): pl.pallas_call(functools.partial(squares_kernel, n, order, len(blocks)),...  4.65 us
    pallas_call x1, Pallas kernels, fetch(): pl.pallas_call(functools.partial(fetch_kernel, n, order), out_shape=(pltp...  3.72 us
    pallas_call x1, Pallas kernels, output(): pl.pallas_call(functools.partial(output_kernel, n), out_shape=jax.ShapeDt...  2.37 us
  transfers between devices with their start and end apart: 10, of which 4 were waited for; matrix products, arithmetic and copies ran while one was open for 0% of the time, Pallas kernels for 25%

profile of v9, /device:TPU:0, one launch (start us, length us, event | category | flops | bytes accessed | tf_op | source)
XLA Modules:
  0.0 51.8 jit_solution(10539443609196492177)
XLA Ops:
  0.0 5.0 %collective-permute-start.2 = (bf16[32,768]{1,0:T(8,128)(2,1)}, bf16[32,768]{1,0:T(8,128)(2,1)S(1)}, u32[]{:S(2)}, u32[]{:S(2)}) collective-permute-start(bf16[32,768]{1,0:T(8,128)(2,1)} %bitcast.17), channel_id=1, source_target_pairs={{0,12},{1,13},{2,14},{3,15},{4,8},{5,9},{6,10},{7,11},{8,4},{9,5},... | collective-permute-start | bytes 147464 | tf_op jit(solution)/shard_map/ppermute | solution.py:29
  5.1 0.6 %collective-permute-start = (bf16[32,768]{1,0:T(8,128)(2,1)}, bf16[32,768]{1,0:T(8,128)(2,1)S(1)}, u32[]{:S(2)}, u32[]{:S(2)}) collective-permute-start(bf16[32,768]{1,0:T(8,128)(2,1)} %bitcast.19), channel_id=1, source_target_pairs={{0,4},{1,5},{2,6},{3,7},{4,0},{5,1},{6,2},{7,3},{8,12},{9,13},{10,... | collective-permute-start | bytes 147464 | tf_op jit(solution)/shard_map/ppermute | solution.py:29
  5.6 3.7 %shard_map.118 = (bf16[32,768]{1,0:T(8,128)(2,1)S(1)}, f32[16,1,768]{2,1,0:T(1,128)S(1)}, bf16[5,768,1152]{2,1,0:T(8,128)(2,1)S(1)}, s32[1,96]{1,0:T(1,128)S(1)}...) custom-call(s32[1]{0:T(128)} %bitcast.rest_0_.me_ref, bf16[32,768]{1,0:T(8,128)(2,1)} %bitcast.20, f32[16,1,768]{2,1,0:T(1,128)} %bitcast.26, ...), custom_call_target="tpu_custom_call" | custom-call | bytes 15000000 | tf_op jit(solution)/shard_map/pallas_call | solution.py:138
  9.4 0.0 collective-permute-done.2
  9.4 0.9 %collective-permute-done.1 = bf16[32,768]{1,0:T(8,128)(2,1)S(1)} collective-permute-done((bf16[32,768]{1,0:T(8,128)(2,1)}, bf16[32,768]{1,0:T(8,128)(2,1)S(1)}, u32[]{:S(2)}, u32[]{:S(2)}) %collective-permute-start.1) | collective-permute-done | bytes 49184 | tf_op jit(solution)/shard_map/ppermute | solution.py:29
  10.3 1.6 %collective-permute-start.3 = (bf16[4,32,768]{2,1,0:T(8,128)(2,1)S(1)}, bf16[4,32,768]{2,1,0:T(8,128)(2,1)S(1)}, u32[]{:S(2)}, u32[]{:S(2)}) collective-permute-start(bf16[4,32,768]{2,1,0:T(8,128)(2,1)S(1)} %pad_maximum_fusion.rest_0_), channel_id=1, source_target_pairs={{0,2},{1,3},{2,0},{3,1},{4,6},{5,7},{6,4},{7,5},{8,10},{9,11},{10,... | collective-permute-start | bytes 589832 | tf_op jit(solution)/shard_map/ppermute | solution.py:29
  11.9 4.6 %shard_map.119 = (f32[32,768]{1,0:T(8,128)S(1)}, bf16[7,768,1152]{2,1,0:T(8,128)(2,1)S(1)}) custom-call(s32[1]{0:T(128)} %bitcast.rest_0_.me_ref, bf16[12288,1152]{1,0:T(8,128)(2,1)} %weight_ref.3, bf16[4,32,768]{2,1,0:T(8,128)(2,1)S(1)} %pad_maximum_fusion.rest_0_), custom_call_target="tpu_custom_call" | custom-call | bytes 14699999 | tf_op jit(solution)/shard_map/pallas_call | solution.py:187
  16.6 0.1 collective-permute-start.4
  18.0 0.1 shard_map.120
  18.1 0.3 collective-permute-done.4.other_ref
  18.4 4.7 %shard_map.121 = bf16[16,18,128]{2,1,0:T(8,128)(2,1)S(1)} custom-call(s32[1]{0:T(128)} %bitcast.rest_0_.me_ref, f32[16,1,768]{2,1,0:T(1,128)S(1)} %get-tuple-element.25.gain_ref, f32[32,768]{1,0:T(8,128)S(1)} %get-tuple-element.31.before_ref, bf16[8,32,768]{2,1,0:T(8,128)(2,1)S(1)} %constant_dynamic-update-slice_fusion.mine_ref, ...), custom_call_target="tpu_custom_call" | custom-call | bytes 18000000 | tf_op jit(solution)/shard_map/pallas_call | solution.py:309
  23.2 12.1 %all_to_all.5.received_ref = bf16[16,18,128]{2,1,0:T(8,128)(2,1)S(1)} all-to-all(bf16[16,18,128]{2,1,0:T(8,128)(2,1)S(1)} %shard_map.121), channel_id=1, replica_groups=mesh['groups'=2,'gx'=16] {'gx'}, dimensions={0} | all-to-all | bytes 147456 | tf_op jit(solution)/shard_map/all_to_all | solution.py:532
  35.2 1.1 %shard_map.122.block_ref = bf16[48,256]{1,0:T(8,128)(2,1)S(1)} custom-call(bf16[16,18,128]{2,1,0:T(8,128)(2,1)S(1)} %all_to_all.5.received_ref, f32[2,1,128]{2,1,0:T(1,128)S(1)} %get-tuple-element.34.cos_ref, f32[2,1,128]{2,1,0:T(1,128)S(1)} %get-tuple-element.35.sin_ref, f32[1,96]{1,0:T(1,128)S(1)} %get-tuple-element.36.allowed_ref, ...), custom_call_target="tpu_custom_call" | custom-call | bytes 30000000 | tf_op jit(solution)/shard_map/pallas_call | solution.py:416
  36.4 0.0 copy-start.3
  36.4 0.7 %collective-permute-start.7 = (bf16[48,256]{1,0:T(8,128)(2,1)S(1)}, bf16[48,256]{1,0:T(8,128)(2,1)S(1)}, u32[]{:S(2)}, u32[]{:S(2)}) collective-permute-start(bf16[48,256]{1,0:T(8,128)(2,1)S(1)} %shard_map.122.block_ref), channel_id=1, source_target_pairs={{0,12},{1,13},{2,14},{3,15},{4,8},{5,9},{6,10},{7,11},{8,4},{9,5},... | collective-permute-start | bytes 73736 | tf_op jit(solution)/shard_map/ppermute | solution.py:29
  37.1 0.6 %collective-permute-start.6 = (bf16[48,256]{1,0:T(8,128)(2,1)S(1)}, bf16[48,256]{1,0:T(8,128)(2,1)S(1)}, u32[]{:S(2)}, u32[]{:S(2)}) collective-permute-start(bf16[48,256]{1,0:T(8,128)(2,1)S(1)} %shard_map.122.block_ref), channel_id=1, source_target_pairs={{0,8},{1,9},{2,10},{3,11},{4,12},{5,13},{6,14},{7,15},{8,0},{9,1},... | collective-permute-start | bytes 73736 | tf_op jit(solution)/shard_map/ppermute | solution.py:29
  37.7 3.2 %collective-permute-start.5 = (bf16[48,256]{1,0:T(8,128)(2,1)S(1)}, bf16[48,256]{1,0:T(8,128)(2,1)S(1)}, u32[]{:S(2)}, u32[]{:S(2)}) collective-permute-start(bf16[48,256]{1,0:T(8,128)(2,1)S(1)} %shard_map.122.block_ref), channel_id=1, source_target_pairs={{0,4},{1,5},{2,6},{3,7},{4,0},{5,1},{6,2},{7,3},{8,12},{9,13},{10,... | collective-permute-start | bytes 73736 | tf_op jit(solution)/shard_map/ppermute | solution.py:29
  40.8 2.3 %shard_map.123 = (bf16[48,256]{1,0:T(8,128)(2,1)S(1)}, bf16[3072,768]{1,0:T(8,128)(2,1)S(1)}) custom-call(bf16[48,256]{1,0:T(8,128)(2,1)S(1)} %shard_map.122.block_ref, bf16[6144,768]{1,0:T(8,128)(2,1)} %from_ref.3), custom_call_target="tpu_custom_call" | custom-call | bytes 6000000 | tf_op jit(solution)/shard_map/pallas_call | solution.py:471
  43.3 0.1 collective-permute-start.8
  43.3 2.3 %shard_map.124 = (bf16[4,48,256]{2,1,0:T(8,128)(2,1)S(1)}, bf16[3072,768]{1,0:T(8,128)(2,1)S(1)}) custom-call(bf16[4,48,256]{2,1,0:T(8,128)(2,1)S(1)} %pad_maximum_fusion.1.block_ref, bf16[6144,768]{1,0:T(8,128)(2,1)} %from_ref.3), custom_call_target="tpu_custom_call" | custom-call | bytes 6000000 | tf_op jit(solution)/shard_map/pallas_call | solution.py:471
  45.7 2.2 %collective-permute-done.8 = bf16[4,48,256]{2,1,0:T(8,128)(2,1)S(1)} collective-permute-done((bf16[4,48,256]{2,1,0:T(8,128)(2,1)S(1)}, bf16[4,48,256]{2,1,0:T(8,128)(2,1)S(1)}, u32[]{:S(2)}, u32[]{:S(2)}) %collective-permute-start.8) | collective-permute-done | bytes 98336 | tf_op jit(solution)/shard_map/ppermute | solution.py:29
  48.0 0.1 collective-permute-start.9
  48.0 1.4 %collective-permute-done.9.other_ref = bf16[8,48,256]{2,1,0:T(8,128)(2,1)S(1)} collective-permute-done((bf16[8,48,256]{2,1,0:T(8,128)(2,1)S(1)}, bf16[8,48,256]{2,1,0:T(8,128)(2,1)S(1)}, u32[]{:S(2)}, u32[]{:S(2)}) %collective-permute-start.9) | collective-permute-done | bytes 196640 | tf_op jit(solution)/shard_map/ppermute | solution.py:29
  49.5 2.4 %shard_map.125 = bf16[2,16,768]{2,1,0:T(8,128)(2,1)} custom-call(s32[1]{0:T(128)} %bitcast.rest_0_.me_ref, bf16[8,48,256]{2,1,0:T(8,128)(2,1)S(1)} %constant_dynamic-update-slice_fusion.5.mine_ref, bf16[8,48,256]{2,1,0:T(8,128)(2,1)S(1)} %collective-permute-done.9.other_ref, bf16[2,16,768]{2,1,0:T(8,128)(2,1)S(1)} %copy-done.3, ...), custom_call_target="tpu_custom_call" | custom-call | tf_op jit(solution)/shard_map/pallas_call | solution.py:498
  (22 shorter events, 0.1 us)
Async XLA Ops:
  0.0 9.4 %collective-permute-start.2 = (bf16[32,768]{1,0:T(8,128)(2,1)}, bf16[32,768]{1,0:T(8,128)(2,1)S(1)}, u32[]{:S(2)}, u32[]{:S(2)}) collective-permute-start(bf16[32,768]{1,0:T(8,128)(2,1)} %bitcast.17), channel_id=1, source_target_pairs={{0,12},{1,13},{2,14},{3,15},{4,8},{5,9},{6,10},{7,11},{8,4},{9,5},... | collective-permute-start | bytes 147464 | tf_op jit(solution)/shard_map/ppermute | solution.py:29
  5.0 5.2 %collective-permute-start.1 = (bf16[32,768]{1,0:T(8,128)(2,1)}, bf16[32,768]{1,0:T(8,128)(2,1)S(1)}, u32[]{:S(2)}, u32[]{:S(2)}) collective-permute-start(bf16[32,768]{1,0:T(8,128)(2,1)} %bitcast.18), channel_id=1, source_target_pairs={{0,8},{1,9},{2,10},{3,11},{4,12},{5,13},{6,14},{7,15},{8,0},{9,1},... | collective-permute-start | bytes 147464 | tf_op jit(solution)/shard_map/ppermute | solution.py:29
  5.1 5.2 %collective-permute-start = (bf16[32,768]{1,0:T(8,128)(2,1)}, bf16[32,768]{1,0:T(8,128)(2,1)S(1)}, u32[]{:S(2)}, u32[]{:S(2)}) collective-permute-start(bf16[32,768]{1,0:T(8,128)(2,1)} %bitcast.19), channel_id=1, source_target_pairs={{0,4},{1,5},{2,6},{3,7},{4,0},{5,1},{6,2},{7,3},{8,12},{9,13},{10,... | collective-permute-start | bytes 147464 | tf_op jit(solution)/shard_map/ppermute | solution.py:29
  10.3 6.3 %collective-permute-start.3 = (bf16[4,32,768]{2,1,0:T(8,128)(2,1)S(1)}, bf16[4,32,768]{2,1,0:T(8,128)(2,1)S(1)}, u32[]{:S(2)}, u32[]{:S(2)}) collective-permute-start(bf16[4,32,768]{2,1,0:T(8,128)(2,1)S(1)} %pad_maximum_fusion.rest_0_), channel_id=1, source_target_pairs={{0,2},{1,3},{2,0},{3,1},{4,6},{5,7},{6,4},{7,5},{8,10},{9,11},{10,... | collective-permute-start | bytes 589832 | tf_op jit(solution)/shard_map/ppermute | solution.py:29
  16.6 1.8 %collective-permute-start.4 = (bf16[8,32,768]{2,1,0:T(8,128)(2,1)S(1)}, bf16[8,32,768]{2,1,0:T(8,128)(2,1)S(1)}, u32[]{:S(2)}, u32[]{:S(2)}) collective-permute-start(bf16[8,32,768]{2,1,0:T(8,128)(2,1)S(1)} %constant_dynamic-update-slice_fusion.mine_ref), channel_id=1, source_target_pairs={{0,1},{1,0},{2,3},{3,2},{4,5},{5,4},{6,7},{7,6},{8,9},{9,8},{10,11... | collective-permute-start | bytes 1179656 | tf_op jit(solution)/shard_map/ppermute | solution.py:29
  18.4 16.8 %copy-start = (bf16[6,16,6144]{2,1,0:T(8,128)(2,1)S(1)}, bf16[6,16,6144]{2,1,0:T(8,128)(2,1)}, u32[]{:S(2)}) copy-start(bf16[6,16,6144]{2,1,0:T(8,128)(2,1)} %values_ref.1) | copy-start | bytes 3538948
  18.4 16.8 %copy-start.1 = (bf16[6,16,3072]{2,1,0:T(8,128)(2,1)S(1)}, bf16[6,16,3072]{2,1,0:T(8,128)(2,1)}, u32[]{:S(2)}) copy-start(bf16[6,16,3072]{2,1,0:T(8,128)(2,1)} %keys_one_ref.1) | copy-start | bytes 1769476
  18.4 16.8 %copy-start.2 = (bf16[6,16,3072]{2,1,0:T(8,128)(2,1)S(1)}, bf16[6,16,3072]{2,1,0:T(8,128)(2,1)}, u32[]{:S(2)}) copy-start(bf16[6,16,3072]{2,1,0:T(8,128)(2,1)} %keys_two_ref.1) | copy-start | bytes 1769476
  36.4 13.1 %copy-start.3 = (bf16[2,16,768]{2,1,0:T(8,128)(2,1)S(1)}, bf16[2,16,768]{2,1,0:T(8,128)(2,1)}, u32[]{:S(2)}) copy-start(bf16[2,16,768]{2,1,0:T(8,128)(2,1)} %inputs_ref.1) | copy-start | bytes 147460
  36.4 6.8 %collective-permute-start.7 = (bf16[48,256]{1,0:T(8,128)(2,1)S(1)}, bf16[48,256]{1,0:T(8,128)(2,1)S(1)}, u32[]{:S(2)}, u32[]{:S(2)}) collective-permute-start(bf16[48,256]{1,0:T(8,128)(2,1)S(1)} %shard_map.122.block_ref), channel_id=1, source_target_pairs={{0,12},{1,13},{2,14},{3,15},{4,8},{5,9},{6,10},{7,11},{8,4},{9,5},... | collective-permute-start | bytes 73736 | tf_op jit(solution)/shard_map/ppermute | solution.py:29
  37.1 6.1 %collective-permute-start.6 = (bf16[48,256]{1,0:T(8,128)(2,1)S(1)}, bf16[48,256]{1,0:T(8,128)(2,1)S(1)}, u32[]{:S(2)}, u32[]{:S(2)}) collective-permute-start(bf16[48,256]{1,0:T(8,128)(2,1)S(1)} %shard_map.122.block_ref), channel_id=1, source_target_pairs={{0,8},{1,9},{2,10},{3,11},{4,12},{5,13},{6,14},{7,15},{8,0},{9,1},... | collective-permute-start | bytes 73736 | tf_op jit(solution)/shard_map/ppermute | solution.py:29
  37.7 5.5 %collective-permute-start.5 = (bf16[48,256]{1,0:T(8,128)(2,1)S(1)}, bf16[48,256]{1,0:T(8,128)(2,1)S(1)}, u32[]{:S(2)}, u32[]{:S(2)}) collective-permute-start(bf16[48,256]{1,0:T(8,128)(2,1)S(1)} %shard_map.122.block_ref), channel_id=1, source_target_pairs={{0,4},{1,5},{2,6},{3,7},{4,0},{5,1},{6,2},{7,3},{8,12},{9,13},{10,... | collective-permute-start | bytes 73736 | tf_op jit(solution)/shard_map/ppermute | solution.py:29
  43.3 4.7 %collective-permute-start.8 = (bf16[4,48,256]{2,1,0:T(8,128)(2,1)S(1)}, bf16[4,48,256]{2,1,0:T(8,128)(2,1)S(1)}, u32[]{:S(2)}, u32[]{:S(2)}) collective-permute-start(bf16[4,48,256]{2,1,0:T(8,128)(2,1)S(1)} %pad_maximum_fusion.1.block_ref), channel_id=1, source_target_pairs={{0,2},{1,3},{2,0},{3,1},{4,6},{5,7},{6,4},{7,5},{8,10},{9,11},{10,... | collective-permute-start | bytes 294920 | tf_op jit(solution)/shard_map/ppermute | solution.py:29
  48.0 1.5 %collective-permute-start.9 = (bf16[8,48,256]{2,1,0:T(8,128)(2,1)S(1)}, bf16[8,48,256]{2,1,0:T(8,128)(2,1)S(1)}, u32[]{:S(2)}, u32[]{:S(2)}) collective-permute-start(bf16[8,48,256]{2,1,0:T(8,128)(2,1)S(1)} %constant_dynamic-update-slice_fusion.5.mine_ref), channel_id=1, source_target_pairs={{0,1},{1,0},{2,3},{3,2},{4,5},{5,4},{6,7},{7,6},{8,9},{9,8},{10,11... | collective-permute-start | bytes 589832 | tf_op jit(solution)/shard_map/ppermute | solution.py:29

commit v10 on v9

--- a/solution.py
+++ b/solution.py
@@ -39,9 +39,12 @@
     return mine, swap(mine, n, 1)
 
 
-def owner(me, entry, core, n):
+def owner(me, entry, core, n, far_first=False):
     outer, middle = radices(n)
-    mask = (entry % outer) * (2 * middle) + (entry // outer) * 2 + core
+    place = entry % outer
+    if far_first:
+        place = (outer - place) % outer
+    mask = place * (2 * middle) + (entry // outer) * 2 + core
     return jnp.bitwise_xor(me, mask)
 
 
@@ -78,7 +81,7 @@
     part = from_ref.shape[0] // n
     copies = []
     for slot, (entry, core) in enumerate(order):
-        start = pl.multiple_of(owner(me, entry, core, n) * part, part)
+        start = pl.multiple_of(owner(me, entry, core, n, True) * part, part)
         copies.append(
             pltpu.make_async_copy(
                 from_ref.at[pl.ds(start, part), :], to_ref.at[slot], sems.at[slot]
@@ -254,7 +257,7 @@
         summed = None
         for (entry, core), (held, slot) in picked:
             values = (mine_ref, other_ref)[core][entry].astype(F32)
-            normed = (values * factor * gain_ref[owner(me, entry, core, n)]).astype(BF16)
+            normed = (values * factor * gain_ref[owner(me, entry, core, n, True)]).astype(BF16)
             product = jnp.dot(normed, held[slot], preferred_element_type=F32)
             summed = product if summed is None else summed + product
         return summed
@@ -293,7 +296,7 @@
     order = slots(n)
     first, second = 5 * n // 16, 3 * n // 4
 
-    arrived = [swap(block, n, o * 2 * middle) for o in range(1, outer)]
+    arrived = [swap(block, n, o * 2 * middle) for o in range(outer - 1, 0, -1)]
     held, gain, weight_a, place, weights, head_gain = fetch(
         me, block, gain, weight, n, order[:first], small, capacity
     )

time: 52.1 us -> 52.1 us (level)
  blocking collectives: 12.1 us -> 10.6 us
  waiting for transfers between devices: 4.89 us -> 6.34 us
    all_to_all x1, blocking collectives: 12.1 us -> 10.6 us  [local(): received = lax.all_to_all(sent, 'gx', 0, 0)]
    ppermute x10, waiting for transfers between devices: 4.89 us -> 6.34 us  [swap(): return lax.ppermute(block, 'gx', [(i, i ^ mask) for i in range(n)])]
where the time goes in v10:
time: 52.1 us; the launch traced here: 51.9 us
  Pallas kernels  21.4 us (41%)
  starting transfers between devices  11.9 us (23%)
  blocking collectives  10.6 us (20%)
  waiting for transfers between devices  6.34 us (12%)
  between operations  1.5 us (3%)
    ppermute x10, starting transfers between devices, swap(): return lax.ppermute(block, 'gx', [(i, i ^ mask) for i in range(n)])  11.9 us
    all_to_all x1, blocking collectives, local(): received = lax.all_to_all(sent, 'gx', 0, 0)  10.6 us
    ppermute x10, waiting for transfers between devices, swap(): return lax.ppermute(block, 'gx', [(i, i ^ mask) for i in range(n)])  6.34 us
    pallas_call x1, Pallas kernels, project(): pl.pallas_call(functools.partial(project_kernel, n, order[second:]), out_...  4.75 us
    pallas_call x2, Pallas kernels, keep(): pl.pallas_call(functools.partial(keep_kernel, half), out_shape=(jax.Shape...  4.69 us
    pallas_call x1, Pallas kernels, squares_beside(): pl.pallas_call(functools.partial(squares_kernel, n, order, len(blocks)),...  4.65 us
    pallas_call x1, Pallas kernels, fetch(): pl.pallas_call(functools.partial(fetch_kernel, n, order), out_shape=(pltp...  3.72 us
    pallas_call x1, Pallas kernels, output(): pl.pallas_call(functools.partial(output_kernel, n), out_shape=jax.ShapeDt...  2.37 us
  transfers between devices with their start and end apart: 10, of which 4 were waited for; matrix products, arithmetic and copies ran while one was open for 0% of the time, Pallas kernels for 25%

profile of v10, /device:TPU:0, one launch (start us, length us, event | category | flops | bytes accessed | tf_op | source)
XLA Modules:
  0.0 51.9 jit_solution(5025457933310183132)
XLA Ops:
  0.0 3.0 %collective-permute-start.2 = (bf16[32,768]{1,0:T(8,128)(2,1)}, bf16[32,768]{1,0:T(8,128)(2,1)S(1)}, u32[]{:S(2)}, u32[]{:S(2)}) collective-permute-start(bf16[32,768]{1,0:T(8,128)(2,1)} %bitcast.17), channel_id=1, source_target_pairs={{0,4},{1,5},{2,6},{3,7},{4,0},{5,1},{6,2},{7,3},{8,12},{9,13},{10,... | collective-permute-start | bytes 147464 | tf_op jit(solution)/shard_map/ppermute | solution.py:29
  3.0 2.6 %collective-permute-start.1 = (bf16[32,768]{1,0:T(8,128)(2,1)}, bf16[32,768]{1,0:T(8,128)(2,1)S(1)}, u32[]{:S(2)}, u32[]{:S(2)}) collective-permute-start(bf16[32,768]{1,0:T(8,128)(2,1)} %bitcast.18), channel_id=1, source_target_pairs={{0,8},{1,9},{2,10},{3,11},{4,12},{5,13},{6,14},{7,15},{8,0},{9,1},... | collective-permute-start | bytes 147464 | tf_op jit(solution)/shard_map/ppermute | solution.py:29
  5.6 0.0 collective-permute-start
  5.6 3.7 %shard_map.118 = (bf16[32,768]{1,0:T(8,128)(2,1)S(1)}, f32[16,1,768]{2,1,0:T(1,128)S(1)}, bf16[5,768,1152]{2,1,0:T(8,128)(2,1)S(1)}, s32[1,96]{1,0:T(1,128)S(1)}...) custom-call(s32[1]{0:T(128)} %bitcast.rest_0_.me_ref, bf16[32,768]{1,0:T(8,128)(2,1)} %bitcast.20, f32[16,1,768]{2,1,0:T(1,128)} %bitcast.26, ...), custom_call_target="tpu_custom_call" | custom-call | bytes 15000000 | tf_op jit(solution)/shard_map/pallas_call | solution.py:141
  9.4 2.3 %collective-permute-done = bf16[32,768]{1,0:T(8,128)(2,1)S(1)} collective-permute-done((bf16[32,768]{1,0:T(8,128)(2,1)}, bf16[32,768]{1,0:T(8,128)(2,1)S(1)}, u32[]{:S(2)}, u32[]{:S(2)}) %collective-permute-start) | collective-permute-done | bytes 49184 | tf_op jit(solution)/shard_map/ppermute | solution.py:29
  11.7 1.6 %collective-permute-start.3 = (bf16[4,32,768]{2,1,0:T(8,128)(2,1)S(1)}, bf16[4,32,768]{2,1,0:T(8,128)(2,1)S(1)}, u32[]{:S(2)}, u32[]{:S(2)}) collective-permute-start(bf16[4,32,768]{2,1,0:T(8,128)(2,1)S(1)} %pad_maximum_fusion.rest_0_), channel_id=1, source_target_pairs={{0,2},{1,3},{2,0},{3,1},{4,6},{5,7},{6,4},{7,5},{8,10},{9,11},{10,... | collective-permute-start | bytes 589832 | tf_op jit(solution)/shard_map/ppermute | solution.py:29
  13.3 4.6 %shard_map.119 = (f32[32,768]{1,0:T(8,128)S(1)}, bf16[7,768,1152]{2,1,0:T(8,128)(2,1)S(1)}) custom-call(s32[1]{0:T(128)} %bitcast.rest_0_.me_ref, bf16[12288,1152]{1,0:T(8,128)(2,1)} %weight_ref.3, bf16[4,32,768]{2,1,0:T(8,128)(2,1)S(1)} %pad_maximum_fusion.rest_0_), custom_call_target="tpu_custom_call" | custom-call | bytes 14699999 | tf_op jit(solution)/shard_map/pallas_call | solution.py:190
  18.1 0.1 collective-permute-start.4
  19.4 0.1 shard_map.120
  19.5 0.3 collective-permute-done.4.other_ref
  19.9 4.7 %shard_map.121 = bf16[16,18,128]{2,1,0:T(8,128)(2,1)S(1)} custom-call(s32[1]{0:T(128)} %bitcast.rest_0_.me_ref, f32[16,1,768]{2,1,0:T(1,128)S(1)} %get-tuple-element.25.gain_ref, f32[32,768]{1,0:T(8,128)S(1)} %get-tuple-element.31.before_ref, bf16[8,32,768]{2,1,0:T(8,128)(2,1)S(1)} %constant_dynamic-update-slice_fusion.mine_ref, ...), custom_call_target="tpu_custom_call" | custom-call | bytes 18000000 | tf_op jit(solution)/shard_map/pallas_call | solution.py:312
  24.6 10.6 %all_to_all.5.received_ref = bf16[16,18,128]{2,1,0:T(8,128)(2,1)S(1)} all-to-all(bf16[16,18,128]{2,1,0:T(8,128)(2,1)S(1)} %shard_map.121), channel_id=1, replica_groups=mesh['groups'=2,'gx'=16] {'gx'}, dimensions={0} | all-to-all | bytes 147456 | tf_op jit(solution)/shard_map/all_to_all | solution.py:535
  35.2 1.1 %shard_map.122.block_ref = bf16[48,256]{1,0:T(8,128)(2,1)S(1)} custom-call(bf16[16,18,128]{2,1,0:T(8,128)(2,1)S(1)} %all_to_all.5.received_ref, f32[2,1,128]{2,1,0:T(1,128)S(1)} %get-tuple-element.34.cos_ref, f32[2,1,128]{2,1,0:T(1,128)S(1)} %get-tuple-element.35.sin_ref, f32[1,96]{1,0:T(1,128)S(1)} %get-tuple-element.36.allowed_ref, ...), custom_call_target="tpu_custom_call" | custom-call | bytes 30000000 | tf_op jit(solution)/shard_map/pallas_call | solution.py:419
  36.4 0.0 copy-start.3
  36.4 0.7 %collective-permute-start.7 = (bf16[48,256]{1,0:T(8,128)(2,1)S(1)}, bf16[48,256]{1,0:T(8,128)(2,1)S(1)}, u32[]{:S(2)}, u32[]{:S(2)}) collective-permute-start(bf16[48,256]{1,0:T(8,128)(2,1)S(1)} %shard_map.122.block_ref), channel_id=1, source_target_pairs={{0,12},{1,13},{2,14},{3,15},{4,8},{5,9},{6,10},{7,11},{8,4},{9,5},... | collective-permute-start | bytes 73736 | tf_op jit(solution)/shard_map/ppermute | solution.py:29
  37.1 0.6 %collective-permute-start.6 = (bf16[48,256]{1,0:T(8,128)(2,1)S(1)}, bf16[48,256]{1,0:T(8,128)(2,1)S(1)}, u32[]{:S(2)}, u32[]{:S(2)}) collective-permute-start(bf16[48,256]{1,0:T(8,128)(2,1)S(1)} %shard_map.122.block_ref), channel_id=1, source_target_pairs={{0,8},{1,9},{2,10},{3,11},{4,12},{5,13},{6,14},{7,15},{8,0},{9,1},... | collective-permute-start | bytes 73736 | tf_op jit(solution)/shard_map/ppermute | solution.py:29
  37.7 3.2 %collective-permute-start.5 = (bf16[48,256]{1,0:T(8,128)(2,1)S(1)}, bf16[48,256]{1,0:T(8,128)(2,1)S(1)}, u32[]{:S(2)}, u32[]{:S(2)}) collective-permute-start(bf16[48,256]{1,0:T(8,128)(2,1)S(1)} %shard_map.122.block_ref), channel_id=1, source_target_pairs={{0,4},{1,5},{2,6},{3,7},{4,0},{5,1},{6,2},{7,3},{8,12},{9,13},{10,... | collective-permute-start | bytes 73736 | tf_op jit(solution)/shard_map/ppermute | solution.py:29
  40.9 2.3 %shard_map.123 = (bf16[48,256]{1,0:T(8,128)(2,1)S(1)}, bf16[3072,768]{1,0:T(8,128)(2,1)S(1)}) custom-call(bf16[48,256]{1,0:T(8,128)(2,1)S(1)} %shard_map.122.block_ref, bf16[6144,768]{1,0:T(8,128)(2,1)} %from_ref.3), custom_call_target="tpu_custom_call" | custom-call | bytes 6000000 | tf_op jit(solution)/shard_map/pallas_call | solution.py:474
  43.3 0.1 collective-permute-start.8
  43.3 2.3 %shard_map.124 = (bf16[4,48,256]{2,1,0:T(8,128)(2,1)S(1)}, bf16[3072,768]{1,0:T(8,128)(2,1)S(1)}) custom-call(bf16[4,48,256]{2,1,0:T(8,128)(2,1)S(1)} %pad_maximum_fusion.1.block_ref, bf16[6144,768]{1,0:T(8,128)(2,1)} %from_ref.3), custom_call_target="tpu_custom_call" | custom-call | bytes 6000000 | tf_op jit(solution)/shard_map/pallas_call | solution.py:474
  45.7 2.2 %collective-permute-done.8 = bf16[4,48,256]{2,1,0:T(8,128)(2,1)S(1)} collective-permute-done((bf16[4,48,256]{2,1,0:T(8,128)(2,1)S(1)}, bf16[4,48,256]{2,1,0:T(8,128)(2,1)S(1)}, u32[]{:S(2)}, u32[]{:S(2)}) %collective-permute-start.8) | collective-permute-done | bytes 98336 | tf_op jit(solution)/shard_map/ppermute | solution.py:29
  48.0 0.1 collective-permute-start.9
  48.1 1.4 %collective-permute-done.9.other_ref = bf16[8,48,256]{2,1,0:T(8,128)(2,1)S(1)} collective-permute-done((bf16[8,48,256]{2,1,0:T(8,128)(2,1)S(1)}, bf16[8,48,256]{2,1,0:T(8,128)(2,1)S(1)}, u32[]{:S(2)}, u32[]{:S(2)}) %collective-permute-start.9) | collective-permute-done | bytes 196640 | tf_op jit(solution)/shard_map/ppermute | solution.py:29
  49.5 2.4 %shard_map.125 = bf16[2,16,768]{2,1,0:T(8,128)(2,1)} custom-call(s32[1]{0:T(128)} %bitcast.rest_0_.me_ref, bf16[8,48,256]{2,1,0:T(8,128)(2,1)S(1)} %constant_dynamic-update-slice_fusion.5.mine_ref, bf16[8,48,256]{2,1,0:T(8,128)(2,1)S(1)} %collective-permute-done.9.other_ref, bf16[2,16,768]{2,1,0:T(8,128)(2,1)S(1)} %copy-done.3, ...), custom_call_target="tpu_custom_call" | custom-call | tf_op jit(solution)/shard_map/pallas_call | solution.py:501
  (22 shorter events, 0.1 us)
Async XLA Ops:
  0.0 9.4 %collective-permute-start.2 = (bf16[32,768]{1,0:T(8,128)(2,1)}, bf16[32,768]{1,0:T(8,128)(2,1)S(1)}, u32[]{:S(2)}, u32[]{:S(2)}) collective-permute-start(bf16[32,768]{1,0:T(8,128)(2,1)} %bitcast.17), channel_id=1, source_target_pairs={{0,4},{1,5},{2,6},{3,7},{4,0},{5,1},{6,2},{7,3},{8,12},{9,13},{10,... | collective-permute-start | bytes 147464 | tf_op jit(solution)/shard_map/ppermute | solution.py:29
  3.0 6.3 %collective-permute-start.1 = (bf16[32,768]{1,0:T(8,128)(2,1)}, bf16[32,768]{1,0:T(8,128)(2,1)S(1)}, u32[]{:S(2)}, u32[]{:S(2)}) collective-permute-start(bf16[32,768]{1,0:T(8,128)(2,1)} %bitcast.18), channel_id=1, source_target_pairs={{0,8},{1,9},{2,10},{3,11},{4,12},{5,13},{6,14},{7,15},{8,0},{9,1},... | collective-permute-start | bytes 147464 | tf_op jit(solution)/shard_map/ppermute | solution.py:29
  5.6 6.1 %collective-permute-start = (bf16[32,768]{1,0:T(8,128)(2,1)}, bf16[32,768]{1,0:T(8,128)(2,1)S(1)}, u32[]{:S(2)}, u32[]{:S(2)}) collective-permute-start(bf16[32,768]{1,0:T(8,128)(2,1)} %bitcast.19), channel_id=1, source_target_pairs={{0,12},{1,13},{2,14},{3,15},{4,8},{5,9},{6,10},{7,11},{8,4},{9,5},... | collective-permute-start | bytes 147464 | tf_op jit(solution)/shard_map/ppermute | solution.py:29
  11.7 6.3 %collective-permute-start.3 = (bf16[4,32,768]{2,1,0:T(8,128)(2,1)S(1)}, bf16[4,32,768]{2,1,0:T(8,128)(2,1)S(1)}, u32[]{:S(2)}, u32[]{:S(2)}) collective-permute-start(bf16[4,32,768]{2,1,0:T(8,128)(2,1)S(1)} %pad_maximum_fusion.rest_0_), channel_id=1, source_target_pairs={{0,2},{1,3},{2,0},{3,1},{4,6},{5,7},{6,4},{7,5},{8,10},{9,11},{10,... | collective-permute-start | bytes 589832 | tf_op jit(solution)/shard_map/ppermute | solution.py:29
  18.1 1.8 %collective-permute-start.4 = (bf16[8,32,768]{2,1,0:T(8,128)(2,1)S(1)}, bf16[8,32,768]{2,1,0:T(8,128)(2,1)S(1)}, u32[]{:S(2)}, u32[]{:S(2)}) collective-permute-start(bf16[8,32,768]{2,1,0:T(8,128)(2,1)S(1)} %constant_dynamic-update-slice_fusion.mine_ref), channel_id=1, source_target_pairs={{0,1},{1,0},{2,3},{3,2},{4,5},{5,4},{6,7},{7,6},{8,9},{9,8},{10,11... | collective-permute-start | bytes 1179656 | tf_op jit(solution)/shard_map/ppermute | solution.py:29
  19.8 15.4 %copy-start = (bf16[6,16,6144]{2,1,0:T(8,128)(2,1)S(1)}, bf16[6,16,6144]{2,1,0:T(8,128)(2,1)}, u32[]{:S(2)}) copy-start(bf16[6,16,6144]{2,1,0:T(8,128)(2,1)} %values_ref.1) | copy-start | bytes 3538948
  19.9 15.4 %copy-start.1 = (bf16[6,16,3072]{2,1,0:T(8,128)(2,1)S(1)}, bf16[6,16,3072]{2,1,0:T(8,128)(2,1)}, u32[]{:S(2)}) copy-start(bf16[6,16,3072]{2,1,0:T(8,128)(2,1)} %keys_one_ref.1) | copy-start | bytes 1769476
  19.9 15.4 %copy-start.2 = (bf16[6,16,3072]{2,1,0:T(8,128)(2,1)S(1)}, bf16[6,16,3072]{2,1,0:T(8,128)(2,1)}, u32[]{:S(2)}) copy-start(bf16[6,16,3072]{2,1,0:T(8,128)(2,1)} %keys_two_ref.1) | copy-start | bytes 1769476
  36.4 13.1 %copy-start.3 = (bf16[2,16,768]{2,1,0:T(8,128)(2,1)S(1)}, bf16[2,16,768]{2,1,0:T(8,128)(2,1)}, u32[]{:S(2)}) copy-start(bf16[2,16,768]{2,1,0:T(8,128)(2,1)} %inputs_ref.1) | copy-start | bytes 147460
  36.4 6.8 %collective-permute-start.7 = (bf16[48,256]{1,0:T(8,128)(2,1)S(1)}, bf16[48,256]{1,0:T(8,128)(2,1)S(1)}, u32[]{:S(2)}, u32[]{:S(2)}) collective-permute-start(bf16[48,256]{1,0:T(8,128)(2,1)S(1)} %shard_map.122.block_ref), channel_id=1, source_target_pairs={{0,12},{1,13},{2,14},{3,15},{4,8},{5,9},{6,10},{7,11},{8,4},{9,5},... | collective-permute-start | bytes 73736 | tf_op jit(solution)/shard_map/ppermute | solution.py:29
  37.1 6.1 %collective-permute-start.6 = (bf16[48,256]{1,0:T(8,128)(2,1)S(1)}, bf16[48,256]{1,0:T(8,128)(2,1)S(1)}, u32[]{:S(2)}, u32[]{:S(2)}) collective-permute-start(bf16[48,256]{1,0:T(8,128)(2,1)S(1)} %shard_map.122.block_ref), channel_id=1, source_target_pairs={{0,8},{1,9},{2,10},{3,11},{4,12},{5,13},{6,14},{7,15},{8,0},{9,1},... | collective-permute-start | bytes 73736 | tf_op jit(solution)/shard_map/ppermute | solution.py:29
  37.7 5.5 %collective-permute-start.5 = (bf16[48,256]{1,0:T(8,128)(2,1)S(1)}, bf16[48,256]{1,0:T(8,128)(2,1)S(1)}, u32[]{:S(2)}, u32[]{:S(2)}) collective-permute-start(bf16[48,256]{1,0:T(8,128)(2,1)S(1)} %shard_map.122.block_ref), channel_id=1, source_target_pairs={{0,4},{1,5},{2,6},{3,7},{4,0},{5,1},{6,2},{7,3},{8,12},{9,13},{10,... | collective-permute-start | bytes 73736 | tf_op jit(solution)/shard_map/ppermute | solution.py:29
  43.3 4.7 %collective-permute-start.8 = (bf16[4,48,256]{2,1,0:T(8,128)(2,1)S(1)}, bf16[4,48,256]{2,1,0:T(8,128)(2,1)S(1)}, u32[]{:S(2)}, u32[]{:S(2)}) collective-permute-start(bf16[4,48,256]{2,1,0:T(8,128)(2,1)S(1)} %pad_maximum_fusion.1.block_ref), channel_id=1, source_target_pairs={{0,2},{1,3},{2,0},{3,1},{4,6},{5,7},{6,4},{7,5},{8,10},{9,11},{10,... | collective-permute-start | bytes 294920 | tf_op jit(solution)/shard_map/ppermute | solution.py:29
  48.0 1.5 %collective-permute-start.9 = (bf16[8,48,256]{2,1,0:T(8,128)(2,1)S(1)}, bf16[8,48,256]{2,1,0:T(8,128)(2,1)S(1)}, u32[]{:S(2)}, u32[]{:S(2)}) collective-permute-start(bf16[8,48,256]{2,1,0:T(8,128)(2,1)S(1)} %constant_dynamic-update-slice_fusion.5.mine_ref), channel_id=1, source_target_pairs={{0,1},{1,0},{2,3},{3,2},{4,5},{5,4},{6,7},{7,6},{8,9},{9,8},{10,11... | collective-permute-start | bytes 589832 | tf_op jit(solution)/shard_map/ppermute | solution.py:29

commit v11 on v10

--- a/solution.py
+++ b/solution.py
@@ -54,23 +54,6 @@
 
 def hint(us):
     return pl.CostEstimate(flops=0, bytes_accessed=int(us * 3_000_000), transcendentals=0)
-
-
-def fetches(n, first, count, cores, me, from_ref, to_ref, sems):
-    part = from_ref.shape[0] // n
-    copies = []
-    for index, core in enumerate(cores):
-        for entry in range(count):
-            slot = index * count + entry
-            start = pl.multiple_of(owner(me, first + entry, core, n) * part, part)
-            copies.append(
-                pltpu.make_async_copy(
-                    from_ref.at[pl.ds(start, part), :],
-                    to_ref.at[slot],
-                    sems.at[slot],
-                )
-            )
-    return copies
 
 
 def slots(n):
@@ -294,7 +277,7 @@
     pieces = rows // n * (columns // 128)
     outer, middle = radices(n)
     order = slots(n)
-    first, second = 5 * n // 16, 3 * n // 4
+    first, second = n // 4, 3 * n // 4
 
     arrived = [swap(block, n, o * 2 * middle) for o in range(outer - 1, 0, -1)]
     held, gain, weight_a, place, weights, head_gain = fetch(

time: 52.1 us -> 52 us (level)
  blocking collectives: 10.6 us -> 9.99 us
  waiting for transfers between devices: 6.34 us -> 6.87 us
    all_to_all x1, blocking collectives: 10.6 us -> 9.99 us  [local(): received = lax.all_to_all(sent, 'gx', 0, 0)]
    ppermute x10, waiting for transfers between devices: 6.34 us -> 6.87 us  [swap(): return lax.ppermute(block, 'gx', [(i, i ^ mask) for i in range(n)])]
  transfers between devices with their start and end apart: 10 -> 10, of which waited for: 4 -> 5; matrix products, arithmetic and copies ran while one was open for 0% -> 0% of each run, Pallas kernels for 25% -> 25%
where the time goes in v11:
time: 52 us; the launch traced here: 51.7 us
  Pallas kernels  21.4 us (41%)
  starting transfers between devices  11.9 us (23%)
  blocking collectives  9.99 us (19%)
  waiting for transfers between devices  6.87 us (13%)
  between operations  1.49 us (3%)
    ppermute x10, starting transfers between devices, swap(): return lax.ppermute(block, 'gx', [(i, i ^ mask) for i in range(n)])  11.9 us
    all_to_all x1, blocking collectives, local(): received = lax.all_to_all(sent, 'gx', 0, 0)  9.99 us
    ppermute x10, waiting for transfers between devices, swap(): return lax.ppermute(block, 'gx', [(i, i ^ mask) for i in range(n)])  6.87 us
    pallas_call x1, Pallas kernels, squares_beside(): pl.pallas_call(functools.partial(squares_kernel, n, order, len(blocks)),...  5.16 us
    pallas_call x1, Pallas kernels, project(): pl.pallas_call(functools.partial(project_kernel, n, order[second:]), out_...  4.75 us
    pallas_call x2, Pallas kernels, keep(): pl.pallas_call(functools.partial(keep_kernel, half), out_shape=(jax.Shape...  4.69 us
    pallas_call x1, Pallas kernels, fetch(): pl.pallas_call(functools.partial(fetch_kernel, n, order), out_shape=(pltp...  3.21 us
    pallas_call x1, Pallas kernels, output(): pl.pallas_call(functools.partial(output_kernel, n), out_shape=jax.ShapeDt...  2.37 us
  transfers between devices with their start and end apart: 10, of which 5 were waited for; matrix products, arithmetic and copies ran while one was open for 0% of the time, Pallas kernels for 25%

profile of v11, /device:TPU:0, one launch (start us, length us, event | category | flops | bytes accessed | tf_op | source)
XLA Modules:
  0.0 51.7 jit_solution(12905427426448646721)
XLA Ops:
  0.0 3.0 %collective-permute-start.2 = (bf16[32,768]{1,0:T(8,128)(2,1)}, bf16[32,768]{1,0:T(8,128)(2,1)S(1)}, u32[]{:S(2)}, u32[]{:S(2)}) collective-permute-start(bf16[32,768]{1,0:T(8,128)(2,1)} %bitcast.17), channel_id=1, source_target_pairs={{0,4},{1,5},{2,6},{3,7},{4,0},{5,1},{6,2},{7,3},{8,12},{9,13},{10,... | collective-permute-start | bytes 147464 | tf_op jit(solution)/shard_map/ppermute | solution.py:29
  3.0 2.6 %collective-permute-start.1 = (bf16[32,768]{1,0:T(8,128)(2,1)}, bf16[32,768]{1,0:T(8,128)(2,1)S(1)}, u32[]{:S(2)}, u32[]{:S(2)}) collective-permute-start(bf16[32,768]{1,0:T(8,128)(2,1)} %bitcast.18), channel_id=1, source_target_pairs={{0,8},{1,9},{2,10},{3,11},{4,12},{5,13},{6,14},{7,15},{8,0},{9,1},... | collective-permute-start | bytes 147464 | tf_op jit(solution)/shard_map/ppermute | solution.py:29
  5.6 3.2 %shard_map.118 = (bf16[32,768]{1,0:T(8,128)(2,1)S(1)}, f32[16,1,768]{2,1,0:T(1,128)S(1)}, bf16[4,768,1152]{2,1,0:T(8,128)(2,1)S(1)}, s32[1,96]{1,0:T(1,128)S(1)}...) custom-call(s32[1]{0:T(128)} %bitcast.rest_0_.me_ref, bf16[32,768]{1,0:T(8,128)(2,1)} %bitcast.20, f32[16,1,768]{2,1,0:T(1,128)} %bitcast.26, ...), custom_call_target="tpu_custom_call" | custom-call | bytes 15000000 | tf_op jit(solution)/shard_map/pallas_call | solution.py:124
  8.9 0.3 collective-permute-done.1
  9.2 2.6 %collective-permute-done = bf16[32,768]{1,0:T(8,128)(2,1)S(1)} collective-permute-done((bf16[32,768]{1,0:T(8,128)(2,1)}, bf16[32,768]{1,0:T(8,128)(2,1)S(1)}, u32[]{:S(2)}, u32[]{:S(2)}) %collective-permute-start) | collective-permute-done | bytes 49184 | tf_op jit(solution)/shard_map/ppermute | solution.py:29
  11.7 1.6 %collective-permute-start.3 = (bf16[4,32,768]{2,1,0:T(8,128)(2,1)S(1)}, bf16[4,32,768]{2,1,0:T(8,128)(2,1)S(1)}, u32[]{:S(2)}, u32[]{:S(2)}) collective-permute-start(bf16[4,32,768]{2,1,0:T(8,128)(2,1)S(1)} %pad_maximum_fusion.rest_0_), channel_id=1, source_target_pairs={{0,2},{1,3},{2,0},{3,1},{4,6},{5,7},{6,4},{7,5},{8,10},{9,11},{10,... | collective-permute-start | bytes 589832 | tf_op jit(solution)/shard_map/ppermute | solution.py:29
  13.3 5.2 %shard_map.119 = (f32[32,768]{1,0:T(8,128)S(1)}, bf16[8,768,1152]{2,1,0:T(8,128)(2,1)S(1)}) custom-call(s32[1]{0:T(128)} %bitcast.rest_0_.me_ref, bf16[12288,1152]{1,0:T(8,128)(2,1)} %weight_ref.3, bf16[4,32,768]{2,1,0:T(8,128)(2,1)S(1)} %pad_maximum_fusion.rest_0_), custom_call_target="tpu_custom_call" | custom-call | bytes 16800000 | tf_op jit(solution)/shard_map/pallas_call | solution.py:173
  18.6 0.1 collective-permute-start.4
  19.9 0.1 shard_map.120
  20.0 0.3 collective-permute-done.4.other_ref
  20.4 4.7 %shard_map.121 = bf16[16,18,128]{2,1,0:T(8,128)(2,1)S(1)} custom-call(s32[1]{0:T(128)} %bitcast.rest_0_.me_ref, f32[16,1,768]{2,1,0:T(1,128)S(1)} %get-tuple-element.25.gain_ref, f32[32,768]{1,0:T(8,128)S(1)} %get-tuple-element.31.before_ref, bf16[8,32,768]{2,1,0:T(8,128)(2,1)S(1)} %constant_dynamic-update-slice_fusion.mine_ref, ...), custom_call_target="tpu_custom_call" | custom-call | bytes 18000000 | tf_op jit(solution)/shard_map/pallas_call | solution.py:295
  25.1 10.0 %all_to_all.5.received_ref = bf16[16,18,128]{2,1,0:T(8,128)(2,1)S(1)} all-to-all(bf16[16,18,128]{2,1,0:T(8,128)(2,1)S(1)} %shard_map.121), channel_id=1, replica_groups=mesh['groups'=2,'gx'=16] {'gx'}, dimensions={0} | all-to-all | bytes 147456 | tf_op jit(solution)/shard_map/all_to_all | solution.py:518
  35.1 1.1 %shard_map.122.block_ref = bf16[48,256]{1,0:T(8,128)(2,1)S(1)} custom-call(bf16[16,18,128]{2,1,0:T(8,128)(2,1)S(1)} %all_to_all.5.received_ref, f32[2,1,128]{2,1,0:T(1,128)S(1)} %get-tuple-element.34.cos_ref, f32[2,1,128]{2,1,0:T(1,128)S(1)} %get-tuple-element.35.sin_ref, f32[1,96]{1,0:T(1,128)S(1)} %get-tuple-element.36.allowed_ref, ...), custom_call_target="tpu_custom_call" | custom-call | bytes 30000000 | tf_op jit(solution)/shard_map/pallas_call | solution.py:402
  36.3 0.6 %collective-permute-start.7 = (bf16[48,256]{1,0:T(8,128)(2,1)S(1)}, bf16[48,256]{1,0:T(8,128)(2,1)S(1)}, u32[]{:S(2)}, u32[]{:S(2)}) collective-permute-start(bf16[48,256]{1,0:T(8,128)(2,1)S(1)} %shard_map.122.block_ref), channel_id=1, source_target_pairs={{0,12},{1,13},{2,14},{3,15},{4,8},{5,9},{6,10},{7,11},{8,4},{9,5},... | collective-permute-start | bytes 73736 | tf_op jit(solution)/shard_map/ppermute | solution.py:29
  36.9 0.6 %collective-permute-start.6 = (bf16[48,256]{1,0:T(8,128)(2,1)S(1)}, bf16[48,256]{1,0:T(8,128)(2,1)S(1)}, u32[]{:S(2)}, u32[]{:S(2)}) collective-permute-start(bf16[48,256]{1,0:T(8,128)(2,1)S(1)} %shard_map.122.block_ref), channel_id=1, source_target_pairs={{0,8},{1,9},{2,10},{3,11},{4,12},{5,13},{6,14},{7,15},{8,0},{9,1},... | collective-permute-start | bytes 73736 | tf_op jit(solution)/shard_map/ppermute | solution.py:29
  37.5 3.2 %collective-permute-start.5 = (bf16[48,256]{1,0:T(8,128)(2,1)S(1)}, bf16[48,256]{1,0:T(8,128)(2,1)S(1)}, u32[]{:S(2)}, u32[]{:S(2)}) collective-permute-start(bf16[48,256]{1,0:T(8,128)(2,1)S(1)} %shard_map.122.block_ref), channel_id=1, source_target_pairs={{0,4},{1,5},{2,6},{3,7},{4,0},{5,1},{6,2},{7,3},{8,12},{9,13},{10,... | collective-permute-start | bytes 73736 | tf_op jit(solution)/shard_map/ppermute | solution.py:29
  40.7 2.3 %shard_map.123 = (bf16[48,256]{1,0:T(8,128)(2,1)S(1)}, bf16[3072,768]{1,0:T(8,128)(2,1)S(1)}) custom-call(bf16[48,256]{1,0:T(8,128)(2,1)S(1)} %shard_map.122.block_ref, bf16[6144,768]{1,0:T(8,128)(2,1)} %from_ref.3), custom_call_target="tpu_custom_call" | custom-call | bytes 6000000 | tf_op jit(solution)/shard_map/pallas_call | solution.py:457
  43.1 0.0 copy-start.3
  43.1 0.1 collective-permute-start.8
  43.2 2.3 %shard_map.124 = (bf16[4,48,256]{2,1,0:T(8,128)(2,1)S(1)}, bf16[3072,768]{1,0:T(8,128)(2,1)S(1)}) custom-call(bf16[4,48,256]{2,1,0:T(8,128)(2,1)S(1)} %pad_maximum_fusion.1.block_ref, bf16[6144,768]{1,0:T(8,128)(2,1)} %from_ref.3), custom_call_target="tpu_custom_call" | custom-call | bytes 6000000 | tf_op jit(solution)/shard_map/pallas_call | solution.py:457
  45.6 2.2 %collective-permute-done.8 = bf16[4,48,256]{2,1,0:T(8,128)(2,1)S(1)} collective-permute-done((bf16[4,48,256]{2,1,0:T(8,128)(2,1)S(1)}, bf16[4,48,256]{2,1,0:T(8,128)(2,1)S(1)}, u32[]{:S(2)}, u32[]{:S(2)}) %collective-permute-start.8) | collective-permute-done | bytes 98336 | tf_op jit(solution)/shard_map/ppermute | solution.py:29
  47.9 0.1 collective-permute-start.9
  47.9 1.4 %collective-permute-done.9.other_ref = bf16[8,48,256]{2,1,0:T(8,128)(2,1)S(1)} collective-permute-done((bf16[8,48,256]{2,1,0:T(8,128)(2,1)S(1)}, bf16[8,48,256]{2,1,0:T(8,128)(2,1)S(1)}, u32[]{:S(2)}, u32[]{:S(2)}) %collective-permute-start.9) | collective-permute-done | bytes 196640 | tf_op jit(solution)/shard_map/ppermute | solution.py:29
  49.4 2.4 %shard_map.125 = bf16[2,16,768]{2,1,0:T(8,128)(2,1)} custom-call(s32[1]{0:T(128)} %bitcast.rest_0_.me_ref, bf16[8,48,256]{2,1,0:T(8,128)(2,1)S(1)} %constant_dynamic-update-slice_fusion.5.mine_ref, bf16[8,48,256]{2,1,0:T(8,128)(2,1)S(1)} %collective-permute-done.9.other_ref, bf16[2,16,768]{2,1,0:T(8,128)(2,1)S(1)} %copy-done.3, ...), custom_call_target="tpu_custom_call" | custom-call | tf_op jit(solution)/shard_map/pallas_call | solution.py:484
  (22 shorter events, 0.1 us)
Async XLA Ops:
  0.0 8.8 %collective-permute-start.2 = (bf16[32,768]{1,0:T(8,128)(2,1)}, bf16[32,768]{1,0:T(8,128)(2,1)S(1)}, u32[]{:S(2)}, u32[]{:S(2)}) collective-permute-start(bf16[32,768]{1,0:T(8,128)(2,1)} %bitcast.17), channel_id=1, source_target_pairs={{0,4},{1,5},{2,6},{3,7},{4,0},{5,1},{6,2},{7,3},{8,12},{9,13},{10,... | collective-permute-start | bytes 147464 | tf_op jit(solution)/shard_map/ppermute | solution.py:29
  3.0 6.1 %collective-permute-start.1 = (bf16[32,768]{1,0:T(8,128)(2,1)}, bf16[32,768]{1,0:T(8,128)(2,1)S(1)}, u32[]{:S(2)}, u32[]{:S(2)}) collective-permute-start(bf16[32,768]{1,0:T(8,128)(2,1)} %bitcast.18), channel_id=1, source_target_pairs={{0,8},{1,9},{2,10},{3,11},{4,12},{5,13},{6,14},{7,15},{8,0},{9,1},... | collective-permute-start | bytes 147464 | tf_op jit(solution)/shard_map/ppermute | solution.py:29
  5.6 6.1 %collective-permute-start = (bf16[32,768]{1,0:T(8,128)(2,1)}, bf16[32,768]{1,0:T(8,128)(2,1)S(1)}, u32[]{:S(2)}, u32[]{:S(2)}) collective-permute-start(bf16[32,768]{1,0:T(8,128)(2,1)} %bitcast.19), channel_id=1, source_target_pairs={{0,12},{1,13},{2,14},{3,15},{4,8},{5,9},{6,10},{7,11},{8,4},{9,5},... | collective-permute-start | bytes 147464 | tf_op jit(solution)/shard_map/ppermute | solution.py:29
  11.7 6.8 %collective-permute-start.3 = (bf16[4,32,768]{2,1,0:T(8,128)(2,1)S(1)}, bf16[4,32,768]{2,1,0:T(8,128)(2,1)S(1)}, u32[]{:S(2)}, u32[]{:S(2)}) collective-permute-start(bf16[4,32,768]{2,1,0:T(8,128)(2,1)S(1)} %pad_maximum_fusion.rest_0_), channel_id=1, source_target_pairs={{0,2},{1,3},{2,0},{3,1},{4,6},{5,7},{6,4},{7,5},{8,10},{9,11},{10,... | collective-permute-start | bytes 589832 | tf_op jit(solution)/shard_map/ppermute | solution.py:29
  18.6 1.8 %collective-permute-start.4 = (bf16[8,32,768]{2,1,0:T(8,128)(2,1)S(1)}, bf16[8,32,768]{2,1,0:T(8,128)(2,1)S(1)}, u32[]{:S(2)}, u32[]{:S(2)}) collective-permute-start(bf16[8,32,768]{2,1,0:T(8,128)(2,1)S(1)} %constant_dynamic-update-slice_fusion.mine_ref), channel_id=1, source_target_pairs={{0,1},{1,0},{2,3},{3,2},{4,5},{5,4},{6,7},{7,6},{8,9},{9,8},{10,11... | collective-permute-start | bytes 1179656 | tf_op jit(solution)/shard_map/ppermute | solution.py:29
  20.4 14.8 %copy-start = (bf16[6,16,6144]{2,1,0:T(8,128)(2,1)S(1)}, bf16[6,16,6144]{2,1,0:T(8,128)(2,1)}, u32[]{:S(2)}) copy-start(bf16[6,16,6144]{2,1,0:T(8,128)(2,1)} %values_ref.1) | copy-start | bytes 3538948
  20.4 14.8 %copy-start.1 = (bf16[6,16,3072]{2,1,0:T(8,128)(2,1)S(1)}, bf16[6,16,3072]{2,1,0:T(8,128)(2,1)}, u32[]{:S(2)}) copy-start(bf16[6,16,3072]{2,1,0:T(8,128)(2,1)} %keys_one_ref.1) | copy-start | bytes 1769476
  20.4 14.8 %copy-start.2 = (bf16[6,16,3072]{2,1,0:T(8,128)(2,1)S(1)}, bf16[6,16,3072]{2,1,0:T(8,128)(2,1)}, u32[]{:S(2)}) copy-start(bf16[6,16,3072]{2,1,0:T(8,128)(2,1)} %keys_two_ref.1) | copy-start | bytes 1769476
  36.3 6.8 %collective-permute-start.7 = (bf16[48,256]{1,0:T(8,128)(2,1)S(1)}, bf16[48,256]{1,0:T(8,128)(2,1)S(1)}, u32[]{:S(2)}, u32[]{:S(2)}) collective-permute-start(bf16[48,256]{1,0:T(8,128)(2,1)S(1)} %shard_map.122.block_ref), channel_id=1, source_target_pairs={{0,12},{1,13},{2,14},{3,15},{4,8},{5,9},{6,10},{7,11},{8,4},{9,5},... | collective-permute-start | bytes 73736 | tf_op jit(solution)/shard_map/ppermute | solution.py:29
  36.9 6.2 %collective-permute-start.6 = (bf16[48,256]{1,0:T(8,128)(2,1)S(1)}, bf16[48,256]{1,0:T(8,128)(2,1)S(1)}, u32[]{:S(2)}, u32[]{:S(2)}) collective-permute-start(bf16[48,256]{1,0:T(8,128)(2,1)S(1)} %shard_map.122.block_ref), channel_id=1, source_target_pairs={{0,8},{1,9},{2,10},{3,11},{4,12},{5,13},{6,14},{7,15},{8,0},{9,1},... | collective-permute-start | bytes 73736 | tf_op jit(solution)/shard_map/ppermute | solution.py:29
  37.5 5.6 %collective-permute-start.5 = (bf16[48,256]{1,0:T(8,128)(2,1)S(1)}, bf16[48,256]{1,0:T(8,128)(2,1)S(1)}, u32[]{:S(2)}, u32[]{:S(2)}) collective-permute-start(bf16[48,256]{1,0:T(8,128)(2,1)S(1)} %shard_map.122.block_ref), channel_id=1, source_target_pairs={{0,4},{1,5},{2,6},{3,7},{4,0},{5,1},{6,2},{7,3},{8,12},{9,13},{10,... | collective-permute-start | bytes 73736 | tf_op jit(solution)/shard_map/ppermute | solution.py:29
  43.1 6.3 %copy-start.3 = (bf16[2,16,768]{2,1,0:T(8,128)(2,1)S(1)}, bf16[2,16,768]{2,1,0:T(8,128)(2,1)}, u32[]{:S(2)}) copy-start(bf16[2,16,768]{2,1,0:T(8,128)(2,1)} %inputs_ref.1) | copy-start | bytes 147460
  43.1 4.7 %collective-permute-start.8 = (bf16[4,48,256]{2,1,0:T(8,128)(2,1)S(1)}, bf16[4,48,256]{2,1,0:T(8,128)(2,1)S(1)}, u32[]{:S(2)}, u32[]{:S(2)}) collective-permute-start(bf16[4,48,256]{2,1,0:T(8,128)(2,1)S(1)} %pad_maximum_fusion.1.block_ref), channel_id=1, source_target_pairs={{0,2},{1,3},{2,0},{3,1},{4,6},{5,7},{6,4},{7,5},{8,10},{9,11},{10,... | collective-permute-start | bytes 294920 | tf_op jit(solution)/shard_map/ppermute | solution.py:29
  47.9 1.5 %collective-permute-start.9 = (bf16[8,48,256]{2,1,0:T(8,128)(2,1)S(1)}, bf16[8,48,256]{2,1,0:T(8,128)(2,1)S(1)}, u32[]{:S(2)}, u32[]{:S(2)}) collective-permute-start(bf16[8,48,256]{2,1,0:T(8,128)(2,1)S(1)} %constant_dynamic-update-slice_fusion.5.mine_ref), channel_id=1, source_target_pairs={{0,1},{1,0},{2,3},{3,2},{4,5},{5,4},{6,7},{7,6},{8,9},{9,8},{10,11... | collective-permute-start | bytes 589832 | tf_op jit(solution)/shard_map/ppermute | solution.py:29

commit v12 on v11

--- a/solution.py
+++ b/solution.py
@@ -39,12 +39,9 @@
     return mine, swap(mine, n, 1)
 
 
-def owner(me, entry, core, n, far_first=False):
+def owner(me, entry, core, n):
     outer, middle = radices(n)
-    place = entry % outer
-    if far_first:
-        place = (outer - place) % outer
-    mask = place * (2 * middle) + (entry // outer) * 2 + core
+    mask = (entry % outer) * (2 * middle) + (entry // outer) * 2 + core
     return jnp.bitwise_xor(me, mask)
 
 
@@ -64,7 +61,7 @@
     part = from_ref.shape[0] // n
     copies = []
     for slot, (entry, core) in enumerate(order):
-        start = pl.multiple_of(owner(me, entry, core, n, True) * part, part)
+        start = pl.multiple_of(owner(me, entry, core, n) * part, part)
         copies.append(
             pltpu.make_async_copy(
                 from_ref.at[pl.ds(start, part), :], to_ref.at[slot], sems.at[slot]
@@ -240,7 +237,7 @@
         summed = None
         for (entry, core), (held, slot) in picked:
             values = (mine_ref, other_ref)[core][entry].astype(F32)
-            normed = (values * factor * gain_ref[owner(me, entry, core, n, True)]).astype(BF16)
+            normed = (values * factor * gain_ref[owner(me, entry, core, n)]).astype(BF16)
             product = jnp.dot(normed, held[slot], preferred_element_type=F32)
             summed = product if summed is None else summed + product
         return summed
@@ -279,7 +276,7 @@
     order = slots(n)
     first, second = n // 4, 3 * n // 4
 
-    arrived = [swap(block, n, o * 2 * middle) for o in range(outer - 1, 0, -1)]
+    arrived = [swap(block, n, o * 2 * middle) for o in range(1, outer)]
     held, gain, weight_a, place, weights, head_gain = fetch(
         me, block, gain, weight, n, order[:first], small, capacity
     )

time: 52 us -> 51.6 us (level)
  waiting for transfers between devices: 6.87 us -> 5.41 us
  blocking collectives: 9.99 us -> 11 us
    ppermute x10, waiting for transfers between devices: 6.87 us -> 5.41 us  [swap(): return lax.ppermute(block, 'gx', [(i, i ^ mask) for i in range(n)])]
    all_to_all x1, blocking collectives: 9.99 us -> 11 us  [local(): received = lax.all_to_all(sent, 'gx', 0, 0)]
  transfers between devices with their start and end apart: 10 -> 10, of which waited for: 5 -> 4; matrix products, arithmetic and copies ran while one was open for 0% -> 0% of each run, Pallas kernels for 25% -> 26%
where the time goes in v12:
time: 51.6 us; the launch traced here: 51.3 us
  Pallas kernels  21.4 us (41%)
  starting transfers between devices  11.9 us (23%)
  blocking collectives  11 us (21%)
  waiting for transfers between devices  5.41 us (10%)
  between operations  1.49 us (3%)
    ppermute x10, starting transfers between devices, swap(): return lax.ppermute(block, 'gx', [(i, i ^ mask) for i in range(n)])  11.9 us
    all_to_all x1, blocking collectives, local(): received = lax.all_to_all(sent, 'gx', 0, 0)  11 us
    ppermute x10, waiting for transfers between devices, swap(): return lax.ppermute(block, 'gx', [(i, i ^ mask) for i in range(n)])  5.41 us
    pallas_call x1, Pallas kernels, squares_beside(): pl.pallas_call(functools.partial(squares_kernel, n, order, len(blocks)),...  5.16 us
    pallas_call x1, Pallas kernels, project(): pl.pallas_call(functools.partial(project_kernel, n, order[second:]), out_...  4.75 us
    pallas_call x2, Pallas kernels, keep(): pl.pallas_call(functools.partial(keep_kernel, half), out_shape=(jax.Shape...  4.69 us
    pallas_call x1, Pallas kernels, fetch(): pl.pallas_call(functools.partial(fetch_kernel, n, order), out_shape=(pltp...  3.21 us
    pallas_call x1, Pallas kernels, output(): pl.pallas_call(functools.partial(output_kernel, n), out_shape=jax.ShapeDt...  2.37 us
  transfers between devices with their start and end apart: 10, of which 4 were waited for; matrix products, arithmetic and copies ran while one was open for 0% of the time, Pallas kernels for 26%

profile of v12, /device:TPU:0, one launch (start us, length us, event | category | flops | bytes accessed | tf_op | source)
XLA Modules:
  0.0 51.3 jit_solution(17980181308736969501)
XLA Ops:
  0.0 5.0 %collective-permute-start.2 = (bf16[32,768]{1,0:T(8,128)(2,1)}, bf16[32,768]{1,0:T(8,128)(2,1)S(1)}, u32[]{:S(2)}, u32[]{:S(2)}) collective-permute-start(bf16[32,768]{1,0:T(8,128)(2,1)} %bitcast.17), channel_id=1, source_target_pairs={{0,12},{1,13},{2,14},{3,15},{4,8},{5,9},{6,10},{7,11},{8,4},{9,5},... | collective-permute-start | bytes 147464 | tf_op jit(solution)/shard_map/ppermute | solution.py:29
  5.0 0.0 collective-permute-start.1
  5.1 0.6 %collective-permute-start = (bf16[32,768]{1,0:T(8,128)(2,1)}, bf16[32,768]{1,0:T(8,128)(2,1)S(1)}, u32[]{:S(2)}, u32[]{:S(2)}) collective-permute-start(bf16[32,768]{1,0:T(8,128)(2,1)} %bitcast.19), channel_id=1, source_target_pairs={{0,4},{1,5},{2,6},{3,7},{4,0},{5,1},{6,2},{7,3},{8,12},{9,13},{10,... | collective-permute-start | bytes 147464 | tf_op jit(solution)/shard_map/ppermute | solution.py:29
  5.6 3.2 %shard_map.118 = (bf16[32,768]{1,0:T(8,128)(2,1)S(1)}, f32[16,1,768]{2,1,0:T(1,128)S(1)}, bf16[4,768,1152]{2,1,0:T(8,128)(2,1)S(1)}, s32[1,96]{1,0:T(1,128)S(1)}...) custom-call(s32[1]{0:T(128)} %bitcast.rest_0_.me_ref, bf16[32,768]{1,0:T(8,128)(2,1)} %bitcast.20, f32[16,1,768]{2,1,0:T(1,128)} %bitcast.26, ...), custom_call_target="tpu_custom_call" | custom-call | bytes 15000000 | tf_op jit(solution)/shard_map/pallas_call | solution.py:121
  8.9 1.4 %collective-permute-done.1 = bf16[32,768]{1,0:T(8,128)(2,1)S(1)} collective-permute-done((bf16[32,768]{1,0:T(8,128)(2,1)}, bf16[32,768]{1,0:T(8,128)(2,1)S(1)}, u32[]{:S(2)}, u32[]{:S(2)}) %collective-permute-start.1) | collective-permute-done | bytes 49184 | tf_op jit(solution)/shard_map/ppermute | solution.py:29
  10.3 1.6 %collective-permute-start.3 = (bf16[4,32,768]{2,1,0:T(8,128)(2,1)S(1)}, bf16[4,32,768]{2,1,0:T(8,128)(2,1)S(1)}, u32[]{:S(2)}, u32[]{:S(2)}) collective-permute-start(bf16[4,32,768]{2,1,0:T(8,128)(2,1)S(1)} %pad_maximum_fusion.rest_0_), channel_id=1, source_target_pairs={{0,2},{1,3},{2,0},{3,1},{4,6},{5,7},{6,4},{7,5},{8,10},{9,11},{10,... | collective-permute-start | bytes 589832 | tf_op jit(solution)/shard_map/ppermute | solution.py:29
  11.9 5.2 %shard_map.119 = (f32[32,768]{1,0:T(8,128)S(1)}, bf16[8,768,1152]{2,1,0:T(8,128)(2,1)S(1)}) custom-call(s32[1]{0:T(128)} %bitcast.rest_0_.me_ref, bf16[12288,1152]{1,0:T(8,128)(2,1)} %weight_ref.3, bf16[4,32,768]{2,1,0:T(8,128)(2,1)S(1)} %pad_maximum_fusion.rest_0_), custom_call_target="tpu_custom_call" | custom-call | bytes 16800000 | tf_op jit(solution)/shard_map/pallas_call | solution.py:170
  17.1 0.1 collective-permute-start.4
  18.5 0.1 shard_map.120
  18.6 0.3 collective-permute-done.4.other_ref
  18.9 4.7 %shard_map.121 = bf16[16,18,128]{2,1,0:T(8,128)(2,1)S(1)} custom-call(s32[1]{0:T(128)} %bitcast.rest_0_.me_ref, f32[16,1,768]{2,1,0:T(1,128)S(1)} %get-tuple-element.25.gain_ref, f32[32,768]{1,0:T(8,128)S(1)} %get-tuple-element.31.before_ref, bf16[8,32,768]{2,1,0:T(8,128)(2,1)S(1)} %constant_dynamic-update-slice_fusion.mine_ref, ...), custom_call_target="tpu_custom_call" | custom-call | bytes 18000000 | tf_op jit(solution)/shard_map/pallas_call | solution.py:292
  23.7 11.0 %all_to_all.5.received_ref = bf16[16,18,128]{2,1,0:T(8,128)(2,1)S(1)} all-to-all(bf16[16,18,128]{2,1,0:T(8,128)(2,1)S(1)} %shard_map.121), channel_id=1, replica_groups=mesh['groups'=2,'gx'=16] {'gx'}, dimensions={0} | all-to-all | bytes 147456 | tf_op jit(solution)/shard_map/all_to_all | solution.py:515
  34.7 1.1 %shard_map.122.block_ref = bf16[48,256]{1,0:T(8,128)(2,1)S(1)} custom-call(bf16[16,18,128]{2,1,0:T(8,128)(2,1)S(1)} %all_to_all.5.received_ref, f32[2,1,128]{2,1,0:T(1,128)S(1)} %get-tuple-element.34.cos_ref, f32[2,1,128]{2,1,0:T(1,128)S(1)} %get-tuple-element.35.sin_ref, f32[1,96]{1,0:T(1,128)S(1)} %get-tuple-element.36.allowed_ref, ...), custom_call_target="tpu_custom_call" | custom-call | bytes 30000000 | tf_op jit(solution)/shard_map/pallas_call | solution.py:399
  35.9 0.7 %collective-permute-start.7 = (bf16[48,256]{1,0:T(8,128)(2,1)S(1)}, bf16[48,256]{1,0:T(8,128)(2,1)S(1)}, u32[]{:S(2)}, u32[]{:S(2)}) collective-permute-start(bf16[48,256]{1,0:T(8,128)(2,1)S(1)} %shard_map.122.block_ref), channel_id=1, source_target_pairs={{0,12},{1,13},{2,14},{3,15},{4,8},{5,9},{6,10},{7,11},{8,4},{9,5},... | collective-permute-start | bytes 73736 | tf_op jit(solution)/shard_map/ppermute | solution.py:29
  36.6 0.6 %collective-permute-start.6 = (bf16[48,256]{1,0:T(8,128)(2,1)S(1)}, bf16[48,256]{1,0:T(8,128)(2,1)S(1)}, u32[]{:S(2)}, u32[]{:S(2)}) collective-permute-start(bf16[48,256]{1,0:T(8,128)(2,1)S(1)} %shard_map.122.block_ref), channel_id=1, source_target_pairs={{0,8},{1,9},{2,10},{3,11},{4,12},{5,13},{6,14},{7,15},{8,0},{9,1},... | collective-permute-start | bytes 73736 | tf_op jit(solution)/shard_map/ppermute | solution.py:29
  37.2 3.2 %collective-permute-start.5 = (bf16[48,256]{1,0:T(8,128)(2,1)S(1)}, bf16[48,256]{1,0:T(8,128)(2,1)S(1)}, u32[]{:S(2)}, u32[]{:S(2)}) collective-permute-start(bf16[48,256]{1,0:T(8,128)(2,1)S(1)} %shard_map.122.block_ref), channel_id=1, source_target_pairs={{0,4},{1,5},{2,6},{3,7},{4,0},{5,1},{6,2},{7,3},{8,12},{9,13},{10,... | collective-permute-start | bytes 73736 | tf_op jit(solution)/shard_map/ppermute | solution.py:29
  40.3 2.3 %shard_map.123 = (bf16[48,256]{1,0:T(8,128)(2,1)S(1)}, bf16[3072,768]{1,0:T(8,128)(2,1)S(1)}) custom-call(bf16[48,256]{1,0:T(8,128)(2,1)S(1)} %shard_map.122.block_ref, bf16[6144,768]{1,0:T(8,128)(2,1)} %from_ref.3), custom_call_target="tpu_custom_call" | custom-call | bytes 6000000 | tf_op jit(solution)/shard_map/pallas_call | solution.py:454
  42.7 0.0 copy-start.3
  42.7 0.1 collective-permute-start.8
  42.8 2.3 %shard_map.124 = (bf16[4,48,256]{2,1,0:T(8,128)(2,1)S(1)}, bf16[3072,768]{1,0:T(8,128)(2,1)S(1)}) custom-call(bf16[4,48,256]{2,1,0:T(8,128)(2,1)S(1)} %pad_maximum_fusion.1.block_ref, bf16[6144,768]{1,0:T(8,128)(2,1)} %from_ref.3), custom_call_target="tpu_custom_call" | custom-call | bytes 6000000 | tf_op jit(solution)/shard_map/pallas_call | solution.py:454
  45.2 2.2 %collective-permute-done.8 = bf16[4,48,256]{2,1,0:T(8,128)(2,1)S(1)} collective-permute-done((bf16[4,48,256]{2,1,0:T(8,128)(2,1)S(1)}, bf16[4,48,256]{2,1,0:T(8,128)(2,1)S(1)}, u32[]{:S(2)}, u32[]{:S(2)}) %collective-permute-start.8) | collective-permute-done | bytes 98336 | tf_op jit(solution)/shard_map/ppermute | solution.py:29
  47.5 0.1 collective-permute-start.9
  47.5 1.4 %collective-permute-done.9.other_ref = bf16[8,48,256]{2,1,0:T(8,128)(2,1)S(1)} collective-permute-done((bf16[8,48,256]{2,1,0:T(8,128)(2,1)S(1)}, bf16[8,48,256]{2,1,0:T(8,128)(2,1)S(1)}, u32[]{:S(2)}, u32[]{:S(2)}) %collective-permute-start.9) | collective-permute-done | bytes 196640 | tf_op jit(solution)/shard_map/ppermute | solution.py:29
  49.0 2.4 %shard_map.125 = bf16[2,16,768]{2,1,0:T(8,128)(2,1)} custom-call(s32[1]{0:T(128)} %bitcast.rest_0_.me_ref, bf16[8,48,256]{2,1,0:T(8,128)(2,1)S(1)} %constant_dynamic-update-slice_fusion.5.mine_ref, bf16[8,48,256]{2,1,0:T(8,128)(2,1)S(1)} %collective-permute-done.9.other_ref, bf16[2,16,768]{2,1,0:T(8,128)(2,1)S(1)} %copy-done.3, ...), custom_call_target="tpu_custom_call" | custom-call | tf_op jit(solution)/shard_map/pallas_call | solution.py:481
  (22 shorter events, 0.1 us)
Async XLA Ops:
  0.0 8.8 %collective-permute-start.2 = (bf16[32,768]{1,0:T(8,128)(2,1)}, bf16[32,768]{1,0:T(8,128)(2,1)S(1)}, u32[]{:S(2)}, u32[]{:S(2)}) collective-permute-start(bf16[32,768]{1,0:T(8,128)(2,1)} %bitcast.17), channel_id=1, source_target_pairs={{0,12},{1,13},{2,14},{3,15},{4,8},{5,9},{6,10},{7,11},{8,4},{9,5},... | collective-permute-start | bytes 147464 | tf_op jit(solution)/shard_map/ppermute | solution.py:29
  5.0 5.2 %collective-permute-start.1 = (bf16[32,768]{1,0:T(8,128)(2,1)}, bf16[32,768]{1,0:T(8,128)(2,1)S(1)}, u32[]{:S(2)}, u32[]{:S(2)}) collective-permute-start(bf16[32,768]{1,0:T(8,128)(2,1)} %bitcast.18), channel_id=1, source_target_pairs={{0,8},{1,9},{2,10},{3,11},{4,12},{5,13},{6,14},{7,15},{8,0},{9,1},... | collective-permute-start | bytes 147464 | tf_op jit(solution)/shard_map/ppermute | solution.py:29
  5.1 5.2 %collective-permute-start = (bf16[32,768]{1,0:T(8,128)(2,1)}, bf16[32,768]{1,0:T(8,128)(2,1)S(1)}, u32[]{:S(2)}, u32[]{:S(2)}) collective-permute-start(bf16[32,768]{1,0:T(8,128)(2,1)} %bitcast.19), channel_id=1, source_target_pairs={{0,4},{1,5},{2,6},{3,7},{4,0},{5,1},{6,2},{7,3},{8,12},{9,13},{10,... | collective-permute-start | bytes 147464 | tf_op jit(solution)/shard_map/ppermute | solution.py:29
  10.3 6.8 %collective-permute-start.3 = (bf16[4,32,768]{2,1,0:T(8,128)(2,1)S(1)}, bf16[4,32,768]{2,1,0:T(8,128)(2,1)S(1)}, u32[]{:S(2)}, u32[]{:S(2)}) collective-permute-start(bf16[4,32,768]{2,1,0:T(8,128)(2,1)S(1)} %pad_maximum_fusion.rest_0_), channel_id=1, source_target_pairs={{0,2},{1,3},{2,0},{3,1},{4,6},{5,7},{6,4},{7,5},{8,10},{9,11},{10,... | collective-permute-start | bytes 589832 | tf_op jit(solution)/shard_map/ppermute | solution.py:29
  17.1 1.8 %collective-permute-start.4 = (bf16[8,32,768]{2,1,0:T(8,128)(2,1)S(1)}, bf16[8,32,768]{2,1,0:T(8,128)(2,1)S(1)}, u32[]{:S(2)}, u32[]{:S(2)}) collective-permute-start(bf16[8,32,768]{2,1,0:T(8,128)(2,1)S(1)} %constant_dynamic-update-slice_fusion.mine_ref), channel_id=1, source_target_pairs={{0,1},{1,0},{2,3},{3,2},{4,5},{5,4},{6,7},{7,6},{8,9},{9,8},{10,11... | collective-permute-start | bytes 1179656 | tf_op jit(solution)/shard_map/ppermute | solution.py:29
  18.9 15.8 %copy-start = (bf16[6,16,6144]{2,1,0:T(8,128)(2,1)S(1)}, bf16[6,16,6144]{2,1,0:T(8,128)(2,1)}, u32[]{:S(2)}) copy-start(bf16[6,16,6144]{2,1,0:T(8,128)(2,1)} %values_ref.1) | copy-start | bytes 3538948
  18.9 15.8 %copy-start.1 = (bf16[6,16,3072]{2,1,0:T(8,128)(2,1)S(1)}, bf16[6,16,3072]{2,1,0:T(8,128)(2,1)}, u32[]{:S(2)}) copy-start(bf16[6,16,3072]{2,1,0:T(8,128)(2,1)} %keys_one_ref.1) | copy-start | bytes 1769476
  18.9 15.8 %copy-start.2 = (bf16[6,16,3072]{2,1,0:T(8,128)(2,1)S(1)}, bf16[6,16,3072]{2,1,0:T(8,128)(2,1)}, u32[]{:S(2)}) copy-start(bf16[6,16,3072]{2,1,0:T(8,128)(2,1)} %keys_two_ref.1) | copy-start | bytes 1769476
  35.9 6.8 %collective-permute-start.7 = (bf16[48,256]{1,0:T(8,128)(2,1)S(1)}, bf16[48,256]{1,0:T(8,128)(2,1)S(1)}, u32[]{:S(2)}, u32[]{:S(2)}) collective-permute-start(bf16[48,256]{1,0:T(8,128)(2,1)S(1)} %shard_map.122.block_ref), channel_id=1, source_target_pairs={{0,12},{1,13},{2,14},{3,15},{4,8},{5,9},{6,10},{7,11},{8,4},{9,5},... | collective-permute-start | bytes 73736 | tf_op jit(solution)/shard_map/ppermute | solution.py:29
  36.6 6.1 %collective-permute-start.6 = (bf16[48,256]{1,0:T(8,128)(2,1)S(1)}, bf16[48,256]{1,0:T(8,128)(2,1)S(1)}, u32[]{:S(2)}, u32[]{:S(2)}) collective-permute-start(bf16[48,256]{1,0:T(8,128)(2,1)S(1)} %shard_map.122.block_ref), channel_id=1, source_target_pairs={{0,8},{1,9},{2,10},{3,11},{4,12},{5,13},{6,14},{7,15},{8,0},{9,1},... | collective-permute-start | bytes 73736 | tf_op jit(solution)/shard_map/ppermute | solution.py:29
  37.2 5.6 %collective-permute-start.5 = (bf16[48,256]{1,0:T(8,128)(2,1)S(1)}, bf16[48,256]{1,0:T(8,128)(2,1)S(1)}, u32[]{:S(2)}, u32[]{:S(2)}) collective-permute-start(bf16[48,256]{1,0:T(8,128)(2,1)S(1)} %shard_map.122.block_ref), channel_id=1, source_target_pairs={{0,4},{1,5},{2,6},{3,7},{4,0},{5,1},{6,2},{7,3},{8,12},{9,13},{10,... | collective-permute-start | bytes 73736 | tf_op jit(solution)/shard_map/ppermute | solution.py:29
  42.7 6.3 %copy-start.3 = (bf16[2,16,768]{2,1,0:T(8,128)(2,1)S(1)}, bf16[2,16,768]{2,1,0:T(8,128)(2,1)}, u32[]{:S(2)}) copy-start(bf16[2,16,768]{2,1,0:T(8,128)(2,1)} %inputs_ref.1) | copy-start | bytes 147460
  42.7 4.7 %collective-permute-start.8 = (bf16[4,48,256]{2,1,0:T(8,128)(2,1)S(1)}, bf16[4,48,256]{2,1,0:T(8,128)(2,1)S(1)}, u32[]{:S(2)}, u32[]{:S(2)}) collective-permute-start(bf16[4,48,256]{2,1,0:T(8,128)(2,1)S(1)} %pad_maximum_fusion.1.block_ref), channel_id=1, source_target_pairs={{0,2},{1,3},{2,0},{3,1},{4,6},{5,7},{6,4},{7,5},{8,10},{9,11},{10,... | collective-permute-start | bytes 294920 | tf_op jit(solution)/shard_map/ppermute | solution.py:29
  47.5 1.5 %collective-permute-start.9 = (bf16[8,48,256]{2,1,0:T(8,128)(2,1)S(1)}, bf16[8,48,256]{2,1,0:T(8,128)(2,1)S(1)}, u32[]{:S(2)}, u32[]{:S(2)}) collective-permute-start(bf16[8,48,256]{2,1,0:T(8,128)(2,1)S(1)} %constant_dynamic-update-slice_fusion.5.mine_ref), channel_id=1, source_target_pairs={{0,1},{1,0},{2,3},{3,2},{4,5},{5,4},{6,7},{7,6},{8,9},{9,8},{10,11... | collective-permute-start | bytes 589832 | tf_op jit(solution)/shard_map/ppermute | solution.py:29

commit v13 on v12

--- a/solution.py
+++ b/solution.py
@@ -253,10 +253,13 @@
         total[...] = products(blocks[:early], factor)
         kept[...] = jnp.broadcast_to(factor, kept.shape)
 
-    for copy in copies:
-        copy.wait()
     factor = kept[:, :1]
-    summed = total[...] + products(blocks[early:], factor)
+    summed = total[...]
+    half = -(-len(copies) // 2)
+    for group in (slice(0, half), slice(half, len(copies))):
+        for copy in copies[group]:
+            copy.wait()
+        summed = summed + products(blocks[early:][group], factor)
     columns = summed.shape[1] // 128
     steps = rows // n
     for block in range(columns):
@@ -274,7 +277,7 @@
     pieces = rows // n * (columns // 128)
     outer, middle = radices(n)
     order = slots(n)
-    first, second = n // 4, 3 * n // 4
+    first, second = n // 4, 5 * n // 8
 
     arrived = [swap(block, n, o * 2 * middle) for o in range(1, outer)]
     held, gain, weight_a, place, weights, head_gain = fetch(

time: 51.6 us -> 52.1 us (level)
  blocking collectives: 11 us -> 12 us
    pallas_call x1, Pallas kernels: 5.16 us -> 4.14 us  [squares_beside(): pl.pallas_call(functools.partial(squares_kernel, n, order, len(blocks)),...]
    all_to_all x1, blocking collectives: 11 us -> 12 us  [local(): received = lax.all_to_all(sent, 'gx', 0, 0)]
  transfers between devices with their start and end apart: 10 -> 10, of which waited for: 4 -> 4; matrix products, arithmetic and copies ran while one was open for 0% -> 0% of each run, Pallas kernels for 26% -> 23%
where the time goes in v13:
time: 52.1 us; the launch traced here: 51.9 us
  Pallas kernels  20.9 us (40%)
  blocking collectives  12 us (23%)
  starting transfers between devices  11.9 us (23%)
  waiting for transfers between devices  5.45 us (10%)
  between operations  1.48 us (3%)
    all_to_all x1, blocking collectives, local(): received = lax.all_to_all(sent, 'gx', 0, 0)  12 us
    ppermute x10, starting transfers between devices, swap(): return lax.ppermute(block, 'gx', [(i, i ^ mask) for i in range(n)])  11.9 us
    ppermute x10, waiting for transfers between devices, swap(): return lax.ppermute(block, 'gx', [(i, i ^ mask) for i in range(n)])  5.45 us
    pallas_call x1, Pallas kernels, project(): pl.pallas_call(functools.partial(project_kernel, n, order[second:]), out_...  5.27 us
    pallas_call x2, Pallas kernels, keep(): pl.pallas_call(functools.partial(keep_kernel, half), out_shape=(jax.Shape...  4.69 us
    pallas_call x1, Pallas kernels, squares_beside(): pl.pallas_call(functools.partial(squares_kernel, n, order, len(blocks)),...  4.14 us
    pallas_call x1, Pallas kernels, fetch(): pl.pallas_call(functools.partial(fetch_kernel, n, order), out_shape=(pltp...  3.21 us
    pallas_call x1, Pallas kernels, output(): pl.pallas_call(functools.partial(output_kernel, n), out_shape=jax.ShapeDt...  2.37 us
  transfers between devices with their start and end apart: 10, of which 4 were waited for; matrix products, arithmetic and copies ran while one was open for 0% of the time, Pallas kernels for 23%

profile of v13, /device:TPU:0, one launch (start us, length us, event | category | flops | bytes accessed | tf_op | source)
XLA Modules:
  0.0 51.9 jit_solution(8383364145168040613)
XLA Ops:
  0.0 5.0 %collective-permute-start.2 = (bf16[32,768]{1,0:T(8,128)(2,1)}, bf16[32,768]{1,0:T(8,128)(2,1)S(1)}, u32[]{:S(2)}, u32[]{:S(2)}) collective-permute-start(bf16[32,768]{1,0:T(8,128)(2,1)} %bitcast.17), channel_id=1, source_target_pairs={{0,12},{1,13},{2,14},{3,15},{4,8},{5,9},{6,10},{7,11},{8,4},{9,5},... | collective-permute-start | bytes 147464 | tf_op jit(solution)/shard_map/ppermute | solution.py:29
  5.1 0.6 %collective-permute-start = (bf16[32,768]{1,0:T(8,128)(2,1)}, bf16[32,768]{1,0:T(8,128)(2,1)S(1)}, u32[]{:S(2)}, u32[]{:S(2)}) collective-permute-start(bf16[32,768]{1,0:T(8,128)(2,1)} %bitcast.19), channel_id=1, source_target_pairs={{0,4},{1,5},{2,6},{3,7},{4,0},{5,1},{6,2},{7,3},{8,12},{9,13},{10,... | collective-permute-start | bytes 147464 | tf_op jit(solution)/shard_map/ppermute | solution.py:29
  5.6 3.2 %shard_map.118 = (bf16[32,768]{1,0:T(8,128)(2,1)S(1)}, f32[16,1,768]{2,1,0:T(1,128)S(1)}, bf16[4,768,1152]{2,1,0:T(8,128)(2,1)S(1)}, s32[1,96]{1,0:T(1,128)S(1)}...) custom-call(s32[1]{0:T(128)} %bitcast.rest_0_.me_ref, bf16[32,768]{1,0:T(8,128)(2,1)} %bitcast.20, f32[16,1,768]{2,1,0:T(1,128)} %bitcast.26, ...), custom_call_target="tpu_custom_call" | custom-call | bytes 15000000 | tf_op jit(solution)/shard_map/pallas_call | solution.py:121
  8.9 1.4 %collective-permute-done.1 = bf16[32,768]{1,0:T(8,128)(2,1)S(1)} collective-permute-done((bf16[32,768]{1,0:T(8,128)(2,1)}, bf16[32,768]{1,0:T(8,128)(2,1)S(1)}, u32[]{:S(2)}, u32[]{:S(2)}) %collective-permute-start.1) | collective-permute-done | bytes 49184 | tf_op jit(solution)/shard_map/ppermute | solution.py:29
  10.3 1.6 %collective-permute-start.3 = (bf16[4,32,768]{2,1,0:T(8,128)(2,1)S(1)}, bf16[4,32,768]{2,1,0:T(8,128)(2,1)S(1)}, u32[]{:S(2)}, u32[]{:S(2)}) collective-permute-start(bf16[4,32,768]{2,1,0:T(8,128)(2,1)S(1)} %pad_maximum_fusion.rest_0_), channel_id=1, source_target_pairs={{0,2},{1,3},{2,0},{3,1},{4,6},{5,7},{6,4},{7,5},{8,10},{9,11},{10,... | collective-permute-start | bytes 589832 | tf_op jit(solution)/shard_map/ppermute | solution.py:29
  11.9 4.1 %shard_map.119 = (f32[32,768]{1,0:T(8,128)S(1)}, bf16[6,768,1152]{2,1,0:T(8,128)(2,1)S(1)}) custom-call(s32[1]{0:T(128)} %bitcast.rest_0_.me_ref, bf16[12288,1152]{1,0:T(8,128)(2,1)} %weight_ref.3, bf16[4,32,768]{2,1,0:T(8,128)(2,1)S(1)} %pad_maximum_fusion.rest_0_), custom_call_target="tpu_custom_call" | custom-call | bytes 12599999 | tf_op jit(solution)/shard_map/pallas_call | solution.py:170
  16.1 0.0 collective-permute-done.3.rest_0_
  16.1 0.1 collective-permute-start.4
  17.5 0.1 shard_map.120
  17.6 0.3 collective-permute-done.4.other_ref
  17.9 5.3 %shard_map.121 = bf16[16,18,128]{2,1,0:T(8,128)(2,1)S(1)} custom-call(s32[1]{0:T(128)} %bitcast.rest_0_.me_ref, f32[16,1,768]{2,1,0:T(1,128)S(1)} %get-tuple-element.25.gain_ref, f32[32,768]{1,0:T(8,128)S(1)} %get-tuple-element.31.before_ref, bf16[8,32,768]{2,1,0:T(8,128)(2,1)S(1)} %constant_dynamic-update-slice_fusion.mine_ref, ...), custom_call_target="tpu_custom_call" | custom-call | bytes 18000000 | tf_op jit(solution)/shard_map/pallas_call | solution.py:295
  23.2 12.0 %all_to_all.5.received_ref = bf16[16,18,128]{2,1,0:T(8,128)(2,1)S(1)} all-to-all(bf16[16,18,128]{2,1,0:T(8,128)(2,1)S(1)} %shard_map.121), channel_id=1, replica_groups=mesh['groups'=2,'gx'=16] {'gx'}, dimensions={0} | all-to-all | bytes 147456 | tf_op jit(solution)/shard_map/all_to_all | solution.py:518
  35.2 1.1 %shard_map.122.block_ref = bf16[48,256]{1,0:T(8,128)(2,1)S(1)} custom-call(bf16[16,18,128]{2,1,0:T(8,128)(2,1)S(1)} %all_to_all.5.received_ref, f32[2,1,128]{2,1,0:T(1,128)S(1)} %get-tuple-element.34.cos_ref, f32[2,1,128]{2,1,0:T(1,128)S(1)} %get-tuple-element.35.sin_ref, f32[1,96]{1,0:T(1,128)S(1)} %get-tuple-element.36.allowed_ref, ...), custom_call_target="tpu_custom_call" | custom-call | bytes 30000000 | tf_op jit(solution)/shard_map/pallas_call | solution.py:402
  36.4 0.7 %collective-permute-start.7 = (bf16[48,256]{1,0:T(8,128)(2,1)S(1)}, bf16[48,256]{1,0:T(8,128)(2,1)S(1)}, u32[]{:S(2)}, u32[]{:S(2)}) collective-permute-start(bf16[48,256]{1,0:T(8,128)(2,1)S(1)} %shard_map.122.block_ref), channel_id=1, source_target_pairs={{0,12},{1,13},{2,14},{3,15},{4,8},{5,9},{6,10},{7,11},{8,4},{9,5},... | collective-permute-start | bytes 73736 | tf_op jit(solution)/shard_map/ppermute | solution.py:29
  37.1 0.6 %collective-permute-start.6 = (bf16[48,256]{1,0:T(8,128)(2,1)S(1)}, bf16[48,256]{1,0:T(8,128)(2,1)S(1)}, u32[]{:S(2)}, u32[]{:S(2)}) collective-permute-start(bf16[48,256]{1,0:T(8,128)(2,1)S(1)} %shard_map.122.block_ref), channel_id=1, source_target_pairs={{0,8},{1,9},{2,10},{3,11},{4,12},{5,13},{6,14},{7,15},{8,0},{9,1},... | collective-permute-start | bytes 73736 | tf_op jit(solution)/shard_map/ppermute | solution.py:29
  37.7 3.2 %collective-permute-start.5 = (bf16[48,256]{1,0:T(8,128)(2,1)S(1)}, bf16[48,256]{1,0:T(8,128)(2,1)S(1)}, u32[]{:S(2)}, u32[]{:S(2)}) collective-permute-start(bf16[48,256]{1,0:T(8,128)(2,1)S(1)} %shard_map.122.block_ref), channel_id=1, source_target_pairs={{0,4},{1,5},{2,6},{3,7},{4,0},{5,1},{6,2},{7,3},{8,12},{9,13},{10,... | collective-permute-start | bytes 73736 | tf_op jit(solution)/shard_map/ppermute | solution.py:29
  40.8 2.3 %shard_map.123 = (bf16[48,256]{1,0:T(8,128)(2,1)S(1)}, bf16[3072,768]{1,0:T(8,128)(2,1)S(1)}) custom-call(bf16[48,256]{1,0:T(8,128)(2,1)S(1)} %shard_map.122.block_ref, bf16[6144,768]{1,0:T(8,128)(2,1)} %from_ref.3), custom_call_target="tpu_custom_call" | custom-call | bytes 6000000 | tf_op jit(solution)/shard_map/pallas_call | solution.py:457
  43.2 0.0 copy-start.3
  43.3 0.1 collective-permute-start.8
  43.3 2.3 %shard_map.124 = (bf16[4,48,256]{2,1,0:T(8,128)(2,1)S(1)}, bf16[3072,768]{1,0:T(8,128)(2,1)S(1)}) custom-call(bf16[4,48,256]{2,1,0:T(8,128)(2,1)S(1)} %pad_maximum_fusion.1.block_ref, bf16[6144,768]{1,0:T(8,128)(2,1)} %from_ref.3), custom_call_target="tpu_custom_call" | custom-call | bytes 6000000 | tf_op jit(solution)/shard_map/pallas_call | solution.py:457
  45.7 2.2 %collective-permute-done.8 = bf16[4,48,256]{2,1,0:T(8,128)(2,1)S(1)} collective-permute-done((bf16[4,48,256]{2,1,0:T(8,128)(2,1)S(1)}, bf16[4,48,256]{2,1,0:T(8,128)(2,1)S(1)}, u32[]{:S(2)}, u32[]{:S(2)}) %collective-permute-start.8) | collective-permute-done | bytes 98336 | tf_op jit(solution)/shard_map/ppermute | solution.py:29
  48.0 0.1 collective-permute-start.9
  48.1 1.4 %collective-permute-done.9.other_ref = bf16[8,48,256]{2,1,0:T(8,128)(2,1)S(1)} collective-permute-done((bf16[8,48,256]{2,1,0:T(8,128)(2,1)S(1)}, bf16[8,48,256]{2,1,0:T(8,128)(2,1)S(1)}, u32[]{:S(2)}, u32[]{:S(2)}) %collective-permute-start.9) | collective-permute-done | bytes 196640 | tf_op jit(solution)/shard_map/ppermute | solution.py:29
  49.5 2.4 %shard_map.125 = bf16[2,16,768]{2,1,0:T(8,128)(2,1)} custom-call(s32[1]{0:T(128)} %bitcast.rest_0_.me_ref, bf16[8,48,256]{2,1,0:T(8,128)(2,1)S(1)} %constant_dynamic-update-slice_fusion.5.mine_ref, bf16[8,48,256]{2,1,0:T(8,128)(2,1)S(1)} %collective-permute-done.9.other_ref, bf16[2,16,768]{2,1,0:T(8,128)(2,1)S(1)} %copy-done.3, ...), custom_call_target="tpu_custom_call" | custom-call | tf_op jit(solution)/shard_map/pallas_call | solution.py:484
  (22 shorter events, 0.1 us)
Async XLA Ops:
  0.0 8.8 %collective-permute-start.2 = (bf16[32,768]{1,0:T(8,128)(2,1)}, bf16[32,768]{1,0:T(8,128)(2,1)S(1)}, u32[]{:S(2)}, u32[]{:S(2)}) collective-permute-start(bf16[32,768]{1,0:T(8,128)(2,1)} %bitcast.17), channel_id=1, source_target_pairs={{0,12},{1,13},{2,14},{3,15},{4,8},{5,9},{6,10},{7,11},{8,4},{9,5},... | collective-permute-start | bytes 147464 | tf_op jit(solution)/shard_map/ppermute | solution.py:29
  5.0 5.2 %collective-permute-start.1 = (bf16[32,768]{1,0:T(8,128)(2,1)}, bf16[32,768]{1,0:T(8,128)(2,1)S(1)}, u32[]{:S(2)}, u32[]{:S(2)}) collective-permute-start(bf16[32,768]{1,0:T(8,128)(2,1)} %bitcast.18), channel_id=1, source_target_pairs={{0,8},{1,9},{2,10},{3,11},{4,12},{5,13},{6,14},{7,15},{8,0},{9,1},... | collective-permute-start | bytes 147464 | tf_op jit(solution)/shard_map/ppermute | solution.py:29
  5.1 5.2 %collective-permute-start = (bf16[32,768]{1,0:T(8,128)(2,1)}, bf16[32,768]{1,0:T(8,128)(2,1)S(1)}, u32[]{:S(2)}, u32[]{:S(2)}) collective-permute-start(bf16[32,768]{1,0:T(8,128)(2,1)} %bitcast.19), channel_id=1, source_target_pairs={{0,4},{1,5},{2,6},{3,7},{4,0},{5,1},{6,2},{7,3},{8,12},{9,13},{10,... | collective-permute-start | bytes 147464 | tf_op jit(solution)/shard_map/ppermute | solution.py:29
  10.3 5.8 %collective-permute-start.3 = (bf16[4,32,768]{2,1,0:T(8,128)(2,1)S(1)}, bf16[4,32,768]{2,1,0:T(8,128)(2,1)S(1)}, u32[]{:S(2)}, u32[]{:S(2)}) collective-permute-start(bf16[4,32,768]{2,1,0:T(8,128)(2,1)S(1)} %pad_maximum_fusion.rest_0_), channel_id=1, source_target_pairs={{0,2},{1,3},{2,0},{3,1},{4,6},{5,7},{6,4},{7,5},{8,10},{9,11},{10,... | collective-permute-start | bytes 589832 | tf_op jit(solution)/shard_map/ppermute | solution.py:29
  16.1 1.8 %collective-permute-start.4 = (bf16[8,32,768]{2,1,0:T(8,128)(2,1)S(1)}, bf16[8,32,768]{2,1,0:T(8,128)(2,1)S(1)}, u32[]{:S(2)}, u32[]{:S(2)}) collective-permute-start(bf16[8,32,768]{2,1,0:T(8,128)(2,1)S(1)} %constant_dynamic-update-slice_fusion.mine_ref), channel_id=1, source_target_pairs={{0,1},{1,0},{2,3},{3,2},{4,5},{5,4},{6,7},{7,6},{8,9},{9,8},{10,11... | collective-permute-start | bytes 1179656 | tf_op jit(solution)/shard_map/ppermute | solution.py:29
  17.9 17.3 %copy-start = (bf16[6,16,6144]{2,1,0:T(8,128)(2,1)S(1)}, bf16[6,16,6144]{2,1,0:T(8,128)(2,1)}, u32[]{:S(2)}) copy-start(bf16[6,16,6144]{2,1,0:T(8,128)(2,1)} %values_ref.1) | copy-start | bytes 3538948
  17.9 17.3 %copy-start.1 = (bf16[6,16,3072]{2,1,0:T(8,128)(2,1)S(1)}, bf16[6,16,3072]{2,1,0:T(8,128)(2,1)}, u32[]{:S(2)}) copy-start(bf16[6,16,3072]{2,1,0:T(8,128)(2,1)} %keys_one_ref.1) | copy-start | bytes 1769476
  17.9 17.3 %copy-start.2 = (bf16[6,16,3072]{2,1,0:T(8,128)(2,1)S(1)}, bf16[6,16,3072]{2,1,0:T(8,128)(2,1)}, u32[]{:S(2)}) copy-start(bf16[6,16,3072]{2,1,0:T(8,128)(2,1)} %keys_two_ref.1) | copy-start | bytes 1769476
  36.4 6.8 %collective-permute-start.7 = (bf16[48,256]{1,0:T(8,128)(2,1)S(1)}, bf16[48,256]{1,0:T(8,128)(2,1)S(1)}, u32[]{:S(2)}, u32[]{:S(2)}) collective-permute-start(bf16[48,256]{1,0:T(8,128)(2,1)S(1)} %shard_map.122.block_ref), channel_id=1, source_target_pairs={{0,12},{1,13},{2,14},{3,15},{4,8},{5,9},{6,10},{7,11},{8,4},{9,5},... | collective-permute-start | bytes 73736 | tf_op jit(solution)/shard_map/ppermute | solution.py:29
  37.1 6.1 %collective-permute-start.6 = (bf16[48,256]{1,0:T(8,128)(2,1)S(1)}, bf16[48,256]{1,0:T(8,128)(2,1)S(1)}, u32[]{:S(2)}, u32[]{:S(2)}) collective-permute-start(bf16[48,256]{1,0:T(8,128)(2,1)S(1)} %shard_map.122.block_ref), channel_id=1, source_target_pairs={{0,8},{1,9},{2,10},{3,11},{4,12},{5,13},{6,14},{7,15},{8,0},{9,1},... | collective-permute-start | bytes 73736 | tf_op jit(solution)/shard_map/ppermute | solution.py:29
  37.7 5.6 %collective-permute-start.5 = (bf16[48,256]{1,0:T(8,128)(2,1)S(1)}, bf16[48,256]{1,0:T(8,128)(2,1)S(1)}, u32[]{:S(2)}, u32[]{:S(2)}) collective-permute-start(bf16[48,256]{1,0:T(8,128)(2,1)S(1)} %shard_map.122.block_ref), channel_id=1, source_target_pairs={{0,4},{1,5},{2,6},{3,7},{4,0},{5,1},{6,2},{7,3},{8,12},{9,13},{10,... | collective-permute-start | bytes 73736 | tf_op jit(solution)/shard_map/ppermute | solution.py:29
  43.2 6.3 %copy-start.3 = (bf16[2,16,768]{2,1,0:T(8,128)(2,1)S(1)}, bf16[2,16,768]{2,1,0:T(8,128)(2,1)}, u32[]{:S(2)}) copy-start(bf16[2,16,768]{2,1,0:T(8,128)(2,1)} %inputs_ref.1) | copy-start | bytes 147460
  43.3 4.7 %collective-permute-start.8 = (bf16[4,48,256]{2,1,0:T(8,128)(2,1)S(1)}, bf16[4,48,256]{2,1,0:T(8,128)(2,1)S(1)}, u32[]{:S(2)}, u32[]{:S(2)}) collective-permute-start(bf16[4,48,256]{2,1,0:T(8,128)(2,1)S(1)} %pad_maximum_fusion.1.block_ref), channel_id=1, source_target_pairs={{0,2},{1,3},{2,0},{3,1},{4,6},{5,7},{6,4},{7,5},{8,10},{9,11},{10,... | collective-permute-start | bytes 294920 | tf_op jit(solution)/shard_map/ppermute | solution.py:29
  48.0 1.5 %collective-permute-start.9 = (bf16[8,48,256]{2,1,0:T(8,128)(2,1)S(1)}, bf16[8,48,256]{2,1,0:T(8,128)(2,1)S(1)}, u32[]{:S(2)}, u32[]{:S(2)}) collective-permute-start(bf16[8,48,256]{2,1,0:T(8,128)(2,1)S(1)} %constant_dynamic-update-slice_fusion.5.mine_ref), channel_id=1, source_target_pairs={{0,1},{1,0},{2,3},{3,2},{4,5},{5,4},{6,7},{7,6},{8,9},{9,8},{10,11... | collective-permute-start | bytes 589832 | tf_op jit(solution)/shard_map/ppermute | solution.py:29

commit v14 on v12

--- a/solution.py
+++ b/solution.py
@@ -31,7 +31,7 @@
 
 def gather_blocks(block, n, first_aside, second_aside):
     outer, middle = radices(n)
-    arrived = [swap(block, n, o * 2 * middle) for o in range(1, outer)]
+    arrived = [swap(block, n, o * 2 * middle) for o in range(outer - 1, 0, -1)]
     rows = jnp.stack([first_aside(block)] + arrived)
     others = [swap(rows, n, m * 2) for m in range(1, middle)]
     rows, others = lax.optimization_barrier((second_aside(rows), others))
@@ -39,9 +39,12 @@
     return mine, swap(mine, n, 1)
 
 
-def owner(me, entry, core, n):
+def owner(me, entry, core, n, reverse=False):
     outer, middle = radices(n)
-    mask = (entry % outer) * (2 * middle) + (entry // outer) * 2 + core
+    place = entry % outer
+    if reverse:
+        place = (outer - place) % outer
+    mask = place * (2 * middle) + (entry // outer) * 2 + core
     return jnp.bitwise_xor(me, mask)
 
 
@@ -415,7 +418,7 @@
     lanes = width // 128
     for entry in range(half):
         for core, ref in ((0, mine_ref), (1, other_ref)):
-            start = pl.multiple_of(owner(me, entry, core, n) * heads, 8)
+            start = pl.multiple_of(owner(me, entry, core, n, True) * heads, 8)
             block = ref[entry].astype(F32)
             for lane in range(lanes):
                 rows_ref[lane, pl.ds(start, heads), :] = block[:, lane * 128 : (lane + 1) * 128]

time: 51.6 us -> 51.6 us (level)
  starting transfers between devices: 11.9 us -> 12.6 us
  waiting for transfers between devices: 5.41 us -> 4.73 us
    ppermute x10, starting transfers between devices: 11.9 us -> 12.6 us  [swap(): return lax.ppermute(block, 'gx', [(i, i ^ mask) for i in range(n)])]
    ppermute x10, waiting for transfers between devices: 5.41 us -> 4.73 us  [swap(): return lax.ppermute(block, 'gx', [(i, i ^ mask) for i in range(n)])]
where the time goes in v14:
time: 51.6 us; the launch traced here: 51.4 us
  Pallas kernels  21.4 us (41%)
  starting transfers between devices  12.6 us (24%)
  blocking collectives  11 us (21%)
  waiting for transfers between devices  4.73 us (9%)
  between operations  1.48 us (3%)
    ppermute x10, starting transfers between devices, swap(): return lax.ppermute(block, 'gx', [(i, i ^ mask) for i in range(n)])  12.6 us
    all_to_all x1, blocking collectives, local(): received = lax.all_to_all(sent, 'gx', 0, 0)  11 us
    pallas_call x1, Pallas kernels, squares_beside(): pl.pallas_call(functools.partial(squares_kernel, n, order, len(blocks)),...  5.16 us
    pallas_call x1, Pallas kernels, project(): pl.pallas_call(functools.partial(project_kernel, n, order[second:]), out_...  4.75 us
    ppermute x10, waiting for transfers between devices, swap(): return lax.ppermute(block, 'gx', [(i, i ^ mask) for i in range(n)])  4.73 us
    pallas_call x2, Pallas kernels, keep(): pl.pallas_call(functools.partial(keep_kernel, half), out_shape=(jax.Shape...  4.69 us
    pallas_call x1, Pallas kernels, fetch(): pl.pallas_call(functools.partial(fetch_kernel, n, order), out_shape=(pltp...  3.21 us
    pallas_call x1, Pallas kernels, output(): pl.pallas_call(functools.partial(output_kernel, n), out_shape=jax.ShapeDt...  2.37 us
  transfers between devices with their start and end apart: 10, of which 4 were waited for; matrix products, arithmetic and copies ran while one was open for 0% of the time, Pallas kernels for 26%

profile of v14, /device:TPU:0, one launch (start us, length us, event | category | flops | bytes accessed | tf_op | source)
XLA Modules:
  0.0 51.4 jit_solution(14664505987858837681)
XLA Ops:
  0.0 5.0 %collective-permute-start.2 = (bf16[32,768]{1,0:T(8,128)(2,1)}, bf16[32,768]{1,0:T(8,128)(2,1)S(1)}, u32[]{:S(2)}, u32[]{:S(2)}) collective-permute-start(bf16[32,768]{1,0:T(8,128)(2,1)} %bitcast.17), channel_id=1, source_target_pairs={{0,12},{1,13},{2,14},{3,15},{4,8},{5,9},{6,10},{7,11},{8,4},{9,5},... | collective-permute-start | bytes 147464 | tf_op jit(solution)/shard_map/ppermute | solution.py:29
  5.1 0.6 %collective-permute-start = (bf16[32,768]{1,0:T(8,128)(2,1)}, bf16[32,768]{1,0:T(8,128)(2,1)S(1)}, u32[]{:S(2)}, u32[]{:S(2)}) collective-permute-start(bf16[32,768]{1,0:T(8,128)(2,1)} %bitcast.19), channel_id=1, source_target_pairs={{0,4},{1,5},{2,6},{3,7},{4,0},{5,1},{6,2},{7,3},{8,12},{9,13},{10,... | collective-permute-start | bytes 147464 | tf_op jit(solution)/shard_map/ppermute | solution.py:29
  5.6 3.2 %shard_map.118 = (bf16[32,768]{1,0:T(8,128)(2,1)S(1)}, f32[16,1,768]{2,1,0:T(1,128)S(1)}, bf16[4,768,1152]{2,1,0:T(8,128)(2,1)S(1)}, s32[1,96]{1,0:T(1,128)S(1)}...) custom-call(s32[1]{0:T(128)} %bitcast.rest_0_.me_ref, bf16[32,768]{1,0:T(8,128)(2,1)} %bitcast.20, f32[16,1,768]{2,1,0:T(1,128)} %bitcast.26, ...), custom_call_target="tpu_custom_call" | custom-call | bytes 15000000 | tf_op jit(solution)/shard_map/pallas_call | solution.py:124
  8.9 1.4 %collective-permute-done.1 = bf16[32,768]{1,0:T(8,128)(2,1)S(1)} collective-permute-done((bf16[32,768]{1,0:T(8,128)(2,1)}, bf16[32,768]{1,0:T(8,128)(2,1)S(1)}, u32[]{:S(2)}, u32[]{:S(2)}) %collective-permute-start.1) | collective-permute-done | bytes 49184 | tf_op jit(solution)/shard_map/ppermute | solution.py:29
  10.3 1.6 %collective-permute-start.3 = (bf16[4,32,768]{2,1,0:T(8,128)(2,1)S(1)}, bf16[4,32,768]{2,1,0:T(8,128)(2,1)S(1)}, u32[]{:S(2)}, u32[]{:S(2)}) collective-permute-start(bf16[4,32,768]{2,1,0:T(8,128)(2,1)S(1)} %pad_maximum_fusion.rest_0_), channel_id=1, source_target_pairs={{0,2},{1,3},{2,0},{3,1},{4,6},{5,7},{6,4},{7,5},{8,10},{9,11},{10,... | collective-permute-start | bytes 589832 | tf_op jit(solution)/shard_map/ppermute | solution.py:29
  11.9 5.2 %shard_map.119 = (f32[32,768]{1,0:T(8,128)S(1)}, bf16[8,768,1152]{2,1,0:T(8,128)(2,1)S(1)}) custom-call(s32[1]{0:T(128)} %bitcast.rest_0_.me_ref, bf16[12288,1152]{1,0:T(8,128)(2,1)} %weight_ref.3, bf16[4,32,768]{2,1,0:T(8,128)(2,1)S(1)} %pad_maximum_fusion.rest_0_), custom_call_target="tpu_custom_call" | custom-call | bytes 16800000 | tf_op jit(solution)/shard_map/pallas_call | solution.py:173
  17.1 0.1 collective-permute-start.4
  18.5 0.1 shard_map.120
  18.6 0.3 collective-permute-done.4.other_ref
  18.9 4.7 %shard_map.121 = bf16[16,18,128]{2,1,0:T(8,128)(2,1)S(1)} custom-call(s32[1]{0:T(128)} %bitcast.rest_0_.me_ref, f32[16,1,768]{2,1,0:T(1,128)S(1)} %get-tuple-element.25.gain_ref, f32[32,768]{1,0:T(8,128)S(1)} %get-tuple-element.31.before_ref, bf16[8,32,768]{2,1,0:T(8,128)(2,1)S(1)} %constant_dynamic-update-slice_fusion.mine_ref, ...), custom_call_target="tpu_custom_call" | custom-call | bytes 18000000 | tf_op jit(solution)/shard_map/pallas_call | solution.py:295
  23.7 11.0 %all_to_all.5.received_ref = bf16[16,18,128]{2,1,0:T(8,128)(2,1)S(1)} all-to-all(bf16[16,18,128]{2,1,0:T(8,128)(2,1)S(1)} %shard_map.121), channel_id=1, replica_groups=mesh['groups'=2,'gx'=16] {'gx'}, dimensions={0} | all-to-all | bytes 147456 | tf_op jit(solution)/shard_map/all_to_all | solution.py:518
  34.7 1.1 %shard_map.122.block_ref = bf16[48,256]{1,0:T(8,128)(2,1)S(1)} custom-call(bf16[16,18,128]{2,1,0:T(8,128)(2,1)S(1)} %all_to_all.5.received_ref, f32[2,1,128]{2,1,0:T(1,128)S(1)} %get-tuple-element.34.cos_ref, f32[2,1,128]{2,1,0:T(1,128)S(1)} %get-tuple-element.35.sin_ref, f32[1,96]{1,0:T(1,128)S(1)} %get-tuple-element.36.allowed_ref, ...), custom_call_target="tpu_custom_call" | custom-call | bytes 30000000 | tf_op jit(solution)/shard_map/pallas_call | solution.py:402
  35.9 0.1 collective-permute-start.7
  35.9 1.2 %collective-permute-start.6 = (bf16[48,256]{1,0:T(8,128)(2,1)S(1)}, bf16[48,256]{1,0:T(8,128)(2,1)S(1)}, u32[]{:S(2)}, u32[]{:S(2)}) collective-permute-start(bf16[48,256]{1,0:T(8,128)(2,1)S(1)} %shard_map.122.block_ref), channel_id=1, source_target_pairs={{0,8},{1,9},{2,10},{3,11},{4,12},{5,13},{6,14},{7,15},{8,0},{9,1},... | collective-permute-start | bytes 73736 | tf_op jit(solution)/shard_map/ppermute | solution.py:29
  37.1 3.2 %collective-permute-start.5 = (bf16[48,256]{1,0:T(8,128)(2,1)S(1)}, bf16[48,256]{1,0:T(8,128)(2,1)S(1)}, u32[]{:S(2)}, u32[]{:S(2)}) collective-permute-start(bf16[48,256]{1,0:T(8,128)(2,1)S(1)} %shard_map.122.block_ref), channel_id=1, source_target_pairs={{0,12},{1,13},{2,14},{3,15},{4,8},{5,9},{6,10},{7,11},{8,4},{9,5},... | collective-permute-start | bytes 73736 | tf_op jit(solution)/shard_map/ppermute | solution.py:29
  40.3 2.3 %shard_map.123 = (bf16[48,256]{1,0:T(8,128)(2,1)S(1)}, bf16[3072,768]{1,0:T(8,128)(2,1)S(1)}) custom-call(bf16[48,256]{1,0:T(8,128)(2,1)S(1)} %shard_map.122.block_ref, bf16[6144,768]{1,0:T(8,128)(2,1)} %from_ref.3), custom_call_target="tpu_custom_call" | custom-call | bytes 6000000 | tf_op jit(solution)/shard_map/pallas_call | solution.py:457
  42.7 0.0 copy-start.3
  42.7 0.0 collective-permute-done.5
  42.8 0.8 %collective-permute-start.8 = (bf16[4,48,256]{2,1,0:T(8,128)(2,1)S(1)}, bf16[4,48,256]{2,1,0:T(8,128)(2,1)S(1)}, u32[]{:S(2)}, u32[]{:S(2)}) collective-permute-start(bf16[4,48,256]{2,1,0:T(8,128)(2,1)S(1)} %pad_maximum_fusion.1.block_ref), channel_id=1, source_target_pairs={{0,2},{1,3},{2,0},{3,1},{4,6},{5,7},{6,4},{7,5},{8,10},{9,11},{10,... | collective-permute-start | bytes 294920 | tf_op jit(solution)/shard_map/ppermute | solution.py:29
  43.6 2.3 %shard_map.124 = (bf16[4,48,256]{2,1,0:T(8,128)(2,1)S(1)}, bf16[3072,768]{1,0:T(8,128)(2,1)S(1)}) custom-call(bf16[4,48,256]{2,1,0:T(8,128)(2,1)S(1)} %pad_maximum_fusion.1.block_ref, bf16[6144,768]{1,0:T(8,128)(2,1)} %from_ref.3), custom_call_target="tpu_custom_call" | custom-call | bytes 6000000 | tf_op jit(solution)/shard_map/pallas_call | solution.py:457
  45.9 1.5 %collective-permute-done.8 = bf16[4,48,256]{2,1,0:T(8,128)(2,1)S(1)} collective-permute-done((bf16[4,48,256]{2,1,0:T(8,128)(2,1)S(1)}, bf16[4,48,256]{2,1,0:T(8,128)(2,1)S(1)}, u32[]{:S(2)}, u32[]{:S(2)}) %collective-permute-start.8) | collective-permute-done | bytes 98336 | tf_op jit(solution)/shard_map/ppermute | solution.py:29
  47.5 0.1 collective-permute-start.9
  47.6 1.4 %collective-permute-done.9.other_ref = bf16[8,48,256]{2,1,0:T(8,128)(2,1)S(1)} collective-permute-done((bf16[8,48,256]{2,1,0:T(8,128)(2,1)S(1)}, bf16[8,48,256]{2,1,0:T(8,128)(2,1)S(1)}, u32[]{:S(2)}, u32[]{:S(2)}) %collective-permute-start.9) | collective-permute-done | bytes 196640 | tf_op jit(solution)/shard_map/ppermute | solution.py:29
  49.0 2.4 %shard_map.125 = bf16[2,16,768]{2,1,0:T(8,128)(2,1)} custom-call(s32[1]{0:T(128)} %bitcast.rest_0_.me_ref, bf16[8,48,256]{2,1,0:T(8,128)(2,1)S(1)} %constant_dynamic-update-slice_fusion.5.mine_ref, bf16[8,48,256]{2,1,0:T(8,128)(2,1)S(1)} %collective-permute-done.9.other_ref, bf16[2,16,768]{2,1,0:T(8,128)(2,1)S(1)} %copy-done.3, ...), custom_call_target="tpu_custom_call" | custom-call | tf_op jit(solution)/shard_map/pallas_call | solution.py:484
  (22 shorter events, 0.1 us)
Async XLA Ops:
  0.0 8.8 %collective-permute-start.2 = (bf16[32,768]{1,0:T(8,128)(2,1)}, bf16[32,768]{1,0:T(8,128)(2,1)S(1)}, u32[]{:S(2)}, u32[]{:S(2)}) collective-permute-start(bf16[32,768]{1,0:T(8,128)(2,1)} %bitcast.17), channel_id=1, source_target_pairs={{0,12},{1,13},{2,14},{3,15},{4,8},{5,9},{6,10},{7,11},{8,4},{9,5},... | collective-permute-start | bytes 147464 | tf_op jit(solution)/shard_map/ppermute | solution.py:29
  5.0 5.2 %collective-permute-start.1 = (bf16[32,768]{1,0:T(8,128)(2,1)}, bf16[32,768]{1,0:T(8,128)(2,1)S(1)}, u32[]{:S(2)}, u32[]{:S(2)}) collective-permute-start(bf16[32,768]{1,0:T(8,128)(2,1)} %bitcast.18), channel_id=1, source_target_pairs={{0,8},{1,9},{2,10},{3,11},{4,12},{5,13},{6,14},{7,15},{8,0},{9,1},... | collective-permute-start | bytes 147464 | tf_op jit(solution)/shard_map/ppermute | solution.py:29
  5.1 5.2 %collective-permute-start = (bf16[32,768]{1,0:T(8,128)(2,1)}, bf16[32,768]{1,0:T(8,128)(2,1)S(1)}, u32[]{:S(2)}, u32[]{:S(2)}) collective-permute-start(bf16[32,768]{1,0:T(8,128)(2,1)} %bitcast.19), channel_id=1, source_target_pairs={{0,4},{1,5},{2,6},{3,7},{4,0},{5,1},{6,2},{7,3},{8,12},{9,13},{10,... | collective-permute-start | bytes 147464 | tf_op jit(solution)/shard_map/ppermute | solution.py:29
  10.3 6.8 %collective-permute-start.3 = (bf16[4,32,768]{2,1,0:T(8,128)(2,1)S(1)}, bf16[4,32,768]{2,1,0:T(8,128)(2,1)S(1)}, u32[]{:S(2)}, u32[]{:S(2)}) collective-permute-start(bf16[4,32,768]{2,1,0:T(8,128)(2,1)S(1)} %pad_maximum_fusion.rest_0_), channel_id=1, source_target_pairs={{0,2},{1,3},{2,0},{3,1},{4,6},{5,7},{6,4},{7,5},{8,10},{9,11},{10,... | collective-permute-start | bytes 589832 | tf_op jit(solution)/shard_map/ppermute | solution.py:29
  17.1 1.8 %collective-permute-start.4 = (bf16[8,32,768]{2,1,0:T(8,128)(2,1)S(1)}, bf16[8,32,768]{2,1,0:T(8,128)(2,1)S(1)}, u32[]{:S(2)}, u32[]{:S(2)}) collective-permute-start(bf16[8,32,768]{2,1,0:T(8,128)(2,1)S(1)} %constant_dynamic-update-slice_fusion.mine_ref), channel_id=1, source_target_pairs={{0,1},{1,0},{2,3},{3,2},{4,5},{5,4},{6,7},{7,6},{8,9},{9,8},{10,11... | collective-permute-start | bytes 1179656 | tf_op jit(solution)/shard_map/ppermute | solution.py:29
  18.9 15.8 %copy-start = (bf16[6,16,6144]{2,1,0:T(8,128)(2,1)S(1)}, bf16[6,16,6144]{2,1,0:T(8,128)(2,1)}, u32[]{:S(2)}) copy-start(bf16[6,16,6144]{2,1,0:T(8,128)(2,1)} %values_ref.1) | copy-start | bytes 3538948
  18.9 15.8 %copy-start.1 = (bf16[6,16,3072]{2,1,0:T(8,128)(2,1)S(1)}, bf16[6,16,3072]{2,1,0:T(8,128)(2,1)}, u32[]{:S(2)}) copy-start(bf16[6,16,3072]{2,1,0:T(8,128)(2,1)} %keys_one_ref.1) | copy-start | bytes 1769476
  18.9 15.8 %copy-start.2 = (bf16[6,16,3072]{2,1,0:T(8,128)(2,1)S(1)}, bf16[6,16,3072]{2,1,0:T(8,128)(2,1)}, u32[]{:S(2)}) copy-start(bf16[6,16,3072]{2,1,0:T(8,128)(2,1)} %keys_two_ref.1) | copy-start | bytes 1769476
  35.9 6.8 %collective-permute-start.7 = (bf16[48,256]{1,0:T(8,128)(2,1)S(1)}, bf16[48,256]{1,0:T(8,128)(2,1)S(1)}, u32[]{:S(2)}, u32[]{:S(2)}) collective-permute-start(bf16[48,256]{1,0:T(8,128)(2,1)S(1)} %shard_map.122.block_ref), channel_id=1, source_target_pairs={{0,4},{1,5},{2,6},{3,7},{4,0},{5,1},{6,2},{7,3},{8,12},{9,13},{10,... | collective-permute-start | bytes 73736 | tf_op jit(solution)/shard_map/ppermute | solution.py:29
  35.9 6.8 %collective-permute-start.6 = (bf16[48,256]{1,0:T(8,128)(2,1)S(1)}, bf16[48,256]{1,0:T(8,128)(2,1)S(1)}, u32[]{:S(2)}, u32[]{:S(2)}) collective-permute-start(bf16[48,256]{1,0:T(8,128)(2,1)S(1)} %shard_map.122.block_ref), channel_id=1, source_target_pairs={{0,8},{1,9},{2,10},{3,11},{4,12},{5,13},{6,14},{7,15},{8,0},{9,1},... | collective-permute-start | bytes 73736 | tf_op jit(solution)/shard_map/ppermute | solution.py:29
  37.1 5.6 %collective-permute-start.5 = (bf16[48,256]{1,0:T(8,128)(2,1)S(1)}, bf16[48,256]{1,0:T(8,128)(2,1)S(1)}, u32[]{:S(2)}, u32[]{:S(2)}) collective-permute-start(bf16[48,256]{1,0:T(8,128)(2,1)S(1)} %shard_map.122.block_ref), channel_id=1, source_target_pairs={{0,12},{1,13},{2,14},{3,15},{4,8},{5,9},{6,10},{7,11},{8,4},{9,5},... | collective-permute-start | bytes 73736 | tf_op jit(solution)/shard_map/ppermute | solution.py:29
  42.7 6.3 %copy-start.3 = (bf16[2,16,768]{2,1,0:T(8,128)(2,1)S(1)}, bf16[2,16,768]{2,1,0:T(8,128)(2,1)}, u32[]{:S(2)}) copy-start(bf16[2,16,768]{2,1,0:T(8,128)(2,1)} %inputs_ref.1) | copy-start | bytes 147460
  42.8 4.7 %collective-permute-start.8 = (bf16[4,48,256]{2,1,0:T(8,128)(2,1)S(1)}, bf16[4,48,256]{2,1,0:T(8,128)(2,1)S(1)}, u32[]{:S(2)}, u32[]{:S(2)}) collective-permute-start(bf16[4,48,256]{2,1,0:T(8,128)(2,1)S(1)} %pad_maximum_fusion.1.block_ref), channel_id=1, source_target_pairs={{0,2},{1,3},{2,0},{3,1},{4,6},{5,7},{6,4},{7,5},{8,10},{9,11},{10,... | collective-permute-start | bytes 294920 | tf_op jit(solution)/shard_map/ppermute | solution.py:29
  47.5 1.5 %collective-permute-start.9 = (bf16[8,48,256]{2,1,0:T(8,128)(2,1)S(1)}, bf16[8,48,256]{2,1,0:T(8,128)(2,1)S(1)}, u32[]{:S(2)}, u32[]{:S(2)}) collective-permute-start(bf16[8,48,256]{2,1,0:T(8,128)(2,1)S(1)} %constant_dynamic-update-slice_fusion.5.mine_ref), channel_id=1, source_target_pairs={{0,1},{1,0},{2,3},{3,2},{4,5},{5,4},{6,7},{7,6},{8,9},{9,8},{10,11... | collective-permute-start | bytes 589832 | tf_op jit(solution)/shard_map/ppermute | solution.py:29

commit v15 on v12

--- a/solution.py
+++ b/solution.py
@@ -31,9 +31,9 @@
 
 def gather_blocks(block, n, first_aside, second_aside):
     outer, middle = radices(n)
-    arrived = [swap(block, n, o * 2 * middle) for o in range(1, outer)]
+    arrived = [swap(block, n, m * 2) for m in range(1, middle)]
     rows = jnp.stack([first_aside(block)] + arrived)
-    others = [swap(rows, n, m * 2) for m in range(1, middle)]
+    others = [swap(rows, n, o * 2 * middle) for o in range(1, outer)]
     rows, others = lax.optimization_barrier((second_aside(rows), others))
     mine = jnp.concatenate([rows] + others)
     return mine, swap(mine, n, 1)
@@ -415,7 +415,8 @@
     lanes = width // 128
     for entry in range(half):
         for core, ref in ((0, mine_ref), (1, other_ref)):
-            start = pl.multiple_of(owner(me, entry, core, n) * heads, 8)
+            source = jnp.bitwise_xor(me, 2 * entry + core)
+            start = pl.multiple_of(source * heads, 8)
             block = ref[entry].astype(F32)
             for lane in range(lanes):
                 rows_ref[lane, pl.ds(start, heads), :] = block[:, lane * 128 : (lane + 1) * 128]

time: 51.6 us -> 50.7 us (0.983)
  waiting for transfers between devices: 5.41 us -> 4.61 us
    ppermute x10, waiting for transfers between devices: 5.41 us -> 4.61 us  [swap(): return lax.ppermute(block, 'gx', [(i, i ^ mask) for i in range(n)])]
where the time goes in v15:
time: 50.7 us; the launch traced here: 50.5 us
  Pallas kernels  21.4 us (42%)
  starting transfers between devices  11.8 us (23%)
  blocking collectives  11 us (22%)
  waiting for transfers between devices  4.61 us (9%)
  between operations  1.51 us (3%)
    ppermute x10, starting transfers between devices, swap(): return lax.ppermute(block, 'gx', [(i, i ^ mask) for i in range(n)])  11.8 us
    all_to_all x1, blocking collectives, local(): received = lax.all_to_all(sent, 'gx', 0, 0)  11 us
    pallas_call x1, Pallas kernels, squares_beside(): pl.pallas_call(functools.partial(squares_kernel, n, order, len(blocks)),...  5.16 us
    pallas_call x1, Pallas kernels, project(): pl.pallas_call(functools.partial(project_kernel, n, order[second:]), out_...  4.75 us
    pallas_call x2, Pallas kernels, keep(): pl.pallas_call(functools.partial(keep_kernel, half), out_shape=(jax.Shape...  4.69 us
    ppermute x10, waiting for transfers between devices, swap(): return lax.ppermute(block, 'gx', [(i, i ^ mask) for i in range(n)])  4.61 us
    pallas_call x1, Pallas kernels, fetch(): pl.pallas_call(functools.partial(fetch_kernel, n, order), out_shape=(pltp...  3.21 us
    pallas_call x1, Pallas kernels, output(): pl.pallas_call(functools.partial(output_kernel, n), out_shape=jax.ShapeDt...  2.37 us
  transfers between devices with their start and end apart: 10, of which 4 were waited for; matrix products, arithmetic and copies ran while one was open for 0% of the time, Pallas kernels for 26%

profile of v15, /device:TPU:0, one launch (start us, length us, event | category | flops | bytes accessed | tf_op | source)
XLA Modules:
  0.0 50.5 jit_solution(782850713150446059)
XLA Ops:
  0.0 5.0 %collective-permute-start.2 = (bf16[32,768]{1,0:T(8,128)(2,1)}, bf16[32,768]{1,0:T(8,128)(2,1)S(1)}, u32[]{:S(2)}, u32[]{:S(2)}) collective-permute-start(bf16[32,768]{1,0:T(8,128)(2,1)} %bitcast.15), channel_id=1, source_target_pairs={{0,12},{1,13},{2,14},{3,15},{4,8},{5,9},{6,10},{7,11},{8,4},{9,5},... | collective-permute-start | bytes 147464 | tf_op jit(solution)/shard_map/ppermute | solution.py:29
  5.0 0.0 collective-permute-start.1
  5.1 0.6 %collective-permute-start = (bf16[32,768]{1,0:T(8,128)(2,1)}, bf16[32,768]{1,0:T(8,128)(2,1)S(1)}, u32[]{:S(2)}, u32[]{:S(2)}) collective-permute-start(bf16[32,768]{1,0:T(8,128)(2,1)} %bitcast.17), channel_id=1, source_target_pairs={{0,4},{1,5},{2,6},{3,7},{4,0},{5,1},{6,2},{7,3},{8,12},{9,13},{10,... | collective-permute-start | bytes 147464 | tf_op jit(solution)/shard_map/ppermute | solution.py:29
  5.6 3.2 %shard_map.118 = (bf16[32,768]{1,0:T(8,128)(2,1)S(1)}, f32[16,1,768]{2,1,0:T(1,128)S(1)}, bf16[4,768,1152]{2,1,0:T(8,128)(2,1)S(1)}, s32[1,96]{1,0:T(1,128)S(1)}...) custom-call(s32[1]{0:T(128)} %bitcast.rest_0_.me_ref, bf16[32,768]{1,0:T(8,128)(2,1)} %bitcast.18, f32[16,1,768]{2,1,0:T(1,128)} %bitcast.24, ...), custom_call_target="tpu_custom_call" | custom-call | bytes 15000000 | tf_op jit(solution)/shard_map/pallas_call | solution.py:121
  8.9 1.4 %collective-permute-done.1 = bf16[32,768]{1,0:T(8,128)(2,1)S(1)} collective-permute-done((bf16[32,768]{1,0:T(8,128)(2,1)}, bf16[32,768]{1,0:T(8,128)(2,1)S(1)}, u32[]{:S(2)}, u32[]{:S(2)}) %collective-permute-start.1) | collective-permute-done | bytes 49184 | tf_op jit(solution)/shard_map/ppermute | solution.py:29
  10.3 1.6 %collective-permute-start.3 = (bf16[4,32,768]{2,1,0:T(8,128)(2,1)S(1)}, bf16[4,32,768]{2,1,0:T(8,128)(2,1)S(1)}, u32[]{:S(2)}, u32[]{:S(2)}) collective-permute-start(bf16[4,32,768]{2,1,0:T(8,128)(2,1)S(1)} %pad_maximum_fusion.rest_0_), channel_id=1, source_target_pairs={{0,2},{1,3},{2,0},{3,1},{4,6},{5,7},{6,4},{7,5},{8,10},{9,11},{10,... | collective-permute-start | bytes 589832 | tf_op jit(solution)/shard_map/ppermute | solution.py:29
  11.9 5.2 %shard_map.119 = (f32[32,768]{1,0:T(8,128)S(1)}, bf16[8,768,1152]{2,1,0:T(8,128)(2,1)S(1)}) custom-call(s32[1]{0:T(128)} %bitcast.rest_0_.me_ref, bf16[12288,1152]{1,0:T(8,128)(2,1)} %weight_ref.3, bf16[4,32,768]{2,1,0:T(8,128)(2,1)S(1)} %pad_maximum_fusion.rest_0_), custom_call_target="tpu_custom_call" | custom-call | bytes 16800000 | tf_op jit(solution)/shard_map/pallas_call | solution.py:170
  17.1 0.1 collective-permute-start.4
  18.5 0.1 shard_map.120
  18.6 0.3 collective-permute-done.4.other_ref
  18.9 4.7 %shard_map.121 = bf16[16,18,128]{2,1,0:T(8,128)(2,1)S(1)} custom-call(s32[1]{0:T(128)} %bitcast.rest_0_.me_ref, f32[16,1,768]{2,1,0:T(1,128)S(1)} %get-tuple-element.27.gain_ref, f32[32,768]{1,0:T(8,128)S(1)} %get-tuple-element.33.before_ref, bf16[8,32,768]{2,1,0:T(8,128)(2,1)S(1)} %constant_dynamic-update-slice_fusion.mine_ref, ...), custom_call_target="tpu_custom_call" | custom-call | bytes 18000000 | tf_op jit(solution)/shard_map/pallas_call | solution.py:292
  23.7 11.0 %all_to_all.5.received_ref = bf16[16,18,128]{2,1,0:T(8,128)(2,1)S(1)} all-to-all(bf16[16,18,128]{2,1,0:T(8,128)(2,1)S(1)} %shard_map.121), channel_id=1, replica_groups=mesh['groups'=2,'gx'=16] {'gx'}, dimensions={0} | all-to-all | bytes 147456 | tf_op jit(solution)/shard_map/all_to_all | solution.py:516
  34.7 1.1 %shard_map.122.block_ref = bf16[48,256]{1,0:T(8,128)(2,1)S(1)} custom-call(bf16[16,18,128]{2,1,0:T(8,128)(2,1)S(1)} %all_to_all.5.received_ref, f32[2,1,128]{2,1,0:T(1,128)S(1)} %get-tuple-element.36.cos_ref, f32[2,1,128]{2,1,0:T(1,128)S(1)} %get-tuple-element.37.sin_ref, f32[1,96]{1,0:T(1,128)S(1)} %get-tuple-element.38.allowed_ref, ...), custom_call_target="tpu_custom_call" | custom-call | bytes 30000000 | tf_op jit(solution)/shard_map/pallas_call | solution.py:399
  35.9 0.1 collective-permute-start.5
  35.9 2.3 %shard_map.123 = (bf16[48,256]{1,0:T(8,128)(2,1)S(1)}, bf16[3072,768]{1,0:T(8,128)(2,1)S(1)}) custom-call(bf16[48,256]{1,0:T(8,128)(2,1)S(1)} %shard_map.122.block_ref, bf16[6144,768]{1,0:T(8,128)(2,1)} %from_ref.3), custom_call_target="tpu_custom_call" | custom-call | bytes 6000000 | tf_op jit(solution)/shard_map/pallas_call | solution.py:455
  38.3 0.0 copy-start.3
  38.3 1.4 %collective-permute-done.5 = bf16[48,256]{1,0:T(8,128)(2,1)S(1)} collective-permute-done((bf16[48,256]{1,0:T(8,128)(2,1)S(1)}, bf16[48,256]{1,0:T(8,128)(2,1)S(1)}, u32[]{:S(2)}, u32[]{:S(2)}) %collective-permute-start.5) | collective-permute-done | bytes 24608 | tf_op jit(solution)/shard_map/ppermute | solution.py:29
  39.8 0.6 %collective-permute-start.8 = (bf16[2,48,256]{2,1,0:T(8,128)(2,1)S(1)}, bf16[2,48,256]{2,1,0:T(8,128)(2,1)S(1)}, u32[]{:S(2)}, u32[]{:S(2)}) collective-permute-start(bf16[2,48,256]{2,1,0:T(8,128)(2,1)S(1)} %pad_maximum_fusion.1.block_ref), channel_id=1, source_target_pairs={{0,12},{1,13},{2,14},{3,15},{4,8},{5,9},{6,10},{7,11},{8,4},{9,5},... | collective-permute-start | bytes 147464 | tf_op jit(solution)/shard_map/ppermute | solution.py:29
  40.4 0.6 %collective-permute-start.7 = (bf16[2,48,256]{2,1,0:T(8,128)(2,1)S(1)}, bf16[2,48,256]{2,1,0:T(8,128)(2,1)S(1)}, u32[]{:S(2)}, u32[]{:S(2)}) collective-permute-start(bf16[2,48,256]{2,1,0:T(8,128)(2,1)S(1)} %pad_maximum_fusion.1.block_ref), channel_id=1, source_target_pairs={{0,8},{1,9},{2,10},{3,11},{4,12},{5,13},{6,14},{7,15},{8,0},{9,1},... | collective-permute-start | bytes 147464 | tf_op jit(solution)/shard_map/ppermute | solution.py:29
  41.0 3.2 %collective-permute-start.6 = (bf16[2,48,256]{2,1,0:T(8,128)(2,1)S(1)}, bf16[2,48,256]{2,1,0:T(8,128)(2,1)S(1)}, u32[]{:S(2)}, u32[]{:S(2)}) collective-permute-start(bf16[2,48,256]{2,1,0:T(8,128)(2,1)S(1)} %pad_maximum_fusion.1.block_ref), channel_id=1, source_target_pairs={{0,4},{1,5},{2,6},{3,7},{4,0},{5,1},{6,2},{7,3},{8,12},{9,13},{10,... | collective-permute-start | bytes 147464 | tf_op jit(solution)/shard_map/ppermute | solution.py:29
  44.2 2.3 %shard_map.124 = (bf16[2,48,256]{2,1,0:T(8,128)(2,1)S(1)}, bf16[3072,768]{1,0:T(8,128)(2,1)S(1)}) custom-call(bf16[2,48,256]{2,1,0:T(8,128)(2,1)S(1)} %pad_maximum_fusion.1.block_ref, bf16[6144,768]{1,0:T(8,128)(2,1)} %from_ref.3), custom_call_target="tpu_custom_call" | custom-call | bytes 6000000 | tf_op jit(solution)/shard_map/pallas_call | solution.py:455
  46.6 0.1 collective-permute-start.9
  46.7 1.4 %collective-permute-done.9.other_ref = bf16[8,48,256]{2,1,0:T(8,128)(2,1)S(1)} collective-permute-done((bf16[8,48,256]{2,1,0:T(8,128)(2,1)S(1)}, bf16[8,48,256]{2,1,0:T(8,128)(2,1)S(1)}, u32[]{:S(2)}, u32[]{:S(2)}) %collective-permute-start.9) | collective-permute-done | bytes 196640 | tf_op jit(solution)/shard_map/ppermute | solution.py:29
  48.1 2.4 %shard_map.125 = bf16[2,16,768]{2,1,0:T(8,128)(2,1)} custom-call(s32[1]{0:T(128)} %bitcast.rest_0_.me_ref, bf16[8,48,256]{2,1,0:T(8,128)(2,1)S(1)} %constant_dynamic-update-slice_fusion.5.mine_ref, bf16[8,48,256]{2,1,0:T(8,128)(2,1)S(1)} %collective-permute-done.9.other_ref, bf16[2,16,768]{2,1,0:T(8,128)(2,1)S(1)} %copy-done.3, ...), custom_call_target="tpu_custom_call" | custom-call | tf_op jit(solution)/shard_map/pallas_call | solution.py:482
  (24 shorter events, 0.1 us)
Async XLA Ops:
  0.0 8.8 %collective-permute-start.2 = (bf16[32,768]{1,0:T(8,128)(2,1)}, bf16[32,768]{1,0:T(8,128)(2,1)S(1)}, u32[]{:S(2)}, u32[]{:S(2)}) collective-permute-start(bf16[32,768]{1,0:T(8,128)(2,1)} %bitcast.15), channel_id=1, source_target_pairs={{0,12},{1,13},{2,14},{3,15},{4,8},{5,9},{6,10},{7,11},{8,4},{9,5},... | collective-permute-start | bytes 147464 | tf_op jit(solution)/shard_map/ppermute | solution.py:29
  5.0 5.2 %collective-permute-start.1 = (bf16[32,768]{1,0:T(8,128)(2,1)}, bf16[32,768]{1,0:T(8,128)(2,1)S(1)}, u32[]{:S(2)}, u32[]{:S(2)}) collective-permute-start(bf16[32,768]{1,0:T(8,128)(2,1)} %bitcast.16), channel_id=1, source_target_pairs={{0,8},{1,9},{2,10},{3,11},{4,12},{5,13},{6,14},{7,15},{8,0},{9,1},... | collective-permute-start | bytes 147464 | tf_op jit(solution)/shard_map/ppermute | solution.py:29
  5.1 5.2 %collective-permute-start = (bf16[32,768]{1,0:T(8,128)(2,1)}, bf16[32,768]{1,0:T(8,128)(2,1)S(1)}, u32[]{:S(2)}, u32[]{:S(2)}) collective-permute-start(bf16[32,768]{1,0:T(8,128)(2,1)} %bitcast.17), channel_id=1, source_target_pairs={{0,4},{1,5},{2,6},{3,7},{4,0},{5,1},{6,2},{7,3},{8,12},{9,13},{10,... | collective-permute-start | bytes 147464 | tf_op jit(solution)/shard_map/ppermute | solution.py:29
  10.3 6.8 %collective-permute-start.3 = (bf16[4,32,768]{2,1,0:T(8,128)(2,1)S(1)}, bf16[4,32,768]{2,1,0:T(8,128)(2,1)S(1)}, u32[]{:S(2)}, u32[]{:S(2)}) collective-permute-start(bf16[4,32,768]{2,1,0:T(8,128)(2,1)S(1)} %pad_maximum_fusion.rest_0_), channel_id=1, source_target_pairs={{0,2},{1,3},{2,0},{3,1},{4,6},{5,7},{6,4},{7,5},{8,10},{9,11},{10,... | collective-permute-start | bytes 589832 | tf_op jit(solution)/shard_map/ppermute | solution.py:29
  17.1 1.8 %collective-permute-start.4 = (bf16[8,32,768]{2,1,0:T(8,128)(2,1)S(1)}, bf16[8,32,768]{2,1,0:T(8,128)(2,1)S(1)}, u32[]{:S(2)}, u32[]{:S(2)}) collective-permute-start(bf16[8,32,768]{2,1,0:T(8,128)(2,1)S(1)} %constant_dynamic-update-slice_fusion.mine_ref), channel_id=1, source_target_pairs={{0,1},{1,0},{2,3},{3,2},{4,5},{5,4},{6,7},{7,6},{8,9},{9,8},{10,11... | collective-permute-start | bytes 1179656 | tf_op jit(solution)/shard_map/ppermute | solution.py:29
  18.9 15.8 %copy-start = (bf16[6,16,6144]{2,1,0:T(8,128)(2,1)S(1)}, bf16[6,16,6144]{2,1,0:T(8,128)(2,1)}, u32[]{:S(2)}) copy-start(bf16[6,16,6144]{2,1,0:T(8,128)(2,1)} %values_ref.1) | copy-start | bytes 3538948
  18.9 15.8 %copy-start.1 = (bf16[6,16,3072]{2,1,0:T(8,128)(2,1)S(1)}, bf16[6,16,3072]{2,1,0:T(8,128)(2,1)}, u32[]{:S(2)}) copy-start(bf16[6,16,3072]{2,1,0:T(8,128)(2,1)} %keys_one_ref.1) | copy-start | bytes 1769476
  18.9 15.8 %copy-start.2 = (bf16[6,16,3072]{2,1,0:T(8,128)(2,1)S(1)}, bf16[6,16,3072]{2,1,0:T(8,128)(2,1)}, u32[]{:S(2)}) copy-start(bf16[6,16,3072]{2,1,0:T(8,128)(2,1)} %keys_two_ref.1) | copy-start | bytes 1769476
  35.9 3.9 %collective-permute-start.5 = (bf16[48,256]{1,0:T(8,128)(2,1)S(1)}, bf16[48,256]{1,0:T(8,128)(2,1)S(1)}, u32[]{:S(2)}, u32[]{:S(2)}) collective-permute-start(bf16[48,256]{1,0:T(8,128)(2,1)S(1)} %shard_map.122.block_ref), channel_id=1, source_target_pairs={{0,2},{1,3},{2,0},{3,1},{4,6},{5,7},{6,4},{7,5},{8,10},{9,11},{10,... | collective-permute-start | bytes 73736 | tf_op jit(solution)/shard_map/ppermute | solution.py:29
  38.3 9.8 %copy-start.3 = (bf16[2,16,768]{2,1,0:T(8,128)(2,1)S(1)}, bf16[2,16,768]{2,1,0:T(8,128)(2,1)}, u32[]{:S(2)}) copy-start(bf16[2,16,768]{2,1,0:T(8,128)(2,1)} %inputs_ref.1) | copy-start | bytes 147460
  39.8 6.7 %collective-permute-start.8 = (bf16[2,48,256]{2,1,0:T(8,128)(2,1)S(1)}, bf16[2,48,256]{2,1,0:T(8,128)(2,1)S(1)}, u32[]{:S(2)}, u32[]{:S(2)}) collective-permute-start(bf16[2,48,256]{2,1,0:T(8,128)(2,1)S(1)} %pad_maximum_fusion.1.block_ref), channel_id=1, source_target_pairs={{0,12},{1,13},{2,14},{3,15},{4,8},{5,9},{6,10},{7,11},{8,4},{9,5},... | collective-permute-start | bytes 147464 | tf_op jit(solution)/shard_map/ppermute | solution.py:29
  40.4 6.1 %collective-permute-start.7 = (bf16[2,48,256]{2,1,0:T(8,128)(2,1)S(1)}, bf16[2,48,256]{2,1,0:T(8,128)(2,1)S(1)}, u32[]{:S(2)}, u32[]{:S(2)}) collective-permute-start(bf16[2,48,256]{2,1,0:T(8,128)(2,1)S(1)} %pad_maximum_fusion.1.block_ref), channel_id=1, source_target_pairs={{0,8},{1,9},{2,10},{3,11},{4,12},{5,13},{6,14},{7,15},{8,0},{9,1},... | collective-permute-start | bytes 147464 | tf_op jit(solution)/shard_map/ppermute | solution.py:29
  41.0 5.5 %collective-permute-start.6 = (bf16[2,48,256]{2,1,0:T(8,128)(2,1)S(1)}, bf16[2,48,256]{2,1,0:T(8,128)(2,1)S(1)}, u32[]{:S(2)}, u32[]{:S(2)}) collective-permute-start(bf16[2,48,256]{2,1,0:T(8,128)(2,1)S(1)} %pad_maximum_fusion.1.block_ref), channel_id=1, source_target_pairs={{0,4},{1,5},{2,6},{3,7},{4,0},{5,1},{6,2},{7,3},{8,12},{9,13},{10,... | collective-permute-start | bytes 147464 | tf_op jit(solution)/shard_map/ppermute | solution.py:29
  46.6 1.5 %collective-permute-start.9 = (bf16[8,48,256]{2,1,0:T(8,128)(2,1)S(1)}, bf16[8,48,256]{2,1,0:T(8,128)(2,1)S(1)}, u32[]{:S(2)}, u32[]{:S(2)}) collective-permute-start(bf16[8,48,256]{2,1,0:T(8,128)(2,1)S(1)} %constant_dynamic-update-slice_fusion.5.mine_ref), channel_id=1, source_target_pairs={{0,1},{1,0},{2,3},{3,2},{4,5},{5,4},{6,7},{7,6},{8,9},{9,8},{10,11... | collective-permute-start | bytes 589832 | tf_op jit(solution)/shard_map/ppermute | solution.py:29

commit v16 on v15

--- a/solution.py
+++ b/solution.py
@@ -33,7 +33,7 @@
     outer, middle = radices(n)
     arrived = [swap(block, n, m * 2) for m in range(1, middle)]
     rows = jnp.stack([first_aside(block)] + arrived)
-    others = [swap(rows, n, o * 2 * middle) for o in range(1, outer)]
+    others = [swap(rows, n, o * 2 * middle) for o in range(outer - 1, 0, -1)]
     rows, others = lax.optimization_barrier((second_aside(rows), others))
     mine = jnp.concatenate([rows] + others)
     return mine, swap(mine, n, 1)
@@ -413,9 +413,11 @@
     half, heads, width = mine_ref.shape
     steps = heads // H
     lanes = width // 128
+    outer, middle = radices(n)
     for entry in range(half):
         for core, ref in ((0, mine_ref), (1, other_ref)):
-            source = jnp.bitwise_xor(me, 2 * entry + core)
+            along = (outer - entry // middle) % outer
+            source = jnp.bitwise_xor(me, 2 * (along * middle + entry % middle) + core)
             start = pl.multiple_of(source * heads, 8)
             block = ref[entry].astype(F32)
             for lane in range(lanes):

time: 50.7 us -> 51 us (level)
  transfers between devices with their start and end apart: 10 -> 10, of which waited for: 4 -> 5; matrix products, arithmetic and copies ran while one was open for 0% -> 0% of each run, Pallas kernels for 26% -> 26%
where the time goes in v16:
time: 51 us; the launch traced here: 50.8 us
  Pallas kernels  21.4 us (42%)
  starting transfers between devices  11.8 us (23%)
  blocking collectives  11 us (22%)
  waiting for transfers between devices  4.92 us (10%)
  between operations  1.49 us (3%)
    ppermute x10, starting transfers between devices, swap(): return lax.ppermute(block, 'gx', [(i, i ^ mask) for i in range(n)])  11.8 us
    all_to_all x1, blocking collectives, local(): received = lax.all_to_all(sent, 'gx', 0, 0)  11 us
    pallas_call x1, Pallas kernels, squares_beside(): pl.pallas_call(functools.partial(squares_kernel, n, order, len(blocks)),...  5.16 us
    ppermute x10, waiting for transfers between devices, swap(): return lax.ppermute(block, 'gx', [(i, i ^ mask) for i in range(n)])  4.92 us
    pallas_call x1, Pallas kernels, project(): pl.pallas_call(functools.partial(project_kernel, n, order[second:]), out_...  4.75 us
    pallas_call x2, Pallas kernels, keep(): pl.pallas_call(functools.partial(keep_kernel, half), out_shape=(jax.Shape...  4.69 us
    pallas_call x1, Pallas kernels, fetch(): pl.pallas_call(functools.partial(fetch_kernel, n, order), out_shape=(pltp...  3.21 us
    pallas_call x1, Pallas kernels, output(): pl.pallas_call(functools.partial(output_kernel, n), out_shape=jax.ShapeDt...  2.37 us
  transfers between devices with their start and end apart: 10, of which 5 were waited for; matrix products, arithmetic and copies ran while one was open for 0% of the time, Pallas kernels for 26%

profile of v16, /device:TPU:0, one launch (start us, length us, event | category | flops | bytes accessed | tf_op | source)
XLA Modules:
  0.0 50.8 jit_solution(5874534206473506218)
XLA Ops:
  0.0 5.0 %collective-permute-start.2 = (bf16[32,768]{1,0:T(8,128)(2,1)}, bf16[32,768]{1,0:T(8,128)(2,1)S(1)}, u32[]{:S(2)}, u32[]{:S(2)}) collective-permute-start(bf16[32,768]{1,0:T(8,128)(2,1)} %bitcast.15), channel_id=1, source_target_pairs={{0,12},{1,13},{2,14},{3,15},{4,8},{5,9},{6,10},{7,11},{8,4},{9,5},... | collective-permute-start | bytes 147464 | tf_op jit(solution)/shard_map/ppermute | solution.py:29
  5.0 0.0 collective-permute-start.1
  5.1 0.6 %collective-permute-start = (bf16[32,768]{1,0:T(8,128)(2,1)}, bf16[32,768]{1,0:T(8,128)(2,1)S(1)}, u32[]{:S(2)}, u32[]{:S(2)}) collective-permute-start(bf16[32,768]{1,0:T(8,128)(2,1)} %bitcast.17), channel_id=1, source_target_pairs={{0,4},{1,5},{2,6},{3,7},{4,0},{5,1},{6,2},{7,3},{8,12},{9,13},{10,... | collective-permute-start | bytes 147464 | tf_op jit(solution)/shard_map/ppermute | solution.py:29
  5.6 3.2 %shard_map.118 = (bf16[32,768]{1,0:T(8,128)(2,1)S(1)}, f32[16,1,768]{2,1,0:T(1,128)S(1)}, bf16[4,768,1152]{2,1,0:T(8,128)(2,1)S(1)}, s32[1,96]{1,0:T(1,128)S(1)}...) custom-call(s32[1]{0:T(128)} %bitcast.rest_0_.me_ref, bf16[32,768]{1,0:T(8,128)(2,1)} %bitcast.18, f32[16,1,768]{2,1,0:T(1,128)} %bitcast.24, ...), custom_call_target="tpu_custom_call" | custom-call | bytes 15000000 | tf_op jit(solution)/shard_map/pallas_call | solution.py:121
  8.9 1.4 %collective-permute-done.1 = bf16[32,768]{1,0:T(8,128)(2,1)S(1)} collective-permute-done((bf16[32,768]{1,0:T(8,128)(2,1)}, bf16[32,768]{1,0:T(8,128)(2,1)S(1)}, u32[]{:S(2)}, u32[]{:S(2)}) %collective-permute-start.1) | collective-permute-done | bytes 49184 | tf_op jit(solution)/shard_map/ppermute | solution.py:29
  10.3 1.6 %collective-permute-start.3 = (bf16[4,32,768]{2,1,0:T(8,128)(2,1)S(1)}, bf16[4,32,768]{2,1,0:T(8,128)(2,1)S(1)}, u32[]{:S(2)}, u32[]{:S(2)}) collective-permute-start(bf16[4,32,768]{2,1,0:T(8,128)(2,1)S(1)} %pad_maximum_fusion.rest_0_), channel_id=1, source_target_pairs={{0,2},{1,3},{2,0},{3,1},{4,6},{5,7},{6,4},{7,5},{8,10},{9,11},{10,... | collective-permute-start | bytes 589832 | tf_op jit(solution)/shard_map/ppermute | solution.py:29
  11.9 5.2 %shard_map.119 = (f32[32,768]{1,0:T(8,128)S(1)}, bf16[8,768,1152]{2,1,0:T(8,128)(2,1)S(1)}) custom-call(s32[1]{0:T(128)} %bitcast.rest_0_.me_ref, bf16[12288,1152]{1,0:T(8,128)(2,1)} %weight_ref.3, bf16[4,32,768]{2,1,0:T(8,128)(2,1)S(1)} %pad_maximum_fusion.rest_0_), custom_call_target="tpu_custom_call" | custom-call | bytes 16800000 | tf_op jit(solution)/shard_map/pallas_call | solution.py:170
  17.1 0.1 collective-permute-start.4
  18.5 0.1 shard_map.120
  18.6 0.3 collective-permute-done.4.other_ref
  18.9 4.7 %shard_map.121 = bf16[16,18,128]{2,1,0:T(8,128)(2,1)S(1)} custom-call(s32[1]{0:T(128)} %bitcast.rest_0_.me_ref, f32[16,1,768]{2,1,0:T(1,128)S(1)} %get-tuple-element.27.gain_ref, f32[32,768]{1,0:T(8,128)S(1)} %get-tuple-element.33.before_ref, bf16[8,32,768]{2,1,0:T(8,128)(2,1)S(1)} %constant_dynamic-update-slice_fusion.mine_ref, ...), custom_call_target="tpu_custom_call" | custom-call | bytes 18000000 | tf_op jit(solution)/shard_map/pallas_call | solution.py:292
  23.7 11.0 %all_to_all.5.received_ref = bf16[16,18,128]{2,1,0:T(8,128)(2,1)S(1)} all-to-all(bf16[16,18,128]{2,1,0:T(8,128)(2,1)S(1)} %shard_map.121), channel_id=1, replica_groups=mesh['groups'=2,'gx'=16] {'gx'}, dimensions={0} | all-to-all | bytes 147456 | tf_op jit(solution)/shard_map/all_to_all | solution.py:518
  34.7 1.1 %shard_map.122.block_ref = bf16[48,256]{1,0:T(8,128)(2,1)S(1)} custom-call(bf16[16,18,128]{2,1,0:T(8,128)(2,1)S(1)} %all_to_all.5.received_ref, f32[2,1,128]{2,1,0:T(1,128)S(1)} %get-tuple-element.36.cos_ref, f32[2,1,128]{2,1,0:T(1,128)S(1)} %get-tuple-element.37.sin_ref, f32[1,96]{1,0:T(1,128)S(1)} %get-tuple-element.38.allowed_ref, ...), custom_call_target="tpu_custom_call" | custom-call | bytes 30000000 | tf_op jit(solution)/shard_map/pallas_call | solution.py:399
  35.9 0.1 collective-permute-start.5
  35.9 2.3 %shard_map.123 = (bf16[48,256]{1,0:T(8,128)(2,1)S(1)}, bf16[3072,768]{1,0:T(8,128)(2,1)S(1)}) custom-call(bf16[48,256]{1,0:T(8,128)(2,1)S(1)} %shard_map.122.block_ref, bf16[6144,768]{1,0:T(8,128)(2,1)} %from_ref.3), custom_call_target="tpu_custom_call" | custom-call | bytes 6000000 | tf_op jit(solution)/shard_map/pallas_call | solution.py:457
  38.3 0.0 copy-start.3
  38.3 1.4 %collective-permute-done.5 = bf16[48,256]{1,0:T(8,128)(2,1)S(1)} collective-permute-done((bf16[48,256]{1,0:T(8,128)(2,1)S(1)}, bf16[48,256]{1,0:T(8,128)(2,1)S(1)}, u32[]{:S(2)}, u32[]{:S(2)}) %collective-permute-start.5) | collective-permute-done | bytes 24608 | tf_op jit(solution)/shard_map/ppermute | solution.py:29
  39.8 1.2 %collective-permute-start.7 = (bf16[2,48,256]{2,1,0:T(8,128)(2,1)S(1)}, bf16[2,48,256]{2,1,0:T(8,128)(2,1)S(1)}, u32[]{:S(2)}, u32[]{:S(2)}) collective-permute-start(bf16[2,48,256]{2,1,0:T(8,128)(2,1)S(1)} %pad_maximum_fusion.1.block_ref), channel_id=1, source_target_pairs={{0,8},{1,9},{2,10},{3,11},{4,12},{5,13},{6,14},{7,15},{8,0},{9,1},... | collective-permute-start | bytes 147464 | tf_op jit(solution)/shard_map/ppermute | solution.py:29
  41.0 3.2 %collective-permute-start.6 = (bf16[2,48,256]{2,1,0:T(8,128)(2,1)S(1)}, bf16[2,48,256]{2,1,0:T(8,128)(2,1)S(1)}, u32[]{:S(2)}, u32[]{:S(2)}) collective-permute-start(bf16[2,48,256]{2,1,0:T(8,128)(2,1)S(1)} %pad_maximum_fusion.1.block_ref), channel_id=1, source_target_pairs={{0,12},{1,13},{2,14},{3,15},{4,8},{5,9},{6,10},{7,11},{8,4},{9,5},... | collective-permute-start | bytes 147464 | tf_op jit(solution)/shard_map/ppermute | solution.py:29
  44.2 2.3 %shard_map.124 = (bf16[2,48,256]{2,1,0:T(8,128)(2,1)S(1)}, bf16[3072,768]{1,0:T(8,128)(2,1)S(1)}) custom-call(bf16[2,48,256]{2,1,0:T(8,128)(2,1)S(1)} %pad_maximum_fusion.1.block_ref, bf16[6144,768]{1,0:T(8,128)(2,1)} %from_ref.3), custom_call_target="tpu_custom_call" | custom-call | bytes 6000000 | tf_op jit(solution)/shard_map/pallas_call | solution.py:457
  46.5 0.3 collective-permute-done.6
  46.9 0.1 collective-permute-start.9
  47.0 1.4 %collective-permute-done.9.other_ref = bf16[8,48,256]{2,1,0:T(8,128)(2,1)S(1)} collective-permute-done((bf16[8,48,256]{2,1,0:T(8,128)(2,1)S(1)}, bf16[8,48,256]{2,1,0:T(8,128)(2,1)S(1)}, u32[]{:S(2)}, u32[]{:S(2)}) %collective-permute-start.9) | collective-permute-done | bytes 196640 | tf_op jit(solution)/shard_map/ppermute | solution.py:29
  48.4 2.4 %shard_map.125 = bf16[2,16,768]{2,1,0:T(8,128)(2,1)} custom-call(s32[1]{0:T(128)} %bitcast.rest_0_.me_ref, bf16[8,48,256]{2,1,0:T(8,128)(2,1)S(1)} %constant_dynamic-update-slice_fusion.5.mine_ref, bf16[8,48,256]{2,1,0:T(8,128)(2,1)S(1)} %collective-permute-done.9.other_ref, bf16[2,16,768]{2,1,0:T(8,128)(2,1)S(1)} %copy-done.3, ...), custom_call_target="tpu_custom_call" | custom-call | tf_op jit(solution)/shard_map/pallas_call | solution.py:484
  (24 shorter events, 0.1 us)
Async XLA Ops:
  0.0 8.8 %collective-permute-start.2 = (bf16[32,768]{1,0:T(8,128)(2,1)}, bf16[32,768]{1,0:T(8,128)(2,1)S(1)}, u32[]{:S(2)}, u32[]{:S(2)}) collective-permute-start(bf16[32,768]{1,0:T(8,128)(2,1)} %bitcast.15), channel_id=1, source_target_pairs={{0,12},{1,13},{2,14},{3,15},{4,8},{5,9},{6,10},{7,11},{8,4},{9,5},... | collective-permute-start | bytes 147464 | tf_op jit(solution)/shard_map/ppermute | solution.py:29
  5.0 5.2 %collective-permute-start.1 = (bf16[32,768]{1,0:T(8,128)(2,1)}, bf16[32,768]{1,0:T(8,128)(2,1)S(1)}, u32[]{:S(2)}, u32[]{:S(2)}) collective-permute-start(bf16[32,768]{1,0:T(8,128)(2,1)} %bitcast.16), channel_id=1, source_target_pairs={{0,8},{1,9},{2,10},{3,11},{4,12},{5,13},{6,14},{7,15},{8,0},{9,1},... | collective-permute-start | bytes 147464 | tf_op jit(solution)/shard_map/ppermute | solution.py:29
  5.1 5.2 %collective-permute-start = (bf16[32,768]{1,0:T(8,128)(2,1)}, bf16[32,768]{1,0:T(8,128)(2,1)S(1)}, u32[]{:S(2)}, u32[]{:S(2)}) collective-permute-start(bf16[32,768]{1,0:T(8,128)(2,1)} %bitcast.17), channel_id=1, source_target_pairs={{0,4},{1,5},{2,6},{3,7},{4,0},{5,1},{6,2},{7,3},{8,12},{9,13},{10,... | collective-permute-start | bytes 147464 | tf_op jit(solution)/shard_map/ppermute | solution.py:29
  10.3 6.8 %collective-permute-start.3 = (bf16[4,32,768]{2,1,0:T(8,128)(2,1)S(1)}, bf16[4,32,768]{2,1,0:T(8,128)(2,1)S(1)}, u32[]{:S(2)}, u32[]{:S(2)}) collective-permute-start(bf16[4,32,768]{2,1,0:T(8,128)(2,1)S(1)} %pad_maximum_fusion.rest_0_), channel_id=1, source_target_pairs={{0,2},{1,3},{2,0},{3,1},{4,6},{5,7},{6,4},{7,5},{8,10},{9,11},{10,... | collective-permute-start | bytes 589832 | tf_op jit(solution)/shard_map/ppermute | solution.py:29
  17.1 1.8 %collective-permute-start.4 = (bf16[8,32,768]{2,1,0:T(8,128)(2,1)S(1)}, bf16[8,32,768]{2,1,0:T(8,128)(2,1)S(1)}, u32[]{:S(2)}, u32[]{:S(2)}) collective-permute-start(bf16[8,32,768]{2,1,0:T(8,128)(2,1)S(1)} %constant_dynamic-update-slice_fusion.mine_ref), channel_id=1, source_target_pairs={{0,1},{1,0},{2,3},{3,2},{4,5},{5,4},{6,7},{7,6},{8,9},{9,8},{10,11... | collective-permute-start | bytes 1179656 | tf_op jit(solution)/shard_map/ppermute | solution.py:29
  18.9 15.8 %copy-start = (bf16[6,16,6144]{2,1,0:T(8,128)(2,1)S(1)}, bf16[6,16,6144]{2,1,0:T(8,128)(2,1)}, u32[]{:S(2)}) copy-start(bf16[6,16,6144]{2,1,0:T(8,128)(2,1)} %values_ref.1) | copy-start | bytes 3538948
  18.9 15.8 %copy-start.1 = (bf16[6,16,3072]{2,1,0:T(8,128)(2,1)S(1)}, bf16[6,16,3072]{2,1,0:T(8,128)(2,1)}, u32[]{:S(2)}) copy-start(bf16[6,16,3072]{2,1,0:T(8,128)(2,1)} %keys_one_ref.1) | copy-start | bytes 1769476
  18.9 15.8 %copy-start.2 = (bf16[6,16,3072]{2,1,0:T(8,128)(2,1)S(1)}, bf16[6,16,3072]{2,1,0:T(8,128)(2,1)}, u32[]{:S(2)}) copy-start(bf16[6,16,3072]{2,1,0:T(8,128)(2,1)} %keys_two_ref.1) | copy-start | bytes 1769476
  35.9 3.9 %collective-permute-start.5 = (bf16[48,256]{1,0:T(8,128)(2,1)S(1)}, bf16[48,256]{1,0:T(8,128)(2,1)S(1)}, u32[]{:S(2)}, u32[]{:S(2)}) collective-permute-start(bf16[48,256]{1,0:T(8,128)(2,1)S(1)} %shard_map.122.block_ref), channel_id=1, source_target_pairs={{0,2},{1,3},{2,0},{3,1},{4,6},{5,7},{6,4},{7,5},{8,10},{9,11},{10,... | collective-permute-start | bytes 73736 | tf_op jit(solution)/shard_map/ppermute | solution.py:29
  38.3 10.1 %copy-start.3 = (bf16[2,16,768]{2,1,0:T(8,128)(2,1)S(1)}, bf16[2,16,768]{2,1,0:T(8,128)(2,1)}, u32[]{:S(2)}) copy-start(bf16[2,16,768]{2,1,0:T(8,128)(2,1)} %inputs_ref.1) | copy-start | bytes 147460
  39.8 6.7 %collective-permute-start.8 = (bf16[2,48,256]{2,1,0:T(8,128)(2,1)S(1)}, bf16[2,48,256]{2,1,0:T(8,128)(2,1)S(1)}, u32[]{:S(2)}, u32[]{:S(2)}) collective-permute-start(bf16[2,48,256]{2,1,0:T(8,128)(2,1)S(1)} %pad_maximum_fusion.1.block_ref), channel_id=1, source_target_pairs={{0,4},{1,5},{2,6},{3,7},{4,0},{5,1},{6,2},{7,3},{8,12},{9,13},{10,... | collective-permute-start | bytes 147464 | tf_op jit(solution)/shard_map/ppermute | solution.py:29
  39.8 6.7 %collective-permute-start.7 = (bf16[2,48,256]{2,1,0:T(8,128)(2,1)S(1)}, bf16[2,48,256]{2,1,0:T(8,128)(2,1)S(1)}, u32[]{:S(2)}, u32[]{:S(2)}) collective-permute-start(bf16[2,48,256]{2,1,0:T(8,128)(2,1)S(1)} %pad_maximum_fusion.1.block_ref), channel_id=1, source_target_pairs={{0,8},{1,9},{2,10},{3,11},{4,12},{5,13},{6,14},{7,15},{8,0},{9,1},... | collective-permute-start | bytes 147464 | tf_op jit(solution)/shard_map/ppermute | solution.py:29
  41.0 5.9 %collective-permute-start.6 = (bf16[2,48,256]{2,1,0:T(8,128)(2,1)S(1)}, bf16[2,48,256]{2,1,0:T(8,128)(2,1)S(1)}, u32[]{:S(2)}, u32[]{:S(2)}) collective-permute-start(bf16[2,48,256]{2,1,0:T(8,128)(2,1)S(1)} %pad_maximum_fusion.1.block_ref), channel_id=1, source_target_pairs={{0,12},{1,13},{2,14},{3,15},{4,8},{5,9},{6,10},{7,11},{8,4},{9,5},... | collective-permute-start | bytes 147464 | tf_op jit(solution)/shard_map/ppermute | solution.py:29
  46.9 1.5 %collective-permute-start.9 = (bf16[8,48,256]{2,1,0:T(8,128)(2,1)S(1)}, bf16[8,48,256]{2,1,0:T(8,128)(2,1)S(1)}, u32[]{:S(2)}, u32[]{:S(2)}) collective-permute-start(bf16[8,48,256]{2,1,0:T(8,128)(2,1)S(1)} %constant_dynamic-update-slice_fusion.5.mine_ref), channel_id=1, source_target_pairs={{0,1},{1,0},{2,3},{3,2},{4,5},{5,4},{6,7},{7,6},{8,9},{9,8},{10,11... | collective-permute-start | bytes 589832 | tf_op jit(solution)/shard_map/ppermute | solution.py:29

commit v17 on v15

--- a/solution.py
+++ b/solution.py
@@ -274,7 +274,7 @@
     pieces = rows // n * (columns // 128)
     outer, middle = radices(n)
     order = slots(n)
-    first, second = n // 4, 3 * n // 4
+    first, second = 5 * n // 16, 3 * n // 4
 
     arrived = [swap(block, n, o * 2 * middle) for o in range(1, outer)]
     held, gain, weight_a, place, weights, head_gain = fetch(

time: 50.7 us -> 51.2 us (level)
  blocking collectives: 11 us -> 12.1 us
    all_to_all x1, blocking collectives: 11 us -> 12.1 us  [local(): received = lax.all_to_all(sent, 'gx', 0, 0)]
    pallas_call x1, Pallas kernels: 3.21 us -> 3.72 us  [fetch(): pl.pallas_call(functools.partial(fetch_kernel, n, order), out_shape=(pltp...]
    pallas_call x1, Pallas kernels: 5.16 us -> 4.65 us  [squares_beside(): pl.pallas_call(functools.partial(squares_kernel, n, order, len(blocks)),...]
where the time goes in v17:
time: 51.2 us; the launch traced here: 51 us
  Pallas kernels  21.4 us (42%)
  blocking collectives  12.1 us (24%)
  starting transfers between devices  11.8 us (23%)
  waiting for transfers between devices  4.1 us (8%)
  between operations  1.51 us (3%)
    all_to_all x1, blocking collectives, local(): received = lax.all_to_all(sent, 'gx', 0, 0)  12.1 us
    ppermute x10, starting transfers between devices, swap(): return lax.ppermute(block, 'gx', [(i, i ^ mask) for i in range(n)])  11.8 us
    pallas_call x1, Pallas kernels, project(): pl.pallas_call(functools.partial(project_kernel, n, order[second:]), out_...  4.75 us
    pallas_call x2, Pallas kernels, keep(): pl.pallas_call(functools.partial(keep_kernel, half), out_shape=(jax.Shape...  4.69 us
    pallas_call x1, Pallas kernels, squares_beside(): pl.pallas_call(functools.partial(squares_kernel, n, order, len(blocks)),...  4.65 us
    ppermute x10, waiting for transfers between devices, swap(): return lax.ppermute(block, 'gx', [(i, i ^ mask) for i in range(n)])  4.1 us
    pallas_call x1, Pallas kernels, fetch(): pl.pallas_call(functools.partial(fetch_kernel, n, order), out_shape=(pltp...  3.72 us
    pallas_call x1, Pallas kernels, output(): pl.pallas_call(functools.partial(output_kernel, n), out_shape=jax.ShapeDt...  2.37 us
  transfers between devices with their start and end apart: 10, of which 4 were waited for; matrix products, arithmetic and copies ran while one was open for 0% of the time, Pallas kernels for 26%

profile of v17, /device:TPU:0, one launch (start us, length us, event | category | flops | bytes accessed | tf_op | source)
XLA Modules:
  0.0 51.0 jit_solution(10942488459250864196)
XLA Ops:
  0.0 5.0 %collective-permute-start.2 = (bf16[32,768]{1,0:T(8,128)(2,1)}, bf16[32,768]{1,0:T(8,128)(2,1)S(1)}, u32[]{:S(2)}, u32[]{:S(2)}) collective-permute-start(bf16[32,768]{1,0:T(8,128)(2,1)} %bitcast.15), channel_id=1, source_target_pairs={{0,12},{1,13},{2,14},{3,15},{4,8},{5,9},{6,10},{7,11},{8,4},{9,5},... | collective-permute-start | bytes 147464 | tf_op jit(solution)/shard_map/ppermute | solution.py:29
  5.0 0.0 collective-permute-start.1
  5.1 0.6 %collective-permute-start = (bf16[32,768]{1,0:T(8,128)(2,1)}, bf16[32,768]{1,0:T(8,128)(2,1)S(1)}, u32[]{:S(2)}, u32[]{:S(2)}) collective-permute-start(bf16[32,768]{1,0:T(8,128)(2,1)} %bitcast.17), channel_id=1, source_target_pairs={{0,4},{1,5},{2,6},{3,7},{4,0},{5,1},{6,2},{7,3},{8,12},{9,13},{10,... | collective-permute-start | bytes 147464 | tf_op jit(solution)/shard_map/ppermute | solution.py:29
  5.6 3.7 %shard_map.118 = (bf16[32,768]{1,0:T(8,128)(2,1)S(1)}, f32[16,1,768]{2,1,0:T(1,128)S(1)}, bf16[5,768,1152]{2,1,0:T(8,128)(2,1)S(1)}, s32[1,96]{1,0:T(1,128)S(1)}...) custom-call(s32[1]{0:T(128)} %bitcast.rest_0_.me_ref, bf16[32,768]{1,0:T(8,128)(2,1)} %bitcast.18, f32[16,1,768]{2,1,0:T(1,128)} %bitcast.24, ...), custom_call_target="tpu_custom_call" | custom-call | bytes 15000000 | tf_op jit(solution)/shard_map/pallas_call | solution.py:121
  9.4 0.9 %collective-permute-done.1 = bf16[32,768]{1,0:T(8,128)(2,1)S(1)} collective-permute-done((bf16[32,768]{1,0:T(8,128)(2,1)}, bf16[32,768]{1,0:T(8,128)(2,1)S(1)}, u32[]{:S(2)}, u32[]{:S(2)}) %collective-permute-start.1) | collective-permute-done | bytes 49184 | tf_op jit(solution)/shard_map/ppermute | solution.py:29
  10.3 1.6 %collective-permute-start.3 = (bf16[4,32,768]{2,1,0:T(8,128)(2,1)S(1)}, bf16[4,32,768]{2,1,0:T(8,128)(2,1)S(1)}, u32[]{:S(2)}, u32[]{:S(2)}) collective-permute-start(bf16[4,32,768]{2,1,0:T(8,128)(2,1)S(1)} %pad_maximum_fusion.rest_0_), channel_id=1, source_target_pairs={{0,2},{1,3},{2,0},{3,1},{4,6},{5,7},{6,4},{7,5},{8,10},{9,11},{10,... | collective-permute-start | bytes 589832 | tf_op jit(solution)/shard_map/ppermute | solution.py:29
  11.9 4.6 %shard_map.119 = (f32[32,768]{1,0:T(8,128)S(1)}, bf16[7,768,1152]{2,1,0:T(8,128)(2,1)S(1)}) custom-call(s32[1]{0:T(128)} %bitcast.rest_0_.me_ref, bf16[12288,1152]{1,0:T(8,128)(2,1)} %weight_ref.3, bf16[4,32,768]{2,1,0:T(8,128)(2,1)S(1)} %pad_maximum_fusion.rest_0_), custom_call_target="tpu_custom_call" | custom-call | bytes 14699999 | tf_op jit(solution)/shard_map/pallas_call | solution.py:170
  16.6 0.1 collective-permute-start.4
  18.0 0.1 shard_map.120
  18.1 0.3 collective-permute-done.4.other_ref
  18.4 4.7 %shard_map.121 = bf16[16,18,128]{2,1,0:T(8,128)(2,1)S(1)} custom-call(s32[1]{0:T(128)} %bitcast.rest_0_.me_ref, f32[16,1,768]{2,1,0:T(1,128)S(1)} %get-tuple-element.27.gain_ref, f32[32,768]{1,0:T(8,128)S(1)} %get-tuple-element.33.before_ref, bf16[8,32,768]{2,1,0:T(8,128)(2,1)S(1)} %constant_dynamic-update-slice_fusion.mine_ref, ...), custom_call_target="tpu_custom_call" | custom-call | bytes 18000000 | tf_op jit(solution)/shard_map/pallas_call | solution.py:292
  23.2 12.1 %all_to_all.5.received_ref = bf16[16,18,128]{2,1,0:T(8,128)(2,1)S(1)} all-to-all(bf16[16,18,128]{2,1,0:T(8,128)(2,1)S(1)} %shard_map.121), channel_id=1, replica_groups=mesh['groups'=2,'gx'=16] {'gx'}, dimensions={0} | all-to-all | bytes 147456 | tf_op jit(solution)/shard_map/all_to_all | solution.py:516
  35.2 1.1 %shard_map.122.block_ref = bf16[48,256]{1,0:T(8,128)(2,1)S(1)} custom-call(bf16[16,18,128]{2,1,0:T(8,128)(2,1)S(1)} %all_to_all.5.received_ref, f32[2,1,128]{2,1,0:T(1,128)S(1)} %get-tuple-element.36.cos_ref, f32[2,1,128]{2,1,0:T(1,128)S(1)} %get-tuple-element.37.sin_ref, f32[1,96]{1,0:T(1,128)S(1)} %get-tuple-element.38.allowed_ref, ...), custom_call_target="tpu_custom_call" | custom-call | bytes 30000000 | tf_op jit(solution)/shard_map/pallas_call | solution.py:399
  36.4 0.0 copy-start.3
  36.4 0.1 collective-permute-start.5
  36.5 2.3 %shard_map.123 = (bf16[48,256]{1,0:T(8,128)(2,1)S(1)}, bf16[3072,768]{1,0:T(8,128)(2,1)S(1)}) custom-call(bf16[48,256]{1,0:T(8,128)(2,1)S(1)} %shard_map.122.block_ref, bf16[6144,768]{1,0:T(8,128)(2,1)} %from_ref.3), custom_call_target="tpu_custom_call" | custom-call | bytes 6000000 | tf_op jit(solution)/shard_map/pallas_call | solution.py:455
  38.8 1.5 %collective-permute-done.5 = bf16[48,256]{1,0:T(8,128)(2,1)S(1)} collective-permute-done((bf16[48,256]{1,0:T(8,128)(2,1)S(1)}, bf16[48,256]{1,0:T(8,128)(2,1)S(1)}, u32[]{:S(2)}, u32[]{:S(2)}) %collective-permute-start.5) | collective-permute-done | bytes 24608 | tf_op jit(solution)/shard_map/ppermute | solution.py:29
  40.3 0.6 %collective-permute-start.8 = (bf16[2,48,256]{2,1,0:T(8,128)(2,1)S(1)}, bf16[2,48,256]{2,1,0:T(8,128)(2,1)S(1)}, u32[]{:S(2)}, u32[]{:S(2)}) collective-permute-start(bf16[2,48,256]{2,1,0:T(8,128)(2,1)S(1)} %pad_maximum_fusion.1.block_ref), channel_id=1, source_target_pairs={{0,12},{1,13},{2,14},{3,15},{4,8},{5,9},{6,10},{7,11},{8,4},{9,5},... | collective-permute-start | bytes 147464 | tf_op jit(solution)/shard_map/ppermute | solution.py:29
  40.9 0.6 %collective-permute-start.7 = (bf16[2,48,256]{2,1,0:T(8,128)(2,1)S(1)}, bf16[2,48,256]{2,1,0:T(8,128)(2,1)S(1)}, u32[]{:S(2)}, u32[]{:S(2)}) collective-permute-start(bf16[2,48,256]{2,1,0:T(8,128)(2,1)S(1)} %pad_maximum_fusion.1.block_ref), channel_id=1, source_target_pairs={{0,8},{1,9},{2,10},{3,11},{4,12},{5,13},{6,14},{7,15},{8,0},{9,1},... | collective-permute-start | bytes 147464 | tf_op jit(solution)/shard_map/ppermute | solution.py:29
  41.5 3.2 %collective-permute-start.6 = (bf16[2,48,256]{2,1,0:T(8,128)(2,1)S(1)}, bf16[2,48,256]{2,1,0:T(8,128)(2,1)S(1)}, u32[]{:S(2)}, u32[]{:S(2)}) collective-permute-start(bf16[2,48,256]{2,1,0:T(8,128)(2,1)S(1)} %pad_maximum_fusion.1.block_ref), channel_id=1, source_target_pairs={{0,4},{1,5},{2,6},{3,7},{4,0},{5,1},{6,2},{7,3},{8,12},{9,13},{10,... | collective-permute-start | bytes 147464 | tf_op jit(solution)/shard_map/ppermute | solution.py:29
  44.7 2.3 %shard_map.124 = (bf16[2,48,256]{2,1,0:T(8,128)(2,1)S(1)}, bf16[3072,768]{1,0:T(8,128)(2,1)S(1)}) custom-call(bf16[2,48,256]{2,1,0:T(8,128)(2,1)S(1)} %pad_maximum_fusion.1.block_ref, bf16[6144,768]{1,0:T(8,128)(2,1)} %from_ref.3), custom_call_target="tpu_custom_call" | custom-call | bytes 6000000 | tf_op jit(solution)/shard_map/pallas_call | solution.py:455
  47.1 0.1 collective-permute-start.9
  47.2 1.4 %collective-permute-done.9.other_ref = bf16[8,48,256]{2,1,0:T(8,128)(2,1)S(1)} collective-permute-done((bf16[8,48,256]{2,1,0:T(8,128)(2,1)S(1)}, bf16[8,48,256]{2,1,0:T(8,128)(2,1)S(1)}, u32[]{:S(2)}, u32[]{:S(2)}) %collective-permute-start.9) | collective-permute-done | bytes 196640 | tf_op jit(solution)/shard_map/ppermute | solution.py:29
  48.6 2.4 %shard_map.125 = bf16[2,16,768]{2,1,0:T(8,128)(2,1)} custom-call(s32[1]{0:T(128)} %bitcast.rest_0_.me_ref, bf16[8,48,256]{2,1,0:T(8,128)(2,1)S(1)} %constant_dynamic-update-slice_fusion.5.mine_ref, bf16[8,48,256]{2,1,0:T(8,128)(2,1)S(1)} %collective-permute-done.9.other_ref, bf16[2,16,768]{2,1,0:T(8,128)(2,1)S(1)} %copy-done.3, ...), custom_call_target="tpu_custom_call" | custom-call | tf_op jit(solution)/shard_map/pallas_call | solution.py:482
  (24 shorter events, 0.1 us)
Async XLA Ops:
  0.0 9.4 %collective-permute-start.2 = (bf16[32,768]{1,0:T(8,128)(2,1)}, bf16[32,768]{1,0:T(8,128)(2,1)S(1)}, u32[]{:S(2)}, u32[]{:S(2)}) collective-permute-start(bf16[32,768]{1,0:T(8,128)(2,1)} %bitcast.15), channel_id=1, source_target_pairs={{0,12},{1,13},{2,14},{3,15},{4,8},{5,9},{6,10},{7,11},{8,4},{9,5},... | collective-permute-start | bytes 147464 | tf_op jit(solution)/shard_map/ppermute | solution.py:29
  5.0 5.2 %collective-permute-start.1 = (bf16[32,768]{1,0:T(8,128)(2,1)}, bf16[32,768]{1,0:T(8,128)(2,1)S(1)}, u32[]{:S(2)}, u32[]{:S(2)}) collective-permute-start(bf16[32,768]{1,0:T(8,128)(2,1)} %bitcast.16), channel_id=1, source_target_pairs={{0,8},{1,9},{2,10},{3,11},{4,12},{5,13},{6,14},{7,15},{8,0},{9,1},... | collective-permute-start | bytes 147464 | tf_op jit(solution)/shard_map/ppermute | solution.py:29
  5.1 5.2 %collective-permute-start = (bf16[32,768]{1,0:T(8,128)(2,1)}, bf16[32,768]{1,0:T(8,128)(2,1)S(1)}, u32[]{:S(2)}, u32[]{:S(2)}) collective-permute-start(bf16[32,768]{1,0:T(8,128)(2,1)} %bitcast.17), channel_id=1, source_target_pairs={{0,4},{1,5},{2,6},{3,7},{4,0},{5,1},{6,2},{7,3},{8,12},{9,13},{10,... | collective-permute-start | bytes 147464 | tf_op jit(solution)/shard_map/ppermute | solution.py:29
  10.3 6.3 %collective-permute-start.3 = (bf16[4,32,768]{2,1,0:T(8,128)(2,1)S(1)}, bf16[4,32,768]{2,1,0:T(8,128)(2,1)S(1)}, u32[]{:S(2)}, u32[]{:S(2)}) collective-permute-start(bf16[4,32,768]{2,1,0:T(8,128)(2,1)S(1)} %pad_maximum_fusion.rest_0_), channel_id=1, source_target_pairs={{0,2},{1,3},{2,0},{3,1},{4,6},{5,7},{6,4},{7,5},{8,10},{9,11},{10,... | collective-permute-start | bytes 589832 | tf_op jit(solution)/shard_map/ppermute | solution.py:29
  16.6 1.8 %collective-permute-start.4 = (bf16[8,32,768]{2,1,0:T(8,128)(2,1)S(1)}, bf16[8,32,768]{2,1,0:T(8,128)(2,1)S(1)}, u32[]{:S(2)}, u32[]{:S(2)}) collective-permute-start(bf16[8,32,768]{2,1,0:T(8,128)(2,1)S(1)} %constant_dynamic-update-slice_fusion.mine_ref), channel_id=1, source_target_pairs={{0,1},{1,0},{2,3},{3,2},{4,5},{5,4},{6,7},{7,6},{8,9},{9,8},{10,11... | collective-permute-start | bytes 1179656 | tf_op jit(solution)/shard_map/ppermute | solution.py:29
  18.4 16.8 %copy-start = (bf16[6,16,6144]{2,1,0:T(8,128)(2,1)S(1)}, bf16[6,16,6144]{2,1,0:T(8,128)(2,1)}, u32[]{:S(2)}) copy-start(bf16[6,16,6144]{2,1,0:T(8,128)(2,1)} %values_ref.1) | copy-start | bytes 3538948
  18.4 16.8 %copy-start.1 = (bf16[6,16,3072]{2,1,0:T(8,128)(2,1)S(1)}, bf16[6,16,3072]{2,1,0:T(8,128)(2,1)}, u32[]{:S(2)}) copy-start(bf16[6,16,3072]{2,1,0:T(8,128)(2,1)} %keys_one_ref.1) | copy-start | bytes 1769476
  18.4 16.8 %copy-start.2 = (bf16[6,16,3072]{2,1,0:T(8,128)(2,1)S(1)}, bf16[6,16,3072]{2,1,0:T(8,128)(2,1)}, u32[]{:S(2)}) copy-start(bf16[6,16,3072]{2,1,0:T(8,128)(2,1)} %keys_two_ref.1) | copy-start | bytes 1769476
  36.4 12.2 %copy-start.3 = (bf16[2,16,768]{2,1,0:T(8,128)(2,1)S(1)}, bf16[2,16,768]{2,1,0:T(8,128)(2,1)}, u32[]{:S(2)}) copy-start(bf16[2,16,768]{2,1,0:T(8,128)(2,1)} %inputs_ref.1) | copy-start | bytes 147460
  36.4 3.9 %collective-permute-start.5 = (bf16[48,256]{1,0:T(8,128)(2,1)S(1)}, bf16[48,256]{1,0:T(8,128)(2,1)S(1)}, u32[]{:S(2)}, u32[]{:S(2)}) collective-permute-start(bf16[48,256]{1,0:T(8,128)(2,1)S(1)} %shard_map.122.block_ref), channel_id=1, source_target_pairs={{0,2},{1,3},{2,0},{3,1},{4,6},{5,7},{6,4},{7,5},{8,10},{9,11},{10,... | collective-permute-start | bytes 73736 | tf_op jit(solution)/shard_map/ppermute | solution.py:29
  40.3 6.7 %collective-permute-start.8 = (bf16[2,48,256]{2,1,0:T(8,128)(2,1)S(1)}, bf16[2,48,256]{2,1,0:T(8,128)(2,1)S(1)}, u32[]{:S(2)}, u32[]{:S(2)}) collective-permute-start(bf16[2,48,256]{2,1,0:T(8,128)(2,1)S(1)} %pad_maximum_fusion.1.block_ref), channel_id=1, source_target_pairs={{0,12},{1,13},{2,14},{3,15},{4,8},{5,9},{6,10},{7,11},{8,4},{9,5},... | collective-permute-start | bytes 147464 | tf_op jit(solution)/shard_map/ppermute | solution.py:29
  40.9 6.1 %collective-permute-start.7 = (bf16[2,48,256]{2,1,0:T(8,128)(2,1)S(1)}, bf16[2,48,256]{2,1,0:T(8,128)(2,1)S(1)}, u32[]{:S(2)}, u32[]{:S(2)}) collective-permute-start(bf16[2,48,256]{2,1,0:T(8,128)(2,1)S(1)} %pad_maximum_fusion.1.block_ref), channel_id=1, source_target_pairs={{0,8},{1,9},{2,10},{3,11},{4,12},{5,13},{6,14},{7,15},{8,0},{9,1},... | collective-permute-start | bytes 147464 | tf_op jit(solution)/shard_map/ppermute | solution.py:29
  41.5 5.5 %collective-permute-start.6 = (bf16[2,48,256]{2,1,0:T(8,128)(2,1)S(1)}, bf16[2,48,256]{2,1,0:T(8,128)(2,1)S(1)}, u32[]{:S(2)}, u32[]{:S(2)}) collective-permute-start(bf16[2,48,256]{2,1,0:T(8,128)(2,1)S(1)} %pad_maximum_fusion.1.block_ref), channel_id=1, source_target_pairs={{0,4},{1,5},{2,6},{3,7},{4,0},{5,1},{6,2},{7,3},{8,12},{9,13},{10,... | collective-permute-start | bytes 147464 | tf_op jit(solution)/shard_map/ppermute | solution.py:29
  47.1 1.5 %collective-permute-start.9 = (bf16[8,48,256]{2,1,0:T(8,128)(2,1)S(1)}, bf16[8,48,256]{2,1,0:T(8,128)(2,1)S(1)}, u32[]{:S(2)}, u32[]{:S(2)}) collective-permute-start(bf16[8,48,256]{2,1,0:T(8,128)(2,1)S(1)} %constant_dynamic-update-slice_fusion.5.mine_ref), channel_id=1, source_target_pairs={{0,1},{1,0},{2,3},{3,2},{4,5},{5,4},{6,7},{7,6},{8,9},{9,8},{10,11... | collective-permute-start | bytes 589832 | tf_op jit(solution)/shard_map/ppermute | solution.py:29

commit v18 on v15

--- a/solution.py
+++ b/solution.py
@@ -253,10 +253,13 @@
         total[...] = products(blocks[:early], factor)
         kept[...] = jnp.broadcast_to(factor, kept.shape)
 
-    for copy in copies:
-        copy.wait()
     factor = kept[:, :1]
-    summed = total[...] + products(blocks[early:], factor)
+    summed = total[...]
+    half = -(-len(copies) // 2)
+    for group in (slice(0, half), slice(half, len(copies))):
+        for copy in copies[group]:
+            copy.wait()
+        summed = summed + products(blocks[early:][group], factor)
     columns = summed.shape[1] // 128
     steps = rows // n
     for block in range(columns):

time: 50.7 us -> 50.8 us (level)
  no operation moved by 1% of the time
where the time goes in v18:
time: 50.8 us; the launch traced here: 50.6 us
  Pallas kernels  21.5 us (42%)
  starting transfers between devices  11.8 us (23%)
  blocking collectives  11 us (22%)
  waiting for transfers between devices  4.61 us (9%)
  between operations  1.51 us (3%)
    ppermute x10, starting transfers between devices, swap(): return lax.ppermute(block, 'gx', [(i, i ^ mask) for i in range(n)])  11.8 us
    all_to_all x1, blocking collectives, local(): received = lax.all_to_all(sent, 'gx', 0, 0)  11 us
    pallas_call x1, Pallas kernels, squares_beside(): pl.pallas_call(functools.partial(squares_kernel, n, order, len(blocks)),...  5.16 us
    pallas_call x1, Pallas kernels, project(): pl.pallas_call(functools.partial(project_kernel, n, order[second:]), out_...  4.87 us
    pallas_call x2, Pallas kernels, keep(): pl.pallas_call(functools.partial(keep_kernel, half), out_shape=(jax.Shape...  4.69 us
    ppermute x10, waiting for transfers between devices, swap(): return lax.ppermute(block, 'gx', [(i, i ^ mask) for i in range(n)])  4.61 us
    pallas_call x1, Pallas kernels, fetch(): pl.pallas_call(functools.partial(fetch_kernel, n, order), out_shape=(pltp...  3.21 us
    pallas_call x1, Pallas kernels, output(): pl.pallas_call(functools.partial(output_kernel, n), out_shape=jax.ShapeDt...  2.37 us
  transfers between devices with their start and end apart: 10, of which 4 were waited for; matrix products, arithmetic and copies ran while one was open for 0% of the time, Pallas kernels for 26%

profile of v18, /device:TPU:0, one launch (start us, length us, event | category | flops | bytes accessed | tf_op | source)
XLA Modules:
  0.0 50.6 jit_solution(2830645203211965446)
XLA Ops:
  0.0 5.0 %collective-permute-start.2 = (bf16[32,768]{1,0:T(8,128)(2,1)}, bf16[32,768]{1,0:T(8,128)(2,1)S(1)}, u32[]{:S(2)}, u32[]{:S(2)}) collective-permute-start(bf16[32,768]{1,0:T(8,128)(2,1)} %bitcast.15), channel_id=1, source_target_pairs={{0,12},{1,13},{2,14},{3,15},{4,8},{5,9},{6,10},{7,11},{8,4},{9,5},... | collective-permute-start | bytes 147464 | tf_op jit(solution)/shard_map/ppermute | solution.py:29
  5.1 0.6 %collective-permute-start = (bf16[32,768]{1,0:T(8,128)(2,1)}, bf16[32,768]{1,0:T(8,128)(2,1)S(1)}, u32[]{:S(2)}, u32[]{:S(2)}) collective-permute-start(bf16[32,768]{1,0:T(8,128)(2,1)} %bitcast.17), channel_id=1, source_target_pairs={{0,4},{1,5},{2,6},{3,7},{4,0},{5,1},{6,2},{7,3},{8,12},{9,13},{10,... | collective-permute-start | bytes 147464 | tf_op jit(solution)/shard_map/ppermute | solution.py:29
  5.6 3.2 %shard_map.118 = (bf16[32,768]{1,0:T(8,128)(2,1)S(1)}, f32[16,1,768]{2,1,0:T(1,128)S(1)}, bf16[4,768,1152]{2,1,0:T(8,128)(2,1)S(1)}, s32[1,96]{1,0:T(1,128)S(1)}...) custom-call(s32[1]{0:T(128)} %bitcast.rest_0_.me_ref, bf16[32,768]{1,0:T(8,128)(2,1)} %bitcast.18, f32[16,1,768]{2,1,0:T(1,128)} %bitcast.24, ...), custom_call_target="tpu_custom_call" | custom-call | bytes 15000000 | tf_op jit(solution)/shard_map/pallas_call | solution.py:121
  8.9 1.4 %collective-permute-done.1 = bf16[32,768]{1,0:T(8,128)(2,1)S(1)} collective-permute-done((bf16[32,768]{1,0:T(8,128)(2,1)}, bf16[32,768]{1,0:T(8,128)(2,1)S(1)}, u32[]{:S(2)}, u32[]{:S(2)}) %collective-permute-start.1) | collective-permute-done | bytes 49184 | tf_op jit(solution)/shard_map/ppermute | solution.py:29
  10.3 1.6 %collective-permute-start.3 = (bf16[4,32,768]{2,1,0:T(8,128)(2,1)S(1)}, bf16[4,32,768]{2,1,0:T(8,128)(2,1)S(1)}, u32[]{:S(2)}, u32[]{:S(2)}) collective-permute-start(bf16[4,32,768]{2,1,0:T(8,128)(2,1)S(1)} %pad_maximum_fusion.rest_0_), channel_id=1, source_target_pairs={{0,2},{1,3},{2,0},{3,1},{4,6},{5,7},{6,4},{7,5},{8,10},{9,11},{10,... | collective-permute-start | bytes 589832 | tf_op jit(solution)/shard_map/ppermute | solution.py:29
  11.9 5.2 %shard_map.119 = (f32[32,768]{1,0:T(8,128)S(1)}, bf16[8,768,1152]{2,1,0:T(8,128)(2,1)S(1)}) custom-call(s32[1]{0:T(128)} %bitcast.rest_0_.me_ref, bf16[12288,1152]{1,0:T(8,128)(2,1)} %weight_ref.3, bf16[4,32,768]{2,1,0:T(8,128)(2,1)S(1)} %pad_maximum_fusion.rest_0_), custom_call_target="tpu_custom_call" | custom-call | bytes 16800000 | tf_op jit(solution)/shard_map/pallas_call | solution.py:170
  17.1 0.0 collective-permute-done.3.rest_0_
  17.1 0.1 collective-permute-start.4
  18.5 0.1 shard_map.120
  18.6 0.3 collective-permute-done.4.other_ref
  18.9 4.9 %shard_map.121 = bf16[16,18,128]{2,1,0:T(8,128)(2,1)S(1)} custom-call(s32[1]{0:T(128)} %bitcast.rest_0_.me_ref, f32[16,1,768]{2,1,0:T(1,128)S(1)} %get-tuple-element.27.gain_ref, f32[32,768]{1,0:T(8,128)S(1)} %get-tuple-element.33.before_ref, bf16[8,32,768]{2,1,0:T(8,128)(2,1)S(1)} %constant_dynamic-update-slice_fusion.mine_ref, ...), custom_call_target="tpu_custom_call" | custom-call | bytes 18000000 | tf_op jit(solution)/shard_map/pallas_call | solution.py:295
  23.8 11.0 %all_to_all.5.received_ref = bf16[16,18,128]{2,1,0:T(8,128)(2,1)S(1)} all-to-all(bf16[16,18,128]{2,1,0:T(8,128)(2,1)S(1)} %shard_map.121), channel_id=1, replica_groups=mesh['groups'=2,'gx'=16] {'gx'}, dimensions={0} | all-to-all | bytes 147456 | tf_op jit(solution)/shard_map/all_to_all | solution.py:519
  34.8 1.1 %shard_map.122.block_ref = bf16[48,256]{1,0:T(8,128)(2,1)S(1)} custom-call(bf16[16,18,128]{2,1,0:T(8,128)(2,1)S(1)} %all_to_all.5.received_ref, f32[2,1,128]{2,1,0:T(1,128)S(1)} %get-tuple-element.36.cos_ref, f32[2,1,128]{2,1,0:T(1,128)S(1)} %get-tuple-element.37.sin_ref, f32[1,96]{1,0:T(1,128)S(1)} %get-tuple-element.38.allowed_ref, ...), custom_call_target="tpu_custom_call" | custom-call | bytes 30000000 | tf_op jit(solution)/shard_map/pallas_call | solution.py:402
  36.0 0.1 collective-permute-start.5
  36.1 2.3 %shard_map.123 = (bf16[48,256]{1,0:T(8,128)(2,1)S(1)}, bf16[3072,768]{1,0:T(8,128)(2,1)S(1)}) custom-call(bf16[48,256]{1,0:T(8,128)(2,1)S(1)} %shard_map.122.block_ref, bf16[6144,768]{1,0:T(8,128)(2,1)} %from_ref.3), custom_call_target="tpu_custom_call" | custom-call | bytes 6000000 | tf_op jit(solution)/shard_map/pallas_call | solution.py:458
  38.4 0.0 copy-start.3
  38.4 1.4 %collective-permute-done.5 = bf16[48,256]{1,0:T(8,128)(2,1)S(1)} collective-permute-done((bf16[48,256]{1,0:T(8,128)(2,1)S(1)}, bf16[48,256]{1,0:T(8,128)(2,1)S(1)}, u32[]{:S(2)}, u32[]{:S(2)}) %collective-permute-start.5) | collective-permute-done | bytes 24608 | tf_op jit(solution)/shard_map/ppermute | solution.py:29
  39.9 0.6 %collective-permute-start.8 = (bf16[2,48,256]{2,1,0:T(8,128)(2,1)S(1)}, bf16[2,48,256]{2,1,0:T(8,128)(2,1)S(1)}, u32[]{:S(2)}, u32[]{:S(2)}) collective-permute-start(bf16[2,48,256]{2,1,0:T(8,128)(2,1)S(1)} %pad_maximum_fusion.1.block_ref), channel_id=1, source_target_pairs={{0,12},{1,13},{2,14},{3,15},{4,8},{5,9},{6,10},{7,11},{8,4},{9,5},... | collective-permute-start | bytes 147464 | tf_op jit(solution)/shard_map/ppermute | solution.py:29
  40.5 0.6 %collective-permute-start.7 = (bf16[2,48,256]{2,1,0:T(8,128)(2,1)S(1)}, bf16[2,48,256]{2,1,0:T(8,128)(2,1)S(1)}, u32[]{:S(2)}, u32[]{:S(2)}) collective-permute-start(bf16[2,48,256]{2,1,0:T(8,128)(2,1)S(1)} %pad_maximum_fusion.1.block_ref), channel_id=1, source_target_pairs={{0,8},{1,9},{2,10},{3,11},{4,12},{5,13},{6,14},{7,15},{8,0},{9,1},... | collective-permute-start | bytes 147464 | tf_op jit(solution)/shard_map/ppermute | solution.py:29
  41.1 3.2 %collective-permute-start.6 = (bf16[2,48,256]{2,1,0:T(8,128)(2,1)S(1)}, bf16[2,48,256]{2,1,0:T(8,128)(2,1)S(1)}, u32[]{:S(2)}, u32[]{:S(2)}) collective-permute-start(bf16[2,48,256]{2,1,0:T(8,128)(2,1)S(1)} %pad_maximum_fusion.1.block_ref), channel_id=1, source_target_pairs={{0,4},{1,5},{2,6},{3,7},{4,0},{5,1},{6,2},{7,3},{8,12},{9,13},{10,... | collective-permute-start | bytes 147464 | tf_op jit(solution)/shard_map/ppermute | solution.py:29
  44.3 2.3 %shard_map.124 = (bf16[2,48,256]{2,1,0:T(8,128)(2,1)S(1)}, bf16[3072,768]{1,0:T(8,128)(2,1)S(1)}) custom-call(bf16[2,48,256]{2,1,0:T(8,128)(2,1)S(1)} %pad_maximum_fusion.1.block_ref, bf16[6144,768]{1,0:T(8,128)(2,1)} %from_ref.3), custom_call_target="tpu_custom_call" | custom-call | bytes 6000000 | tf_op jit(solution)/shard_map/pallas_call | solution.py:458
  46.7 0.1 collective-permute-start.9
  46.8 1.4 %collective-permute-done.9.other_ref = bf16[8,48,256]{2,1,0:T(8,128)(2,1)S(1)} collective-permute-done((bf16[8,48,256]{2,1,0:T(8,128)(2,1)S(1)}, bf16[8,48,256]{2,1,0:T(8,128)(2,1)S(1)}, u32[]{:S(2)}, u32[]{:S(2)}) %collective-permute-start.9) | collective-permute-done | bytes 196640 | tf_op jit(solution)/shard_map/ppermute | solution.py:29
  48.2 2.4 %shard_map.125 = bf16[2,16,768]{2,1,0:T(8,128)(2,1)} custom-call(s32[1]{0:T(128)} %bitcast.rest_0_.me_ref, bf16[8,48,256]{2,1,0:T(8,128)(2,1)S(1)} %constant_dynamic-update-slice_fusion.5.mine_ref, bf16[8,48,256]{2,1,0:T(8,128)(2,1)S(1)} %collective-permute-done.9.other_ref, bf16[2,16,768]{2,1,0:T(8,128)(2,1)S(1)} %copy-done.3, ...), custom_call_target="tpu_custom_call" | custom-call | tf_op jit(solution)/shard_map/pallas_call | solution.py:485
  (24 shorter events, 0.1 us)
Async XLA Ops:
  0.0 8.8 %collective-permute-start.2 = (bf16[32,768]{1,0:T(8,128)(2,1)}, bf16[32,768]{1,0:T(8,128)(2,1)S(1)}, u32[]{:S(2)}, u32[]{:S(2)}) collective-permute-start(bf16[32,768]{1,0:T(8,128)(2,1)} %bitcast.15), channel_id=1, source_target_pairs={{0,12},{1,13},{2,14},{3,15},{4,8},{5,9},{6,10},{7,11},{8,4},{9,5},... | collective-permute-start | bytes 147464 | tf_op jit(solution)/shard_map/ppermute | solution.py:29
  5.0 5.2 %collective-permute-start.1 = (bf16[32,768]{1,0:T(8,128)(2,1)}, bf16[32,768]{1,0:T(8,128)(2,1)S(1)}, u32[]{:S(2)}, u32[]{:S(2)}) collective-permute-start(bf16[32,768]{1,0:T(8,128)(2,1)} %bitcast.16), channel_id=1, source_target_pairs={{0,8},{1,9},{2,10},{3,11},{4,12},{5,13},{6,14},{7,15},{8,0},{9,1},... | collective-permute-start | bytes 147464 | tf_op jit(solution)/shard_map/ppermute | solution.py:29
  5.1 5.2 %collective-permute-start = (bf16[32,768]{1,0:T(8,128)(2,1)}, bf16[32,768]{1,0:T(8,128)(2,1)S(1)}, u32[]{:S(2)}, u32[]{:S(2)}) collective-permute-start(bf16[32,768]{1,0:T(8,128)(2,1)} %bitcast.17), channel_id=1, source_target_pairs={{0,4},{1,5},{2,6},{3,7},{4,0},{5,1},{6,2},{7,3},{8,12},{9,13},{10,... | collective-permute-start | bytes 147464 | tf_op jit(solution)/shard_map/ppermute | solution.py:29
  10.3 6.8 %collective-permute-start.3 = (bf16[4,32,768]{2,1,0:T(8,128)(2,1)S(1)}, bf16[4,32,768]{2,1,0:T(8,128)(2,1)S(1)}, u32[]{:S(2)}, u32[]{:S(2)}) collective-permute-start(bf16[4,32,768]{2,1,0:T(8,128)(2,1)S(1)} %pad_maximum_fusion.rest_0_), channel_id=1, source_target_pairs={{0,2},{1,3},{2,0},{3,1},{4,6},{5,7},{6,4},{7,5},{8,10},{9,11},{10,... | collective-permute-start | bytes 589832 | tf_op jit(solution)/shard_map/ppermute | solution.py:29
  17.1 1.8 %collective-permute-start.4 = (bf16[8,32,768]{2,1,0:T(8,128)(2,1)S(1)}, bf16[8,32,768]{2,1,0:T(8,128)(2,1)S(1)}, u32[]{:S(2)}, u32[]{:S(2)}) collective-permute-start(bf16[8,32,768]{2,1,0:T(8,128)(2,1)S(1)} %constant_dynamic-update-slice_fusion.mine_ref), channel_id=1, source_target_pairs={{0,1},{1,0},{2,3},{3,2},{4,5},{5,4},{6,7},{7,6},{8,9},{9,8},{10,11... | collective-permute-start | bytes 1179656 | tf_op jit(solution)/shard_map/ppermute | solution.py:29
  18.9 15.9 %copy-start = (bf16[6,16,6144]{2,1,0:T(8,128)(2,1)S(1)}, bf16[6,16,6144]{2,1,0:T(8,128)(2,1)}, u32[]{:S(2)}) copy-start(bf16[6,16,6144]{2,1,0:T(8,128)(2,1)} %values_ref.1) | copy-start | bytes 3538948
  18.9 15.9 %copy-start.1 = (bf16[6,16,3072]{2,1,0:T(8,128)(2,1)S(1)}, bf16[6,16,3072]{2,1,0:T(8,128)(2,1)}, u32[]{:S(2)}) copy-start(bf16[6,16,3072]{2,1,0:T(8,128)(2,1)} %keys_one_ref.1) | copy-start | bytes 1769476
  18.9 15.9 %copy-start.2 = (bf16[6,16,3072]{2,1,0:T(8,128)(2,1)S(1)}, bf16[6,16,3072]{2,1,0:T(8,128)(2,1)}, u32[]{:S(2)}) copy-start(bf16[6,16,3072]{2,1,0:T(8,128)(2,1)} %keys_two_ref.1) | copy-start | bytes 1769476
  36.0 3.9 %collective-permute-start.5 = (bf16[48,256]{1,0:T(8,128)(2,1)S(1)}, bf16[48,256]{1,0:T(8,128)(2,1)S(1)}, u32[]{:S(2)}, u32[]{:S(2)}) collective-permute-start(bf16[48,256]{1,0:T(8,128)(2,1)S(1)} %shard_map.122.block_ref), channel_id=1, source_target_pairs={{0,2},{1,3},{2,0},{3,1},{4,6},{5,7},{6,4},{7,5},{8,10},{9,11},{10,... | collective-permute-start | bytes 73736 | tf_op jit(solution)/shard_map/ppermute | solution.py:29
  38.4 9.8 %copy-start.3 = (bf16[2,16,768]{2,1,0:T(8,128)(2,1)S(1)}, bf16[2,16,768]{2,1,0:T(8,128)(2,1)}, u32[]{:S(2)}) copy-start(bf16[2,16,768]{2,1,0:T(8,128)(2,1)} %inputs_ref.1) | copy-start | bytes 147460
  39.9 6.7 %collective-permute-start.8 = (bf16[2,48,256]{2,1,0:T(8,128)(2,1)S(1)}, bf16[2,48,256]{2,1,0:T(8,128)(2,1)S(1)}, u32[]{:S(2)}, u32[]{:S(2)}) collective-permute-start(bf16[2,48,256]{2,1,0:T(8,128)(2,1)S(1)} %pad_maximum_fusion.1.block_ref), channel_id=1, source_target_pairs={{0,12},{1,13},{2,14},{3,15},{4,8},{5,9},{6,10},{7,11},{8,4},{9,5},... | collective-permute-start | bytes 147464 | tf_op jit(solution)/shard_map/ppermute | solution.py:29
  40.5 6.1 %collective-permute-start.7 = (bf16[2,48,256]{2,1,0:T(8,128)(2,1)S(1)}, bf16[2,48,256]{2,1,0:T(8,128)(2,1)S(1)}, u32[]{:S(2)}, u32[]{:S(2)}) collective-permute-start(bf16[2,48,256]{2,1,0:T(8,128)(2,1)S(1)} %pad_maximum_fusion.1.block_ref), channel_id=1, source_target_pairs={{0,8},{1,9},{2,10},{3,11},{4,12},{5,13},{6,14},{7,15},{8,0},{9,1},... | collective-permute-start | bytes 147464 | tf_op jit(solution)/shard_map/ppermute | solution.py:29
  41.1 5.5 %collective-permute-start.6 = (bf16[2,48,256]{2,1,0:T(8,128)(2,1)S(1)}, bf16[2,48,256]{2,1,0:T(8,128)(2,1)S(1)}, u32[]{:S(2)}, u32[]{:S(2)}) collective-permute-start(bf16[2,48,256]{2,1,0:T(8,128)(2,1)S(1)} %pad_maximum_fusion.1.block_ref), channel_id=1, source_target_pairs={{0,4},{1,5},{2,6},{3,7},{4,0},{5,1},{6,2},{7,3},{8,12},{9,13},{10,... | collective-permute-start | bytes 147464 | tf_op jit(solution)/shard_map/ppermute | solution.py:29
  46.7 1.5 %collective-permute-start.9 = (bf16[8,48,256]{2,1,0:T(8,128)(2,1)S(1)}, bf16[8,48,256]{2,1,0:T(8,128)(2,1)S(1)}, u32[]{:S(2)}, u32[]{:S(2)}) collective-permute-start(bf16[8,48,256]{2,1,0:T(8,128)(2,1)S(1)} %constant_dynamic-update-slice_fusion.5.mine_ref), channel_id=1, source_target_pairs={{0,1},{1,0},{2,3},{3,2},{4,5},{5,4},{6,7},{7,6},{8,9},{9,8},{10,11... | collective-permute-start | bytes 589832 | tf_op jit(solution)/shard_map/ppermute | solution.py:29
